TPU v7x, 32 devices: a whole 2x2x4 slice. The times are simulated.
32 devices in a mesh: dp: 8 (over z, y), tensor: 4 (over x, core).
Axes of the slice: x: 2, y: 2, z: 4, core: 2. Of those that a mesh axis runs over, the one named last changes fastest.
Arguments:
- tokens: bfloat16 [3072, 8, 768], P(None, 'dp'), may hold values from -6 to 6
- cotangent: bfloat16 [3072, 8, 768], P(None, 'dp'), may hold values from -6 to 6
- lengths: int32 [16], replicated, may hold values from 1024 to 2048, as said below
- dealing: int32 [16], replicated, may hold values from 0 to 15, as said below
- w_qkv: bfloat16 [768, 3, 768], P(None, None, 'tensor'), may hold values from -0.3125 to 0.3125
- w_out: bfloat16 [768, 768], P(None, 'tensor'), may hold values from -0.875 to 0.875
- w_gu: bfloat16 [768, 2, 3072], P(None, None, 'tensor'), may hold values from -0.21875 to 0.21875
- w_down: bfloat16 [768, 3072], P(None, 'tensor'), may hold values from -0.15625 to 0.15625
- gains: float32 [768, 2], replicated, may hold values from 0.25 to 1.75
- shifts: float32 [768, 2], replicated, may hold values from -1.8 to 1.8
Outputs:
- result: bfloat16 [3072, 8, 768], P(None, 'dp')
- input_grad: bfloat16 [3072, 8, 768], P(None, 'dp')
- grad_qkv: float32 [768, 3, 768], P('dp', None, 'tensor')
- grad_out: float32 [768, 768], P('dp', 'tensor')
- grad_gu: float32 [768, 2, 3072], P('dp', None, 'tensor')
- grad_down: float32 [768, 3072], P('dp', 'tensor')
- grad_gains: float32 [768, 2], P(('dp', 'tensor'))
- grad_shifts: float32 [768, 2], P(('dp', 'tensor'))
Inputs may be any that keep to these rules, and one draw needn't show every extreme that they name: Group g's two sequences, dealing[2g] and dealing[2g+1], have lengths adding to 3072; some group holds one of 2048 and one of 1024. `dealing`: a permutation of the sequences.
All inputs are finite; a program needn't handle non-finite values.
Results may differ from a plain program's by a relative error of at most 0.025.
The roundings to bfloat16 on the way count: a program that leaves them out, or rounds other values in their place, can miss the bound.
Values may be sent and summed in bfloat16 or wider, within the bound.
A program may use at most 192 MiB of HBM per device.

v0:
```python
import jax
import jax.numpy as jnp
from jax import lax
from jax.sharding import PartitionSpec as P

HEAD = 64


EPSILON = 1e-05
NEGATIVE = -1000000000.0


def rope_tables(positions):
    half_width = HEAD // 2
    frequency = 1000.0 ** (-(jnp.arange(half_width, dtype=jnp.float32) * 2.0) / HEAD)
    angles = positions.astype(jnp.float32)[:, None] * frequency[None, :]
    return (jnp.cos(angles)[:, None, :], jnp.sin(angles)[:, None, :])


def rotate(head_rows, cosine_table, sine_table):
    half_width = head_rows.shape[-1] // 2
    first_half = head_rows[..., :half_width]
    second_half = head_rows[..., half_width:]
    return jnp.concatenate(
        [
            first_half * cosine_table - second_half * sine_table,
            second_half * cosine_table + first_half * sine_table,
        ],
        -1,
    )


def unrotate(grad_rows, cosine_table, sine_table):
    half_width = grad_rows.shape[-1] // 2
    first_half = grad_rows[..., :half_width]
    second_half = grad_rows[..., half_width:]
    return jnp.concatenate(
        [
            first_half * cosine_table + second_half * sine_table,
            second_half * cosine_table - first_half * sine_table,
        ],
        -1,
    )


def norm_forward(resid_rows, gain_vec, shift_vec):
    row_mean = jnp.mean(resid_rows, -1, keepdims=True)
    centred = resid_rows - row_mean
    inverse = lax.rsqrt(jnp.mean(centred * centred, -1, keepdims=True) + EPSILON)
    unit_rows = centred * inverse
    return (unit_rows * gain_vec + shift_vec, unit_rows, inverse)


def norm_backward(upstream, unit_rows, inverse, gain_vec):
    scaled = upstream * gain_vec
    inner_term = (
        scaled
        - jnp.mean(scaled, -1, keepdims=True)
        - unit_rows * jnp.mean(scaled * unit_rows, -1, keepdims=True)
    )
    return (inner_term * inverse, jnp.sum(upstream * unit_rows, 0), jnp.sum(upstream, 0))


def slot_spans(offsets, lengths, seq_ids, source, groups):
    seq_start = offsets[seq_ids]
    seq_stop = seq_start + lengths[seq_ids]
    low_row = (seq_start - source + groups - 1) // groups
    high_row = (seq_stop - source + groups - 1) // groups
    return (low_row, high_row - low_row)


def local(tokens, cotangent, lengths, dealing, w_qkv, w_out, w_gu, w_down, gains, shifts):
    groups = lax.axis_size("dp")
    member = lax.axis_index("dp")
    tensor_size = lax.axis_size("tensor")
    tensor_id = lax.axis_index("tensor")
    local_tok = tokens.shape[0]
    model_width = tokens.shape[2]
    seq_count = lengths.shape[0]
    slot_count = local_tok // groups + 2
    offsets = jnp.cumsum(lengths) - lengths
    dealt_pairs = dealing.reshape(groups, 2)
    slot_grid = jnp.arange(slot_count, dtype=jnp.int32)[None, :]
    low_first, count_first = slot_spans(offsets, lengths, dealt_pairs[:, 0], member, groups)
    low_second, count_second = slot_spans(offsets, lengths, dealt_pairs[:, 1], member, groups)
    rows_out = jnp.where(
        slot_grid < count_first[:, None],
        low_first[:, None] + slot_grid,
        low_second[:, None] + slot_grid - count_first[:, None],
    )
    live_out = (slot_grid < (count_first + count_second)[:, None])[..., None]
    rows_out = jnp.clip(rows_out, 0, local_tok - 1)
    flat_in = tokens.reshape(local_tok, model_width)
    flat_cot = cotangent.reshape(local_tok, model_width)
    send_in = jnp.where(live_out, jnp.take(flat_in, rows_out, axis=0), jnp.zeros((), jnp.bfloat16))
    send_cot = jnp.where(
        live_out, jnp.take(flat_cot, rows_out, axis=0), jnp.zeros((), jnp.bfloat16)
    )
    recv_in, recv_cot = (
        lax.all_to_all(send_in, "dp", split_axis=0, concat_axis=0, tiled=True),
        lax.all_to_all(send_cot, "dp", split_axis=0, concat_axis=0, tiled=True),
    )
    mine_first = dealing[2 * member]
    mine_second = dealing[2 * member + 1]
    sources = jnp.arange(groups, dtype=jnp.int32)
    rlow_first, rcount_first = slot_spans(offsets, lengths, mine_first, sources, groups)
    rlow_second, rcount_second = slot_spans(offsets, lengths, mine_second, sources, groups)
    in_first = slot_grid < rcount_first[:, None]
    in_any = slot_grid < (rcount_first + rcount_second)[:, None]
    local_rows = jnp.where(
        in_first,
        rlow_first[:, None] + slot_grid,
        rlow_second[:, None] + slot_grid - rcount_first[:, None],
    )
    token_ids = local_rows * groups + sources[:, None]
    segment_grid = jnp.where(in_first, 0, jnp.where(in_any, 1, -1)).astype(jnp.int32)
    position_grid = jnp.where(
        in_first, token_ids - offsets[mine_first], token_ids - offsets[mine_second]
    )
    position_grid = jnp.where(in_any, position_grid, 0)
    received = groups * slot_count
    padded = (local_tok + 511) // 512 * 512
    block_rows = min(512, padded)
    live_count = rcount_first + rcount_second
    live_start = jnp.cumsum(live_count) - live_count
    compact_ids = jnp.arange(padded, dtype=jnp.int32)
    source_of = jnp.sum((live_start[None, :] <= compact_ids[:, None]).astype(jnp.int32), 1) - 1
    slot_of = compact_ids - live_start[source_of]
    pick_rows = jnp.clip(source_of * slot_count + slot_of, 0, received - 1)
    real_row = compact_ids < local_tok
    x_rows = jnp.where(
        real_row[:, None],
        jnp.take(recv_in.reshape(received, model_width), pick_rows, axis=0),
        jnp.zeros((), jnp.bfloat16),
    )
    cot_rows = jnp.where(
        real_row[:, None],
        jnp.take(recv_cot.reshape(received, model_width), pick_rows, axis=0),
        jnp.zeros((), jnp.bfloat16),
    )
    segment = jnp.where(real_row, jnp.take(segment_grid.reshape(received), pick_rows), -1)
    positions = jnp.where(real_row, jnp.take(position_grid.reshape(received), pick_rows), 0)
    share_rows = padded // tensor_size
    first_row = tensor_id * share_rows
    local_width = w_qkv.shape[2]
    heads_here = local_width // HEAD
    score_scale = HEAD ** (-0.5)
    blocks = padded // block_rows
    cosine_table, sine_table = rope_tables(positions)
    projected = jnp.einsum("rd,dcn->rcn", x_rows, w_qkv, preferred_element_type=jnp.float32)
    query_rot = rotate(
        projected[:, 0].reshape(padded, heads_here, HEAD), cosine_table, sine_table
    ).astype(jnp.bfloat16)
    keys_rot = rotate(
        projected[:, 1].reshape(padded, heads_here, HEAD), cosine_table, sine_table
    ).astype(jnp.bfloat16)
    values_all = projected[:, 2].reshape(padded, heads_here, HEAD).astype(jnp.bfloat16)

    def block_scores(block_index):
        row_start = block_index * block_rows
        query_block = lax.dynamic_slice_in_dim(query_rot, row_start, block_rows, 0)
        segment_block = lax.dynamic_slice_in_dim(segment, row_start, block_rows, 0)
        scores = (
            jnp.einsum("qhe,khe->hqk", query_block, keys_rot, preferred_element_type=jnp.float32)
            * score_scale
        )
        same_seq = (segment_block[:, None] == segment[None, :])[None]
        return (jnp.where(same_seq, scores, NEGATIVE), query_block, row_start)

    def attend(block_index):
        scores, query_block, row_start = block_scores(block_index)
        row_max = jnp.max(scores, -1, keepdims=True)
        weights = jnp.exp(scores - row_max)
        row_total = jnp.sum(weights, -1, keepdims=True)
        soft_weights = (weights / row_total).astype(jnp.bfloat16)
        block_out = jnp.einsum(
            "hqk,khe->qhe", soft_weights, values_all, preferred_element_type=jnp.float32
        )
        return (block_out.astype(jnp.bfloat16), (row_max + jnp.log(row_total))[..., 0])

    block_outs, log_totals = lax.map(attend, jnp.arange(blocks, dtype=jnp.int32))
    attn_out = block_outs.reshape(padded, local_width)
    row_piece = attn_out
    attn_branch = lax.psum_scatter(
        lax.dot_general(
            row_piece, w_out, (((1,), (1,)), ((), ())), preferred_element_type=jnp.float32
        ).astype(jnp.bfloat16),
        "tensor",
        scatter_dimension=0,
        tiled=True,
    ).astype(jnp.float32)
    x_share = lax.dynamic_slice_in_dim(x_rows, first_row, share_rows, 0).astype(jnp.float32)
    normed_one, unit_one, inverse_one = norm_forward(
        x_share + attn_branch, gains[:, 0], shifts[:, 0]
    )
    normed_full = lax.all_gather(normed_one.astype(jnp.bfloat16), "tensor", axis=0, tiled=True)
    gate_up = jnp.einsum("rd,dcf->rcf", normed_full, w_gu, preferred_element_type=jnp.float32)
    gate_act = gate_up[:, 0]
    up_act = gate_up[:, 1]
    sigmoid_gate = jax.nn.sigmoid(gate_act)
    swish_gate = gate_act * sigmoid_gate
    hidden = (swish_gate * up_act).astype(jnp.bfloat16)
    row_piece = hidden
    mlp_branch = lax.psum_scatter(
        lax.dot_general(
            row_piece, w_down, (((1,), (1,)), ((), ())), preferred_element_type=jnp.float32
        ).astype(jnp.bfloat16),
        "tensor",
        scatter_dimension=0,
        tiled=True,
    ).astype(jnp.float32)
    result_share, unit_two, inverse_two = norm_forward(
        normed_one + mlp_branch, gains[:, 1], shifts[:, 1]
    )
    cot_share = lax.dynamic_slice_in_dim(cot_rows, first_row, share_rows, 0).astype(jnp.float32)
    grad_two, gain_two, shift_two = norm_backward(cot_share, unit_two, inverse_two, gains[:, 1])
    grad_mlp_full = lax.all_gather(grad_two.astype(jnp.bfloat16), "tensor", axis=0, tiled=True)
    grad_hidden = jnp.dot(grad_mlp_full, w_down, preferred_element_type=jnp.float32)
    grad_gate = grad_hidden * up_act * sigmoid_gate * (1.0 + gate_act * (1.0 - sigmoid_gate))
    grad_up = grad_hidden * swish_gate
    grad_gu = jnp.stack([grad_gate, grad_up], 1).astype(jnp.bfloat16)
    row_piece = grad_gu
    back_normed = lax.psum_scatter(
        jnp.einsum("rcf,dcf->rd", row_piece, w_gu, preferred_element_type=jnp.float32).astype(
            jnp.bfloat16
        ),
        "tensor",
        scatter_dimension=0,
        tiled=True,
    ).astype(jnp.float32)
    d_w_gu = jnp.einsum("rd,rcf->dcf", normed_full, grad_gu, preferred_element_type=jnp.float32)
    d_w_down = jnp.einsum("rd,rf->df", grad_mlp_full, hidden, preferred_element_type=jnp.float32)
    grad_one, gain_one, shift_one = norm_backward(
        grad_two + back_normed, unit_one, inverse_one, gains[:, 0]
    )
    grad_attn_full = lax.all_gather(grad_one.astype(jnp.bfloat16), "tensor", axis=0, tiled=True)
    grad_heads = jnp.dot(grad_attn_full, w_out, preferred_element_type=jnp.float32).astype(
        jnp.bfloat16
    )
    grad_heads = grad_heads.reshape(padded, heads_here, HEAD)
    d_w_out = jnp.einsum("rd,rn->dn", grad_attn_full, attn_out, preferred_element_type=jnp.float32)

    def attend_back(carried, block_index):
        grad_keys, grad_values = carried
        scores, query_block, row_start = block_scores(block_index)
        grad_block = lax.dynamic_slice_in_dim(grad_heads, row_start, block_rows, 0)
        soft_exact = jnp.exp(scores - log_totals[block_index][..., None])
        grad_soft = jnp.einsum(
            "qhe,khe->hqk", grad_block, values_all, preferred_element_type=jnp.float32
        )
        grad_scores = (
            soft_exact * (grad_soft - jnp.sum(soft_exact * grad_soft, -1, keepdims=True))
        ).astype(jnp.bfloat16)
        grad_query = (
            jnp.einsum("hqk,khe->qhe", grad_scores, keys_rot, preferred_element_type=jnp.float32)
            * score_scale
        )
        grad_keys = (
            grad_keys
            + jnp.einsum(
                "hqk,qhe->khe", grad_scores, query_block, preferred_element_type=jnp.float32
            )
            * score_scale
        )
        grad_values = grad_values + jnp.einsum(
            "hqk,qhe->khe",
            soft_exact.astype(jnp.bfloat16),
            grad_block,
            preferred_element_type=jnp.float32,
        )
        return ((grad_keys, grad_values), grad_query)

    zero_heads = jnp.zeros((padded, heads_here, HEAD), jnp.float32)
    (grad_keys, grad_values), grad_queries = lax.scan(
        attend_back, (zero_heads, zero_heads), jnp.arange(blocks, dtype=jnp.int32)
    )
    grad_queries = grad_queries.reshape(padded, heads_here, HEAD)
    grad_proj = jnp.stack(
        [
            unrotate(grad_queries, cosine_table, sine_table).reshape(padded, local_width),
            unrotate(grad_keys, cosine_table, sine_table).reshape(padded, local_width),
            grad_values.reshape(padded, local_width),
        ],
        1,
    ).astype(jnp.bfloat16)
    row_piece = grad_proj
    back_inputs = lax.psum_scatter(
        jnp.einsum("rcn,dcn->rd", row_piece, w_qkv, preferred_element_type=jnp.float32).astype(
            jnp.bfloat16
        ),
        "tensor",
        scatter_dimension=0,
        tiled=True,
    ).astype(jnp.float32)
    grad_input_share = (grad_one + back_inputs).astype(jnp.bfloat16)
    d_w_qkv = jnp.einsum("rd,rcn->dcn", x_rows, grad_proj, preferred_element_type=jnp.float32)
    gain_grads = jnp.stack([gain_one, gain_two], 1)
    shift_grads = jnp.stack([shift_one, shift_two], 1)
    gain_sum, shift_sum = (
        lax.psum_scatter(gain_grads, ("dp", "tensor"), scatter_dimension=0, tiled=True),
        lax.psum_scatter(shift_grads, ("dp", "tensor"), scatter_dimension=0, tiled=True),
    )
    qkv_sum, out_sum, gu_sum, down_sum = (
        lax.psum_scatter(d_w_qkv, "dp", scatter_dimension=0, tiled=True),
        lax.psum_scatter(d_w_out, "dp", scatter_dimension=0, tiled=True),
        lax.psum_scatter(d_w_gu, "dp", scatter_dimension=0, tiled=True),
        lax.psum_scatter(d_w_down, "dp", scatter_dimension=0, tiled=True),
    )
    result_full, input_full = (
        lax.all_gather(result_share.astype(jnp.bfloat16), "tensor", axis=0, tiled=True),
        lax.all_gather(grad_input_share, "tensor", axis=0, tiled=True),
    )
    back_pick = jnp.clip(live_start[:, None] + slot_grid, 0, padded - 1).reshape(received)
    back_live = (slot_grid < live_count[:, None])[..., None]
    back_result = jnp.where(
        back_live,
        jnp.take(result_full, back_pick, axis=0).reshape(groups, slot_count, model_width),
        jnp.zeros((), jnp.bfloat16),
    )
    back_input = jnp.where(
        back_live,
        jnp.take(input_full, back_pick, axis=0).reshape(groups, slot_count, model_width),
        jnp.zeros((), jnp.bfloat16),
    )
    home_result, home_input = (
        lax.all_to_all(back_result, "dp", split_axis=0, concat_axis=0, tiled=True),
        lax.all_to_all(back_input, "dp", split_axis=0, concat_axis=0, tiled=True),
    )
    arrival_rows = jnp.arange(local_tok, dtype=jnp.int32)
    arrival_ids = arrival_rows * groups + member
    seq_of = jnp.sum((offsets[None, :] <= arrival_ids[:, None]).astype(jnp.int32), 1) - 1
    seq_range = jnp.arange(seq_count, dtype=jnp.int32)
    dealt_place = jnp.sum(jnp.where(dealing[None, :] == seq_of[:, None], seq_range[None, :], 0), 1)
    owner_group = dealt_place // 2
    is_second = dealt_place % 2
    seq_low = (offsets[seq_of] - member + groups - 1) // groups
    owner_low, owner_count = slot_spans(offsets, lengths, dealing[2 * owner_group], member, groups)
    slot_ids = arrival_rows - seq_low + is_second * owner_count
    flat_slots = owner_group * slot_count + slot_ids
    result = jnp.take(home_result.reshape(groups * slot_count, model_width), flat_slots, axis=0)
    input_grad = jnp.take(home_input.reshape(groups * slot_count, model_width), flat_slots, axis=0)
    return (
        result.reshape(local_tok, 1, model_width),
        input_grad.reshape(local_tok, 1, model_width),
        qkv_sum,
        out_sum,
        gu_sum,
        down_sum,
        gain_sum,
        shift_sum,
    )


def solution(mesh):
    placed = (
        P(None, "dp", None),
        P(None, "dp", None),
        P(),
        P(),
        P(None, None, "tensor"),
        P(None, "tensor"),
        P(None, None, "tensor"),
        P(None, "tensor"),
        P(),
        P(),
    )
    return jax.shard_map(
        local,
        mesh=mesh,
        in_specs=placed,
        out_specs=(
            P(None, "dp", None),
            P(None, "dp", None),
            P("dp", None, "tensor"),
            P("dp", "tensor"),
            P("dp", None, "tensor"),
            P("dp", "tensor"),
            P(("dp", "tensor"), None),
            P(("dp", "tensor"), None),
        ),
        check_vma=False,
    )
```

profile of v0, /device:TPU:0, one launch (start us, length us, event | category | flops | bytes accessed | tf_op | source)
XLA Modules:
  0.0 1852.5 jit_solution(3296396813574628752)
XLA Ops:
  28.1 15.8 gather_fusion.10
  48.5 15.8 gather_fusion.4
  94.2 17.4 gather_fusion.7
  111.6 17.4 gather_fusion.6
  131.2 59.6 %all-to-all-done = bf16[8,386,768]{2,1,0:T(8,128)(2,1)} async-done(((bf16[8,386,768]{2,1,0:T(8,128)(2,1)}), bf16[8,386,768]{2,1,0:T(8,128)(2,1)}, u32[]{:S(2)}, u32[]{:S(2)}) %all-to-all-start) | async-done | bytes 4743200 | tf_op jit(solution)/shard_map/all_to_all | solution.py:100
  195.3 17.5 gather_fusion.5
  223.2 176.6 %while.27 = (s32[]{:T(128)}, bf16[6,512,3,64]{1,3,2,0:T(8,128)(2,1)}, f32[6,3,512]{2,1,0:T(4,128)}, s32[6]{0:T(128)S(1)}, s32[3072]{0:T(1024)S(1)}, /*index=5*/b...) while((s32[]{:T(128)}, ...), condition=%wide.region_6.10_spmd, body=%wide.region_3.9_spmd.sunk | while | flops 1266252288 | bytes 145953024 | solution.py:181
  242.2 9.9 fusion.166
  271.6 9.9 fusion.166
  301.0 9.9 fusion.166
  330.4 9.9 fusion.166
  359.8 9.9 fusion.166
  389.2 9.9 fusion.166
  409.7 44.2 %reduce-scatter.11.cloned.1.call-done = bf16[768,768]{1,0:T(8,128)(2,1)} async-done(((bf16[3072,768]{1,0:T(8,128)(2,1)}), bf16[768,768]{1,0:T(8,128)(2,1)}) %reduce-scatter.11.cloned.1.call-update) | async-done | bytes 1179664 | tf_op jit(solution)/shard_map/reduce_scatter | solution.py:184
  461.5 37.6 %all-gather.6.cloned.1.call-done = bf16[3072,768]{1,0:T(8,128)(2,1)} async-done(((bf16[768,768]{1,0:T(8,128)(2,1)}), bf16[3072,768]{1,0:T(8,128)(2,1)}) %all-gather.6.cloned.1.call-update) | async-done | bytes 4718608 | tf_op jit(solution)/shard_map/all_gather | solution.py:196
  499.1 9.7 fusion.43
  531.4 104.4 %all-to-all-done.2 = bf16[8,386,768]{2,1,0:T(8,128)(2,1)} async-done(((bf16[8,386,768]{2,1,0:T(8,128)(2,1)}), bf16[8,386,768]{2,1,0:T(8,128)(2,1)}, u32[]{:S(2)}, u32[]{:S(2)}) %all-to-all-start.2) | async-done | bytes 4743200 | tf_op jit(solution)/shard_map/all_to_all | solution.py:101
  640.4 18.3 gather_fusion.11
  668.6 35.7 %all-gather.10.cloned.1.call-done = bf16[3072,768]{1,0:T(8,128)(2,1)} async-done(((bf16[768,768]{1,0:T(8,128)(2,1)}), bf16[3072,768]{1,0:T(8,128)(2,1)}) %all-gather.10.cloned.1.call-update) | async-done | bytes 4718608 | tf_op jit(solution)/shard_map/all_gather | solution.py:217
  704.2 13.1 fusion.45
  720.9 9.1 bitcast_convert_fusion.1
  730.1 47.9 %reduce-scatter.15.cloned.1.call-done = bf16[768,768]{1,0:T(8,128)(2,1)} async-done(((bf16[3072,768]{1,0:T(8,128)(2,1)}), bf16[768,768]{1,0:T(8,128)(2,1)}) %reduce-scatter.15.cloned.1.call-update) | async-done | bytes 1179664 | tf_op jit(solution)/shard_map/reduce_scatter | solution.py:223
  786.2 37.5 %all-gather.12.cloned.1.call-done = bf16[3072,768]{1,0:T(8,128)(2,1)} async-done(((bf16[768,768]{1,0:T(8,128)(2,1)}), bf16[3072,768]{1,0:T(8,128)(2,1)}) %all-gather.12.cloned.1.call-update) | async-done | bytes 4718608 | tf_op jit(solution)/shard_map/all_gather | solution.py:236
  828.9 410.2 %while.28 = (s32[]{:T(128)}, f32[3072,3,64]{0,2,1:T(8,128)}, f32[3072,3,64]{0,2,1:T(8,128)}, f32[6,512,3,64]{1,0,3,2:T(8,128)}, s32[6]{0:T(128)S(1)}, /*index=5*...) while((s32[]{:T(128)}, f32[3072,3,64]{0,2,1:T(8,128)}, ...), condition=%wide.region_22.27_spmd.clone, body=%wide.region_20.26_spmd.clone.sunk | while | flops 3095296512 | bytes 258011472 | solution.py:274
  852.0 14.4 multiply_reduce_fusion.7
  866.3 13.8 multiply_convert_fusion.5
  887.7 8.9 dynamic_update_slice.20
  911.5 8.8 fusion.178
  920.4 14.3 multiply_reduce_fusion.7
  934.7 13.8 multiply_convert_fusion.5
  956.1 8.9 dynamic_update_slice.20
  979.9 8.8 fusion.178
  988.8 14.4 multiply_reduce_fusion.7
  1003.2 13.8 multiply_convert_fusion.5
  1024.5 8.9 dynamic_update_slice.20
  1048.4 8.8 fusion.178
  1057.2 14.4 multiply_reduce_fusion.7
  1071.6 13.8 multiply_convert_fusion.5
  1092.9 8.9 dynamic_update_slice.20
  1116.8 8.8 fusion.178
  1125.6 14.3 multiply_reduce_fusion.7
  1140.0 13.8 multiply_convert_fusion.5
  1161.3 8.9 dynamic_update_slice.20
  1185.2 8.8 fusion.178
  1194.0 14.3 multiply_reduce_fusion.7
  1208.4 13.8 multiply_convert_fusion.5
  1229.7 8.9 dynamic_update_slice.20
  1256.1 47.2 %reduce-scatter.17.cloned.1.call-done = bf16[768,768]{1,0:T(8,128)(2,1)} async-done(((bf16[3072,768]{1,0:T(8,128)(2,1)}), bf16[768,768]{1,0:T(8,128)(2,1)}) %reduce-scatter.17.cloned.1.call-update) | async-done | bytes 1179664 | tf_op jit(solution)/shard_map/reduce_scatter | solution.py:287
  1307.4 13.2 fusion.37
  1320.6 21.7 %all-gather.8.cloned.1.call-done = bf16[3072,768]{1,0:T(8,128)(2,1)} async-done(((bf16[768,768]{1,0:T(8,128)(2,1)}), bf16[3072,768]{1,0:T(8,128)(2,1)}) %all-gather.8.cloned.1.call-update) | async-done | bytes 4718608 | tf_op jit(solution)/shard_map/all_gather | solution.py:310
  1342.3 15.8 gather_fusion.8
  1358.1 23.2 %all-gather.14.cloned.1.call-done = bf16[3072,768]{1,0:T(8,128)(2,1)} async-done(((bf16[768,768]{1,0:T(8,128)(2,1)}), bf16[3072,768]{1,0:T(8,128)(2,1)}) %all-gather.14.cloned.1.call-update) | async-done | bytes 4718608 | tf_op jit(solution)/shard_map/all_gather | solution.py:311
  1381.4 15.8 gather_fusion.12
  1397.2 9.0 broadcast_select_fusion.2
  1415.4 8.5 broadcast_select_fusion
  1429.5 9.2 fusion.121
  1438.8 117.3 %all-to-all-done.3 = bf16[8,386,768]{2,1,0:T(8,128)(2,1)} async-done(((bf16[8,386,768]{2,1,0:T(8,128)(2,1)}), bf16[8,386,768]{2,1,0:T(8,128)(2,1)}, u32[]{:S(2)}, u32[]{:S(2)}) %all-to-all-start.3) | async-done | bytes 4743200 | tf_op jit(solution)/shard_map/all_to_all | solution.py:327
  1594.1 10.9 compare_and_fusion.2
  1607.6 99.6 %all-reduce.2 = (f32[768,2]{0,1:T(2,128)S(1)}, f32[768,2]{0,1:T(2,128)S(1)}) all-reduce(f32[768,2]{0,1:T(2,128)S(1)} %pad_maximum_fusion.12, f32[768,2]{0,1:T(2,128)S(1)} %pad_maximum_fusion.13), channel_id=10, replica_groups=mesh['dp'=8,'tensor'=4] {'dp','tensor'}, use_global_device_ids=true, to_apply=%region_30.35.clone | all-reduce | flops 3072 | bytes 24576
  1712.9 17.5 gather_fusion.13
  1734.9 17.5 gather_fusion.9
  1752.5 8.7 select_bitcast_fusion
  1761.2 12.2 reduce-scatter.21.cloned.1.call-done
  1773.4 72.4 %reduce-scatter.19.cloned.1.call-done = f32[96,3,192]{2,0,1:T(8,128)} async-done(((f32[768,3,192]{2,0,1:T(8,128)}), f32[96,3,192]{2,0,1:T(8,128)}) %reduce-scatter.19.cloned.1.call-update) | async-done | bytes 221200 | tf_op jit(solution)/shard_map/reduce_scatter | solution.py:304
  (410 shorter events, 463.0 us)
Async XLA Ops:
  7.2 491.9 %copy-start = (bf16[768,2,768]{2,1,0:T(2,128)(2,1)S(1)}, bf16[768,2,768]{2,1,0:T(2,128)(2,1)}, u32[]{:S(2)}) copy-start(bf16[768,2,768]{2,1,0:T(2,128)(2,1)} %param.28) | copy-start | bytes 7077892
  12.4 31.5 %copy-start.3 = (s32[16]{0:T(128)}, s32[16]{0:T(128)S(1)}, u32[]{:S(2)}) copy-start(s32[16]{0:T(128)S(1)} %sub.473) | copy-start | bytes 196
  27.8 57.0 %copy-start.45 = (s32[8]{0:T(128)}, s32[8]{0:T(128)S(1)}, u32[]{:S(2)}) copy-start(s32[8]{0:T(128)S(1)} %get-tuple-element.397) | copy-start | bytes 100
  27.8 59.9 %copy-start.35 = (s32[8]{0:T(128)}, s32[8]{0:T(128)S(1)}, u32[]{:S(2)}) copy-start(s32[8]{0:T(128)S(1)} %get-tuple-element.396) | copy-start | bytes 100
  76.9 113.9 %all-to-all-start = ((bf16[8,386,768]{2,1,0:T(8,128)(2,1)}), bf16[8,386,768]{2,1,0:T(8,128)(2,1)}, u32[]{:S(2)}, u32[]{:S(2)}) async-start(bf16[8,386,768]{2,1,0:T(8,128)(2,1)} %get-tuple-element.325), calls=%async_computation | async-start | bytes 9633792 | tf_op jit(solution)/shard_map/all_to_all | solution.py:100
  84.2 369.7 %reduce-scatter.11.cloned.1.call-start = ((), (), s32[]{:S(2)}) async-start(), calls=%async_computation.12 | async-start | bytes 5898240 | tf_op jit(solution)/shard_map/reduce_scatter | solution.py:184
  87.0 24.6 %copy-start.29 = (s32[3088]{0:T(1024)}, s32[3088]{0:T(1024)S(1)}, u32[]{:S(2)}) copy-start(s32[3088]{0:T(1024)S(1)} %lt.256) | copy-start | bytes 37060
  92.8 102.5 %copy-start.26 = (s32[3072]{0:T(1024)}, s32[3072]{0:T(1024)S(1)}, u32[]{:S(2)}) copy-start(s32[3072]{0:T(1024)S(1)} %broadcast_clamp_fusion.1) | copy-start | bytes 36868
  129.1 83.8 %copy-start.39 = (pred[3072]{0:T(1024)(128)(4,1)}, pred[3072]{0:T(1024)(128)(4,1)S(1)}, u32[]{:S(2)}) copy-start(pred[3072]{0:T(1024)(128)(4,1)S(1)} %iota_compare_fusion.4) | copy-start | bytes 9220
  129.7 83.1 %copy-start.38 = (pred[3072]{0:T(1024)(128)(4,1)}, pred[3072]{0:T(1024)(128)(4,1)S(1)}, u32[]{:S(2)}) copy-start(pred[3072]{0:T(1024)(128)(4,1)S(1)} %get-tuple-element.286) | copy-start | bytes 9220
  131.2 90.1 %copy-start.20 = (f32[3072,32]{0,1:T(8,128)}, f32[3072,32]{0,1:T(8,128)S(1)}, u32[]{:S(2)}) copy-start(f32[3072,32]{0,1:T(8,128)S(1)} %get-tuple-element.318) | copy-start | bytes 1179652
  131.2 90.1 %copy-start.22 = (f32[3072,32]{0,1:T(8,128)}, f32[3072,32]{0,1:T(8,128)S(1)}, u32[]{:S(2)}) copy-start(f32[3072,32]{0,1:T(8,128)S(1)} %get-tuple-element.319) | copy-start | bytes 1179652
  230.6 6.5 copy-start.8
  237.1 5.2 copy-start.9
  260.0 6.5 copy-start.8
  266.5 5.2 copy-start.9
  289.4 6.5 copy-start.8
  295.9 5.2 copy-start.9
  318.8 6.5 copy-start.8
  325.3 5.2 copy-start.9
  348.2 6.5 copy-start.8
  354.6 5.2 copy-start.9
  377.6 6.5 copy-start.8
  384.0 5.2 copy-start.9
  406.9 92.2 %all-gather.6.cloned.1.call-start = ((), (), s32[]{:S(2)}) async-start(), calls=%async_computation.13 | async-start | bytes 5898240 | tf_op jit(solution)/shard_map/all_gather | solution.py:196
  461.5 197.2 %reduce-scatter.13.cloned.1.call-start = ((), (), s32[]{:S(2)}) async-start(), calls=%async_computation.14 | async-start | bytes 5898240 | tf_op jit(solution)/shard_map/reduce_scatter | solution.py:204
  508.8 6.7 copy-start.14
  508.8 8.8 copy-start.48
  523.2 112.6 %all-to-all-start.2 = ((bf16[8,386,768]{2,1,0:T(8,128)(2,1)}), bf16[8,386,768]{2,1,0:T(8,128)(2,1)}, u32[]{:S(2)}, u32[]{:S(2)}) async-start(bf16[8,386,768]{2,1,0:T(8,128)(2,1)} %get-tuple-element.324), calls=%async_computation.4 | async-start | bytes 9633792 | tf_op jit(solution)/shard_map/all_to_all | solution.py:101
  528.8 175.5 %all-gather.10.cloned.1.call-start = ((), (), s32[]{:S(2)}) async-start(), calls=%async_computation.16 | async-start | bytes 5898240 | tf_op jit(solution)/shard_map/all_gather | solution.py:217
  668.5 109.5 %reduce-scatter.15.cloned.1.call-start = ((), (), s32[]{:S(2)}) async-start(), calls=%async_computation.17 | async-start | bytes 5898240 | tf_op jit(solution)/shard_map/reduce_scatter | solution.py:223
  730.0 48.0 %copy-start.11 = (bf16[768,768]{1,0:T(8,128)(2,1)S(1)}, bf16[768,768]{1,0:T(8,128)(2,1)}, u32[]{:S(2)}) copy-start(bf16[768,768]{1,0:T(8,128)(2,1)} %reduce-scatter.11.cloned.1.call-done) | copy-start | bytes 3538948
  730.0 93.8 %all-gather.12.cloned.1.call-start = ((), (), s32[]{:S(2)}) async-start(), calls=%async_computation.18 | async-start | bytes 5898240 | tf_op jit(solution)/shard_map/all_gather | solution.py:236
  786.1 517.1 %reduce-scatter.17.cloned.1.call-start = ((), (), s32[]{:S(2)}) async-start(), calls=%async_computation.19 | async-start | bytes 5898240 | tf_op jit(solution)/shard_map/reduce_scatter | solution.py:287
  837.5 6.5 copy-start.2
  886.1 10.5 copy-start.6
  905.1 6.5 copy-start.2
  954.5 10.5 copy-start.6
  973.5 6.5 copy-start.2
  1023.0 10.5 copy-start.6
  1041.9 6.5 copy-start.2
  1091.4 10.5 copy-start.6
  1110.3 6.5 copy-start.2
  1159.8 10.5 copy-start.6
  1178.7 6.5 copy-start.2
  1228.2 10.5 copy-start.6
  1248.2 7.0 copy-start.24
  1248.3 6.9 copy-start.25
  1255.2 48.0 %copy-start.15 = (f32[768,768]{1,0:T(8,128)S(1)}, f32[768,768]{1,0:T(8,128)}, u32[]{:S(2)}) copy-start(f32[768,768]{1,0:T(8,128)} %get-tuple-element.269) | copy-start | bytes 7077892
  1255.3 87.0 %all-gather.8.cloned.1.call-start = ((), (), s32[]{:S(2)}) async-start(), calls=%async_computation.15 | async-start | bytes 5898240 | tf_op jit(solution)/shard_map/all_gather | solution.py:310
  1256.0 125.4 %all-gather.14.cloned.1.call-start = ((), (), s32[]{:S(2)}) async-start(), calls=%async_computation.20 | async-start | bytes 5898240 | tf_op jit(solution)/shard_map/all_gather | solution.py:311
  1305.8 299.4 %reduce-scatter.23.cloned.1.call-start = ((), (), s32[]{:S(2)}) async-start(), calls=%async_computation.23 | async-start | bytes 5308416 | tf_op jit(solution)/shard_map/reduce_scatter | solution.py:306
  1423.9 132.2 %all-to-all-start.3 = ((bf16[8,386,768]{2,1,0:T(8,128)(2,1)}), bf16[8,386,768]{2,1,0:T(8,128)(2,1)}, u32[]{:S(2)}, u32[]{:S(2)}) async-start(bf16[8,386,768]{2,1,0:T(8,128)(2,1)} %get-tuple-element.326), calls=%async_computation.7 | async-start | bytes 9633792 | tf_op jit(solution)/shard_map/all_to_all | solution.py:327
  1429.3 331.9 %reduce-scatter.25.cloned.1.call-start = ((), (), s32[]{:S(2)}) async-start(), calls=%async_computation.24 | async-start | bytes 2654208 | tf_op jit(solution)/shard_map/reduce_scatter | solution.py:307
  1556.1 5.0 copy-start.28
  1556.1 9.8 copy-start.17
  1556.1 174.4 %all-to-all-start.1 = ((bf16[8,386,768]{2,1,0:T(8,128)(2,1)}), bf16[8,386,768]{2,1,0:T(8,128)(2,1)}, u32[]{:S(2)}, u32[]{:S(2)}) async-start(bf16[8,386,768]{2,1,0:T(8,128)(2,1)} %get-tuple-element.327), calls=%async_computation.3 | async-start | bytes 9633792 | tf_op jit(solution)/shard_map/all_to_all | solution.py:326
  1560.8 212.6 %reduce-scatter.21.cloned.1.call-start = ((), (), s32[]{:S(2)}) async-start(), calls=%async_computation.22 | async-start | bytes 884736 | tf_op jit(solution)/shard_map/reduce_scatter | solution.py:305
  1570.7 275.1 %reduce-scatter.19.cloned.1.call-start = ((), (), s32[]{:S(2)}) async-start(), calls=%async_computation.21 | async-start | bytes 2654208 | tf_op jit(solution)/shard_map/reduce_scatter | solution.py:304
  1584.5 20.6 %copy-start.42 = (f32[768]{0:T(1024)S(1)}, f32[768]{0:T(1024)}, u32[]{:S(2)}) copy-start(f32[768]{0:T(1024)} %get-tuple-element.189) | copy-start | bytes 9220
  1584.5 20.6 %copy-start.41 = (f32[768]{0:T(1024)S(1)}, f32[768]{0:T(1024)}, u32[]{:S(2)}) copy-start(f32[768]{0:T(1024)} %get-tuple-element.194) | copy-start | bytes 9220
  1584.5 20.6 %copy-start.44 = (f32[768]{0:T(1024)S(1)}, f32[768]{0:T(1024)}, u32[]{:S(2)}) copy-start(f32[768]{0:T(1024)} %get-tuple-element.187) | copy-start | bytes 9220
  1584.5 20.6 %copy-start.43 = (f32[768]{0:T(1024)S(1)}, f32[768]{0:T(1024)}, u32[]{:S(2)}) copy-start(f32[768]{0:T(1024)} %get-tuple-element.192) | copy-start | bytes 9220
  1752.5 93.3 %copy-start.1 = (bf16[768,2,768]{2,1,0:T(2,128)(2,1)S(1)}, bf16[768,2,768]{2,1,0:T(2,128)(2,1)}, u32[]{:S(2)}) copy-start(bf16[768,2,768]{2,1,0:T(2,128)(2,1)} %param.28) | copy-start | bytes 7077892
  (31 other events, 89.3 us)
Sparse Core Ops, SparseCore 0:
  407.0 46.8 reduce-scatter.10
  461.6 37.4 all-gather.5
  523.3 47.8 reduce-scatter.12
  668.6 35.5 all-gather.9
  730.1 47.8 reduce-scatter.14
  786.3 37.4 all-gather.11
  1255.4 47.8 reduce-scatter.16
  1304.8 37.4 all-gather.7
  1343.9 37.4 all-gather.13
  1385.4 167.9 reduce-scatter.22
  1557.5 150.5 reduce-scatter.24
  1711.9 61.4 reduce-scatter.20
  1777.9 67.8 reduce-scatter.18
where the time goes:
time: 1860 us; the launch traced here: 1850 us
  waiting for transfers between devices  662 us (36%)
  local copies, waits for them, and re-layouts  401 us (22%)
  matrix products  375 us (20%)
  other arithmetic  248 us (13%)
  blocking collectives  99.6 us (5%)
  starting transfers between devices  24.2 us (1%)
  between operations  21.6 us (1%)
  loops' own time  20.8 us (1%)
    all_to_all x1, waiting for transfers between devices, local(): lax.all_to_all(back_input, 'dp', split_axis=0, concat_axis=0, tiled=True)  117 us
    all_to_all x1, waiting for transfers between devices, local(): lax.all_to_all(send_cot, 'dp', split_axis=0, concat_axis=0, tiled=True)  104 us
    unnamed x1, blocking collectives  99.6 us
    dot_general x6, matrix products, attend_back(): jnp.einsum('qhe,khe->hqk', grad_block, values_all, preferred_element_type...  86.1 us
    convert_element_type x6, other arithmetic, attend_back(): grad_scores = (soft_exact * (grad_soft - jnp.sum(soft_exact * grad_soft,...  82.8 us
    while x60, local copies, waits for them, and re-layouts  77.6 us
    reduce_scatter x1, waiting for transfers between devices, local(): lax.psum_scatter(d_w_qkv, 'dp', scatter_dimension=0, tiled=True)  72.4 us
    dynamic_update_slice x12, local copies, waits for them, and re-layouts, local(): lax.scan(attend_back, (zero_heads, zero_heads), jnp.arange(blocks, dtype=...  62.7 us
  transfers between devices with their start and end apart: 17, of which 13 were waited for; matrix products, arithmetic and copies ran while one was open for 14% of the time, Pallas kernels for 0%

commit v1 on v0

v1 whole, which is shorter than its diff:
```python
import functools

import jax
import jax.numpy as jnp
from jax import lax
from jax.experimental import pallas as pl
from jax.experimental.pallas import tpu as pltpu
from jax.sharding import PartitionSpec as P

HEAD = 64
HALF = HEAD // 2
BLOCK = 256
EPSILON = 1e-05
NEGATIVE = -1000000000.0
START = -1e30
BF = jnp.bfloat16
F32 = jnp.float32
VMEM_LIMIT = 56 * 1024 * 1024


def mm(a, b, ca, cb):
    return lax.dot_general(a, b, (((ca,), (cb,)), ((), ())), preferred_element_type=F32)


def project_kernel(me_ref, x_ref, w_ref, cos_ref, sin_ref, q_ref, k_ref, v_ref, krow_ref, vrow_ref):
    cols = x_ref.shape[1]
    heads = q_ref.shape[0] // HEAD
    width = heads * HEAD
    projected = mm(w_ref[...], x_ref[0], 1, 1)
    cosine = cos_ref[...]
    sine = sin_ref[...]
    for part, out_ref, scale in ((0, q_ref, HEAD ** (-0.5)), (1, k_ref, 1.0)):
        for head in range(heads):
            base = part * width + head * HEAD
            first = projected[base : base + HALF]
            second = projected[base + HALF : base + HEAD]
            turned = jnp.concatenate(
                [first * cosine - second * sine, second * cosine + first * sine], 0
            )
            out_ref[head * HEAD : (head + 1) * HEAD, :] = (turned.astype(BF) * scale).astype(BF)
            if part == 1:
                krow_ref[head] = turned.T.astype(BF)
    for head in range(heads):
        base = 2 * width + head * HEAD
        value = projected[base : base + HEAD]
        v_ref[head * HEAD : (head + 1) * HEAD, :] = value.astype(BF)
        vrow_ref[head] = value.T.astype(BF)


def project(x_rel, w_t, cosine, sine, me):
    parts, share, width = x_rel.shape
    rows = parts * share
    local = w_t.shape[0] // 3
    heads = local // HEAD
    flat = jax.ShapeDtypeStruct((local, rows), BF)
    tall = jax.ShapeDtypeStruct((heads, rows, HEAD), BF)
    wide_spec = pl.BlockSpec((local, share), lambda i, me: (0, i))
    tall_spec = pl.BlockSpec((heads, share, HEAD), lambda i, me: (0, i, 0))
    table_spec = pl.BlockSpec((HALF, share), lambda i, me: (0, i))
    return pl.pallas_call(
        project_kernel,
        grid_spec=pltpu.PrefetchScalarGridSpec(
            num_scalar_prefetch=1,
            grid=(parts,),
            in_specs=[
                pl.BlockSpec((1, share, width), lambda i, me: (jnp.bitwise_xor(i, me[0]), 0, 0)),
                pl.BlockSpec((3 * local, width), lambda i, me: (0, 0)),
                table_spec,
                table_spec,
            ],
            out_specs=[wide_spec, wide_spec, wide_spec, tall_spec, tall_spec],
        ),
        out_shape=[flat, flat, flat, tall, tall],
        compiler_params=pltpu.CompilerParams(vmem_limit_bytes=VMEM_LIMIT),
        cost_estimate=pl.CostEstimate(
            flops=2 * rows * width * 3 * local, bytes_accessed=8 << 20, transcendentals=0
        ),
        name="project",
    )(me, x_rel, w_t, cosine, sine)


def visit(mixed, index, blocks, body, carry):
    low = jnp.where(index > mixed, mixed + 1, 0)
    high = jnp.where(index > mixed, blocks, jnp.where(index < mixed, mixed, 0))
    carry = lax.fori_loop(low, high, lambda j, c: body(j, False, c), carry)
    low = jnp.where(index == mixed, 0, mixed)
    high = jnp.where(index == mixed, blocks, mixed + 1)
    return lax.fori_loop(low, high, lambda j, c: body(j, True, c), carry)


def attend_kernel(info, q_ref, k_ref, v_ref, segrow_ref, segcol_ref, o_ref, lse_ref, acc_ref):
    index = pl.program_id(0)
    blocks = pl.num_programs(0)
    heads = k_ref.shape[0]
    acc_ref[...] = jnp.zeros_like(acc_ref)
    segrow = segrow_ref[...]

    def body(j, masked, carry):
        keys = pl.ds(pl.multiple_of(j * BLOCK, BLOCK), BLOCK)
        if masked:
            same = segcol_ref[keys, :] == segrow
        out = []
        for head in range(heads):
            top, total = carry[head]
            part = slice(head * HEAD, (head + 1) * HEAD)
            scores = mm(k_ref[head, keys, :], q_ref[part, :], 1, 0)
            if masked:
                scores = jnp.where(same, scores, NEGATIVE)
            new_top = jnp.maximum(top, jnp.max(scores, 0, keepdims=True))
            shrink = jnp.exp(top - new_top)
            weights = jnp.exp(scores - new_top)
            total = total * shrink + jnp.sum(weights, 0, keepdims=True)
            acc_ref[part, :] = acc_ref[part, :] * shrink + mm(
                v_ref[part, keys], weights.astype(BF), 1, 0
            )
            out.append((new_top, total))
        return tuple(out)

    width = q_ref.shape[1]
    start = (jnp.full((1, width), START, F32), jnp.zeros((1, width), F32))
    carry = visit(info[0], index, blocks, body, (start,) * heads)
    for head in range(heads):
        top, total = carry[head]
        part = slice(head * HEAD, (head + 1) * HEAD)
        o_ref[0, part, :] = (acc_ref[part, :] / total).astype(BF)
        lse_ref[head : head + 1, :] = top + jnp.log(total)


def attend(info, q, k_rows, v, seg_row, seg_col, parts):
    local, rows = q.shape
    heads = local // HEAD
    blocks = rows // BLOCK
    each = blocks // parts
    return pl.pallas_call(
        attend_kernel,
        grid_spec=pltpu.PrefetchScalarGridSpec(
            num_scalar_prefetch=1,
            grid=(blocks,),
            in_specs=[
                pl.BlockSpec((local, BLOCK), lambda i, info: (0, i)),
                pl.BlockSpec((heads, rows, HEAD), lambda i, info: (0, 0, 0)),
                pl.BlockSpec((local, rows), lambda i, info: (0, 0)),
                pl.BlockSpec((1, BLOCK), lambda i, info: (0, i)),
                pl.BlockSpec((rows, 1), lambda i, info: (0, 0)),
            ],
            out_specs=[
                pl.BlockSpec(
                    (1, local, BLOCK),
                    lambda i, info: (jnp.bitwise_xor(i // each, info[1]), 0, i % each),
                ),
                pl.BlockSpec((heads, BLOCK), lambda i, info: (0, i)),
            ],
            scratch_shapes=[pltpu.VMEM((local, BLOCK), F32)],
        ),
        out_shape=[
            jax.ShapeDtypeStruct((parts, local, rows // parts), BF),
            jax.ShapeDtypeStruct((heads, rows), F32),
        ],
        compiler_params=pltpu.CompilerParams(vmem_limit_bytes=VMEM_LIMIT),
        cost_estimate=pl.CostEstimate(
            flops=2 * 2 * rows * rows * 256 * heads // 2,
            bytes_accessed=8 << 20,
            transcendentals=heads * rows * rows // 2,
        ),
        name="attend",
    )(info, q, k_rows, v, seg_row, seg_col)


def unturn(first, second, cosine, sine):
    return first * cosine + second * sine, second * cosine - first * sine


def attend_back_kernel(
    info,
    q_ref,
    krow_ref,
    k_ref,
    vrow_ref,
    o_ref,
    do_ref,
    lse_ref,
    segrow_ref,
    segcol_ref,
    cos_ref,
    sin_ref,
    out_ref,
    dq_ref,
    dk_ref,
    dv_ref,
):
    index = pl.program_id(0)
    blocks = pl.num_programs(0)
    heads = krow_ref.shape[0]
    width = heads * HEAD

    @pl.when(index == 0)
    def _():
        dk_ref[...] = jnp.zeros_like(dk_ref)
        dv_ref[...] = jnp.zeros_like(dv_ref)

    dq_ref[...] = jnp.zeros_like(dq_ref)
    segrow = segrow_ref[...]
    deltas = []
    for head in range(heads):
        part = slice(head * HEAD, (head + 1) * HEAD)
        deltas.append(
            jnp.sum(do_ref[0, part, :].astype(F32) * o_ref[0, part, :].astype(F32), 0, keepdims=True)
        )

    def body(j, masked, carry):
        keys = pl.ds(pl.multiple_of(j * BLOCK, BLOCK), BLOCK)
        if masked:
            same = segcol_ref[keys, :] == segrow
        for head in range(heads):
            part = slice(head * HEAD, (head + 1) * HEAD)
            queries = q_ref[part, :]
            upstream = do_ref[0, part, :]
            scores = mm(krow_ref[head, keys, :], queries, 1, 0)
            if masked:
                scores = jnp.where(same, scores, NEGATIVE)
            soft = jnp.exp(scores - lse_ref[head : head + 1, :])
            grad_soft = mm(vrow_ref[head, keys, :], upstream, 1, 0)
            grad_scores = (soft * (grad_soft - deltas[head])).astype(BF)
            dv_ref[head, keys, :] += mm(soft.astype(BF), upstream, 1, 1)
            dk_ref[head, keys, :] += mm(grad_scores, queries, 1, 1)
            dq_ref[part, :] += mm(k_ref[part, keys], grad_scores, 1, 0)
        return carry

    visit(info[0], index, blocks, body, 0)

    columns = pl.ds(pl.multiple_of(index * BLOCK, BLOCK), BLOCK)
    for head in range(heads):
        base = head * HEAD
        grad = dq_ref[base : base + HEAD, :] * HEAD ** (-0.5)
        low, high = unturn(grad[:HALF], grad[HALF:], cos_ref[:, columns], sin_ref[:, columns])
        out_ref[base : base + HALF, columns] = low.astype(BF)
        out_ref[base + HALF : base + HEAD, columns] = high.astype(BF)

    @pl.when(index == blocks - 1)
    def _():
        @pl.loop(0, blocks)
        def _(j):
            rows = pl.ds(pl.multiple_of(j * BLOCK, BLOCK), BLOCK)
            for head in range(heads):
                base = width + head * HEAD
                grad = dk_ref[head, rows, :].T
                low, high = unturn(grad[:HALF], grad[HALF:], cos_ref[:, rows], sin_ref[:, rows])
                out_ref[base : base + HALF, rows] = low.astype(BF)
                out_ref[base + HALF : base + HEAD, rows] = high.astype(BF)
                base = 2 * width + head * HEAD
                out_ref[base : base + HEAD, rows] = dv_ref[head, rows, :].T.astype(BF)


def attend_back(info, q, k_rows, k, v_rows, o, do, lse, seg_row, seg_col, cosine, sine):
    parts = o.shape[0]
    local, rows = q.shape
    heads = local // HEAD
    blocks = rows // BLOCK
    each = blocks // parts
    whole = lambda *shape: pl.BlockSpec(shape, lambda i, info: (0,) * len(shape))
    member = pl.BlockSpec(
        (1, local, BLOCK), lambda i, info: (jnp.bitwise_xor(i // each, info[1]), 0, i % each)
    )
    return pl.pallas_call(
        attend_back_kernel,
        grid_spec=pltpu.PrefetchScalarGridSpec(
            num_scalar_prefetch=1,
            grid=(blocks,),
            in_specs=[
                pl.BlockSpec((local, BLOCK), lambda i, info: (0, i)),
                whole(heads, rows, HEAD),
                whole(local, rows),
                whole(heads, rows, HEAD),
                member,
                member,
                pl.BlockSpec((heads, BLOCK), lambda i, info: (0, i)),
                pl.BlockSpec((1, BLOCK), lambda i, info: (0, i)),
                whole(rows, 1),
                whole(HALF, rows),
                whole(HALF, rows),
            ],
            out_specs=whole(3 * local, rows),
            scratch_shapes=[
                pltpu.VMEM((local, BLOCK), F32),
                pltpu.VMEM((heads, rows, HEAD), F32),
                pltpu.VMEM((heads, rows, HEAD), F32),
            ],
        ),
        out_shape=jax.ShapeDtypeStruct((3 * local, rows), BF),
        compiler_params=pltpu.CompilerParams(vmem_limit_bytes=VMEM_LIMIT),
        cost_estimate=pl.CostEstimate(
            flops=2 * 5 * rows * rows * 256 * heads // 2,
            bytes_accessed=16 << 20,
            transcendentals=heads * rows * rows // 2,
        ),
        name="attend_back",
    )(info, q, k_rows, k, v_rows, o, do, lse, seg_row, seg_col, cosine, sine)


def norm_forward(resid_rows, gain_vec, shift_vec):
    row_mean = jnp.mean(resid_rows, -1, keepdims=True)
    centred = resid_rows - row_mean
    inverse = lax.rsqrt(jnp.mean(centred * centred, -1, keepdims=True) + EPSILON)
    unit_rows = centred * inverse
    return (unit_rows * gain_vec + shift_vec, unit_rows, inverse)


def norm_backward(upstream, unit_rows, inverse, gain_vec):
    scaled = upstream * gain_vec
    inner_term = (
        scaled
        - jnp.mean(scaled, -1, keepdims=True)
        - unit_rows * jnp.mean(scaled * unit_rows, -1, keepdims=True)
    )
    return (inner_term * inverse, jnp.sum(upstream * unit_rows, 0), jnp.sum(upstream, 0))


def swap(array, size, step):
    return lax.ppermute(array, "tensor", [(i, i ^ step) for i in range(size)])


def gather_members(own):
    size = lax.axis_size("tensor")
    across = swap(own, size, 2)
    return [own, swap(own, size, 1), across, swap(across, size, 1)]


def exchange_members(pieces):
    size = lax.axis_size("tensor")
    return [pieces[0]] + [swap(pieces[r], size, r) for r in range(1, size)]


def reduce_members(pieces):
    size = lax.axis_size("tensor")
    near = swap(pieces[1], size, 1)
    far = swap(pieces[3], size, 1)
    other = (pieces[2].astype(F32) + far.astype(F32)).astype(BF)
    across = swap(other, size, 2)
    return pieces[0].astype(F32) + near.astype(F32) + across.astype(F32)


def spans(offset, length, source, groups):
    low = (offset - source + groups - 1) // groups
    high = (offset + length - source + groups - 1) // groups
    return low, high - low


def local(tokens, cotangent, lengths, dealing, w_qkv, w_out, w_gu, w_down, gains, shifts):
    groups = lax.axis_size("dp")
    member = lax.axis_index("dp")
    size = lax.axis_size("tensor")
    me = lax.axis_index("tensor")
    rows = tokens.shape[0]
    width = tokens.shape[2]
    slots = rows // groups
    share = slots // size
    own_rows = rows // size
    subs = own_rows // BLOCK
    sub = share // subs
    extra = 8
    packed = share + extra
    i32 = jnp.int32

    seq_count = lengths.shape[0]
    count_up = jnp.arange(seq_count, dtype=i32)
    offsets = jnp.sum(jnp.where(count_up[None, :] < count_up[:, None], lengths[None, :], 0), 1)
    chosen = dealing[:, None] == count_up[None, :]
    dealt_len = jnp.sum(jnp.where(chosen, lengths[None, :], 0), 1).reshape(groups, 2)
    dealt_off = jnp.sum(jnp.where(chosen, offsets[None, :], 0), 1).reshape(groups, 2)
    group_ids = jnp.arange(groups, dtype=i32)

    low_a, count_a = spans(dealt_off[:, 0], dealt_len[:, 0], member, groups)
    low_b, count_b = spans(dealt_off[:, 1], dealt_len[:, 1], member, groups)
    place = jnp.arange(packed, dtype=i32)[None, :]
    slot = jnp.where(place < share, me * share + place, slots)
    picked = jnp.where(
        slot < count_a[:, None], low_a[:, None] + slot, (low_b - count_a)[:, None] + slot
    )
    picked = jnp.clip(picked, 0, rows - 1).reshape(-1)
    send_x = jnp.take(tokens.reshape(rows, width), picked, axis=0).reshape(groups, packed, width)
    send_c = jnp.take(cotangent.reshape(rows, width), picked, axis=0).reshape(
        groups, packed, width
    )
    recv_x = lax.all_to_all(send_x, "dp", split_axis=0, concat_axis=0, tiled=True)
    recv_c = lax.all_to_all(send_c, "dp", split_axis=0, concat_axis=0, tiled=True)

    mine = group_ids == member
    pick_group = lambda table: jnp.sum(jnp.where(mine[:, None], table, 0), 0)
    my_len = pick_group(dealt_len)
    my_off = pick_group(dealt_off)
    glow_a, gcount_a = spans(my_off[0], my_len[0], group_ids, groups)
    glow_b, gcount_b = spans(my_off[1], my_len[1], group_ids, groups)
    filled = gcount_a + gcount_b
    hole = filled < slots
    over = filled > slots
    before = group_ids[None, :] < group_ids[:, None]
    hole_rank = jnp.sum(jnp.where(before & hole[None, :], 1, 0), 1)
    over_rank = jnp.sum(jnp.where(before & over[None, :], 1, 0), 1)
    match = hole[:, None] & over[None, :] & (hole_rank[:, None] == over_rank[None, :])
    last_token = (glow_b - gcount_a + slots) * groups + group_ids
    hole_token = jnp.sum(jnp.where(match, last_token[None, :], 0), 1)
    match_bf = match.astype(BF)
    is_last = me == size - 1

    def fill(received):
        body = received[:, :share]
        spare = jnp.dot(match_bf, received[:, share], preferred_element_type=F32).astype(BF)
        fix = (hole & is_last)[:, None, None] & (jnp.arange(share) == share - 1)[None, :, None]
        body = jnp.where(fix, spare[:, None, :], body)
        body = body.reshape(groups, subs, sub, width).transpose(1, 0, 2, 3)
        return body.reshape(own_rows, width)

    shape = (size * subs, groups, sub)
    block_id = lax.broadcasted_iota(i32, shape, 0)
    source_id = lax.broadcasted_iota(i32, shape, 1)
    slot_id = block_id * sub + lax.broadcasted_iota(i32, shape, 2)
    spread = lambda vec: vec[None, :, None]
    in_a = slot_id < spread(gcount_a)
    token_id = (
        jnp.where(in_a, spread(glow_a), spread(glow_b - gcount_a)) + slot_id
    ) * groups + source_id
    token_id = jnp.where(spread(hole) & (slot_id == slots - 1), spread(hole_token), token_id)
    positions = (token_id - jnp.where(in_a, my_off[0], my_off[1])).reshape(rows)
    segment = jnp.where(in_a, 0, 1).astype(F32).reshape(rows)
    frequency = 1000.0 ** (-(jnp.arange(HALF, dtype=F32) * 2.0) / HEAD)
    angles = frequency[:, None] * positions.astype(F32)[None, :]
    cosine = jnp.cos(angles)
    sine = jnp.sin(angles)
    seg_row = segment[None, :]
    seg_col = segment[:, None]
    info = jnp.stack([my_len[0] // BLOCK, me]).astype(i32)

    x_own = fill(recv_x)
    x_rel = jnp.stack(gather_members(x_own))
    local_width = w_qkv.shape[2]
    w_qkv_t = w_qkv.transpose(1, 2, 0).reshape(3 * local_width, width)
    q, k, v, k_rows, v_rows = project(x_rel, w_qkv_t, cosine, sine, me[None])
    o_rel, lse = attend(info, q, k_rows, v, seg_row, seg_col, size)

    w_out_t = jnp.concatenate(gather_members(w_out.T), 0)
    gu_parts = gather_members(w_gu.reshape(width, -1))
    down_parts = gather_members(w_down)

    heads_out = jnp.concatenate(exchange_members([o_rel[r] for r in range(size)]), 0)
    x_share = x_own.astype(F32)
    attn = mm(heads_out, w_out_t, 0, 0)
    normed_one, unit_one, inverse_one = norm_forward(x_share + attn, gains[:, 0], shifts[:, 0])
    normed = normed_one.astype(BF)
    hidden_width = w_down.shape[1]
    branch = jnp.zeros((own_rows, width), F32)
    kept = []
    for r in range(size):
        both = mm(normed, gu_parts[r], 1, 0)
        gate = both[:, :hidden_width]
        up = both[:, hidden_width:]
        sig = jax.nn.sigmoid(gate)
        hidden = (gate * sig * up).astype(BF)
        branch = branch + mm(hidden, down_parts[r], 1, 1)
        kept.append((gate, up, sig, hidden))
    result_own, unit_two, inverse_two = norm_forward(
        normed_one + branch, gains[:, 1], shifts[:, 1]
    )
    cot_share = fill(recv_c).astype(F32)
    grad_two, gain_two, shift_two = norm_backward(cot_share, unit_two, inverse_two, gains[:, 1])
    d_branch = grad_two.astype(BF)
    back_normed = jnp.zeros((own_rows, width), F32)
    pieces = []
    for r in range(size):
        gate, up, sig, hidden = kept[r]
        grad_hidden = mm(d_branch, down_parts[r], 1, 0)
        grad_gate = grad_hidden * up * sig * (1.0 + gate * (1.0 - sig))
        grad_up = grad_hidden * gate * sig
        grad_gu = jnp.concatenate([grad_gate, grad_up], 1).astype(BF)
        back_normed = back_normed + mm(grad_gu, gu_parts[r], 1, 1)
        pieces.append([mm(normed, grad_gu, 0, 0), mm(d_branch, hidden, 0, 0)])
    grad_one, gain_one, shift_one = norm_backward(
        grad_two + back_normed, unit_one, inverse_one, gains[:, 0]
    )
    d_attn = grad_one.astype(BF)
    d_heads = mm(w_out_t, d_attn, 1, 1).astype(BF).reshape(size, local_width, own_rows)
    d_out = mm(d_attn, heads_out, 0, 1)
    norm_grads = jnp.stack([gain_one, gain_two, shift_one, shift_two], 1)
    wide = 2 * hidden_width + hidden_width + local_width + 4
    pad = (-wide) % 128
    for r in range(size):
        pieces[r] = jnp.concatenate(
            pieces[r]
            + [
                d_out[:, r * local_width : (r + 1) * local_width],
                norm_grads,
                jnp.zeros((width, pad), F32),
            ],
            1,
        ).astype(BF)

    do_rel = jnp.stack(exchange_members([d_heads[r] for r in range(size)]))
    d_qkv_t = attend_back(
        info, q, k_rows, k, v_rows, o_rel, do_rel, lse, seg_row, seg_col, cosine, sine
    )
    grad_qkv_t = jnp.concatenate(
        [
            mm(d_qkv_t.reshape(3 * local_width, size, own_rows)[:, i], _member(x_rel, i, me), 1, 0)[
                None
            ]
            for i in range(size)
        ],
        0,
    ).sum(0)
    back_parts = []
    for r in range(size):
        columns = lax.dynamic_slice_in_dim(
            d_qkv_t, jnp.bitwise_xor(me, r) * own_rows, own_rows, 1
        )
        back_parts.append(mm(columns, w_qkv_t, 0, 0).astype(BF))
    input_own = (grad_one + reduce_members(back_parts)).astype(BF)

    wide_own = reduce_members(pieces).astype(BF)
    both_grads = jnp.concatenate([wide_own, grad_qkv_t.T.astype(BF)], 1)
    summed = lax.psum_scatter(both_grads, "dp", scatter_dimension=0, tiled=True).astype(F32)
    gu_sum = summed[:, : 2 * hidden_width].reshape(-1, 2, hidden_width)
    down_sum = summed[:, 2 * hidden_width : 3 * hidden_width]
    out_sum = summed[:, 3 * hidden_width : 3 * hidden_width + local_width]
    norm_sum = summed[:, 3 * hidden_width + local_width : wide]
    norm_sum = lax.dynamic_slice_in_dim(
        norm_sum, me * (norm_sum.shape[0] // size), norm_sum.shape[0] // size, 0
    )
    qkv_sum = summed[:, wide + pad :].reshape(-1, 3, local_width)

    row_ids = jnp.arange(rows, dtype=i32)[None, :]
    home_low_a = low_a[:, None]
    home_low_b = low_b[:, None]
    here_a = (row_ids >= home_low_a) & (row_ids < home_low_a + count_a[:, None])
    here_b = (row_ids >= home_low_b) & (row_ids < home_low_b + count_b[:, None])
    home_slot = jnp.where(
        here_a, row_ids - home_low_a, row_ids - home_low_b + count_a[:, None]
    )
    spilled = home_slot >= slots
    home_part = jnp.where(spilled, size - 1, home_slot // share)
    home_place = jnp.where(spilled, share, home_slot - home_part * share)
    home_flat = (
        jnp.bitwise_xor(home_part, me) * groups + group_ids[:, None]
    ) * packed + home_place
    home_flat = jnp.sum(jnp.where(here_a | here_b, home_flat, 0), 0)

    def go_home(own):
        body = own.reshape(subs, groups, sub, width).transpose(1, 0, 2, 3)
        body = body.reshape(groups, share, width)
        spare = lax.dot_general(
            match_bf, body[:, share - 1], (((0,), (0,)), ((), ())), preferred_element_type=F32
        ).astype(BF)
        spare = jnp.broadcast_to(spare[:, None, :], (groups, extra, width))
        sent = jnp.concatenate([body, spare], 1)
        home = lax.all_to_all(sent, "dp", split_axis=0, concat_axis=0, tiled=True)
        every = jnp.concatenate(gather_members(home.reshape(groups * packed, width)), 0)
        return jnp.take(every, home_flat, axis=0).reshape(rows, 1, width)

    result = go_home(result_own.astype(BF))
    input_grad = go_home(input_own)
    return (
        result,
        input_grad,
        qkv_sum,
        out_sum,
        gu_sum,
        down_sum,
        norm_sum[:, :2],
        norm_sum[:, 2:],
    )


def _member(x_rel, absolute, me):
    return lax.dynamic_index_in_dim(x_rel, jnp.bitwise_xor(absolute, me), 0, keepdims=False)


def solution(mesh):
    placed = (
        P(None, "dp", None),
        P(None, "dp", None),
        P(),
        P(),
        P(None, None, "tensor"),
        P(None, "tensor"),
        P(None, None, "tensor"),
        P(None, "tensor"),
        P(),
        P(),
    )
    return jax.shard_map(
        local,
        mesh=mesh,
        in_specs=placed,
        out_specs=(
            P(None, "dp", None),
            P(None, "dp", None),
            P("dp", None, "tensor"),
            P("dp", "tensor"),
            P("dp", None, "tensor"),
            P("dp", "tensor"),
            P(("dp", "tensor"), None),
            P(("dp", "tensor"), None),
        ),
        check_vma=False,
    )
```

time: 1860 us -> 728 us (0.39)
  waiting for transfers between devices: 662 us -> 140 us
  matrix products: 375 us -> 97.3 us
  local copies, waits for them, and re-layouts: 401 us -> 129 us
  other arithmetic: 248 us -> 77 us
  Pallas kernels: 0 us -> 170 us
  blocking collectives: 99.6 us -> 37.8 us
  starting transfers between devices: 24.2 us -> 45.3 us
  loops' own time: 20.8 us -> 0 us
    dot_general x53 -> x39, matrix products: 372 us -> 97.3 us  [the longest x35 96.7 us: mm(): lax.dot_general(a, b, (((ca,), (cb,)), ((), ())), preferred_element_type=...]
    reduce_scatter x8 -> x1, waiting for transfers between devices: 224 us -> 0.01 us  [local(): lax.psum_scatter(both_grads, 'dp', scatter_dimension=0, tiled=True)]
    all_to_all x4 -> x3, waiting for transfers between devices: 281 us -> 76.3 us  [the longest x2 53.5 us: go_home(): home = lax.all_to_all(sent, 'dp', split_axis=0, concat_axis=0, tiled=True)]
    pallas_call x0 -> x3, Pallas kernels: none -> 170 us  [the longest x1 81.1 us: attend(): pl.pallas_call(attend_kernel, grid_spec=pltpu.PrefetchScalarGridSpec(num_...]
    all_gather x5 -> x0, waiting for transfers between devices: 156 us -> none  [the longest x1 37.6 us: local(): lax.all_gather(normed_one.astype(jnp.bfloat16), 'tensor', axis=0, tiled=T...]
    gather x20 -> x4, local copies, waits for them, and re-layouts: 187 us -> 50.1 us  [the longest x2 35.3 us: go_home(): return jnp.take(every, home_flat, axis=0).reshape(rows, 1, width)]
    unnamed x1 -> x0, blocking collectives: 99.6 us -> none
    while x61 -> x0, local copies, waits for them, and re-layouts: 79.6 us -> none
  transfers between devices with their start and end apart: 17 -> 34, of which waited for: 13 -> 7; matrix products, arithmetic and copies ran while one was open for 14% -> 31% of each run, Pallas kernels for 0% -> 24%
where the time goes in v1:
time: 728 us; the launch traced here: 717 us
  Pallas kernels  170 us (23%)
  waiting for transfers between devices  140 us (19%)
  local copies, waits for them, and re-layouts  129 us (18%)
  matrix products  97.3 us (13%)
  other arithmetic  77 us (11%)
  starting transfers between devices  45.3 us (6%)
  blocking collectives  37.8 us (5%)
  between operations  20.9 us (3%)
    dot_general x35, matrix products, mm(): lax.dot_general(a, b, (((ca,), (cb,)), ((), ())), preferred_element_type=...  96.7 us
    pallas_call x1, Pallas kernels, attend(): pl.pallas_call(attend_kernel, grid_spec=pltpu.PrefetchScalarGridSpec(num_...  81.1 us
    pallas_call x1, Pallas kernels, attend_back(): pl.pallas_call(attend_back_kernel, grid_spec=pltpu.PrefetchScalarGridSpec...  80.5 us
    ppermute x30, waiting for transfers between devices, swap(): return lax.ppermute(array, 'tensor', [(i, i ^ step) for i in range(size)])  63.6 us
    all_to_all x2, waiting for transfers between devices, go_home(): home = lax.all_to_all(sent, 'dp', split_axis=0, concat_axis=0, tiled=True)  53.5 us
    all_to_all x1, blocking collectives, local(): lax.all_to_all(send_c, 'dp', split_axis=0, concat_axis=0, tiled=True)  37.8 us
    gather x2, local copies, waits for them, and re-layouts, go_home(): return jnp.take(every, home_flat, axis=0).reshape(rows, 1, width)  35.3 us
    concatenate x4, local copies, waits for them, and re-layouts, local(): jnp.concatenate(pieces[r] + [d_out[:, r * local_width:(r + 1) * local_wid...  27.7 us
  transfers between devices with their start and end apart: 34, of which 7 were waited for; matrix products, arithmetic and copies ran while one was open for 31% of the time, Pallas kernels for 24%

profile of v1, /device:TPU:0, one launch (start us, length us, event | category | flops | bytes accessed | tf_op | source)
XLA Modules:
  0.0 717.3 jit_solution(840249783664544590)
XLA Ops:
  10.4 7.4 %gather_fusion = bf16[832,768]{1,0:T(8,128)(2,1)S(1)} fusion(bf16[3072,768]{1,0:T(8,128)(2,1)} %bitcast.152, s32[1024]{0:T(1024)S(1)} %pad_clamp_fusion), kind=kCustom, calls=%fused_computation.clone | custom fusion | bytes 2559232 | tf_op jit(solution)/shard_map/jit(_take)/gather | solution.py:380
  17.8 7.4 %gather_fusion.2 = bf16[832,768]{1,0:T(8,128)(2,1)S(1)} fusion(bf16[3072,768]{1,0:T(8,128)(2,1)} %bitcast.153, s32[1024]{0:T(1024)S(1)} %pad_clamp_fusion), kind=kCustom, calls=%fused_computation.2.clone | custom fusion | bytes 2559232 | tf_op jit(solution)/shard_map/jit(_take)/gather | solution.py:381
  26.5 37.8 %all_to_all.20 = bf16[8,104,768]{2,1,0:T(8,128)(2,1)S(1)} all-to-all(bf16[8,104,768]{2,1,0:T(8,128)(2,1)S(1)} %bitcast.161), channel_id=1, replica_groups=mesh['dp'=8,'tensor'=4] {'dp'}, dimensions={0} | all-to-all | bytes 2555904 | tf_op jit(solution)/shard_map/all_to_all | solution.py:385
  64.3 4.3 all-to-all-start
  75.8 22.7 %all-to-all-done = bf16[8,104,768]{2,1,0:T(8,128)(2,1)} async-done(((bf16[8,104,768]{2,1,0:T(8,128)(2,1)}), bf16[8,104,768]{2,1,0:T(8,128)(2,1)}, u32[]{:S(2)}, u32[]{:S(2)}) %all-to-all-start) | async-done | bytes 1277984 | tf_op jit(solution)/shard_map/all_to_all | solution.py:384
  99.6 2.6 fusion.67
  109.7 3.6 convert_element_type.208.segcol_ref
  136.0 2.3 multiply_sine_fusion
  139.2 2.5 pad_maximum_fusion.3.x_ref
  141.7 8.2 %project.1 = (bf16[192,3072]{1,0:T(8,128)(2,1)}, bf16[192,3072]{1,0:T(8,128)(2,1)}, bf16[192,3072]{1,0:T(8,128)(2,1)}, bf16[3,3072,64]{2,1,0:T(8,128)(2,1)}, bf16[3,3072,64]{2,1,0:T(8,128)(2,1)}) custom-call(s32[1]{0:T(128)} %bitcast.11.me_ref, bf16[4,768,768]{2,1,0:T(8,128)(2,1)} %pad_maximum_fusion.3.x_ref, bf16[576,768]{1,0:T(8,128)(2,1)} %bitcast.178, ...), custom_call_target="tpu_custom_call" | custom-call | flops 2717908992 | bytes 8388608 | tf_op jit(solution)/shard_map/project/pallas_call | solution.py:60
  149.8 81.1 %attend.1 = (bf16[4,192,768]{2,1,0:T(8,128)(2,1)}, f32[3,3072]{1,0:T(4,128)}) custom-call(s32[2]{0:T(128)} %pad_add_fusion.info, bf16[192,3072]{1,0:T(8,128)(2,1)} %get-tuple-element.17.q_ref, bf16[3,3072,64]{2,1,0:T(8,128)(2,1)} %get-tuple-element.18.k_ref.krow_ref, bf16[192,3072]{1,0:T(8,128)(2,1)} %get-tuple-element.19.v_ref, ...), custom_call_target="tpu_custom_call" | custom-call | flops 14495514624 | bytes 8388608 | tf_op jit(solution)/shard_map/attend/pallas_call | solution.py:134
  237.3 6.1 collective-permute-done.4
  243.4 4.5 collective-permute-done.5
  247.9 3.1 fusion.76
  251.9 4.1 fusion.78
  256.7 4.1 fusion.82
  260.8 2.4 fusion.79
  263.9 2.8 fusion.83
  269.4 2.6 fusion.81
  274.0 11.8 %multiply_convert_fusion.8 = bf16[768,768]{1,0:T(8,128)(2,1)S(1)} fusion(f32[768,1536]{1,0:T(8,128)S(1)} %fusion.84), kind=kLoop, calls=%fused_computation.45 | loop fusion | flops 3538944 | bytes 5898240 | tf_op jit(solution)/shard_map/convert_element_type | solution.py:457
  285.8 3.2 fusion.77
  290.2 2.3 fusion.68
  292.4 3.3 multiply_convert_fusion.7
  295.7 2.2 convolution_convert_fusion.4
  297.9 3.7 fusion.5
  303.2 3.5 convolution_convert_fusion
  308.3 3.7 multiply_convert_fusion.3
  314.1 3.7 fusion.3
  317.8 3.2 multiply_reduce_fusion
  321.7 2.9 convolution_convert_fusion.7
  326.6 7.1 concatenate.71
  334.5 3.9 convolution_convert_fusion.6
  338.4 3.5 convolution_convert_fusion.2
  341.9 7.1 concatenate.69
  349.0 2.3 convolution_convert_fusion.13
  354.3 2.1 convolution_convert_fusion.8
  358.5 6.8 concatenate.68
  365.4 4.2 convolution_convert_fusion.1
  369.6 2.1 convolution_convert_fusion.5
  371.7 6.7 concatenate.70
  378.4 2.4 pad_maximum_fusion.20.do_ref
  380.8 6.2 add_convert_fusion.1
  388.4 80.5 %attend_back.1 = bf16[576,3072]{1,0:T(8,128)(2,1)} custom-call(s32[2]{0:T(128)} %pad_add_fusion.info, bf16[192,3072]{1,0:T(8,128)(2,1)} %get-tuple-element.17.q_ref, bf16[3,3072,64]{2,1,0:T(8,128)(2,1)} %get-tuple-element.18.k_ref.krow_ref, bf16[192,3072]{1,0:T(8,128)(2,1)} %get-tuple-element.21.k_ref, bf16[3,3072,64]{2,1,0:T(8,128)(2,1)} %get-tuple-element.22.vrow_ref, ...), custom_call_target="tpu_custom_call" | custom-call | flops 36238786560 | bytes 16777216 | tf_op jit(solution)/shard_map/attend_back/pallas_call | solution.py:264
  468.9 6.4 reshape.738
  475.3 5.1 fusion.71
  480.4 2.2 fusion.7
  482.6 2.1 fusion.9
  487.5 3.5 convolution_convert_fusion.9
  491.4 4.9 add_convert_fusion
  496.3 2.6 pad_maximum_fusion.2
  501.7 21.6 %all-to-all-start.1 = ((bf16[8,104,768]{2,1,0:T(8,128)(2,1)}), bf16[8,104,768]{2,1,0:T(8,128)(2,1)}, u32[]{:S(2)}, u32[]{:S(2)}) async-start(bf16[8,104,768]{2,1,0:T(8,128)(2,1)} %pad_maximum_fusion.16), calls=%async_computation.1 | async-start | bytes 2555904 | tf_op jit(solution)/shard_map/all_to_all | solution.py:553
  523.3 3.4 convolution_convert_fusion.11
  526.7 3.4 add_convert_fusion.3
  530.7 2.7 convolution_convert_fusion.12
  533.4 25.3 %collective-permute-done.23 = bf16[768,768]{1,0:T(8,128)(2,1)S(1)} collective-permute-done((bf16[768,768]{1,0:T(8,128)(2,1)}, bf16[768,768]{1,0:T(8,128)(2,1)S(1)}, u32[]{:S(2)}, u32[]{:S(2)}) %collective-permute-start.23) | collective-permute-done | bytes 1179680 | tf_op jit(solution)/shard_map/ppermute | solution.py:319
  562.0 22.2 %all-to-all-done.1 = bf16[8,104,768]{2,1,0:T(8,128)(2,1)} async-done(((bf16[8,104,768]{2,1,0:T(8,128)(2,1)}), bf16[8,104,768]{2,1,0:T(8,128)(2,1)}, u32[]{:S(2)}, u32[]{:S(2)}) %all-to-all-start.1) | async-done | bytes 1277984 | tf_op jit(solution)/shard_map/all_to_all | solution.py:553
  584.2 3.8 all-to-all-start.3
  588.5 31.3 %all-to-all-done.3 = bf16[8,104,768]{2,1,0:T(8,128)(2,1)S(1)} async-done(((bf16[8,104,768]{2,1,0:T(8,128)(2,1)}), bf16[8,104,768]{2,1,0:T(8,128)(2,1)S(1)}, u32[]{:S(2)}, u32[]{:S(2)}) %all-to-all-start.3) | async-done | bytes 1277984 | tf_op jit(solution)/shard_map/all_to_all | solution.py:553
  621.9 27.6 %collective-permute-done.25 = bf16[832,768]{1,0:T(8,128)(2,1)S(1)} collective-permute-done((bf16[832,768]{1,0:T(8,128)(2,1)S(1)}, bf16[832,768]{1,0:T(8,128)(2,1)S(1)}, u32[]{:S(2)}, u32[]{:S(2)}) %collective-permute-start.25) | collective-permute-done | bytes 1277984 | tf_op jit(solution)/shard_map/ppermute | solution.py:319
  649.8 5.7 pad_maximum_fusion
  655.5 17.7 %gather_fusion.1 = bf16[3072,768]{1,0:T(8,128)(2,1)} fusion(bf16[3328,768]{1,0:T(8,128)(2,1)} %pad_maximum_fusion, s32[3072]{0:T(1024)S(1)} %fusion.32), kind=kCustom, calls=%fused_computation.1.clone | custom fusion | bytes 9449472 | tf_op jit(solution)/shard_map/jit(_take)/gather | solution.py:555
  673.2 4.5 pad_maximum_fusion.1
  677.7 17.7 %gather_fusion.3 = bf16[3072,768]{1,0:T(8,128)(2,1)} fusion(bf16[3328,768]{1,0:T(8,128)(2,1)} %pad_maximum_fusion.1, s32[3072]{0:T(1024)S(1)} %fusion.32), kind=kCustom, calls=%fused_computation.3.clone | custom fusion | bytes 9449472 | tf_op jit(solution)/shard_map/jit(_take)/gather | solution.py:555
  695.4 8.5 %select_bitcast_fusion = (bf16[3072,1,768]{2,0,1:T(8,128)(2,1)}, bf16[3072,1,768]{2,0,1:T(8,128)(2,1)}) fusion(bf16[3072,768]{1,0:T(8,128)(2,1)} %gather_fusion.3, pred[3072]{0:T(1024)(128)(4,1)S(1)} %compare_and_fusion, bf16[3072,768]{1,0:T(8,128)(2,1)} %gather_fusion.1), kind=kLoop, calls=%fused_computation.10 | loop fusion | flops 4718592 | bytes 18877440 | tf_op jit(solution)/shard_map/reshape | solution.py:555
  (272 shorter events, 86.5 us)
Async XLA Ops:
  64.3 34.3 %all-to-all-start = ((bf16[8,104,768]{2,1,0:T(8,128)(2,1)}), bf16[8,104,768]{2,1,0:T(8,128)(2,1)}, u32[]{:S(2)}, u32[]{:S(2)}) async-start(bf16[8,104,768]{2,1,0:T(8,128)(2,1)} %bitcast.5), calls=%async_computation | async-start | bytes 2555904 | tf_op jit(solution)/shard_map/all_to_all | solution.py:384
  68.5 635.3 %reduce-scatter.2.cloned.1.call-start = ((), (), s32[]{:S(2)}) async-start(), calls=%async_computation.5 | async-start | bytes 5529600 | tf_op jit(solution)/shard_map/reduce_scatter | solution.py:519
  75.6 23.9 %copy-start.20 = (pred[8,8]{1,0:T(8,128)(4,1)}, pred[8,8]{1,0:T(8,128)(4,1)S(1)}, u32[]{:S(2)}) copy-start(pred[8,8]{1,0:T(8,128)(4,1)S(1)} %get-tuple-element.89) | copy-start | bytes 196
  102.3 36.9 %copy-start.3 = (bf16[3,8,32,768]{3,2,1,0:T(8,128)(2,1)}, bf16[3,8,32,768]{3,2,1,0:T(8,128)(2,1)S(1)}, u32[]{:S(2)}) copy-start(bf16[3,8,32,768]{3,2,1,0:T(8,128)(2,1)S(1)} %copy.193) | copy-start | bytes 3538948
  102.3 31.3 %collective-permute-start.1 = (bf16[768,768]{1,0:T(8,128)(2,1)S(1)}, bf16[768,768]{1,0:T(8,128)(2,1)S(1)}, u32[]{:S(2)}, u32[]{:S(2)}) collective-permute-start(bf16[768,768]{1,0:T(8,128)(2,1)S(1)} %bitcast.166), channel_id=1, source_target_pairs={{0,2},{1,3},{2,0},{3,1},{4,6},{5,7},{6,4},{7,5},{8,10},{9,11},{10,... | collective-permute-start | bytes 3538952 | tf_op jit(solution)/shard_map/ppermute | solution.py:319
  103.8 34.7 %collective-permute-start.7 = (bf16[192,768]{1,0:T(8,128)(2,1)}, bf16[192,768]{1,0:T(8,128)(2,1)}, u32[]{:S(2)}, u32[]{:S(2)}) collective-permute-start(bf16[192,768]{1,0:T(8,128)(2,1)} %bitcast.23), channel_id=1, source_target_pairs={{0,2},{1,3},{2,0},{3,1},{4,6},{5,7},{6,4},{7,5},{8,10},{9,11},{10,... | collective-permute-start | bytes 884744 | tf_op jit(solution)/shard_map/ppermute | solution.py:319
  104.4 129.1 %collective-permute-start.6 = (bf16[192,768]{1,0:T(8,128)(2,1)}, bf16[192,768]{1,0:T(8,128)(2,1)}, u32[]{:S(2)}, u32[]{:S(2)}) collective-permute-start(bf16[192,768]{1,0:T(8,128)(2,1)} %bitcast.23), channel_id=1, source_target_pairs={{0,1},{1,0},{2,3},{3,2},{4,5},{5,4},{6,7},{7,6},{8,9},{9,8},{10,11... | collective-permute-start | bytes 884744 | tf_op jit(solution)/shard_map/ppermute | solution.py:319
  106.2 130.6 %collective-permute-start.11 = (bf16[768,1536]{1,0:T(8,128)(2,1)}, bf16[768,1536]{1,0:T(8,128)(2,1)}, u32[]{:S(2)}, u32[]{:S(2)}) collective-permute-start(bf16[768,1536]{1,0:T(8,128)(2,1)} %bitcast.61), channel_id=1, source_target_pairs={{0,2},{1,3},{2,0},{3,1},{4,6},{5,7},{6,4},{7,5},{8,10},{9,11},{10,... | collective-permute-start | bytes 7077896 | tf_op jit(solution)/shard_map/ppermute | solution.py:319
  133.3 5.9 collective-permute-start
  133.6 5.6 collective-permute-start.2
  138.5 97.5 %collective-permute-start.12 = (bf16[768,768]{1,0:T(8,128)(2,1)}, bf16[768,768]{1,0:T(8,128)(2,1)}, u32[]{:S(2)}, u32[]{:S(2)}) collective-permute-start(bf16[768,768]{1,0:T(8,128)(2,1)} %param.21), channel_id=1, source_target_pairs={{0,2},{1,3},{2,0},{3,1},{4,6},{5,7},{6,4},{7,5},{8,10},{9,11},{10,... | collective-permute-start | bytes 3538952 | tf_op jit(solution)/shard_map/ppermute | solution.py:319
  139.2 95.7 %collective-permute-start.8 = (bf16[192,768]{1,0:T(8,128)(2,1)}, bf16[192,768]{1,0:T(8,128)(2,1)}, u32[]{:S(2)}, u32[]{:S(2)}) collective-permute-start(bf16[192,768]{1,0:T(8,128)(2,1)} %collective-permute-done.7), channel_id=1, source_target_pairs={{0,1},{1,0},{2,3},{3,2},{4,5},{5,4},{6,7},{7,6},{8,9},{9,8},{10,11... | collective-permute-start | bytes 884744 | tf_op jit(solution)/shard_map/ppermute | solution.py:319
  232.9 4.0 collective-permute-start.3
  233.4 10.0 %collective-permute-start.4 = (bf16[192,768]{1,0:T(8,128)(2,1)S(1)}, bf16[192,768]{1,0:T(8,128)(2,1)}, u32[]{:S(2)}, u32[]{:S(2)}) collective-permute-start(bf16[192,768]{1,0:T(8,128)(2,1)S(1)} %get-tuple-element.118), channel_id=1, source_target_pairs={{0,2},{1,3},{2,0},{3,1},{4,6},{5,7},{6,4},{7,5},{8,10},{9,11},{10,... | collective-permute-start | bytes 884744 | tf_op jit(solution)/shard_map/ppermute | solution.py:319
  234.9 13.0 %collective-permute-start.5 = (bf16[192,768]{1,0:T(8,128)(2,1)S(1)}, bf16[192,768]{1,0:T(8,128)(2,1)}, u32[]{:S(2)}, u32[]{:S(2)}) collective-permute-start(bf16[192,768]{1,0:T(8,128)(2,1)S(1)} %get-tuple-element.117), channel_id=1, source_target_pairs={{0,3},{1,2},{2,1},{3,0},{4,7},{5,6},{6,5},{7,4},{8,11},{9,10},{10,... | collective-permute-start | bytes 884744 | tf_op jit(solution)/shard_map/ppermute | solution.py:319
  236.1 30.6 %collective-permute-start.9 = (bf16[768,1536]{1,0:T(8,128)(2,1)}, bf16[768,1536]{1,0:T(8,128)(2,1)S(1)}, u32[]{:S(2)}, u32[]{:S(2)}) collective-permute-start(bf16[768,1536]{1,0:T(8,128)(2,1)} %bitcast.61), channel_id=1, source_target_pairs={{0,1},{1,0},{2,3},{3,2},{4,5},{5,4},{6,7},{7,6},{8,9},{9,8},{10,11... | collective-permute-start | bytes 7077896 | tf_op jit(solution)/shard_map/ppermute | solution.py:319
  236.8 32.6 %collective-permute-start.10 = (bf16[768,768]{1,0:T(8,128)(2,1)}, bf16[768,768]{1,0:T(8,128)(2,1)S(1)}, u32[]{:S(2)}, u32[]{:S(2)}) collective-permute-start(bf16[768,768]{1,0:T(8,128)(2,1)} %param.21), channel_id=1, source_target_pairs={{0,1},{1,0},{2,3},{3,2},{4,5},{5,4},{6,7},{7,6},{8,9},{9,8},{10,11... | collective-permute-start | bytes 3538952 | tf_op jit(solution)/shard_map/ppermute | solution.py:319
  236.9 48.9 %collective-permute-start.14 = (bf16[768,768]{1,0:T(8,128)(2,1)}, bf16[768,768]{1,0:T(8,128)(2,1)S(1)}, u32[]{:S(2)}, u32[]{:S(2)}) collective-permute-start(bf16[768,768]{1,0:T(8,128)(2,1)} %collective-permute-done.12), channel_id=1, source_target_pairs={{0,1},{1,0},{2,3},{3,2},{4,5},{5,4},{6,7},{7,6},{8,9},{9,8},{10,11... | collective-permute-start | bytes 3538952 | tf_op jit(solution)/shard_map/ppermute | solution.py:319
  243.4 28.6 %collective-permute-start.13 = (bf16[768,1536]{1,0:T(8,128)(2,1)}, bf16[768,1536]{1,0:T(8,128)(2,1)S(1)}, u32[]{:S(2)}, u32[]{:S(2)}) collective-permute-start(bf16[768,1536]{1,0:T(8,128)(2,1)} %collective-permute-done.11), channel_id=1, source_target_pairs={{0,1},{1,0},{2,3},{3,2},{4,5},{5,4},{6,7},{7,6},{8,9},{9,8},{10,11... | collective-permute-start | bytes 7077896 | tf_op jit(solution)/shard_map/ppermute | solution.py:319
  251.9 20.0 %copy-start.8 = (bf16[768,768]{1,0:T(8,128)(2,1)}, bf16[768,768]{1,0:T(8,128)(2,1)S(1)}, u32[]{:S(2)}) copy-start(bf16[768,768]{1,0:T(8,128)(2,1)S(1)} %fusion.2) | copy-start | bytes 3538948
  256.7 4.1 copy-start.14
  263.8 2.8 copy-start.12
  269.4 2.6 copy-start.19
  292.4 15.8 %copy-start.16 = (bf16[768,768]{1,0:T(8,128)(2,1)}, bf16[768,768]{1,0:T(8,128)(2,1)S(1)}, u32[]{:S(2)}) copy-start(bf16[768,768]{1,0:T(8,128)(2,1)S(1)} %get-tuple-element.86) | copy-start | bytes 3538948
  303.2 3.5 copy-start.34
  308.3 3.8 copy-start.43
  308.3 3.8 copy-start.45
  308.3 3.8 copy-start.32
  321.7 27.3 %copy-start.1 = (f32[768,768]{1,0:T(8,128)}, f32[768,768]{1,0:T(8,128)S(1)}, u32[]{:S(2)}) copy-start(f32[768,768]{1,0:T(8,128)S(1)} %subtract_multiply_fusion) | copy-start | bytes 7077892
  333.8 47.1 %collective-permute-start.28 = (bf16[768,2560]{1,0:T(8,128)(2,1)}, bf16[768,2560]{1,0:T(8,128)(2,1)}, u32[]{:S(2)}, u32[]{:S(2)}) collective-permute-start(bf16[768,2560]{1,0:T(8,128)(2,1)} %concatenate.71), channel_id=1, source_target_pairs={{0,1},{1,0},{2,3},{3,2},{4,5},{5,4},{6,7},{7,6},{8,9},{9,8},{10,11... | collective-permute-start | bytes 11796488 | tf_op jit(solution)/shard_map/ppermute | solution.py:319
  334.5 3.9 copy-start.10
  334.5 3.9 copy-start.44
  334.5 3.9 copy-start.46
  349.0 142.5 %collective-permute-start.27 = (bf16[768,2560]{1,0:T(8,128)(2,1)}, bf16[768,2560]{1,0:T(8,128)(2,1)}, u32[]{:S(2)}, u32[]{:S(2)}) collective-permute-start(bf16[768,2560]{1,0:T(8,128)(2,1)} %concatenate.69), channel_id=1, source_target_pairs={{0,1},{1,0},{2,3},{3,2},{4,5},{5,4},{6,7},{7,6},{8,9},{9,8},{10,11... | collective-permute-start | bytes 11796488 | tf_op jit(solution)/shard_map/ppermute | solution.py:319
  351.3 3.0 copy-start.15
  351.3 3.0 copy-start.17
  352.3 26.1 %collective-permute-start.18 = (bf16[192,768]{1,0:T(8,128)(2,1)}, bf16[192,768]{1,0:T(8,128)(2,1)}, u32[]{:S(2)}, u32[]{:S(2)}) collective-permute-start(bf16[192,768]{1,0:T(8,128)(2,1)} %get-tuple-element.115), channel_id=1, source_target_pairs={{0,1},{1,0},{2,3},{3,2},{4,5},{5,4},{6,7},{7,6},{8,9},{9,8},{10,11... | collective-permute-start | bytes 884744 | tf_op jit(solution)/shard_map/ppermute | solution.py:319
  352.8 25.6 %collective-permute-start.19 = (bf16[192,768]{1,0:T(8,128)(2,1)}, bf16[192,768]{1,0:T(8,128)(2,1)}, u32[]{:S(2)}, u32[]{:S(2)}) collective-permute-start(bf16[192,768]{1,0:T(8,128)(2,1)} %get-tuple-element.114), channel_id=1, source_target_pairs={{0,2},{1,3},{2,0},{3,1},{4,6},{5,7},{6,4},{7,5},{8,10},{9,11},{10,... | collective-permute-start | bytes 884744 | tf_op jit(solution)/shard_map/ppermute | solution.py:319
  354.3 24.1 %collective-permute-start.20 = (bf16[192,768]{1,0:T(8,128)(2,1)}, bf16[192,768]{1,0:T(8,128)(2,1)}, u32[]{:S(2)}, u32[]{:S(2)}) collective-permute-start(bf16[192,768]{1,0:T(8,128)(2,1)} %get-tuple-element.113), channel_id=1, source_target_pairs={{0,3},{1,2},{2,1},{3,0},{4,7},{5,6},{6,5},{7,4},{8,11},{9,10},{10,... | collective-permute-start | bytes 884744 | tf_op jit(solution)/shard_map/ppermute | solution.py:319
  365.4 4.2 copy-start.13
  365.4 4.2 copy-start.18
  387.1 104.4 %collective-permute-start.29 = (bf16[768,2560]{1,0:T(8,128)(2,1)}, bf16[768,2560]{1,0:T(8,128)(2,1)}, u32[]{:S(2)}, u32[]{:S(2)}) collective-permute-start(bf16[768,2560]{1,0:T(8,128)(2,1)} %add_convert_fusion.1), channel_id=1, source_target_pairs={{0,2},{1,3},{2,0},{3,1},{4,6},{5,7},{6,4},{7,5},{8,10},{9,11},{10,... | collective-permute-start | bytes 11796488 | tf_op jit(solution)/shard_map/ppermute | solution.py:319
  475.3 9.5 %slice-start = ((s8[4718592]{0:T(1024)(128)(4,1)}), s8[4194304]{0:T(1024)(128)(4,1)S(1)}, s32[]{:S(2)}) async-start(s8[4718592]{0:T(1024)(128)(4,1)} %bitcast.156), calls=%async_computation.6 | async-start | bytes 8388608
  480.4 4.4 slice-start.1
  487.4 4.0 copy-start
  490.9 35.8 %collective-permute-start.22 = (bf16[768,768]{1,0:T(8,128)(2,1)}, bf16[768,768]{1,0:T(8,128)(2,1)}, u32[]{:S(2)}, u32[]{:S(2)}) collective-permute-start(bf16[768,768]{1,0:T(8,128)(2,1)} %convolution_convert_fusion.9), channel_id=1, source_target_pairs={{0,1},{1,0},{2,3},{3,2},{4,5},{5,4},{6,7},{7,6},{8,9},{9,8},{10,11... | collective-permute-start | bytes 3538952 | tf_op jit(solution)/shard_map/ppermute | solution.py:319
  500.5 22.8 %copy-start.5 = (bf16[576,3072]{1,0:T(8,128)(2,1)S(1)}, bf16[576,3072]{1,0:T(8,128)(2,1)}, u32[]{:S(2)}) copy-start(bf16[576,3072]{1,0:T(8,128)(2,1)} %attend_back.1) | copy-start | bytes 10616836
  501.7 82.6 %all-to-all-start.1 = ((bf16[8,104,768]{2,1,0:T(8,128)(2,1)}), bf16[8,104,768]{2,1,0:T(8,128)(2,1)}, u32[]{:S(2)}, u32[]{:S(2)}) async-start(bf16[8,104,768]{2,1,0:T(8,128)(2,1)} %pad_maximum_fusion.16), calls=%async_computation.1 | async-start | bytes 2555904 | tf_op jit(solution)/shard_map/all_to_all | solution.py:553
  523.3 3.4 copy-start.36
  526.7 6.7 collective-permute-start.21
  530.1 28.6 %copy-start.2 = (f32[768,768]{1,0:T(8,128)S(1)}, f32[768,768]{1,0:T(8,128)}, u32[]{:S(2)}) copy-start(f32[768,768]{1,0:T(8,128)} %copy-done.1) | copy-start | bytes 7077892
  530.1 28.6 %collective-permute-start.23 = (bf16[768,768]{1,0:T(8,128)(2,1)}, bf16[768,768]{1,0:T(8,128)(2,1)S(1)}, u32[]{:S(2)}, u32[]{:S(2)}) collective-permute-start(bf16[768,768]{1,0:T(8,128)(2,1)} %add_convert_fusion.3), channel_id=1, source_target_pairs={{0,2},{1,3},{2,0},{3,1},{4,6},{5,7},{6,4},{7,5},{8,10},{9,11},{10,... | collective-permute-start | bytes 3538952 | tf_op jit(solution)/shard_map/ppermute | solution.py:319
  560.8 88.7 %copy-start.24 = (s32[8]{0:T(128)S(1)}, s32[8]{0:T(128)}, u32[]{:S(2)}) copy-start(s32[8]{0:T(128)} %copy-done.23) | copy-start | bytes 100
  560.8 88.7 %copy-start.26 = (s32[8]{0:T(128)S(1)}, s32[8]{0:T(128)}, u32[]{:S(2)}) copy-start(s32[8]{0:T(128)} %copy-done.25) | copy-start | bytes 100
  560.9 88.7 %copy-start.28 = (s32[8]{0:T(128)S(1)}, s32[8]{0:T(128)}, u32[]{:S(2)}) copy-start(s32[8]{0:T(128)} %get-tuple-element.76) | copy-start | bytes 100
  560.9 88.7 %copy-start.29 = (s32[8]{0:T(128)S(1)}, s32[8]{0:T(128)}, u32[]{:S(2)}) copy-start(s32[8]{0:T(128)} %get-tuple-element.77) | copy-start | bytes 100
  560.9 88.7 %copy-start.30 = (s32[8]{0:T(128)S(1)}, s32[8]{0:T(128)}, u32[]{:S(2)}) copy-start(s32[8]{0:T(128)} %get-tuple-element.78) | copy-start | bytes 100
  584.2 35.6 %all-to-all-start.3 = ((bf16[8,104,768]{2,1,0:T(8,128)(2,1)}), bf16[8,104,768]{2,1,0:T(8,128)(2,1)S(1)}, u32[]{:S(2)}, u32[]{:S(2)}) async-start(bf16[8,104,768]{2,1,0:T(8,128)(2,1)} %pad_maximum_fusion.17), calls=%async_computation.3 | async-start | bytes 2555904 | tf_op jit(solution)/shard_map/all_to_all | solution.py:553
  588.1 33.3 %collective-permute-start.16 = (bf16[832,768]{1,0:T(8,128)(2,1)}, bf16[832,768]{1,0:T(8,128)(2,1)}, u32[]{:S(2)}, u32[]{:S(2)}) collective-permute-start(bf16[832,768]{1,0:T(8,128)(2,1)} %bitcast.28), channel_id=1, source_target_pairs={{0,2},{1,3},{2,0},{3,1},{4,6},{5,7},{6,4},{7,5},{8,10},{9,11},{10,... | collective-permute-start | bytes 3833864 | tf_op jit(solution)/shard_map/ppermute | solution.py:319
  619.8 29.7 %collective-permute-start.25 = (bf16[832,768]{1,0:T(8,128)(2,1)S(1)}, bf16[832,768]{1,0:T(8,128)(2,1)S(1)}, u32[]{:S(2)}, u32[]{:S(2)}) collective-permute-start(bf16[832,768]{1,0:T(8,128)(2,1)S(1)} %bitcast.158), channel_id=1, source_target_pairs={{0,2},{1,3},{2,0},{3,1},{4,6},{5,7},{6,4},{7,5},{8,10},{9,11},{10,... | collective-permute-start | bytes 3833864 | tf_op jit(solution)/shard_map/ppermute | solution.py:319
  621.4 28.4 %collective-permute-start.15 = (bf16[832,768]{1,0:T(8,128)(2,1)}, bf16[832,768]{1,0:T(8,128)(2,1)}, u32[]{:S(2)}, u32[]{:S(2)}) collective-permute-start(bf16[832,768]{1,0:T(8,128)(2,1)} %bitcast.28), channel_id=1, source_target_pairs={{0,1},{1,0},{2,3},{3,2},{4,5},{5,4},{6,7},{7,6},{8,9},{9,8},{10,11... | collective-permute-start | bytes 3833864 | tf_op jit(solution)/shard_map/ppermute | solution.py:319
  621.4 28.4 %collective-permute-start.17 = (bf16[832,768]{1,0:T(8,128)(2,1)}, bf16[832,768]{1,0:T(8,128)(2,1)}, u32[]{:S(2)}, u32[]{:S(2)}) collective-permute-start(bf16[832,768]{1,0:T(8,128)(2,1)} %collective-permute-done.16), channel_id=1, source_target_pairs={{0,1},{1,0},{2,3},{3,2},{4,5},{5,4},{6,7},{7,6},{8,9},{9,8},{10,11... | collective-permute-start | bytes 3833864 | tf_op jit(solution)/shard_map/ppermute | solution.py:319
  621.9 51.3 %collective-permute-start.24 = (bf16[832,768]{1,0:T(8,128)(2,1)S(1)}, bf16[832,768]{1,0:T(8,128)(2,1)}, u32[]{:S(2)}, u32[]{:S(2)}) collective-permute-start(bf16[832,768]{1,0:T(8,128)(2,1)S(1)} %bitcast.159), channel_id=1, source_target_pairs={{0,1},{1,0},{2,3},{3,2},{4,5},{5,4},{6,7},{7,6},{8,9},{9,8},{10,11... | collective-permute-start | bytes 3833864 | tf_op jit(solution)/shard_map/ppermute | solution.py:319
  649.5 23.7 %collective-permute-start.26 = (bf16[832,768]{1,0:T(8,128)(2,1)S(1)}, bf16[832,768]{1,0:T(8,128)(2,1)}, u32[]{:S(2)}, u32[]{:S(2)}) collective-permute-start(bf16[832,768]{1,0:T(8,128)(2,1)S(1)} %collective-permute-done.25), channel_id=1, source_target_pairs={{0,1},{1,0},{2,3},{3,2},{4,5},{5,4},{6,7},{7,6},{8,9},{9,8},{10,11... | collective-permute-start | bytes 3833864 | tf_op jit(solution)/shard_map/ppermute | solution.py:319
  (19 other events, 32.6 us)
Sparse Core Ops, SparseCore 0:
  499.1 156.5 reduce-scatter.1

commit v2 on v1

v2 whole, which is shorter than its diff:
```python
import functools

import jax
import jax.numpy as jnp
from jax import lax
from jax.experimental import pallas as pl
from jax.experimental.pallas import tpu as pltpu
from jax.sharding import PartitionSpec as P

HEAD = 64
HALF = HEAD // 2
BLOCK = 256
QUERIES = 512
PADDED = HEAD + 16
KEYS = 512
LOG_2 = 0.6931471805599453
EPSILON = 1e-05
NEGATIVE = -1000000000.0
START = -1e30
BF = jnp.bfloat16
F32 = jnp.float32
VMEM_LIMIT = 56 * 1024 * 1024


def mm(a, b, ca, cb):
    return lax.dot_general(a, b, (((ca,), (cb,)), ((), ())), preferred_element_type=F32)


def project_kernel(me_ref, x_ref, w_ref, cos_ref, sin_ref, q_ref, k_ref, v_ref, krow_ref, vrow_ref):
    cols = x_ref.shape[1]
    heads = q_ref.shape[0] // HEAD
    width = heads * HEAD
    projected = mm(w_ref[...], x_ref[0], 1, 1)
    cosine = cos_ref[...]
    sine = sin_ref[...]
    for part, out_ref, scale in ((0, q_ref, HEAD ** (-0.5) / LOG_2), (1, k_ref, 1.0)):
        for head in range(heads):
            base = part * width + head * HEAD
            first = projected[base : base + HALF]
            second = projected[base + HALF : base + HEAD]
            turned = jnp.concatenate(
                [first * cosine - second * sine, second * cosine + first * sine], 0
            )
            out_ref[head * HEAD : (head + 1) * HEAD, :] = (turned * scale).astype(BF)
            if part == 1:
                krow_ref[head] = turned.T.astype(BF)
    for head in range(heads):
        base = 2 * width + head * HEAD
        value = projected[base : base + HEAD]
        rest = lax.broadcasted_iota(jnp.int32, (PADDED - HEAD, cols), 0) == 0
        v_ref[head * PADDED : (head + 1) * PADDED, :] = jnp.concatenate(
            [value, jnp.where(rest, 1.0, 0.0)], 0
        ).astype(BF)
        vrow_ref[head] = value.T.astype(BF)


def project(x_rel, w_t, cosine, sine, me):
    parts, share, width = x_rel.shape
    rows = parts * share
    local = w_t.shape[0] // 3
    heads = local // HEAD
    flat = jax.ShapeDtypeStruct((local, rows), BF)
    tall = jax.ShapeDtypeStruct((heads, rows, HEAD), BF)
    wide_spec = pl.BlockSpec((local, share), lambda i, me: (0, i))
    tall_spec = pl.BlockSpec((heads, share, HEAD), lambda i, me: (0, i, 0))
    table_spec = pl.BlockSpec((HALF, share), lambda i, me: (0, i))
    return pl.pallas_call(
        project_kernel,
        grid_spec=pltpu.PrefetchScalarGridSpec(
            num_scalar_prefetch=1,
            grid=(parts,),
            in_specs=[
                pl.BlockSpec((1, share, width), lambda i, me: (jnp.bitwise_xor(i, me[0]), 0, 0)),
                pl.BlockSpec((3 * local, width), lambda i, me: (0, 0)),
                table_spec,
                table_spec,
            ],
            out_specs=[
                wide_spec,
                wide_spec,
                pl.BlockSpec((heads * PADDED, share), lambda i, me: (0, i)),
                tall_spec,
                tall_spec,
            ],
        ),
        out_shape=[
            flat,
            flat,
            jax.ShapeDtypeStruct((heads * PADDED, rows), BF),
            tall,
            tall,
        ],
        compiler_params=pltpu.CompilerParams(vmem_limit_bytes=VMEM_LIMIT),
        cost_estimate=pl.CostEstimate(
            flops=2 * rows * width * 3 * local, bytes_accessed=8 << 20, transcendentals=0
        ),
        name="project",
    )(me, x_rel, w_t, cosine, sine)


def visible(info, index, q_blocks, k_blocks, count):
    is_a = (index + 1) * q_blocks <= info[0]
    is_b = index * q_blocks >= info[1]
    pure = is_a | is_b
    end_a = info[0] // k_blocks
    start_b = (info[1] + k_blocks - 1) // k_blocks
    plain_low = jnp.where(is_b, start_b, 0)
    plain_high = jnp.where(is_b, count, jnp.where(is_a, end_a, 0))
    return plain_low, plain_high, jnp.where(pure, end_a, 0), jnp.where(pure, start_b, count)


def attend_kernel(info, q_ref, k_ref, v_ref, segrow_ref, segcol_ref, o_ref, lse_ref, acc_ref):
    index = pl.program_id(0)
    heads, rows, _ = k_ref.shape
    width = q_ref.shape[1]
    tall = v_ref.shape[0] // heads
    spans_ = visible(info, index, width // BLOCK, KEYS // BLOCK, rows // KEYS)
    acc_ref[...] = jnp.zeros_like(acc_ref)
    segrow = segrow_ref[...]
    ids = range(heads)

    def step(masked, j, tops):
        keys = pl.ds(pl.multiple_of(j * KEYS, KEYS), KEYS)
        scores = [mm(k_ref[h, keys, :], q_ref[h * HEAD : (h + 1) * HEAD, :], 1, 0) for h in ids]
        if masked:
            same = segcol_ref[keys, :] == segrow
            scores = [jnp.where(same, s, NEGATIVE) for s in scores]
        new = [jnp.maximum(tops[h], jnp.max(scores[h], 0, keepdims=True)) for h in ids]
        weights = [jnp.exp2(scores[h] - new[h]).astype(BF) for h in ids]
        shrink = [jnp.exp2(tops[h] - new[h]) for h in ids]
        sums = [mm(v_ref[h * tall : (h + 1) * tall, keys], weights[h], 1, 0) for h in ids]
        for h in ids:
            part = slice(h * tall, (h + 1) * tall)
            acc_ref[part, :] = acc_ref[part, :] * shrink[h] + sums[h]
        return tuple(new)

    tops = (jnp.full((1, width), START, F32),) * heads
    tops = lax.fori_loop(spans_[0], spans_[1], functools.partial(step, False), tops)
    tops = lax.fori_loop(spans_[2], spans_[3], functools.partial(step, True), tops)
    for h in ids:
        total = acc_ref[h * tall + HEAD : h * tall + HEAD + 1, :]
        out = (acc_ref[h * tall : h * tall + HEAD, :] / total).astype(BF)
        each = o_ref.shape[2]
        for i in range(width // each):
            o_ref[i, h * HEAD : (h + 1) * HEAD, :] = out[:, i * each : (i + 1) * each]
        lse_ref[h : h + 1, :] = tops[h] + jnp.log2(total)


def attend(info, q, k_rows, v, seg_row, seg_col):
    local, rows = q.shape
    heads = local // HEAD
    return pl.pallas_call(
        attend_kernel,
        grid_spec=pltpu.PrefetchScalarGridSpec(
            num_scalar_prefetch=1,
            grid=(rows // QUERIES,),
            in_specs=[
                pl.BlockSpec((local, QUERIES), lambda i, info: (0, i)),
                pl.BlockSpec((heads, rows, HEAD), lambda i, info: (0, 0, 0)),
                pl.BlockSpec(v.shape, lambda i, info: (0, 0)),
                pl.BlockSpec((1, QUERIES), lambda i, info: (0, i)),
                pl.BlockSpec((rows, 1), lambda i, info: (0, 0)),
            ],
            out_specs=[
                pl.BlockSpec((QUERIES // BLOCK, local, BLOCK), lambda i, info: (i, 0, 0)),
                pl.BlockSpec((heads, QUERIES), lambda i, info: (0, i)),
            ],
            scratch_shapes=[pltpu.VMEM((v.shape[0], QUERIES), F32)],
        ),
        out_shape=[
            jax.ShapeDtypeStruct((rows // BLOCK, local, BLOCK), BF),
            jax.ShapeDtypeStruct((heads, rows), F32),
        ],
        compiler_params=pltpu.CompilerParams(vmem_limit_bytes=VMEM_LIMIT),
        cost_estimate=pl.CostEstimate(
            flops=2 * 2 * rows * rows * 256 * heads // 2,
            bytes_accessed=8 << 20,
            transcendentals=heads * rows * rows // 2,
        ),
        name="attend",
    )(info, q, k_rows, v, seg_row, seg_col)


def unturn(grad, cosine, sine):
    first = grad[:HALF]
    second = grad[HALF:]
    return jnp.concatenate(
        [first * cosine + second * sine, second * cosine - first * sine], 0
    ).astype(BF)


def attend_back_kernel(
    info,
    q_ref,
    krow_ref,
    k_ref,
    vrow_ref,
    o_ref,
    do_ref,
    lse_ref,
    segrow_ref,
    segcol_ref,
    cos_ref,
    sin_ref,
    out_ref,
    dq_ref,
    dk_ref,
    dv_ref,
):
    index = pl.program_id(0)
    heads, rows, _ = krow_ref.shape
    width = heads * HEAD
    parts, _, share = out_ref.shape
    each = share // BLOCK
    ids = range(heads)
    part = [slice(h * HEAD, (h + 1) * HEAD) for h in ids]

    @pl.when(index == 0)
    def _():
        dk_ref[...] = jnp.zeros_like(dk_ref)
        dv_ref[...] = jnp.zeros_like(dv_ref)

    dq_ref[...] = jnp.zeros_like(dq_ref)
    segrow = segrow_ref[...]
    delta = [
        jnp.sum(do_ref[0, p, :].astype(F32) * o_ref[0, p, :].astype(F32), 0, keepdims=True)
        for p in part
    ]
    spans_ = visible(info, index, 1, KEYS // BLOCK, rows // KEYS)

    def step(masked, j, carry):
        keys = pl.ds(pl.multiple_of(j * KEYS, KEYS), KEYS)
        scores = [mm(krow_ref[h, keys, :], q_ref[part[h], :], 1, 0) for h in ids]
        grad_soft = [mm(vrow_ref[h, keys, :], do_ref[0, part[h], :], 1, 0) for h in ids]
        if masked:
            same = segcol_ref[keys, :] == segrow
            scores = [jnp.where(same, s, NEGATIVE) for s in scores]
        soft = [jnp.exp2(scores[h] - lse_ref[h : h + 1, :]) for h in ids]
        grad_scores = [(soft[h] * (grad_soft[h] - delta[h])).astype(BF) for h in ids]
        soft = [s.astype(BF) for s in soft]
        dv = [mm(do_ref[0, part[h], :], soft[h], 1, 1) for h in ids]
        dk = [mm(q_ref[part[h], :], grad_scores[h], 1, 1) for h in ids]
        dq = [mm(k_ref[part[h], keys], grad_scores[h], 1, 0) for h in ids]
        for h in ids:
            dv_ref[part[h], keys] += dv[h]
            dk_ref[part[h], keys] += dk[h]
            dq_ref[part[h], :] += dq[h]
        return carry

    lax.fori_loop(spans_[0], spans_[1], functools.partial(step, False), 0)
    lax.fori_loop(spans_[2], spans_[3], functools.partial(step, True), 0)

    owner = index // each
    columns = pl.ds(pl.multiple_of(index * BLOCK, BLOCK), BLOCK)
    inside = pl.ds(pl.multiple_of(index % each * BLOCK, BLOCK), BLOCK)
    for h in ids:
        out_ref[owner, part[h], inside] = unturn(
            dq_ref[part[h], :] * HEAD ** (-0.5), cos_ref[:, columns], sin_ref[:, columns]
        )

    @pl.when(index == pl.num_programs(0) - 1)
    def _():
        @pl.loop(0, parts)
        def _(j):
            columns = pl.ds(pl.multiple_of(j * share, share), share)
            for h in ids:
                base = width + h * HEAD
                out_ref[j, base : base + HEAD, :] = unturn(
                    dk_ref[part[h], columns] * LOG_2, cos_ref[:, columns], sin_ref[:, columns]
                )
                base = 2 * width + h * HEAD
                out_ref[j, base : base + HEAD, :] = dv_ref[part[h], columns].astype(BF)


def attend_back(info, q, k_rows, k, v_rows, o, do, lse, seg_row, seg_col, cosine, sine):
    parts = do.shape[0]
    local, rows = q.shape
    heads = local // HEAD
    blocks = rows // BLOCK
    each = blocks // parts
    whole = lambda *shape: pl.BlockSpec(shape, lambda i, info: (0,) * len(shape))
    return pl.pallas_call(
        attend_back_kernel,
        grid_spec=pltpu.PrefetchScalarGridSpec(
            num_scalar_prefetch=1,
            grid=(blocks,),
            in_specs=[
                pl.BlockSpec((local, BLOCK), lambda i, info: (0, i)),
                whole(heads, rows, HEAD),
                whole(local, rows),
                whole(heads, rows, HEAD),
                pl.BlockSpec((1, local, BLOCK), lambda i, info: (i, 0, 0)),
                pl.BlockSpec(
                    (1, local, BLOCK),
                    lambda i, info: (jnp.bitwise_xor(i // each, info[2]), 0, i % each),
                ),
                pl.BlockSpec((heads, BLOCK), lambda i, info: (0, i)),
                pl.BlockSpec((1, BLOCK), lambda i, info: (0, i)),
                whole(rows, 1),
                whole(HALF, rows),
                whole(HALF, rows),
            ],
            out_specs=whole(parts, 3 * local, rows // parts),
            scratch_shapes=[
                pltpu.VMEM((local, BLOCK), F32),
                pltpu.VMEM((local, rows), F32),
                pltpu.VMEM((local, rows), F32),
            ],
        ),
        out_shape=jax.ShapeDtypeStruct((parts, 3 * local, rows // parts), BF),
        compiler_params=pltpu.CompilerParams(vmem_limit_bytes=VMEM_LIMIT),
        cost_estimate=pl.CostEstimate(
            flops=2 * 5 * rows * rows * 256 * heads // 2,
            bytes_accessed=16 << 20,
            transcendentals=heads * rows * rows // 2,
        ),
        name="attend_back",
    )(info, q, k_rows, k, v_rows, o, do, lse, seg_row, seg_col, cosine, sine)


def project_back_kernel(me_ref, d_ref, x_ref, w_ref, back_ref, grad_ref, acc_ref):
    index = pl.program_id(0)

    @pl.when(index == 0)
    def _():
        acc_ref[...] = jnp.zeros_like(acc_ref)

    d_t = d_ref[0]
    back_ref[0] = mm(d_t, w_ref[...], 0, 0).astype(BF)
    acc_ref[...] += mm(d_t, x_ref[0], 1, 0)

    @pl.when(index == pl.num_programs(0) - 1)
    def _():
        grad_ref[...] = acc_ref[...].T.astype(BF)


def project_back(d_qkv_t, x_rel, w_t, me):
    parts, local, share = d_qkv_t.shape
    width = w_t.shape[1]
    relative = lambda i, me: (jnp.bitwise_xor(i, me[0]), 0, 0)
    return pl.pallas_call(
        project_back_kernel,
        grid_spec=pltpu.PrefetchScalarGridSpec(
            num_scalar_prefetch=1,
            grid=(parts,),
            in_specs=[
                pl.BlockSpec((1, local, share), lambda i, me: (i, 0, 0)),
                pl.BlockSpec((1, share, width), relative),
                pl.BlockSpec((local, width), lambda i, me: (0, 0)),
            ],
            out_specs=[
                pl.BlockSpec((1, share, width), relative),
                pl.BlockSpec((width, local), lambda i, me: (0, 0)),
            ],
            scratch_shapes=[pltpu.VMEM((local, width), F32)],
        ),
        out_shape=[
            jax.ShapeDtypeStruct((parts, share, width), BF),
            jax.ShapeDtypeStruct((width, local), BF),
        ],
        compiler_params=pltpu.CompilerParams(vmem_limit_bytes=VMEM_LIMIT),
        cost_estimate=pl.CostEstimate(
            flops=4 * parts * share * local * width, bytes_accessed=15 << 20, transcendentals=0
        ),
        name="project_back",
    )(me, d_qkv_t, x_rel, w_t)


MESH = pl.DeviceIdType.MESH


def greet(groups, steps, d, t):
    barrier = pltpu.get_barrier_semaphore()
    for k in range(1, groups):
        pl.semaphore_signal(
            barrier, inc=1, device_id=(lax.rem(d + k, groups), t), device_id_type=MESH
        )
    for step in steps:
        pl.semaphore_signal(
            barrier, inc=1, device_id=(d, jnp.bitwise_xor(t, step)), device_id_type=MESH
        )
    pl.semaphore_wait(barrier, groups - 1 + len(steps))


def remote(src, dst, send, recv, device):
    return pltpu.make_async_remote_copy(
        src_ref=src,
        dst_ref=dst,
        send_sem=send,
        recv_sem=recv,
        device_id=device,
        device_id_type=MESH,
    )


class Spread:
    def __init__(self, out, sems, groups, d, t):
        self.out, self.sems, self.groups, self.d, self.t = out, sems, groups, d, t

    def at(self, r, k, rest):
        return self.out.at[(r, lax.rem(self.d - k + self.groups, self.groups)) + rest]

    def arrival(self, source, k, rest, where):
        send, recv = self.sems
        to = lax.rem(self.d + k, self.groups)
        return remote(
            source, self.at(0, 0, rest), send.at[(0, k) + where], recv.at[(0, k) + where], (to, self.t)
        )

    def across(self, k, rest, where):
        send, recv = self.sems
        return remote(
            self.at(0, k, rest),
            self.at(2, k, rest),
            send.at[(2, k) + where],
            recv.at[(2, k) + where],
            (self.d, jnp.bitwise_xor(self.t, 2)),
        )

    def beside(self, r, k, rest, where):
        send, recv = self.sems
        return remote(
            self.at(r, k, rest),
            self.at(r + 1, k, rest),
            send.at[(r + 1, k) + where],
            recv.at[(r + 1, k) + where],
            (self.d, jnp.bitwise_xor(self.t, 1)),
        )


def norm_forward(resid_rows, gain_vec, shift_vec):
    row_mean = jnp.mean(resid_rows, -1, keepdims=True)
    centred = resid_rows - row_mean
    inverse = lax.rsqrt(jnp.mean(centred * centred, -1, keepdims=True) + EPSILON)
    unit_rows = centred * inverse
    return (unit_rows * gain_vec + shift_vec, unit_rows, inverse)


def norm_backward(upstream, unit_rows, inverse, gain_vec):
    scaled = upstream * gain_vec
    inner_term = (
        scaled
        - jnp.mean(scaled, -1, keepdims=True)
        - unit_rows * jnp.mean(scaled * unit_rows, -1, keepdims=True)
    )
    return (
        inner_term * inverse,
        jnp.sum(upstream * unit_rows, 0, keepdims=True),
        jnp.sum(upstream, 0, keepdims=True),
    )


def middle_kernel(size, *refs):
    x_ref, cot_ref, norm_ref = refs[:3]
    blocks_ref = refs[3]
    out_hbm, gu_hbm, down_hbm = (refs[4 + i * size : 4 + (i + 1) * size] for i in range(3))
    (
        result_ref,
        grad_one_ref,
        d_heads_ref,
        heads_ref,
        normed_t_ref,
        d_branch_t_ref,
        d_attn_t_ref,
        hidden_ref,
        d_gu_ref,
        norm_grad_ref,
        w_out_ref,
        w_gu_ref,
        w_down_ref,
        slope_ref,
        swish_ref,
        arrived_ref,
        sems,
        sends,
        recvs,
        keep,
    ) = refs[4 + 3 * size :]
    index = pl.program_id(0)
    first = index == 0
    d = lax.axis_index("dp")
    t = lax.axis_index("tensor")
    subs, local, _ = arrived_ref.shape[1:]
    inner = down_hbm[0].shape[1]
    ids = range(size)
    part = [slice(r * local, (r + 1) * local) for r in ids]
    copies_out = [
        pltpu.make_async_copy(out_hbm[r], w_out_ref.at[part[r]], sems.at[0, r]) for r in ids
    ]
    copies_gu = [pltpu.make_async_copy(gu_hbm[r], w_gu_ref.at[r], sems.at[1, r]) for r in ids]
    copies_down = [
        pltpu.make_async_copy(down_hbm[r], w_down_ref.at[r], sems.at[2, r]) for r in ids
    ]

    def heads_copy(r, i):
        other = jnp.bitwise_xor(t, r)
        return remote(
            blocks_ref.at[other * subs + i],
            arrived_ref.at[r, i],
            sends.at[r, i],
            recvs.at[r, i],
            (d, other),
        )

    own_copy = pltpu.make_async_copy(blocks_ref.at[pl.ds(t * subs, subs)], arrived_ref.at[0], keep)

    @pl.when(first)
    def _():
        own_copy.start()
        for copy in copies_out:
            copy.start()
        greet(1, (1, 2, 3), d, t)
        for i in range(subs):
            for r in (2, 3, 1):
                heads_copy(r, i).start()
        own_copy.wait()
        for r in ids:
            copies_gu[r].start()
            copies_down[r].start()
        for copy in copies_out:
            copy.wait()

    for r in ids[1:]:
        heads_copy(r, index).wait_recv()
        heads_copy(r, index).wait_send()
    for r in ids:
        heads_ref[r] = arrived_ref[r, index]
    heads_out = jnp.concatenate([arrived_ref[r, index] for r in ids], 0)
    attn = mm(heads_out, w_out_ref[...], 0, 0)
    gain_one, gain_two, shift_one, shift_two = (norm_ref[i : i + 1, :] for i in range(4))
    normed_one, unit_one, inverse_one = norm_forward(
        x_ref[...].astype(F32) + attn, gain_one, shift_one
    )
    normed = normed_one.astype(BF)
    normed_t_ref[...] = normed_one.T.astype(BF)
    branch = jnp.zeros(normed_one.shape, F32)
    for r in ids:

        @pl.when(first)
        def _():
            copies_gu[r].wait()
            copies_down[r].wait()

        both = mm(normed, w_gu_ref[r], 1, 0)
        gate = both[:, :inner]
        up = both[:, inner:]
        sig = jax.nn.sigmoid(gate)
        swish = gate * sig
        hidden = (swish * up).astype(BF)
        swish_ref[r] = swish
        slope_ref[r] = up * sig * (1.0 + gate * (1.0 - sig))
        hidden_ref[r] = hidden
        branch = branch + mm(hidden, w_down_ref[r], 1, 1)
    result, unit_two, inverse_two = norm_forward(normed_one + branch, gain_two, shift_two)
    result_ref[...] = result.astype(BF)
    grad_two, d_gain_two, d_shift_two = norm_backward(
        cot_ref[...].astype(F32), unit_two, inverse_two, gain_two
    )
    d_branch = grad_two.astype(BF)
    d_branch_t_ref[...] = grad_two.T.astype(BF)
    back = grad_two
    for r in ids:
        grad_hidden = mm(d_branch, w_down_ref[r], 1, 0)
        d_gate = (grad_hidden * slope_ref[r]).astype(BF)
        d_up = (grad_hidden * swish_ref[r]).astype(BF)
        d_gu_ref[r, :, :inner] = d_gate
        d_gu_ref[r, :, inner:] = d_up
        back = back + mm(jnp.concatenate([d_gate, d_up], 1), w_gu_ref[r], 1, 1)
    grad_one, d_gain_one, d_shift_one = norm_backward(back, unit_one, inverse_one, gain_one)
    grad_one_ref[...] = grad_one
    d_attn_t = grad_one.T.astype(BF)
    d_attn_t_ref[...] = d_attn_t
    d_heads = mm(w_out_ref[...], d_attn_t, 1, 0).astype(BF)
    for r in ids:
        d_heads_ref[r] = d_heads[part[r]]

    @pl.when(first)
    def _():
        norm_grad_ref[...] = jnp.zeros_like(norm_grad_ref)

    for i, grad in enumerate((d_gain_one, d_gain_two, d_shift_one, d_shift_two)):
        norm_grad_ref[i : i + 1, :] += grad


def middle(x_own, cot_own, norms, o_blocks, w_out_parts, gu_parts, down_parts):
    rows, width = x_own.shape
    size = len(gu_parts)
    local = o_blocks.shape[1]
    inner = down_parts[0].shape[1]
    block = pl.BlockSpec((BLOCK, width), lambda i: (i, 0))
    turned = pl.BlockSpec((width, BLOCK), lambda i: (0, i))
    anywhere = pl.BlockSpec(memory_space=pl.ANY)
    shape = jax.ShapeDtypeStruct
    return pl.pallas_call(
        functools.partial(middle_kernel, size),
        grid=(rows // BLOCK,),
        in_specs=[block, block, pl.BlockSpec(norms.shape, lambda i: (0, 0))]
        + [anywhere] * (1 + 3 * size),
        out_specs=[
            block,
            block,
            pl.BlockSpec((size, local, BLOCK), lambda i: (0, 0, i)),
            pl.BlockSpec((size, local, BLOCK), lambda i: (0, 0, i)),
            turned,
            turned,
            turned,
            pl.BlockSpec((size, BLOCK, inner), lambda i: (0, i, 0)),
            pl.BlockSpec((size, BLOCK, 2 * inner), lambda i: (0, i, 0)),
            pl.BlockSpec((8, width), lambda i: (0, 0)),
        ],
        out_shape=[
            shape((rows, width), BF),
            shape((rows, width), F32),
            shape((size, local, rows), BF),
            shape((size, local, rows), BF),
            shape((width, rows), BF),
            shape((width, rows), BF),
            shape((width, rows), BF),
            shape((size, rows, inner), BF),
            shape((size, rows, 2 * inner), BF),
            shape((8, width), F32),
        ],
        scratch_shapes=[
            pltpu.VMEM((size * local, width), BF),
            pltpu.VMEM((size, width, 2 * inner), BF),
            pltpu.VMEM((size, width, inner), BF),
            pltpu.VMEM((size, BLOCK, inner), F32),
            pltpu.VMEM((size, BLOCK, inner), F32),
            pltpu.VMEM((size, rows // BLOCK, local, BLOCK), BF),
            pltpu.SemaphoreType.DMA((3, size)),
            pltpu.SemaphoreType.DMA((size, rows // BLOCK)),
            pltpu.SemaphoreType.DMA((size, rows // BLOCK)),
            pltpu.SemaphoreType.DMA,
        ],
        compiler_params=pltpu.CompilerParams(
            collective_id=2, has_side_effects=True, vmem_limit_bytes=VMEM_LIMIT
        ),
        cost_estimate=pl.CostEstimate(
            flops=2 * rows * width * (6 * size * inner + 2 * size * local),
            bytes_accessed=40 << 20,
            transcendentals=rows * size * inner,
        ),
        name="middle",
    )(x_own, cot_own, norms, o_blocks, *w_out_parts, *gu_parts, *down_parts)


def weight_grads_tile(
    normed_t_ref, d_branch_t_ref, d_attn_t_ref, hidden_ref, d_gu_ref, heads_ref, norm_ref, store
):
    inner = hidden_ref.shape[2]
    local = heads_ref.shape[1]
    width = normed_t_ref.shape[0]
    store(0, 2 * inner, mm(normed_t_ref[...], d_gu_ref[0], 1, 0))
    store(2 * inner, 3 * inner, mm(d_branch_t_ref[...], hidden_ref[0], 1, 0))
    d_out = mm(d_attn_t_ref[...], heads_ref[0], 1, 1)
    norm = norm_ref[...].T
    spare = -(local + norm.shape[1]) % 128
    tail = jnp.concatenate([d_out, norm, jnp.zeros((width, spare), F32)], 1)
    store(3 * inner, 3 * inner + tail.shape[1], tail)


def weight_grads_kernel(*refs):
    out_ref = refs[-1]

    def store(low, high, value):
        out_ref[0, :, low:high] = value.astype(BF)

    weight_grads_tile(*refs[:-1], store)


def weight_grads(odd, normed_t, d_branch_t, d_attn_t, hidden, d_gu, heads, norm_grads):
    size, rows, inner = hidden.shape
    local = heads.shape[1]
    width = normed_t.shape[0]
    wide = 3 * inner + local + norm_grads.shape[0]
    wide = (wide + 127) // 128 * 128
    flat = pl.BlockSpec((width, rows), lambda i: (0, 0))
    pick = lambda i: (2 * i + odd, 0, 0)
    return pl.pallas_call(
        weight_grads_kernel,
        grid=(size // 2,),
        in_specs=[
            flat,
            flat,
            flat,
            pl.BlockSpec((1, rows, inner), pick),
            pl.BlockSpec((1, rows, 2 * inner), pick),
            pl.BlockSpec((1, local, rows), pick),
            pl.BlockSpec(norm_grads.shape, lambda i: (0, 0)),
        ],
        out_specs=pl.BlockSpec((1, width, wide), lambda i: (i, 0, 0)),
        out_shape=jax.ShapeDtypeStruct((size // 2, width, wide), BF),
        compiler_params=pltpu.CompilerParams(vmem_limit_bytes=VMEM_LIMIT),
        cost_estimate=pl.CostEstimate(
            flops=size * rows * width * (3 * inner + local), bytes_accessed=20 << 20, transcendentals=0
        ),
        name="weight_grads",
    )(normed_t, d_branch_t, d_attn_t, hidden, d_gu, heads, norm_grads)


def grads_kernel(groups, size, match_ref, *refs):
    tile_refs = refs[:7]
    (
        d_heads_ref,
        result_ref,
        pair_ref,
        do_ref,
        home_ref,
        over_ref,
        sent_ref,
        got_ref,
        own_ref,
        spare_ref,
        s_grad,
        r_grad,
        s_heads,
        r_heads,
        sends,
        recvs,
        s_over,
        r_over,
        keep,
    ) = refs[7:]
    step = pl.program_id(0)
    d = lax.axis_index("dp")
    t = lax.axis_index("tensor")
    chunks, _, sub, width = own_ref.shape
    core = (d, jnp.bitwise_xor(t, 1))
    body = Spread(home_ref, (sends, recvs), groups, d, t)
    extra = Spread(over_ref, (s_over, r_over), groups, d, t)

    def heads_copy(r):
        return remote(
            d_heads_ref.at[r],
            do_ref.at[r],
            s_heads.at[r],
            r_heads.at[r],
            (d, jnp.bitwise_xor(t, r)),
        )

    def grad_copy(i):
        return remote(sent_ref.at[i], got_ref.at[i], s_grad.at[i], r_grad.at[i], core)

    def own_copy(c):
        return pltpu.make_async_copy(own_ref.at[c, d], home_ref.at[0, d, c], keep.at[c])

    load = pltpu.make_async_copy(result_ref, own_ref, keep.at[chunks])
    own_heads = pltpu.make_async_copy(d_heads_ref.at[0], do_ref.at[0], keep.at[chunks + 1])
    own_over = pltpu.make_async_copy(spare_ref.at[d], over_ref.at[0, d], keep.at[chunks + 2])

    def pass_on(c):
        own_copy(c).wait()
        for k in range(groups):
            if k > 0:
                body.arrival(own_ref.at[c, 0], k, (c,), (c,)).wait_recv()
            body.across(k, (c,), (c,)).start()
            body.beside(0, k, (c,), (c,)).start()

    def pass_far(c):
        for k in range(groups):
            body.across(k, (c,), (c,)).wait_recv()
            body.beside(2, k, (c,), (c,)).start()

    @pl.when(step == 0)
    def _():
        load.start()
        own_heads.start()
        greet(groups, (1, 2, 3), d, t)
        for r in (2, 3, 1):
            heads_copy(r).start()
        load.wait()
        for c in range(chunks):
            own_copy(c).start()
            for k in range(1, groups):
                body.arrival(own_ref.at[c, lax.rem(d + k, groups)], k, (c,), (c,)).start()
        last = [own_ref[chunks - 1, g, sub - 16 :, :].astype(F32)[15:16] for g in range(groups)]
        for to in range(groups):
            spare = last[0] * match_ref[to]
            for g in range(1, groups):
                spare = spare + last[g] * match_ref[g * groups + to]
            spare_ref[to] = spare.astype(BF)
        own_over.start()
        for k in range(1, groups):
            extra.arrival(spare_ref.at[lax.rem(d + k, groups)], k, (), ()).start()

    for c in range(2):

        @pl.when(step == c + 2)
        def _():
            pass_on(c)

    @pl.when(step < 2)
    def _():
        def store(low, high, value):
            sent_ref[step, :, low:high] = value.astype(BF)

        weight_grads_tile(*tile_refs, store)
        grad_copy(step).start()

    @pl.when(step >= 2)
    def _():
        grad_copy(step - 2).wait_recv()

        def store(low, high, value):
            other = got_ref[step - 2, :, low:high].astype(F32)
            pair_ref[0, :, low:high] = (value + other).astype(BF)

        weight_grads_tile(*tile_refs, store)

    @pl.when(step == size - 1)
    def _():
        for c in range(2, chunks):
            pass_on(c)
        own_over.wait()
        for k in range(groups):
            if k > 0:
                extra.arrival(spare_ref.at[0], k, (), ()).wait_recv()
            extra.across(k, (), ()).start()
            extra.beside(0, k, (), ()).start()
        for c in range(chunks):
            pass_far(c)
        for k in range(groups):
            extra.across(k, (), ()).wait_recv()
            extra.beside(2, k, (), ()).start()
        own_heads.wait()
        for r in range(1, size):
            heads_copy(r).wait_recv()
            heads_copy(r).wait_send()
        for i in range(2):
            grad_copy(i).wait_send()
        for k in range(groups):
            for c in range(chunks):
                body.beside(0, k, (c,), (c,)).wait_recv()
                body.beside(2, k, (c,), (c,)).wait_recv()
                if k > 0:
                    body.arrival(own_ref.at[c, 0], k, (c,), (c,)).wait_send()
                body.across(k, (c,), (c,)).wait_send()
                body.beside(0, k, (c,), (c,)).wait_send()
                body.beside(2, k, (c,), (c,)).wait_send()
            extra.beside(0, k, (), ()).wait_recv()
            extra.beside(2, k, (), ()).wait_recv()
            if k > 0:
                extra.arrival(spare_ref.at[0], k, (), ()).wait_send()
            extra.across(k, (), ()).wait_send()
            extra.beside(0, k, (), ()).wait_send()
            extra.beside(2, k, (), ()).wait_send()


def grads(
    match, groups, normed_t, d_branch_t, d_attn_t, hidden, d_gu, heads, norm_grads, d_heads, result
):
    size, rows, inner = hidden.shape
    local = heads.shape[1]
    width = normed_t.shape[0]
    chunks = rows // BLOCK
    sub = BLOCK // groups
    wide = 3 * inner + (local + norm_grads.shape[0] + 127) // 128 * 128
    flat = pl.BlockSpec((width, rows), lambda i: (0, 0))
    pick = lambda i: (jnp.where(i < 2, 2 * i + 1, 2 * i - 4), 0, 0)
    anywhere = pl.BlockSpec(memory_space=pl.ANY)
    dma = pltpu.SemaphoreType.DMA
    return pl.pallas_call(
        functools.partial(grads_kernel, groups, size),
        grid=(size,),
        in_specs=[
            pl.BlockSpec(memory_space=pltpu.SMEM),
            flat,
            flat,
            flat,
            pl.BlockSpec((1, rows, inner), pick),
            pl.BlockSpec((1, rows, 2 * inner), pick),
            pl.BlockSpec((1, local, rows), pick),
            pl.BlockSpec(norm_grads.shape, lambda i: (0, 0)),
            anywhere,
            anywhere,
        ],
        out_specs=[
            pl.BlockSpec((1, width, wide), lambda i: (jnp.maximum(i - 2, 0), 0, 0)),
            anywhere,
            anywhere,
            anywhere,
        ],
        out_shape=[
            jax.ShapeDtypeStruct((2, width, wide), BF),
            jax.ShapeDtypeStruct(d_heads.shape, BF),
            jax.ShapeDtypeStruct((size, groups, chunks, sub, width), BF),
            jax.ShapeDtypeStruct((size, groups, 1, width), BF),
        ],
        scratch_shapes=[
            pltpu.VMEM((2, width, wide), BF),
            pltpu.VMEM((2, width, wide), BF),
            pltpu.VMEM((chunks, groups, sub, width), BF),
            pltpu.VMEM((groups, 1, width), BF),
            dma((2,)),
            dma((2,)),
            dma((size,)),
            dma((size,)),
            dma((4, groups, chunks)),
            dma((4, groups, chunks)),
            dma((4, groups)),
            dma((4, groups)),
            dma((chunks + 3,)),
        ],
        compiler_params=pltpu.CompilerParams(
            collective_id=3, has_side_effects=True, vmem_limit_bytes=VMEM_LIMIT
        ),
        cost_estimate=pl.CostEstimate(
            flops=2 * size * rows * width * (3 * inner + local),
            bytes_accessed=80 << 20,
            transcendentals=0,
        ),
        name="grads",
    )(
        match,
        normed_t,
        d_branch_t,
        d_attn_t,
        hidden,
        d_gu,
        heads,
        norm_grads,
        d_heads,
        result.reshape(chunks, groups, sub, width),
    )


def swap(array, size, step):
    return lax.ppermute(array, "tensor", [(i, i ^ step) for i in range(size)])


def gather_members(own):
    size = lax.axis_size("tensor")
    across = swap(own, size, 2)
    return [own, swap(own, size, 1), across, swap(across, size, 1)]


def exchange_members(pieces):
    size = lax.axis_size("tensor")
    return [pieces[0]] + [swap(pieces[r], size, r) for r in range(1, size)]


def reduce_members(pieces):
    size = lax.axis_size("tensor")
    near = swap(pieces[1], size, 1)
    far = swap(pieces[3], size, 1)
    other = (pieces[2].astype(F32) + far.astype(F32)).astype(BF)
    across = swap(other, size, 2)
    return pieces[0].astype(F32) + near.astype(F32) + across.astype(F32)


def route_kernel(groups, size, send_ref, over_ref, out_ref, over_out_ref, sends, recvs, keep):
    d = lax.axis_index("dp")
    t = lax.axis_index("tensor")
    greet(groups, (1, 2), d, t)
    spread = Spread(out_ref, (sends, recvs), groups, d, t)
    own = pltpu.make_async_copy(send_ref.at[d], out_ref.at[0, d], keep.at[0])
    own_over = pltpu.make_async_copy(over_ref.at[d], over_out_ref.at[d], keep.at[1])
    own.start()
    own_over.start()

    def over_copy(k):
        to = lax.rem(d + k, groups)
        return remote(
            over_ref.at[to], over_out_ref.at[d], sends.at[4, k], recvs.at[4, k], (to, t)
        )

    for k in range(1, groups):
        spread.arrival(send_ref.at[lax.rem(d + k, groups)], k, (), ()).start()
    for k in range(1, groups):
        over_copy(k).start()
    own.wait()
    for k in range(groups):
        if k > 0:
            spread.arrival(send_ref.at[0], k, (), ()).wait_recv()
        spread.across(k, (), ()).start()
        spread.beside(0, k, (), ()).start()
        if k > 0:
            spread.across(k - 1, (), ()).wait_recv()
            spread.beside(2, k - 1, (), ()).start()
    spread.across(groups - 1, (), ()).wait_recv()
    spread.beside(2, groups - 1, (), ()).start()
    own_over.wait()
    for k in range(groups):
        spread.beside(0, k, (), ()).wait_recv()
        spread.beside(2, k, (), ()).wait_recv()
        if k > 0:
            over_copy(k).wait_recv()
            over_copy(k).wait_send()
            spread.arrival(send_ref.at[0], k, (), ()).wait_send()
        spread.across(k, (), ()).wait_send()
        spread.beside(0, k, (), ()).wait_send()
        spread.beside(2, k, (), ()).wait_send()


def route(send, over, size):
    groups = send.shape[0]
    anywhere = pl.BlockSpec(memory_space=pl.ANY)
    return pl.pallas_call(
        functools.partial(route_kernel, groups, size),
        in_specs=[anywhere, anywhere],
        out_specs=[anywhere, anywhere],
        out_shape=[
            jax.ShapeDtypeStruct((size,) + send.shape, BF),
            jax.ShapeDtypeStruct(over.shape, BF),
        ],
        scratch_shapes=[
            pltpu.SemaphoreType.DMA((5, groups)),
            pltpu.SemaphoreType.DMA((5, groups)),
            pltpu.SemaphoreType.DMA((2,)),
        ],
        compiler_params=pltpu.CompilerParams(collective_id=0, has_side_effects=True),
        cost_estimate=pl.CostEstimate(flops=0, bytes_accessed=60 << 20, transcendentals=0),
        name="route",
    )(send, over)


def settle_kernel(
    groups,
    size,
    match_ref,
    back_ref,
    one_ref,
    gq_ref,
    home_ref,
    over_ref,
    sum_ref,
    far_ref,
    near_ref,
    pair_ref,
    other_ref,
    own_ref,
    spare_ref,
    gqr_ref,
    sends,
    recvs,
    s_over,
    r_over,
    s_sum,
    r_sum,
    s_gq,
    r_gq,
    keep,
):
    d = lax.axis_index("dp")
    t = lax.axis_index("tensor")
    chunks, _, sub, width = own_ref.shape
    greet(groups, (1, 2), d, t)
    core = (d, jnp.bitwise_xor(t, 1))
    chip = (d, jnp.bitwise_xor(t, 2))

    def rows(c):
        return pl.ds(c * BLOCK, BLOCK)

    def far(c):
        return remote(back_ref.at[3, rows(c)], far_ref.at[c], s_sum.at[0, c], r_sum.at[0, c], core)

    def near(c):
        return remote(back_ref.at[1, rows(c)], near_ref.at[c], s_sum.at[1, c], r_sum.at[1, c], core)

    def other(c):
        return remote(pair_ref.at[c], other_ref.at[c], s_sum.at[2, c], r_sum.at[2, c], chip)

    def gq(k):
        to = lax.rem(d + k, groups)
        return remote(gq_ref.at[to], gqr_ref.at[d], s_gq.at[k], r_gq.at[k], (to, t))

    for c in range(chunks):
        far(c).start()
    for c in range(chunks):
        near(c).start()
    for c in range(chunks):
        far(c).wait_recv()
        pair = back_ref[2, rows(c), :].astype(F32) + far_ref[c].astype(F32)
        pair_ref[c] = pair.astype(BF)
        other(c).start()
    own_gq = pltpu.make_async_copy(gq_ref.at[d], gqr_ref.at[d], keep.at[chunks])
    own_gq.start()

    body = Spread(home_ref, (sends, recvs), groups, d, t)
    extra = Spread(over_ref, (s_over, r_over), groups, d, t)

    def own_copy(c):
        return pltpu.make_async_copy(own_ref.at[c, d], home_ref.at[0, d, c], keep.at[c])

    own_over = pltpu.make_async_copy(spare_ref.at[d], over_ref.at[0, d], keep.at[chunks + 1])

    def pass_on(c):
        own_copy(c).wait()
        for k in range(groups):
            if k > 0:
                body.arrival(own_ref.at[c, 0], k, (c,), (c,)).wait_recv()
            body.across(k, (c,), (c,)).start()
            body.beside(0, k, (c,), (c,)).start()

    def pass_far(c):
        for k in range(groups):
            body.across(k, (c,), (c,)).wait_recv()
            body.beside(2, k, (c,), (c,)).start()

    for c in range(chunks):
        near(c).wait_recv()
        partial = (
            one_ref[rows(c), :] + back_ref[0, rows(c), :].astype(F32) + near_ref[c].astype(F32)
        )
        other(c).wait_recv()
        done = (partial + other_ref[c].astype(F32)).astype(BF)
        for g in range(groups):
            own_ref[c, g] = done[g * sub : (g + 1) * sub]
        own_copy(c).start()
        for k in range(1, groups):
            body.arrival(own_ref.at[c, lax.rem(d + k, groups)], k, (c,), (c,)).start()
        if c == chunks - 1:
            last = [
                own_ref[c, g, sub - 16 :, :].astype(F32)[15:16] for g in range(groups)
            ]
            for to in range(groups):
                spare = last[0] * match_ref[to]
                for g in range(1, groups):
                    spare = spare + last[g] * match_ref[g * groups + to]
                spare_ref[to] = spare.astype(BF)
            own_over.start()
            for k in range(1, groups):
                extra.arrival(spare_ref.at[lax.rem(d + k, groups)], k, (), ()).start()
        if c == 0:
            for k in range(1, groups):
                gq(k).start()
        else:
            pass_on(c - 1)
    pass_on(chunks - 1)
    own_over.wait()
    for k in range(groups):
        if k > 0:
            extra.arrival(spare_ref.at[0], k, (), ()).wait_recv()
        extra.across(k, (), ()).start()
        extra.beside(0, k, (), ()).start()
    own_gq.wait()
    total = gqr_ref[d].astype(F32)
    for k in range(1, groups):
        gq(k).wait_recv()
        total = total + gqr_ref[lax.rem(d - k + groups, groups)].astype(F32)
    sum_ref[...] = total
    for c in range(chunks):
        pass_far(c)
    for k in range(groups):
        extra.across(k, (), ()).wait_recv()
        extra.beside(2, k, (), ()).start()
    for c in range(chunks):
        far(c).wait_send()
        near(c).wait_send()
        other(c).wait_send()
    for k in range(groups):
        for c in range(chunks):
            body.beside(0, k, (c,), (c,)).wait_recv()
            body.beside(2, k, (c,), (c,)).wait_recv()
            if k > 0:
                body.arrival(own_ref.at[c, 0], k, (c,), (c,)).wait_send()
            body.across(k, (c,), (c,)).wait_send()
            body.beside(0, k, (c,), (c,)).wait_send()
            body.beside(2, k, (c,), (c,)).wait_send()
        extra.beside(0, k, (), ()).wait_recv()
        extra.beside(2, k, (), ()).wait_recv()
        if k > 0:
            gq(k).wait_send()
            extra.arrival(spare_ref.at[0], k, (), ()).wait_send()
        extra.across(k, (), ()).wait_send()
        extra.beside(0, k, (), ()).wait_send()
        extra.beside(2, k, (), ()).wait_send()


def settle(match, back_rel, grad_one, grad_qkv):
    size, rows, width = back_rel.shape
    groups, part, local = grad_qkv.shape
    chunks = rows // BLOCK
    sub = BLOCK // groups
    anywhere = pl.BlockSpec(memory_space=pl.ANY)
    vmem = pl.BlockSpec(memory_space=pltpu.VMEM)
    dma = pltpu.SemaphoreType.DMA
    buffer = pltpu.VMEM((chunks, BLOCK, width), BF)
    return pl.pallas_call(
        functools.partial(settle_kernel, groups, size),
        in_specs=[pl.BlockSpec(memory_space=pltpu.SMEM), vmem, vmem, anywhere],
        out_specs=[anywhere, anywhere, vmem],
        out_shape=[
            jax.ShapeDtypeStruct((size, groups, chunks, sub, width), BF),
            jax.ShapeDtypeStruct((size, groups, 1, width), BF),
            jax.ShapeDtypeStruct((part, local), F32),
        ],
        scratch_shapes=[
            buffer,
            buffer,
            buffer,
            buffer,
            pltpu.VMEM((chunks, groups, sub, width), BF),
            pltpu.VMEM((groups, 1, width), BF),
            pltpu.VMEM((groups, part, local), BF),
            dma((4, groups, chunks)),
            dma((4, groups, chunks)),
            dma((4, groups)),
            dma((4, groups)),
            dma((3, chunks)),
            dma((3, chunks)),
            dma((groups,)),
            dma((groups,)),
            dma((chunks + 2,)),
        ],
        compiler_params=pltpu.CompilerParams(
            collective_id=1, has_side_effects=True, vmem_limit_bytes=VMEM_LIMIT
        ),
        cost_estimate=pl.CostEstimate(flops=0, bytes_accessed=150 << 20, transcendentals=0),
        name="settle",
    )(match, back_rel, grad_one, grad_qkv)


ROWS = 32


def unpack_kernel(info, home_ref, over_ref, out_ref, src_ref, dst_ref):
    size, groups, share, _ = home_ref.shape
    rows = out_ref.shape[0]
    slots = size * share
    me = info[0, 0]

    @pl.loop(0, size)
    def _(part):
        source = jnp.bitwise_xor(part, me)
        at = pl.ds(pl.multiple_of(ROWS + part * share, 8), share)
        for g in range(groups):
            src_ref[g, at, :] = home_ref[source, g].astype(F32)

    last = jnp.bitwise_xor(size - 1, me)
    for g in range(groups):
        src_ref[g, ROWS + slots : ROWS + slots + 1, :] = over_ref[last, g].astype(F32)
    row_ids = lax.broadcasted_iota(jnp.int32, (ROWS, 1), 0)

    @pl.loop(0, info.shape[1] - 1)
    def _(j):
        low = info[0, 1 + j]
        count = info[1, 1 + j]
        group = info[2, 1 + j]
        first = info[3, 1 + j]

        @pl.loop(low // ROWS, (low + count + ROWS - 1) // ROWS)
        def _(i):
            start = i * ROWS + first - low + ROWS
            offset = jnp.bitwise_and(start, 7)
            loaded = src_ref[group, pl.ds(pl.multiple_of(start - offset, 8), ROWS + 8), :]
            moved = pltpu.roll(loaded, ROWS + 8 - offset, 0)[:ROWS]
            at = pl.ds(pl.multiple_of(i * ROWS, ROWS), ROWS)
            dst_ref[at, :] = jnp.where(row_ids >= low - i * ROWS, moved, dst_ref[at, :])

    out_ref[...] = dst_ref[:rows, :].astype(BF)


def unpack(info, home, over):
    size, groups, share, width = home.shape
    rows = size * groups * share
    whole = lambda *shape: pl.BlockSpec(shape, lambda i, info: (0,) * len(shape))
    return pl.pallas_call(
        unpack_kernel,
        grid_spec=pltpu.PrefetchScalarGridSpec(
            num_scalar_prefetch=1,
            grid=(1,),
            in_specs=[whole(*home.shape), whole(*over.shape)],
            out_specs=whole(rows, width),
            scratch_shapes=[
                pltpu.VMEM((groups, size * share + 4 * ROWS, width), F32),
                pltpu.VMEM((rows + ROWS, width), F32),
            ],
        ),
        out_shape=jax.ShapeDtypeStruct((rows, width), BF),
        compiler_params=pltpu.CompilerParams(vmem_limit_bytes=VMEM_LIMIT),
        cost_estimate=pl.CostEstimate(flops=0, bytes_accessed=30 << 20, transcendentals=0),
        name="unpack",
    )(info, home, over)


def spans(offset, length, source, groups):
    low = (offset - source + groups - 1) // groups
    high = (offset + length - source + groups - 1) // groups
    return low, high - low


def local(tokens, cotangent, lengths, dealing, w_qkv, w_out, w_gu, w_down, gains, shifts):
    groups = lax.axis_size("dp")
    member = lax.axis_index("dp")
    size = lax.axis_size("tensor")
    me = lax.axis_index("tensor")
    rows = tokens.shape[0]
    width = tokens.shape[2]
    slots = rows // groups
    share = slots // size
    own_rows = rows // size
    subs = own_rows // BLOCK
    sub = share // subs
    i32 = jnp.int32

    seq_count = lengths.shape[0]
    count_up = jnp.arange(seq_count, dtype=i32)
    offsets = jnp.sum(jnp.where(count_up[None, :] < count_up[:, None], lengths[None, :], 0), 1)
    chosen = dealing[:, None] == count_up[None, :]
    dealt_len = jnp.sum(jnp.where(chosen, lengths[None, :], 0), 1).reshape(groups, 2)
    dealt_off = jnp.sum(jnp.where(chosen, offsets[None, :], 0), 1).reshape(groups, 2)
    group_ids = jnp.arange(groups, dtype=i32)

    low_a, count_a = spans(dealt_off[:, 0], dealt_len[:, 0], member, groups)
    low_b, count_b = spans(dealt_off[:, 1], dealt_len[:, 1], member, groups)
    fused = sub % 16 == 0
    body_slots = me * share + jnp.arange(share, dtype=i32)[None, :]

    def pick(slot):
        found = jnp.where(
            slot < count_a[:, None], low_a[:, None] + slot, (low_b - count_a)[:, None] + slot
        )
        return jnp.clip(found, 0, rows - 1).reshape(-1)

    picked = jnp.concatenate([pick(body_slots), pick(jnp.full((1, 1), slots, i32))])

    def pack(array):
        taken = jnp.take(array.reshape(rows, width), picked, axis=0)
        return (
            taken[: groups * share].reshape(groups, share, width),
            taken[groups * share :].reshape(groups, 1, width),
        )

    def over_dp(pair):
        return tuple(
            lax.all_to_all(a, "dp", split_axis=0, concat_axis=0, tiled=True) for a in pair
        )

    send_x = pack(tokens)
    send_c = pack(cotangent)
    far_out, far_down = swap(w_out.T, size, 2), swap(w_down, size, 2)
    if fused:
        recv_x, over_x = route(*send_x, size)
    else:
        recv_x, over_x = over_dp(send_x)
        recv_x = jnp.stack(gather_members(recv_x))
    send_c, recv_x, far_out, far_down = lax.optimization_barrier(
        (send_c, recv_x, far_out, far_down)
    )
    recv_c, over_c = over_dp(send_c)

    mine = group_ids == member
    pick_group = lambda table: jnp.sum(jnp.where(mine[:, None], table, 0), 0)
    my_len = pick_group(dealt_len)
    my_off = pick_group(dealt_off)
    glow_a, gcount_a = spans(my_off[0], my_len[0], group_ids, groups)
    glow_b, gcount_b = spans(my_off[1], my_len[1], group_ids, groups)
    filled = gcount_a + gcount_b
    hole = filled < slots
    over = filled > slots
    before = group_ids[None, :] < group_ids[:, None]
    hole_rank = jnp.sum(jnp.where(before & hole[None, :], 1, 0), 1)
    over_rank = jnp.sum(jnp.where(before & over[None, :], 1, 0), 1)
    match = hole[:, None] & over[None, :] & (hole_rank[:, None] == over_rank[None, :])
    last_token = (glow_b - gcount_a + slots) * groups + group_ids
    hole_token = jnp.sum(jnp.where(match, last_token[None, :], 0), 1)
    match_bf = match.astype(BF)
    relative = jnp.bitwise_xor(jnp.arange(size, dtype=i32), me)

    place_ids = jnp.arange(share, dtype=i32)

    def fill(received, over, last):
        spare = jnp.dot(match_bf, over[:, 0], preferred_element_type=F32).astype(BF)
        fix = last[:, None, None] & (hole[:, None] & (place_ids == share - 1)[None, :])[None]
        body = jnp.where(fix[..., None], spare[None, :, None, :], received)
        body = body.reshape(-1, groups, subs, sub, width).transpose(0, 2, 1, 3, 4)
        return body.reshape(-1, own_rows, width)

    shape = (size * subs, groups, sub)
    block_id = lax.broadcasted_iota(i32, shape, 0)
    source_id = lax.broadcasted_iota(i32, shape, 1)
    slot_id = block_id * sub + lax.broadcasted_iota(i32, shape, 2)
    spread = lambda vec: vec[None, :, None]
    in_a = slot_id < spread(gcount_a)
    token_id = (
        jnp.where(in_a, spread(glow_a), spread(glow_b - gcount_a)) + slot_id
    ) * groups + source_id
    token_id = jnp.where(spread(hole) & (slot_id == slots - 1), spread(hole_token), token_id)
    positions = (token_id - jnp.where(in_a, my_off[0], my_off[1])).reshape(rows)
    segment = jnp.where(in_a, 0, 1).astype(F32).reshape(rows)
    frequency = 1000.0 ** (-(jnp.arange(HALF, dtype=F32) * 2.0) / HEAD)
    angles = frequency[:, None] * positions.astype(F32)[None, :]
    cosine = jnp.cos(angles)
    sine = jnp.sin(angles)
    seg_row = segment[None, :]
    seg_col = segment[:, None]
    first_b = (my_len[0] + BLOCK - 1) // BLOCK
    info = jnp.stack([my_len[0] // BLOCK, first_b, me]).astype(i32)

    x_rel = fill(recv_x, over_x, relative == size - 1)
    x_own = x_rel[0]
    local_width = w_qkv.shape[2]
    w_qkv_t = w_qkv.transpose(1, 2, 0).reshape(3 * local_width, width)
    x_rel, near_gu = lax.optimization_barrier((x_rel, w_gu.reshape(width, -1)))
    far_gu = swap(near_gu, size, 2)
    q, k, v, k_rows, v_rows = project(x_rel, w_qkv_t, cosine, sine, me[None])
    o_blocks, lse = attend(info, q, k_rows, v, seg_row, seg_col)
    o_blocks, far_gu, recv_c = lax.optimization_barrier((o_blocks, far_gu, recv_c))

    spread_parts = lambda near, far: [near, swap(near, size, 1), far, swap(far, size, 1)]
    w_out_parts = spread_parts(w_out.T, far_out)
    down_parts = spread_parts(w_down, far_down)
    gu_parts = spread_parts(near_gu, far_gu)
    cot_own = fill(recv_c[None], over_c, (me == size - 1)[None])[0]
    norms = jnp.concatenate([gains.T, shifts.T], 0)
    (
        result_own,
        grad_one,
        d_heads,
        heads_own,
        normed_t,
        d_branch_t,
        d_attn_t,
        hidden,
        d_gu,
        norm_grads,
    ) = middle(x_own, cot_own, norms, o_blocks, w_out_parts, gu_parts, down_parts)
    grad_args = (normed_t, d_branch_t, d_attn_t, hidden, d_gu, heads_own, norm_grads)
    match_all = match.astype(F32).reshape(-1)
    if fused:
        pair, do_rel, home_result, over_result = grads(
            match_all, groups, *grad_args, d_heads, result_own
        )
        home_result = (home_result.reshape(size, groups, share, width), over_result)
    else:
        sent_grads = weight_grads(1, *grad_args)
        kept_grads = weight_grads(0, *grad_args)
        pair = (kept_grads.astype(F32) + swap(sent_grads, size, 1).astype(F32)).astype(BF)
        do_rel = jnp.stack(exchange_members([d_heads[r] for r in range(size)]))

    d_qkv_t = attend_back(
        info, q, k_rows, k, v_rows, o_blocks, do_rel, lse, seg_row, seg_col, cosine, sine
    )
    back_rel, grad_qkv = project_back(d_qkv_t, x_rel, w_qkv_t, me[None])
    grad_qkv = grad_qkv.reshape(groups, width // groups, 3 * local_width)

    pair = lax.psum_scatter(pair, "dp", scatter_dimension=1, tiled=True)
    spot_low = jnp.stack([low_a, low_b], 1).reshape(-1)
    spot_count = jnp.stack([count_a, count_b], 1).reshape(-1)
    spot_first = jnp.stack([jnp.zeros_like(count_a), count_a], 1).reshape(-1)
    spot_group = jnp.arange(seq_count, dtype=i32) // 2
    table = jnp.stack([spot_low, spot_count, spot_group, spot_first])
    table = jnp.sum(jnp.where(chosen[None], table[:, :, None], 0), 1)
    table = jnp.concatenate([jnp.full((4, 1), me, i32), table], 1)

    def send_back(own):
        body = own.reshape(subs, groups, sub, width).transpose(1, 0, 2, 3)
        body = body.reshape(groups, share, width)
        spare = lax.dot_general(
            match_bf, body[:, share - 1], (((0,), (0,)), ((), ())), preferred_element_type=F32
        ).astype(BF)
        pair = over_dp((body, spare.reshape(groups, 1, width)))
        return tuple(jnp.stack(gather_members(a)) for a in pair)

    if fused:
        home_input, home_over, qkv_sum = settle(
            match_all, back_rel, grad_one, grad_qkv
        )
        home_input = (home_input.reshape(size, groups, share, width), home_over)
        pair, home_input = lax.optimization_barrier((pair, home_input))
    else:
        home_result = send_back(result_own)
        input_own = grad_one + reduce_members([back_rel[r] for r in range(size)])
        home_input = send_back(input_own.astype(BF))
        grad_qkv = lax.all_to_all(grad_qkv, "dp", split_axis=0, concat_axis=0, tiled=True)
        qkv_sum = jnp.sum(grad_qkv.astype(F32), 0)
    qkv_sum = qkv_sum.reshape(-1, 3, local_width)
    summed = pair[0].astype(F32) + swap(pair[1], size, 2).astype(F32)
    inner = w_down.shape[1]
    gu_sum = summed[:, : 2 * inner].reshape(-1, 2, inner)
    down_sum = summed[:, 2 * inner : 3 * inner]
    out_sum = summed[:, 3 * inner : 3 * inner + local_width]
    norm_sum = summed[:, 3 * inner + local_width : 3 * inner + local_width + 4]
    norm_sum = lax.dynamic_slice_in_dim(
        norm_sum, me * (norm_sum.shape[0] // size), norm_sum.shape[0] // size, 0
    )
    if fused:
        arrange = functools.partial(unpack, table)
    else:
        row_ids = jnp.arange(rows, dtype=i32)[None, :]
        here = (row_ids >= spot_low[:, None]) & (row_ids < (spot_low + spot_count)[:, None])
        slot = row_ids + (spot_first - spot_low)[:, None]
        home_part = jnp.minimum(slot // share, size - 1)
        flat = (jnp.bitwise_xor(home_part, me) * groups + spot_group[:, None]) * (share + 1)
        flat = jnp.sum(jnp.where(here, flat + slot - home_part * share, 0), 0)

        def arrange(home, over):
            every = jnp.concatenate([home, over], 2).reshape(-1, width)
            return jnp.take(every, flat, axis=0)

    result = arrange(*home_result).reshape(rows, 1, width)
    input_grad = arrange(*home_input).reshape(rows, 1, width)
    return (
        result,
        input_grad,
        qkv_sum,
        out_sum,
        gu_sum,
        down_sum,
        norm_sum[:, :2],
        norm_sum[:, 2:],
    )


def solution(mesh):
    placed = (
        P(None, "dp", None),
        P(None, "dp", None),
        P(),
        P(),
        P(None, None, "tensor"),
        P(None, "tensor"),
        P(None, None, "tensor"),
        P(None, "tensor"),
        P(),
        P(),
    )
    return jax.shard_map(
        local,
        mesh=mesh,
        in_specs=placed,
        out_specs=(
            P(None, "dp", None),
            P(None, "dp", None),
            P("dp", None, "tensor"),
            P("dp", "tensor"),
            P("dp", None, "tensor"),
            P("dp", "tensor"),
            P(("dp", "tensor"), None),
            P(("dp", "tensor"), None),
        ),
        check_vma=False,
    )
```

time: 728 us -> 508 us (0.70)
  Pallas kernels: 170 us -> 383 us
  waiting for transfers between devices: 140 us -> 0.39 us
  matrix products: 97.3 us -> 1.73 us
  local copies, waits for them, and re-layouts: 129 us -> 48.3 us
  other arithmetic: 77 us -> 24.9 us
  blocking collectives: 37.8 us -> 0 us
  starting transfers between devices: 45.3 us -> 22.5 us
    pallas_call x0 -> x7, Pallas kernels: none -> 283 us  [the longest x1 106 us: settle(): pl.pallas_call(functools.partial(settle_kernel, groups, size), in_specs=[...]
    dot_general x39 -> x2, matrix products: 97.3 us -> 1.73 us  [fill(): spare = jnp.dot(match_bf, over[:, 0], preferred_element_type=F32).astype(BF)]
    all_to_all x3 -> x2, waiting for transfers between devices: 76.3 us -> 0.32 us  [over_dp(): lax.all_to_all(a, 'dp', split_axis=0, concat_axis=0, tiled=True)]
    ppermute x30 -> x10, waiting for transfers between devices: 63.6 us -> 0.03 us  [swap(): return lax.ppermute(array, 'tensor', [(i, i ^ step) for i in range(size)])]
    pallas_call x1, Pallas kernels: 81.1 us -> 32.9 us  [attend(): pl.pallas_call(attend_kernel, grid_spec=pltpu.PrefetchScalarGridSpec(num_...]
    all_to_all x1 -> x0, blocking collectives: 37.8 us -> none  [local(): lax.all_to_all(send_c, 'dp', split_axis=0, concat_axis=0, tiled=True)]
    gather x4 -> x2, local copies, waits for them, and re-layouts: 50.1 us -> 15.4 us  [pack(): taken = jnp.take(array.reshape(rows, width), picked, axis=0)]
    convert_element_type x10 -> x1, other arithmetic: 29.7 us -> 1.27 us  [local(): match_all = match.astype(F32).reshape(-1)]
  transfers between devices with their start and end apart: 34 -> 13, of which waited for: 7 -> 1; matrix products, arithmetic and copies ran while one was open for 31% -> 13% of each run, Pallas kernels for 24% -> 56%
where the time goes in v2:
time: 508 us; the launch traced here: 501 us
  Pallas kernels  383 us (75%)
  local copies, waits for them, and re-layouts  48.3 us (10%)
  other arithmetic  24.9 us (5%)
  starting transfers between devices  22.5 us (4%)
  between operations  20.6 us (4%)
    pallas_call x1, Pallas kernels, settle(): pl.pallas_call(functools.partial(settle_kernel, groups, size), in_specs=[...  106 us
    pallas_call x1, Pallas kernels, attend_back(): pl.pallas_call(attend_back_kernel, grid_spec=pltpu.PrefetchScalarGridSpec...  58.7 us
    pallas_call x1, Pallas kernels, grads(): pl.pallas_call(functools.partial(grads_kernel, groups, size), grid=(size,...  55.3 us
    pallas_call x1, Pallas kernels, middle(): pl.pallas_call(functools.partial(middle_kernel, size), grid=(rows // BLOC...  46.9 us
    pallas_call x1, Pallas kernels, route(): pl.pallas_call(functools.partial(route_kernel, groups, size), in_specs=[a...  41.8 us
    pallas_call x1, Pallas kernels, attend(): pl.pallas_call(attend_kernel, grid_spec=pltpu.PrefetchScalarGridSpec(num_...  32.9 us
    pallas_call x2, Pallas kernels, unpack(): pl.pallas_call(unpack_kernel, grid_spec=pltpu.PrefetchScalarGridSpec(num_...  21.3 us
    all_to_all x2, starting transfers between devices, over_dp(): lax.all_to_all(a, 'dp', split_axis=0, concat_axis=0, tiled=True)  15.9 us
  transfers between devices with their start and end apart: 13, of which 1 were waited for; matrix products, arithmetic and copies ran while one was open for 13% of the time, Pallas kernels for 56%

profile of v2, /device:TPU:0, one launch (start us, length us, event | category | flops | bytes accessed | tf_op | source)
XLA Modules:
  0.0 501.1 jit_solution(3442874233344324244)
XLA Ops:
  7.2 3.0 collective-permute-start
  10.3 0.8 select_reduce_fusion.3
  11.0 0.9 select_reduce_fusion.1
  12.1 0.8 subtract_reduce_fusion
  14.8 1.7 iota_add_fusion.1
  18.8 7.7 %gather_fusion = bf16[776,768]{1,0:T(8,128)(2,1)} fusion(bf16[3072,768]{1,0:T(8,128)(2,1)} %bitcast.53, s32[1024]{0:T(1024)S(1)} %pad_clamp_fusion), kind=kCustom, calls=%fused_computation.clone | custom fusion | bytes 2386976 | tf_op jit(solution)/shard_map/jit(_take)/gather | solution.py:1319
  26.5 7.7 %gather_fusion.1 = bf16[776,768]{1,0:T(8,128)(2,1)} fusion(bf16[3072,768]{1,0:T(8,128)(2,1)} %bitcast.54, s32[1024]{0:T(1024)S(1)} %pad_clamp_fusion), kind=kCustom, calls=%fused_computation.1.clone | custom fusion | bytes 2386976 | tf_op jit(solution)/shard_map/jit(_take)/gather | solution.py:1319
  34.2 1.9 broadcast_select_fusion.2
  36.1 0.6 slice_bitcast_fusion.2
  36.7 0.7 select_convert_fusion
  37.5 0.6 broadcast_and_fusion.1
  38.1 1.3 select_reduce_fusion.4
  39.4 1.2 and_select_fusion.2
  40.6 1.1 slice.93
  44.9 1.1 slice.95
  46.0 1.4 copy.63.over_ref
  47.4 1.8 copy.75
  49.5 0.9 add.490
  50.4 0.7 broadcast_in_dim.231
  51.2 0.7 broadcast_in_dim.233
  51.9 0.7 lt.119
  52.8 0.7 and.400
  53.6 41.8 %route.1 = (bf16[4,8,96,768]{3,2,1,0:T(8,128)(2,1)}, bf16[8,1,768]{2,1,0:T(2,128)(2,1)}) custom-call(bf16[8,96,768]{2,1,0:T(8,128)(2,1)} %bitcast.59, bf16[8,1,768]{2,1,0:T(2,128)(2,1)} %copy.63.over_ref), custom_call_target="tpu_custom_call" | custom-call | bytes 62914560 | tf_op jit(solution)/shard_map/route/pallas_call | solution.py:998
  95.5 0.9 convolution_convert_fusion.1
  96.9 1.8 subtract_convert_fusion
  98.7 2.7 broadcast_select_fusion
  101.4 2.7 copy.86
  104.1 1.5 collective-permute-start.2
  105.6 0.6 pad_add_fusion.3.info
  106.3 0.7 convert_element_type.59.segrow_ref
  106.9 2.8 convert_element_type.66.segcol_ref
  109.7 9.9 %all-to-all-start.1 = ((bf16[8,96,768]{2,1,0:T(8,128)(2,1)}), bf16[8,96,768]{2,1,0:T(8,128)(2,1)S(1)}, u32[]{:S(2)}, u32[]{:S(2)}) async-start(bf16[8,96,768]{2,1,0:T(8,128)(2,1)} %bitcast.8), calls=%async_computation.1 | async-start | bytes 2359296 | tf_op jit(solution)/shard_map/all_to_all | solution.py:1327
  119.6 3.0 multiply_sine_fusion
  122.7 8.2 %project.1 = (bf16[192,3072]{1,0:T(8,128)(2,1)}, bf16[192,3072]{1,0:T(8,128)(2,1)}, bf16[240,3072]{1,0:T(8,128)(2,1)}, bf16[3,3072,64]{2,1,0:T(8,128)(2,1)}, bf16[3,3072,64]{2,1,0:T(8,128)(2,1)}) custom-call(s32[1]{0:T(128)} %bitcast.16.me_ref, bf16[4,768,768]{2,1,0:T(8,128)(2,1)} %bitcast.56, bf16[576,768]{1,0:T(8,128)(2,1)} %bitcast.75, ...), custom_call_target="tpu_custom_call" | custom-call | flops 2717908992 | bytes 8388608 | tf_op jit(solution)/shard_map/project/pallas_call | solution.py:67
  130.9 32.9 %attend.1 = (bf16[12,192,256]{2,1,0:T(8,128)(2,1)}, f32[3,3072]{1,0:T(4,128)}) custom-call(s32[3]{0:T(128)} %pad_add_fusion.3.info, bf16[192,3072]{1,0:T(8,128)(2,1)} %get-tuple-element.55.q_ref, bf16[3,3072,64]{2,1,0:T(8,128)(2,1)} %get-tuple-element.56.k_ref.krow_ref, bf16[240,3072]{1,0:T(8,128)(2,1)} %get-tuple-element.57.v_ref, ...), custom_call_target="tpu_custom_call" | custom-call | flops 14495514624 | bytes 8388608 | tf_op jit(solution)/shard_map/attend/pallas_call | solution.py:152
  165.5 1.2 reduce.8
  166.7 1.3 reshape.719
  168.0 6.0 %all-to-all-start = ((bf16[8,2,384]{2,1,0:T(2,128)(2,1)}), bf16[8,2,384]{2,1,0:T(2,128)(2,1)S(1)}, u32[]{:S(2)}, u32[]{:S(2)}) async-start(bf16[8,2,384]{2,1,0:T(2,128)(2,1)} %reshape.719), calls=%async_computation | async-start | bytes 24576 | tf_op jit(solution)/shard_map/all_to_all | solution.py:1327
  174.1 1.3 pad_maximum_fusion.refs_2_
  175.4 1.3 convert_element_type.64
  176.7 1.2 reshape.691.match_ref
  177.9 2.4 slice.97
  180.6 0.6 reshape.720
  181.2 0.9 convolution_convert_fusion
  182.1 0.8 broadcast_select_fusion.3
  183.0 1.1 copy.67
  184.1 0.7 copy-done.16
  184.8 46.9 %middle.1 = (bf16[768,768]{1,0:T(8,128)(2,1)}, f32[768,768]{1,0:T(8,128)}, bf16[4,192,768]{2,1,0:T(8,128)(2,1)}, bf16[4,192,768]{2,1,0:T(8,128)(2,1)}, bf16[768,...) custom-call(bf16[768,768]{1,0:T(8,128)(2,1)} %bitcast.69, ...), custom_call_target="tpu_custom_call" | custom-call | flops 23555211264 | bytes 41943040 | tf_op jit(solution)/shard_map/middle/pallas_call | solution.py:594
  231.7 55.3 %grads.1 = (bf16[2,768,2560]{2,1,0:T(8,128)(2,1)}, bf16[4,192,768]{2,1,0:T(8,128)(2,1)}, bf16[4,8,3,32,768]{4,3,2,1,0:T(8,128)(2,1)}, bf16[4,8,1,768]{3,2,1,0:T(2,128)(2,1)}) custom-call(f32[64]{0:T(128)} %reshape.691.match_ref, bf16[768,768]{1,0:T(8,128)(2,1)} %get-tuple-element.66.refs_0_, bf16[768,768]{1,0:T(8,128)(2,1)} %get-tuple-element.67.refs_1_, ...), custom_call_target="tpu_custom_call" | custom-call | flops 11777605632 | bytes 83886080 | tf_op jit(solution)/shard_map/grads/pallas_call | solution.py:862
  287.1 0.6 copy-done.6
  287.9 58.7 %attend_back.1.d_ref = bf16[4,576,768]{2,1,0:T(8,128)(2,1)} custom-call(s32[3]{0:T(128)} %pad_add_fusion.3.info, bf16[192,3072]{1,0:T(8,128)(2,1)} %get-tuple-element.55.q_ref, bf16[3,3072,64]{2,1,0:T(8,128)(2,1)} %get-tuple-element.56.k_ref.krow_ref, bf16[192,3072]{1,0:T(8,128)(2,1)} %get-tuple-element.78.k_ref, ...), custom_call_target="tpu_custom_call" | custom-call | flops 36238786560 | bytes 16777216 | tf_op jit(solution)/shard_map/attend_back/pallas_call | solution.py:282
  346.6 11.4 %project_back.1 = (bf16[4,768,768]{2,1,0:T(8,128)(2,1)}, bf16[768,576]{1,0:T(8,128)(2,1)}) custom-call(s32[1]{0:T(128)} %bitcast.16.me_ref, bf16[4,576,768]{2,1,0:T(8,128)(2,1)} %attend_back.1.d_ref, bf16[4,768,768]{2,1,0:T(8,128)(2,1)} %bitcast.58, bf16[576,768]{1,0:T(8,128)(2,1)} %bitcast.76), custom_call_target="tpu_custom_call" | custom-call | flops 5435817984 | bytes 15728640 | tf_op jit(solution)/shard_map/project_back/pallas_call | solution.py:341
  358.0 106.3 %settle.1 = (bf16[4,8,3,32,768]{4,3,2,1,0:T(8,128)(2,1)}, bf16[4,8,1,768]{3,2,1,0:T(2,128)(2,1)}, f32[96,576]{1,0:T(8,128)}) custom-call(f32[64]{0:T(128)} %reshape.691.match_ref, bf16[4,768,768]{2,1,0:T(8,128)(2,1)} %get-tuple-element.82.back_ref, f32[768,768]{1,0:T(8,128)} %get-tuple-element.83.one_ref, bf16[8,96,576]{2,1,0:T(8,128)(2,1)} %bitcast.72), custom_call_target="tpu_custom_call" | custom-call | bytes 157286400 | tf_op jit(solution)/shard_map/settle/pallas_call | solution.py:1179
  464.3 1.1 slice_bitcast_fusion
  465.4 0.8 collective-permute-start.9
  466.6 0.7 concatenate.9.info
  467.4 0.9 copy.70
  468.3 10.6 %unpack.2 = bf16[3072,768]{1,0:T(8,128)(2,1)} custom-call(s32[4,17]{1,0:T(4,128)} %concatenate.9.info, bf16[4,8,96,768]{3,2,1,0:T(8,128)(2,1)} %bitcast.61, bf16[4,8,1,768]{3,2,1,0:T(2,128)(2,1)} %get-tuple-element.76.over_ref), custom_call_target="tpu_custom_call" | custom-call | bytes 31457280 | tf_op jit(solution)/shard_map/unpack/pallas_call | solution.py:1258
  478.9 10.7 %unpack.3 = bf16[3072,768]{1,0:T(8,128)(2,1)} custom-call(s32[4,17]{1,0:T(4,128)} %concatenate.9.info, bf16[4,8,96,768]{3,2,1,0:T(8,128)(2,1)} %bitcast.62, bf16[4,8,1,768]{3,2,1,0:T(2,128)(2,1)} %get-tuple-element.88.over_ref), custom_call_target="tpu_custom_call" | custom-call | bytes 31457280 | tf_op jit(solution)/shard_map/unpack/pallas_call | solution.py:1258
  489.7 0.6 slice.98
  490.4 0.7 slice.100
  491.2 1.2 reshape.690
  492.5 0.6 copy.71
  493.1 0.6 copy.72
  (97 shorter events, 6.3 us)
Async XLA Ops:
  7.2 91.6 %collective-permute-start = (bf16[192,768]{1,0:T(8,128)(2,1)}, bf16[192,768]{1,0:T(8,128)(2,1)}, u32[]{:S(2)}, u32[]{:S(2)}) collective-permute-start(bf16[192,768]{1,0:T(8,128)(2,1)} %bitcast.77), channel_id=1, source_target_pairs={{0,2},{1,3},{2,0},{3,1},{4,6},{5,7},{6,4},{7,5},{8,10},{9,11},{10,... | collective-permute-start | bytes 884744 | tf_op jit(solution)/shard_map/ppermute | solution.py:928
  10.2 88.6 %collective-permute-start.1 = (bf16[768,768]{1,0:T(8,128)(2,1)}, bf16[768,768]{1,0:T(8,128)(2,1)}, u32[]{:S(2)}, u32[]{:S(2)}) collective-permute-start(bf16[768,768]{1,0:T(8,128)(2,1)} %refs_12_.1), channel_id=1, source_target_pairs={{0,2},{1,3},{2,0},{3,1},{4,6},{5,7},{6,4},{7,5},{8,10},{9,11},{10,... | collective-permute-start | bytes 3538952 | tf_op jit(solution)/shard_map/ppermute | solution.py:928
  12.0 14.5 %copy-start.5 = (s32[8,2]{1,0:T(8,128)}, s32[8,2]{1,0:T(8,128)S(1)}, u32[]{:S(2)}) copy-start(s32[8,2]{1,0:T(8,128)S(1)} %reshape.670) | copy-start | bytes 196
  16.6 20.1 %copy-start.11 = (s32[8]{0:T(128)}, s32[8]{0:T(128)S(1)}, u32[]{:S(2)}) copy-start(s32[8]{0:T(128)S(1)} %get-tuple-element.143) | copy-start | bytes 100
  18.4 19.7 %copy-start.12 = (pred[8]{0:T(512)(128)(4,1)}, pred[8]{0:T(512)(128)(4,1)S(1)}, u32[]{:S(2)}) copy-start(pred[8]{0:T(512)(128)(4,1)S(1)} %get-tuple-element.149) | copy-start | bytes 28
  44.9 2.5 copy-start
  47.4 1.8 copy-start.14
  49.2 46.2 %copy-start.13 = (pred[8,96]{1,0:T(8,128)(4,1)S(1)}, pred[8,96]{1,0:T(8,128)(4,1)}, u32[]{:S(2)}) copy-start(pred[8,96]{1,0:T(8,128)(4,1)} %get-tuple-element.160) | copy-start | bytes 2308
  49.2 46.3 %copy-start.8 = (pred[8,8]{1,0:T(8,128)(4,1)S(1)}, pred[8,8]{1,0:T(8,128)(4,1)}, u32[]{:S(2)}) copy-start(pred[8,8]{1,0:T(8,128)(4,1)} %get-tuple-element.140) | copy-start | bytes 196
  101.4 2.7 copy-start.1
  101.4 4.8 copy-start.3
  104.1 59.7 %collective-permute-start.2 = (bf16[768,1536]{1,0:T(8,128)(2,1)S(1)}, bf16[768,1536]{1,0:T(8,128)(2,1)}, u32[]{:S(2)}, u32[]{:S(2)}) collective-permute-start(bf16[768,1536]{1,0:T(8,128)(2,1)S(1)} %bitcast.67), channel_id=1, source_target_pairs={{0,2},{1,3},{2,0},{3,1},{4,6},{5,7},{6,4},{7,5},{8,10},{9,11},{10,... | collective-permute-start | bytes 7077896 | tf_op jit(solution)/shard_map/ppermute | solution.py:928
  109.7 54.1 %all-to-all-start.1 = ((bf16[8,96,768]{2,1,0:T(8,128)(2,1)}), bf16[8,96,768]{2,1,0:T(8,128)(2,1)S(1)}, u32[]{:S(2)}, u32[]{:S(2)}) async-start(bf16[8,96,768]{2,1,0:T(8,128)(2,1)} %bitcast.8), calls=%async_computation.1 | async-start | bytes 2359296 | tf_op jit(solution)/shard_map/all_to_all | solution.py:1327
  122.7 61.4 %collective-permute-start.5 = (bf16[768,1536]{1,0:T(8,128)(2,1)S(1)}, bf16[768,1536]{1,0:T(8,128)(2,1)}, u32[]{:S(2)}, u32[]{:S(2)}) collective-permute-start(bf16[768,1536]{1,0:T(8,128)(2,1)S(1)} %bitcast.68), channel_id=1, source_target_pairs={{0,1},{1,0},{2,3},{3,2},{4,5},{5,4},{6,7},{7,6},{8,9},{9,8},{10,11... | collective-permute-start | bytes 7077896 | tf_op jit(solution)/shard_map/ppermute | solution.py:928
  163.8 20.3 %collective-permute-start.6 = (bf16[768,1536]{1,0:T(8,128)(2,1)}, bf16[768,1536]{1,0:T(8,128)(2,1)}, u32[]{:S(2)}, u32[]{:S(2)}) collective-permute-start(bf16[768,1536]{1,0:T(8,128)(2,1)} %collective-permute-done.2.refs_10_), channel_id=1, source_target_pairs={{0,1},{1,0},{2,3},{3,2},{4,5},{5,4},{6,7},{7,6},{8,9},{9,8},{10,11... | collective-permute-start | bytes 7077896 | tf_op jit(solution)/shard_map/ppermute | solution.py:928
  164.4 19.7 %collective-permute-start.7 = (bf16[768,768]{1,0:T(8,128)(2,1)}, bf16[768,768]{1,0:T(8,128)(2,1)}, u32[]{:S(2)}, u32[]{:S(2)}) collective-permute-start(bf16[768,768]{1,0:T(8,128)(2,1)} %refs_12_.1), channel_id=1, source_target_pairs={{0,1},{1,0},{2,3},{3,2},{4,5},{5,4},{6,7},{7,6},{8,9},{9,8},{10,11... | collective-permute-start | bytes 3538952 | tf_op jit(solution)/shard_map/ppermute | solution.py:928
  164.4 19.6 %collective-permute-start.8 = (bf16[768,768]{1,0:T(8,128)(2,1)}, bf16[768,768]{1,0:T(8,128)(2,1)}, u32[]{:S(2)}, u32[]{:S(2)}) collective-permute-start(bf16[768,768]{1,0:T(8,128)(2,1)} %collective-permute-done.1.refs_14_), channel_id=1, source_target_pairs={{0,1},{1,0},{2,3},{3,2},{4,5},{5,4},{6,7},{7,6},{8,9},{9,8},{10,11... | collective-permute-start | bytes 3538952 | tf_op jit(solution)/shard_map/ppermute | solution.py:928
  164.9 16.4 %collective-permute-start.3 = (bf16[192,768]{1,0:T(8,128)(2,1)}, bf16[192,768]{1,0:T(8,128)(2,1)}, u32[]{:S(2)}, u32[]{:S(2)}) collective-permute-start(bf16[192,768]{1,0:T(8,128)(2,1)} %bitcast.78), channel_id=1, source_target_pairs={{0,1},{1,0},{2,3},{3,2},{4,5},{5,4},{6,7},{7,6},{8,9},{9,8},{10,11... | collective-permute-start | bytes 884744 | tf_op jit(solution)/shard_map/ppermute | solution.py:928
  168.0 12.6 %all-to-all-start = ((bf16[8,2,384]{2,1,0:T(2,128)(2,1)}), bf16[8,2,384]{2,1,0:T(2,128)(2,1)S(1)}, u32[]{:S(2)}, u32[]{:S(2)}) async-start(bf16[8,2,384]{2,1,0:T(2,128)(2,1)} %reshape.719), calls=%async_computation | async-start | bytes 24576 | tf_op jit(solution)/shard_map/all_to_all | solution.py:1327
  174.1 290.2 %reduce-scatter.2.cloned.1.call-start = ((), (), s32[]{:S(2)}) async-start(), calls=%async_computation.3 | async-start | bytes 8847360 | tf_op jit(solution)/shard_map/reduce_scatter | solution.py:1438
  181.2 2.8 collective-permute-start.4
  184.1 0.7 copy-start.16
  287.0 0.7 copy-start.6
  287.1 0.7 copy-start.7
  287.1 0.8 copy-start.9
  287.1 0.7 copy-start.10
  358.0 108.5 %copy-start.15 = (s32[16]{0:T(128)S(1)}, s32[16]{0:T(128)}, u32[]{:S(2)}) copy-start(s32[16]{0:T(128)} %param.15) | copy-start | bytes 196
  464.3 3.0 copy-start.4
  465.4 24.2 %collective-permute-start.9 = (bf16[96,2560]{1,0:T(8,128)(2,1)S(1)}, bf16[96,2560]{1,0:T(8,128)(2,1)S(1)}, u32[]{:S(2)}, u32[]{:S(2)}) collective-permute-start(bf16[96,2560]{1,0:T(8,128)(2,1)S(1)} %slice_bitcast_fusion), channel_id=1, source_target_pairs={{0,2},{1,3},{2,0},{3,1},{4,6},{5,7},{6,4},{7,5},{8,10},{9,11},{10,... | collective-permute-start | bytes 1474568 | tf_op jit(solution)/shard_map/ppermute | solution.py:928
  478.9 10.7 %copy-start.2 = (bf16[2,96,2560]{2,1,0:T(8,128)(2,1)S(1)}, bf16[2,96,2560]{2,1,0:T(8,128)(2,1)}, u32[]{:S(2)}) copy-start(bf16[2,96,2560]{2,1,0:T(8,128)(2,1)} %reduce-scatter.2.cloned.1.call-done) | copy-start | bytes 2949124
Sparse Core Ops, SparseCore 0:
  287.2 168.9 reduce-scatter.1

commit v3 on v2

--- a/solution.py
+++ b/solution.py
@@ -26,16 +26,232 @@
     return lax.dot_general(a, b, (((ca,), (cb,)), ((), ())), preferred_element_type=F32)
 
 
-def project_kernel(me_ref, x_ref, w_ref, cos_ref, sin_ref, q_ref, k_ref, v_ref, krow_ref, vrow_ref):
-    cols = x_ref.shape[1]
+HOLES = 8
+
+
+def extra_of(source, offset, length, groups):
+    turned = lax.rem(source - offset + groups, groups)
+    return turned, jnp.where(turned < lax.rem(length, groups), 1, 0)
+
+
+def pack_kernel(
+    groups,
+    size,
+    lengths,
+    dealing,
+    ids,
+    x_ref,
+    c_ref,
+    send_x_ref,
+    over_x_ref,
+    send_c_ref,
+    meta_ref,
+    table_ref,
+    match_ref,
+):
+    d = ids[0]
+    t = ids[1]
+    rows = x_ref.shape[0]
+    slots = rows // groups
+    share = slots // size
+    window = (share + 31) // 16 * 16
+
+    def lookup(q):
+        seq = dealing[q]
+        offset = lax.fori_loop(0, seq, lambda j, total: total + lengths[j], jnp.int32(0))
+        return seq, offset, lengths[seq]
+
+    def span(offset, length):
+        low = lax.div(offset - d + groups - 1, groups)
+        return low, lax.div(offset + length - d + groups - 1, groups) - low
+
+    def load(ref, row, count):
+        start = jnp.clip(jnp.bitwise_and(row, -16), 0, rows - window)
+        shift = jnp.clip(row - start, 1 - window, window - 1)
+        loaded = ref[pl.ds(pl.multiple_of(start, 16), window), :].astype(F32)
+        return pltpu.roll(loaded, lax.rem(window - shift, window), 0)[:count]
+
+    table_ref[0, 0] = t
+    slot_ids = lax.broadcasted_iota(jnp.int32, (share, 1), 0) + t * share
+
+    @pl.loop(0, groups)
+    def _(g):
+        seq_a, off_a, len_a = lookup(2 * g)
+        seq_b, off_b, len_b = lookup(2 * g + 1)
+        low_a, count_a = span(off_a, len_a)
+        low_b, count_b = span(off_b, len_b)
+        for seq, entries in ((seq_a, (low_a, count_a, g, 0)), (seq_b, (low_b, count_b, g, count_a))):
+            for i, entry in enumerate(entries):
+                table_ref[i, 1 + seq] = jnp.int32(entry)
+        shifted = low_b - count_a
+        for ref, out_ref in ((x_ref, send_x_ref), (c_ref, send_c_ref)):
+            first = load(ref, low_a + t * share, share)
+            second = load(ref, shifted + t * share, share)
+            out_ref[g, :share] = jnp.where(slot_ids < count_a, first, second).astype(BF)
+        over_x_ref[g] = load(x_ref, shifted + slots, 1).astype(BF)
+        spare = send_c_ref.shape[1] - share
+        send_c_ref[g, share:] = load(c_ref, shifted + slots, spare).astype(BF)
+
+    _, off_a, len_a = lookup(2 * d)
+    _, off_b, len_b = lookup(2 * d + 1)
+    off_a = lax.rem(off_a, groups)
+    off_b = lax.rem(off_b, groups)
+    meta_ref[0] = lax.div(len_a, BLOCK)
+    meta_ref[1] = lax.div(len_a + BLOCK - 1, BLOCK)
+    meta_ref[2] = t
+    meta_ref[3] = off_a
+    meta_ref[4] = off_b
+    meta_ref[5] = len_a
+    meta_ref[6] = jnp.int32(0)
+    meta_ref[7] = jnp.int32(0)
+
+    def counts(source):
+        first = lax.div(len_a, groups) + extra_of(source, off_a, len_a, groups)[1]
+        second = lax.div(len_b, groups) + extra_of(source, off_b, len_b, groups)[1]
+        return first, first + second
+
+    @pl.loop(0, groups)
+    def _(hole):
+        lacks = lambda source: jnp.where(counts(source)[1] < slots, 1, 0)
+        rank = lax.fori_loop(0, hole, lambda j, total: total + lacks(j), jnp.int32(0))
+        rank = jnp.where(lacks(hole) == 1, rank, -1)
+
+        def scan(source, carry):
+            seen, found = carry
+            over = jnp.where(counts(source)[1] > slots, 1, 0)
+            hit = (over == 1) & (seen == rank)
+            match_ref[hole * groups + source] = jnp.where(hit, jnp.float32(1.0), jnp.float32(0.0))
+            return seen + over, jnp.where(hit, source, found)
+
+        _, found = lax.fori_loop(0, groups, scan, (jnp.int32(0), jnp.int32(-1)))
+        source = jnp.maximum(found, 0)
+        position = (slots - counts(source)[0]) * groups + extra_of(source, off_b, len_b, groups)[0]
+        meta_ref[HOLES + hole] = jnp.where(found >= 0, position, -1)
+
+
+def pack(lengths, dealing, ids, x, cotangent, groups, size):
+    rows, width = x.shape
+    share = rows // groups // size
+    whole = lambda *shape: pl.BlockSpec(shape, lambda i, *refs: (0,) * len(shape))
+    smem = pl.BlockSpec(memory_space=pltpu.SMEM)
+    shapes = [(groups, share, width), (groups, 1, width), (groups, share + 16, width)]
+    return pl.pallas_call(
+        functools.partial(pack_kernel, groups, size),
+        grid_spec=pltpu.PrefetchScalarGridSpec(
+            num_scalar_prefetch=3,
+            grid=(1,),
+            in_specs=[whole(rows, width)] * 2,
+            out_specs=[whole(*shape) for shape in shapes] + [smem] * 3,
+        ),
+        out_shape=[jax.ShapeDtypeStruct(shape, BF) for shape in shapes]
+        + [
+            jax.ShapeDtypeStruct((HOLES + groups,), jnp.int32),
+            jax.ShapeDtypeStruct((4, 1 + lengths.shape[0]), jnp.int32),
+            jax.ShapeDtypeStruct((groups * groups,), F32),
+        ],
+        compiler_params=pltpu.CompilerParams(vmem_limit_bytes=VMEM_LIMIT),
+        cost_estimate=pl.CostEstimate(flops=0, bytes_accessed=20 << 20, transcendentals=0),
+        name="pack",
+    )(lengths, dealing, ids, x, cotangent)
+
+
+def place(row, groups):
+    sub = BLOCK // groups
+    inside = lax.rem(row, BLOCK)
+    return lax.div(inside, sub), lax.div(row, BLOCK) * sub + lax.rem(inside, sub)
+
+
+def count_first(meta, source, groups):
+    turned, extra = extra_of(source, meta[3], meta[5], groups)
+    return turned, lax.div(meta[5], groups) + extra
+
+
+def in_second(meta, row, groups):
+    source, slot = place(row, groups)
+    return jnp.where(slot < count_first(meta, source, groups)[1], 0, 1)
+
+
+def positions_of(meta, row, groups, slots):
+    source, slot = place(row, groups)
+    turned, count = count_first(meta, source, groups)
+    turned_b = lax.rem(source - meta[4] + groups, groups)
+    position = jnp.where(slot < count, slot * groups + turned, (slot - count) * groups + turned_b)
+    for g in range(groups):
+        fills = meta[HOLES + g]
+        here = (slot == slots - 1) & (source == g) & (fills >= 0)
+        position = jnp.where(here, fills, position)
+    return position
+
+
+def spare_row(match_ref, groups, hole, rows):
+    total = rows[0] * match_ref[hole * groups]
+    flag = match_ref[hole * groups]
+    for source in range(1, groups):
+        weight = match_ref[hole * groups + source]
+        total = total + rows[source] * weight
+        flag = flag + weight
+    return total, flag
+
+
+def project_kernel(
+    groups,
+    packed,
+    meta,
+    match_ref,
+    x_in_ref,
+    over_ref,
+    w_ref,
+    freq_ref,
+    q_ref,
+    k_ref,
+    v_ref,
+    krow_ref,
+    vrow_ref,
+    cos_ref,
+    sin_ref,
+    x_ref,
+    own_ref,
+):
+    index = pl.program_id(0)
+    parts = pl.num_programs(0)
+    share, width = x_ref.shape[1:]
     heads = q_ref.shape[0] // HEAD
-    width = heads * HEAD
+    local = heads * HEAD
+    sub = BLOCK // groups
+    if packed:
+        for i in range(share // BLOCK):
+            for g in range(groups):
+                base = i * BLOCK + g * sub
+                x_ref[0, base : base + sub, :] = x_in_ref[0, g, i * sub : (i + 1) * sub, :]
+
+        @pl.when(index == parts - 1)
+        def _():
+            rows = [over_ref[g].astype(F32) for g in range(groups)]
+            at_end = lax.broadcasted_iota(jnp.int32, (16, 1), 0) == 15
+            for g in range(groups):
+                end = share - BLOCK + (g + 1) * sub
+                spare, _ = spare_row(match_ref, groups, g, rows)
+                old = x_ref[0, end - 16 : end, :].astype(F32)
+                new = jnp.where(at_end & (meta[HOLES + g] >= 0), spare, old)
+                x_ref[0, end - 16 : end, :] = new.astype(BF)
+    else:
+        x_ref[...] = x_in_ref[...]
+
+    @pl.when(index == meta[2])
+    def _():
+        own_ref[...] = x_ref[0]
+
+    row = lax.broadcasted_iota(jnp.int32, (1, share), 1) + index * share
+    position = positions_of(meta, row, groups, parts * share // groups)
+    angles = freq_ref[...] * position.astype(F32)
+    cosine = jnp.cos(angles)
+    sine = jnp.sin(angles)
+    cos_ref[...] = cosine
+    sin_ref[...] = sine
     projected = mm(w_ref[...], x_ref[0], 1, 1)
-    cosine = cos_ref[...]
-    sine = sin_ref[...]
     for part, out_ref, scale in ((0, q_ref, HEAD ** (-0.5) / LOG_2), (1, k_ref, 1.0)):
         for head in range(heads):
-            base = part * width + head * HEAD
+            base = part * local + head * HEAD
             first = projected[base : base + HALF]
             second = projected[base + HALF : base + HEAD]
             turned = jnp.concatenate(
@@ -45,57 +261,70 @@
             if part == 1:
                 krow_ref[head] = turned.T.astype(BF)
     for head in range(heads):
-        base = 2 * width + head * HEAD
+        base = 2 * local + head * HEAD
         value = projected[base : base + HEAD]
-        rest = lax.broadcasted_iota(jnp.int32, (PADDED - HEAD, cols), 0) == 0
+        rest = lax.broadcasted_iota(jnp.int32, (PADDED - HEAD, share), 0) == 0
         v_ref[head * PADDED : (head + 1) * PADDED, :] = jnp.concatenate(
             [value, jnp.where(rest, 1.0, 0.0)], 0
         ).astype(BF)
         vrow_ref[head] = value.T.astype(BF)
 
 
-def project(x_rel, w_t, cosine, sine, me):
-    parts, share, width = x_rel.shape
+def project(meta, match, x_rel, over, w_t, freq, groups, packed):
+    parts = x_rel.shape[0]
+    width = x_rel.shape[-1]
+    share = x_rel.size // parts // width
     rows = parts * share
     local = w_t.shape[0] // 3
     heads = local // HEAD
-    flat = jax.ShapeDtypeStruct((local, rows), BF)
-    tall = jax.ShapeDtypeStruct((heads, rows, HEAD), BF)
-    wide_spec = pl.BlockSpec((local, share), lambda i, me: (0, i))
-    tall_spec = pl.BlockSpec((heads, share, HEAD), lambda i, me: (0, i, 0))
-    table_spec = pl.BlockSpec((HALF, share), lambda i, me: (0, i))
+    shape = jax.ShapeDtypeStruct
+    columns = lambda *lead: pl.BlockSpec(lead + (share,), lambda i, meta: (0,) * len(lead) + (i,))
+    tall_spec = pl.BlockSpec((heads, share, HEAD), lambda i, meta: (0, i, 0))
+    whole = lambda *shape: pl.BlockSpec(shape, lambda i, meta: (0,) * len(shape))
+    lead = x_rel.shape[1:]
     return pl.pallas_call(
-        project_kernel,
+        functools.partial(project_kernel, groups, packed),
         grid_spec=pltpu.PrefetchScalarGridSpec(
             num_scalar_prefetch=1,
             grid=(parts,),
             in_specs=[
-                pl.BlockSpec((1, share, width), lambda i, me: (jnp.bitwise_xor(i, me[0]), 0, 0)),
-                pl.BlockSpec((3 * local, width), lambda i, me: (0, 0)),
-                table_spec,
-                table_spec,
+                pl.BlockSpec(memory_space=pltpu.SMEM),
+                pl.BlockSpec(
+                    (1,) + lead, lambda i, meta: (jnp.bitwise_xor(i, meta[2]),) + (0,) * len(lead)
+                ),
+                whole(*over.shape),
+                whole(3 * local, width),
+                whole(HALF, 1),
             ],
             out_specs=[
-                wide_spec,
-                wide_spec,
-                pl.BlockSpec((heads * PADDED, share), lambda i, me: (0, i)),
+                columns(local),
+                columns(local),
+                columns(heads * PADDED),
                 tall_spec,
                 tall_spec,
+                columns(HALF),
+                columns(HALF),
+                pl.BlockSpec((1, share, width), lambda i, meta: (i, 0, 0)),
+                whole(share, width),
             ],
         ),
         out_shape=[
-            flat,
-            flat,
-            jax.ShapeDtypeStruct((heads * PADDED, rows), BF),
-            tall,
-            tall,
+            shape((local, rows), BF),
+            shape((local, rows), BF),
+            shape((heads * PADDED, rows), BF),
+            shape((heads, rows, HEAD), BF),
+            shape((heads, rows, HEAD), BF),
+            shape((HALF, rows), F32),
+            shape((HALF, rows), F32),
+            shape((parts, share, width), BF),
+            shape((share, width), BF),
         ],
         compiler_params=pltpu.CompilerParams(vmem_limit_bytes=VMEM_LIMIT),
         cost_estimate=pl.CostEstimate(
-            flops=2 * rows * width * 3 * local, bytes_accessed=8 << 20, transcendentals=0
+            flops=2 * rows * width * 3 * local, bytes_accessed=16 << 20, transcendentals=0
         ),
         name="project",
-    )(me, x_rel, w_t, cosine, sine)
+    )(meta, match, x_rel, over, w_t, freq)
 
 
 def visible(info, index, q_blocks, k_blocks, count):
@@ -109,21 +338,22 @@
     return plain_low, plain_high, jnp.where(pure, end_a, 0), jnp.where(pure, start_b, count)
 
 
-def attend_kernel(info, q_ref, k_ref, v_ref, segrow_ref, segcol_ref, o_ref, lse_ref, acc_ref):
+def attend_kernel(groups, info, q_ref, k_ref, v_ref, o_ref, lse_ref, acc_ref):
     index = pl.program_id(0)
     heads, rows, _ = k_ref.shape
     width = q_ref.shape[1]
     tall = v_ref.shape[0] // heads
     spans_ = visible(info, index, width // BLOCK, KEYS // BLOCK, rows // KEYS)
     acc_ref[...] = jnp.zeros_like(acc_ref)
-    segrow = segrow_ref[...]
+    query_ids = lax.broadcasted_iota(jnp.int32, (1, width), 1) + index * width
+    key_ids = lax.broadcasted_iota(jnp.int32, (KEYS, 1), 0)
     ids = range(heads)
 
     def step(masked, j, tops):
         keys = pl.ds(pl.multiple_of(j * KEYS, KEYS), KEYS)
         scores = [mm(k_ref[h, keys, :], q_ref[h * HEAD : (h + 1) * HEAD, :], 1, 0) for h in ids]
         if masked:
-            same = segcol_ref[keys, :] == segrow
+            same = in_second(info, key_ids + j * KEYS, groups) == in_second(info, query_ids, groups)
             scores = [jnp.where(same, s, NEGATIVE) for s in scores]
         new = [jnp.maximum(tops[h], jnp.max(scores[h], 0, keepdims=True)) for h in ids]
         weights = [jnp.exp2(scores[h] - new[h]).astype(BF) for h in ids]
@@ -146,11 +376,11 @@
         lse_ref[h : h + 1, :] = tops[h] + jnp.log2(total)
 
 
-def attend(info, q, k_rows, v, seg_row, seg_col):
+def attend(info, q, k_rows, v, groups):
     local, rows = q.shape
     heads = local // HEAD
     return pl.pallas_call(
-        attend_kernel,
+        functools.partial(attend_kernel, groups),
         grid_spec=pltpu.PrefetchScalarGridSpec(
             num_scalar_prefetch=1,
             grid=(rows // QUERIES,),
@@ -158,8 +388,6 @@
                 pl.BlockSpec((local, QUERIES), lambda i, info: (0, i)),
                 pl.BlockSpec((heads, rows, HEAD), lambda i, info: (0, 0, 0)),
                 pl.BlockSpec(v.shape, lambda i, info: (0, 0)),
-                pl.BlockSpec((1, QUERIES), lambda i, info: (0, i)),
-                pl.BlockSpec((rows, 1), lambda i, info: (0, 0)),
             ],
             out_specs=[
                 pl.BlockSpec((QUERIES // BLOCK, local, BLOCK), lambda i, info: (i, 0, 0)),
@@ -178,7 +406,7 @@
             transcendentals=heads * rows * rows // 2,
         ),
         name="attend",
-    )(info, q, k_rows, v, seg_row, seg_col)
+    )(info, q, k_rows, v)
 
 
 def unturn(grad, cosine, sine):
@@ -190,6 +418,7 @@
 
 
 def attend_back_kernel(
+    groups,
     info,
     q_ref,
     krow_ref,
@@ -198,8 +427,6 @@
     o_ref,
     do_ref,
     lse_ref,
-    segrow_ref,
-    segcol_ref,
     cos_ref,
     sin_ref,
     out_ref,
@@ -221,7 +448,8 @@
         dv_ref[...] = jnp.zeros_like(dv_ref)
 
     dq_ref[...] = jnp.zeros_like(dq_ref)
-    segrow = segrow_ref[...]
+    query_ids = lax.broadcasted_iota(jnp.int32, (1, BLOCK), 1) + index * BLOCK
+    key_ids = lax.broadcasted_iota(jnp.int32, (KEYS, 1), 0)
     delta = [
         jnp.sum(do_ref[0, p, :].astype(F32) * o_ref[0, p, :].astype(F32), 0, keepdims=True)
         for p in part
@@ -233,7 +461,7 @@
         scores = [mm(krow_ref[h, keys, :], q_ref[part[h], :], 1, 0) for h in ids]
         grad_soft = [mm(vrow_ref[h, keys, :], do_ref[0, part[h], :], 1, 0) for h in ids]
         if masked:
-            same = segcol_ref[keys, :] == segrow
+            same = in_second(info, key_ids + j * KEYS, groups) == in_second(info, query_ids, groups)
             scores = [jnp.where(same, s, NEGATIVE) for s in scores]
         soft = [jnp.exp2(scores[h] - lse_ref[h : h + 1, :]) for h in ids]
         grad_scores = [(soft[h] * (grad_soft[h] - delta[h])).astype(BF) for h in ids]
@@ -272,7 +500,7 @@
                 out_ref[j, base : base + HEAD, :] = dv_ref[part[h], columns].astype(BF)
 
 
-def attend_back(info, q, k_rows, k, v_rows, o, do, lse, seg_row, seg_col, cosine, sine):
+def attend_back(info, q, k_rows, k, v_rows, o, do, lse, cosine, sine, groups):
     parts = do.shape[0]
     local, rows = q.shape
     heads = local // HEAD
@@ -280,7 +508,7 @@
     each = blocks // parts
     whole = lambda *shape: pl.BlockSpec(shape, lambda i, info: (0,) * len(shape))
     return pl.pallas_call(
-        attend_back_kernel,
+        functools.partial(attend_back_kernel, groups),
         grid_spec=pltpu.PrefetchScalarGridSpec(
             num_scalar_prefetch=1,
             grid=(blocks,),
@@ -295,8 +523,6 @@
                     lambda i, info: (jnp.bitwise_xor(i // each, info[2]), 0, i % each),
                 ),
                 pl.BlockSpec((heads, BLOCK), lambda i, info: (0, i)),
-                pl.BlockSpec((1, BLOCK), lambda i, info: (0, i)),
-                whole(rows, 1),
                 whole(HALF, rows),
                 whole(HALF, rows),
             ],
@@ -315,10 +541,10 @@
             transcendentals=heads * rows * rows // 2,
         ),
         name="attend_back",
-    )(info, q, k_rows, k, v_rows, o, do, lse, seg_row, seg_col, cosine, sine)
-
-
-def project_back_kernel(me_ref, d_ref, x_ref, w_ref, back_ref, grad_ref, acc_ref):
+    )(info, q, k_rows, k, v_rows, o, do, lse, cosine, sine)
+
+
+def project_back_kernel(meta, d_ref, x_ref, w_ref, back_ref, grad_ref, acc_ref):
     index = pl.program_id(0)
 
     @pl.when(index == 0)
@@ -334,23 +560,24 @@
         grad_ref[...] = acc_ref[...].T.astype(BF)
 
 
-def project_back(d_qkv_t, x_rel, w_t, me):
+def project_back(meta, d_qkv_t, x_all, w_t):
     parts, local, share = d_qkv_t.shape
     width = w_t.shape[1]
-    relative = lambda i, me: (jnp.bitwise_xor(i, me[0]), 0, 0)
+    relative = lambda i, meta: (jnp.bitwise_xor(i, meta[2]), 0, 0)
+    whole = lambda *shape: pl.BlockSpec(shape, lambda i, meta: (0,) * len(shape))
     return pl.pallas_call(
         project_back_kernel,
         grid_spec=pltpu.PrefetchScalarGridSpec(
             num_scalar_prefetch=1,
             grid=(parts,),
             in_specs=[
-                pl.BlockSpec((1, local, share), lambda i, me: (i, 0, 0)),
-                pl.BlockSpec((1, share, width), relative),
-                pl.BlockSpec((local, width), lambda i, me: (0, 0)),
+                pl.BlockSpec((1, local, share), lambda i, meta: (i, 0, 0)),
+                pl.BlockSpec((1, share, width), lambda i, meta: (i, 0, 0)),
+                whole(local, width),
             ],
             out_specs=[
                 pl.BlockSpec((1, share, width), relative),
-                pl.BlockSpec((width, local), lambda i, me: (0, 0)),
+                whole(width, local),
             ],
             scratch_shapes=[pltpu.VMEM((local, width), F32)],
         ),
@@ -363,7 +590,7 @@
             flops=4 * parts * share * local * width, bytes_accessed=15 << 20, transcendentals=0
         ),
         name="project_back",
-    )(me, d_qkv_t, x_rel, w_t)
+    )(meta, d_qkv_t, x_all, w_t)
 
 
 MESH = pl.DeviceIdType.MESH
@@ -450,10 +677,9 @@
     )
 
 
-def middle_kernel(size, *refs):
-    x_ref, cot_ref, norm_ref = refs[:3]
-    blocks_ref = refs[3]
-    out_hbm, gu_hbm, down_hbm = (refs[4 + i * size : 4 + (i + 1) * size] for i in range(3))
+def middle_kernel(size, groups, *refs):
+    x_ref, match_ref, cot_ref, over_ref, norm_ref, blocks_ref = refs[:6]
+    out_hbm, gu_hbm, down_hbm = (refs[6 + i * size : 6 + (i + 1) * size] for i in range(3))
     (
         result_ref,
         grad_one_ref,
@@ -475,7 +701,7 @@
         sends,
         recvs,
         keep,
-    ) = refs[4 + 3 * size :]
+    ) = refs[6 + 3 * size :]
     index = pl.program_id(0)
     first = index == 0
     d = lax.axis_index("dp")
@@ -553,9 +779,21 @@
         branch = branch + mm(hidden, w_down_ref[r], 1, 1)
     result, unit_two, inverse_two = norm_forward(normed_one + branch, gain_two, shift_two)
     result_ref[...] = result.astype(BF)
-    grad_two, d_gain_two, d_shift_two = norm_backward(
-        cot_ref[...].astype(F32), unit_two, inverse_two, gain_two
-    )
+    if groups:
+        sub = BLOCK // groups
+        spares = [over_ref[g, 0:1, :].astype(F32) for g in range(groups)]
+        in_last = jnp.where((index == subs - 1) & (t == size - 1), 1.0, 0.0)
+        ends = lax.broadcasted_iota(jnp.int32, (sub, 1), 0) == sub - 1
+        pieces = []
+        for g in range(groups):
+            piece = cot_ref[g].astype(F32)
+            spare, flag = spare_row(match_ref, groups, g, spares)
+            fix = jnp.where(ends, flag * in_last, 0.0)
+            pieces.append(piece * (1.0 - fix) + spare * fix)
+        cot = jnp.concatenate(pieces, 0)
+    else:
+        cot = cot_ref[...].astype(F32)
+    grad_two, d_gain_two, d_shift_two = norm_backward(cot, unit_two, inverse_two, gain_two)
     d_branch = grad_two.astype(BF)
     d_branch_t_ref[...] = grad_two.T.astype(BF)
     back = grad_two
@@ -582,7 +820,7 @@
         norm_grad_ref[i : i + 1, :] += grad
 
 
-def middle(x_own, cot_own, norms, o_blocks, w_out_parts, gu_parts, down_parts):
+def middle(x_own, match, cot, norms, o_blocks, w_out_parts, gu_parts, down_parts):
     rows, width = x_own.shape
     size = len(gu_parts)
     local = o_blocks.shape[1]
@@ -591,10 +829,22 @@
     turned = pl.BlockSpec((width, BLOCK), lambda i: (0, i))
     anywhere = pl.BlockSpec(memory_space=pl.ANY)
     shape = jax.ShapeDtypeStruct
+    groups = cot.shape[0] if cot.ndim == 3 else 0
+    if groups:
+        sub = BLOCK // groups
+        last = cot.shape[1] // 16 - 1
+        cot_specs = [
+            pl.BlockSpec((groups, sub, width), lambda i: (0, i, 0)),
+            pl.BlockSpec((groups, 16, width), lambda i: (0, last, 0)),
+        ]
+    else:
+        cot_specs = [block, pl.BlockSpec((16, width), lambda i: (0, 0))]
     return pl.pallas_call(
-        functools.partial(middle_kernel, size),
+        functools.partial(middle_kernel, size, groups),
         grid=(rows // BLOCK,),
-        in_specs=[block, block, pl.BlockSpec(norms.shape, lambda i: (0, 0))]
+        in_specs=[block, pl.BlockSpec(memory_space=pltpu.SMEM)]
+        + cot_specs
+        + [pl.BlockSpec(norms.shape, lambda i: (0, 0))]
         + [anywhere] * (1 + 3 * size),
         out_specs=[
             block,
@@ -641,7 +891,7 @@
             transcendentals=rows * size * inner,
         ),
         name="middle",
-    )(x_own, cot_own, norms, o_blocks, *w_out_parts, *gu_parts, *down_parts)
+    )(x_own, match, cot, cot, norms, o_blocks, *w_out_parts, *gu_parts, *down_parts)
 
 
 def weight_grads_tile(
@@ -1274,15 +1524,8 @@
     )(info, home, over)
 
 
-def spans(offset, length, source, groups):
-    low = (offset - source + groups - 1) // groups
-    high = (offset + length - source + groups - 1) // groups
-    return low, high - low
-
-
 def local(tokens, cotangent, lengths, dealing, w_qkv, w_out, w_gu, w_down, gains, shifts):
     groups = lax.axis_size("dp")
-    member = lax.axis_index("dp")
     size = lax.axis_size("tensor")
     me = lax.axis_index("tensor")
     rows = tokens.shape[0]
@@ -1292,117 +1535,62 @@
     own_rows = rows // size
     subs = own_rows // BLOCK
     sub = share // subs
+    fused = sub % 16 == 0
     i32 = jnp.int32
 
-    seq_count = lengths.shape[0]
-    count_up = jnp.arange(seq_count, dtype=i32)
-    offsets = jnp.sum(jnp.where(count_up[None, :] < count_up[:, None], lengths[None, :], 0), 1)
-    chosen = dealing[:, None] == count_up[None, :]
-    dealt_len = jnp.sum(jnp.where(chosen, lengths[None, :], 0), 1).reshape(groups, 2)
-    dealt_off = jnp.sum(jnp.where(chosen, offsets[None, :], 0), 1).reshape(groups, 2)
-    group_ids = jnp.arange(groups, dtype=i32)
-
-    low_a, count_a = spans(dealt_off[:, 0], dealt_len[:, 0], member, groups)
-    low_b, count_b = spans(dealt_off[:, 1], dealt_len[:, 1], member, groups)
-    fused = sub % 16 == 0
-    body_slots = me * share + jnp.arange(share, dtype=i32)[None, :]
-
-    def pick(slot):
-        found = jnp.where(
-            slot < count_a[:, None], low_a[:, None] + slot, (low_b - count_a)[:, None] + slot
-        )
-        return jnp.clip(found, 0, rows - 1).reshape(-1)
-
-    picked = jnp.concatenate([pick(body_slots), pick(jnp.full((1, 1), slots, i32))])
-
-    def pack(array):
-        taken = jnp.take(array.reshape(rows, width), picked, axis=0)
-        return (
-            taken[: groups * share].reshape(groups, share, width),
-            taken[groups * share :].reshape(groups, 1, width),
-        )
-
-    def over_dp(pair):
-        return tuple(
-            lax.all_to_all(a, "dp", split_axis=0, concat_axis=0, tiled=True) for a in pair
-        )
-
-    send_x = pack(tokens)
-    send_c = pack(cotangent)
+    ids = jnp.stack([lax.axis_index("dp"), me]).astype(i32)
+    send_x, over_x, send_c, meta, table, match = pack(
+        lengths,
+        dealing,
+        ids,
+        tokens.reshape(rows, width),
+        cotangent.reshape(rows, width),
+        groups,
+        size,
+    )
+
+    def over_dp(array):
+        return lax.all_to_all(array, "dp", split_axis=0, concat_axis=0, tiled=True)
+
     far_out, far_down = swap(w_out.T, size, 2), swap(w_down, size, 2)
-    if fused:
-        recv_x, over_x = route(*send_x, size)
-    else:
-        recv_x, over_x = over_dp(send_x)
-        recv_x = jnp.stack(gather_members(recv_x))
-    send_c, recv_x, far_out, far_down = lax.optimization_barrier(
-        (send_c, recv_x, far_out, far_down)
-    )
-    recv_c, over_c = over_dp(send_c)
-
-    mine = group_ids == member
-    pick_group = lambda table: jnp.sum(jnp.where(mine[:, None], table, 0), 0)
-    my_len = pick_group(dealt_len)
-    my_off = pick_group(dealt_off)
-    glow_a, gcount_a = spans(my_off[0], my_len[0], group_ids, groups)
-    glow_b, gcount_b = spans(my_off[1], my_len[1], group_ids, groups)
-    filled = gcount_a + gcount_b
-    hole = filled < slots
-    over = filled > slots
-    before = group_ids[None, :] < group_ids[:, None]
-    hole_rank = jnp.sum(jnp.where(before & hole[None, :], 1, 0), 1)
-    over_rank = jnp.sum(jnp.where(before & over[None, :], 1, 0), 1)
-    match = hole[:, None] & over[None, :] & (hole_rank[:, None] == over_rank[None, :])
-    last_token = (glow_b - gcount_a + slots) * groups + group_ids
-    hole_token = jnp.sum(jnp.where(match, last_token[None, :], 0), 1)
-    match_bf = match.astype(BF)
-    relative = jnp.bitwise_xor(jnp.arange(size, dtype=i32), me)
-
-    place_ids = jnp.arange(share, dtype=i32)
+    match_square = match.reshape(groups, groups)
 
     def fill(received, over, last):
-        spare = jnp.dot(match_bf, over[:, 0], preferred_element_type=F32).astype(BF)
-        fix = last[:, None, None] & (hole[:, None] & (place_ids == share - 1)[None, :])[None]
+        spare = jnp.dot(match_square.astype(BF), over, preferred_element_type=F32).astype(BF)
+        hole = (jnp.sum(match_square, 1) > 0)[:, None] & (jnp.arange(share) == share - 1)[None, :]
+        fix = last[:, None, None] & hole[None]
         body = jnp.where(fix[..., None], spare[None, :, None, :], received)
         body = body.reshape(-1, groups, subs, sub, width).transpose(0, 2, 1, 3, 4)
         return body.reshape(-1, own_rows, width)
 
-    shape = (size * subs, groups, sub)
-    block_id = lax.broadcasted_iota(i32, shape, 0)
-    source_id = lax.broadcasted_iota(i32, shape, 1)
-    slot_id = block_id * sub + lax.broadcasted_iota(i32, shape, 2)
-    spread = lambda vec: vec[None, :, None]
-    in_a = slot_id < spread(gcount_a)
-    token_id = (
-        jnp.where(in_a, spread(glow_a), spread(glow_b - gcount_a)) + slot_id
-    ) * groups + source_id
-    token_id = jnp.where(spread(hole) & (slot_id == slots - 1), spread(hole_token), token_id)
-    positions = (token_id - jnp.where(in_a, my_off[0], my_off[1])).reshape(rows)
-    segment = jnp.where(in_a, 0, 1).astype(F32).reshape(rows)
-    frequency = 1000.0 ** (-(jnp.arange(HALF, dtype=F32) * 2.0) / HEAD)
-    angles = frequency[:, None] * positions.astype(F32)[None, :]
-    cosine = jnp.cos(angles)
-    sine = jnp.sin(angles)
-    seg_row = segment[None, :]
-    seg_col = segment[:, None]
-    first_b = (my_len[0] + BLOCK - 1) // BLOCK
-    info = jnp.stack([my_len[0] // BLOCK, first_b, me]).astype(i32)
-
-    x_rel = fill(recv_x, over_x, relative == size - 1)
-    x_own = x_rel[0]
+    if fused:
+        x_rel, over_x = route(send_x, over_x, size)
+        send_c, x_rel, far_out, far_down = lax.optimization_barrier(
+            (send_c, x_rel, far_out, far_down)
+        )
+    else:
+        x_rel = jnp.stack(gather_members(over_dp(send_x)))
+        relative = jnp.bitwise_xor(jnp.arange(size, dtype=i32), me)
+        x_rel = fill(x_rel, over_dp(over_x)[:, 0], relative == size - 1)
+    cot = over_dp(send_c)
+    if not fused:
+        cot = fill(cot[None, :, :share], cot[:, share], (me == size - 1)[None])[0]
+
     local_width = w_qkv.shape[2]
     w_qkv_t = w_qkv.transpose(1, 2, 0).reshape(3 * local_width, width)
     x_rel, near_gu = lax.optimization_barrier((x_rel, w_gu.reshape(width, -1)))
     far_gu = swap(near_gu, size, 2)
-    q, k, v, k_rows, v_rows = project(x_rel, w_qkv_t, cosine, sine, me[None])
-    o_blocks, lse = attend(info, q, k_rows, v, seg_row, seg_col)
-    o_blocks, far_gu, recv_c = lax.optimization_barrier((o_blocks, far_gu, recv_c))
+    frequency = 1000.0 ** (-(jnp.arange(HALF, dtype=F32) * 2.0) / HEAD)
+    q, k, v, k_rows, v_rows, cosine, sine, x_all, x_own = project(
+        meta, match, x_rel, over_x, w_qkv_t, frequency[:, None], groups, fused
+    )
+    o_blocks, lse = attend(meta, q, k_rows, v, groups)
+    o_blocks, far_gu, cot = lax.optimization_barrier((o_blocks, far_gu, cot))
 
     spread_parts = lambda near, far: [near, swap(near, size, 1), far, swap(far, size, 1)]
     w_out_parts = spread_parts(w_out.T, far_out)
     down_parts = spread_parts(w_down, far_down)
     gu_parts = spread_parts(near_gu, far_gu)
-    cot_own = fill(recv_c[None], over_c, (me == size - 1)[None])[0]
     norms = jnp.concatenate([gains.T, shifts.T], 0)
     (
         result_own,
@@ -1415,12 +1603,11 @@
         hidden,
         d_gu,
         norm_grads,
-    ) = middle(x_own, cot_own, norms, o_blocks, w_out_parts, gu_parts, down_parts)
+    ) = middle(x_own, match, cot, norms, o_blocks, w_out_parts, gu_parts, down_parts)
     grad_args = (normed_t, d_branch_t, d_attn_t, hidden, d_gu, heads_own, norm_grads)
-    match_all = match.astype(F32).reshape(-1)
     if fused:
         pair, do_rel, home_result, over_result = grads(
-            match_all, groups, *grad_args, d_heads, result_own
+            match, groups, *grad_args, d_heads, result_own
         )
         home_result = (home_result.reshape(size, groups, share, width), over_result)
     else:
@@ -1430,32 +1617,27 @@
         do_rel = jnp.stack(exchange_members([d_heads[r] for r in range(size)]))
 
     d_qkv_t = attend_back(
-        info, q, k_rows, k, v_rows, o_blocks, do_rel, lse, seg_row, seg_col, cosine, sine
+        meta, q, k_rows, k, v_rows, o_blocks, do_rel, lse, cosine, sine, groups
     )
-    back_rel, grad_qkv = project_back(d_qkv_t, x_rel, w_qkv_t, me[None])
+    back_rel, grad_qkv = project_back(meta, d_qkv_t, x_all, w_qkv_t)
     grad_qkv = grad_qkv.reshape(groups, width // groups, 3 * local_width)
 
     pair = lax.psum_scatter(pair, "dp", scatter_dimension=1, tiled=True)
-    spot_low = jnp.stack([low_a, low_b], 1).reshape(-1)
-    spot_count = jnp.stack([count_a, count_b], 1).reshape(-1)
-    spot_first = jnp.stack([jnp.zeros_like(count_a), count_a], 1).reshape(-1)
-    spot_group = jnp.arange(seq_count, dtype=i32) // 2
-    table = jnp.stack([spot_low, spot_count, spot_group, spot_first])
-    table = jnp.sum(jnp.where(chosen[None], table[:, :, None], 0), 1)
-    table = jnp.concatenate([jnp.full((4, 1), me, i32), table], 1)
-
     def send_back(own):
         body = own.reshape(subs, groups, sub, width).transpose(1, 0, 2, 3)
         body = body.reshape(groups, share, width)
         spare = lax.dot_general(
-            match_bf, body[:, share - 1], (((0,), (0,)), ((), ())), preferred_element_type=F32
+            match_square.astype(BF),
+            body[:, share - 1],
+            (((0,), (0,)), ((), ())),
+            preferred_element_type=F32,
         ).astype(BF)
-        pair = over_dp((body, spare.reshape(groups, 1, width)))
+        pair = (over_dp(body), over_dp(spare.reshape(groups, 1, width)))
         return tuple(jnp.stack(gather_members(a)) for a in pair)
 
     if fused:
         home_input, home_over, qkv_sum = settle(
-            match_all, back_rel, grad_one, grad_qkv
+            match, back_rel, grad_one, grad_qkv
         )
         home_input = (home_input.reshape(size, groups, share, width), home_over)
         pair, home_input = lax.optimization_barrier((pair, home_input))
@@ -1479,10 +1661,11 @@
         arrange = functools.partial(unpack, table)
     else:
         row_ids = jnp.arange(rows, dtype=i32)[None, :]
-        here = (row_ids >= spot_low[:, None]) & (row_ids < (spot_low + spot_count)[:, None])
-        slot = row_ids + (spot_first - spot_low)[:, None]
+        low, count, group, first = (table[i, 1:][:, None] for i in range(4))
+        here = (row_ids >= low) & (row_ids < low + count)
+        slot = row_ids + first - low
         home_part = jnp.minimum(slot // share, size - 1)
-        flat = (jnp.bitwise_xor(home_part, me) * groups + spot_group[:, None]) * (share + 1)
+        flat = (jnp.bitwise_xor(home_part, me) * groups + group) * (share + 1)
         flat = jnp.sum(jnp.where(here, flat + slot - home_part * share, 0), 0)
 
         def arrange(home, over):

time: 508 us -> 463 us (0.911); the launches traced: 501 us -> 463 us
  local copies, waits for them, and re-layouts: 48.3 us -> 11.1 us
  Pallas kernels: 383 us -> 409 us
  other arithmetic: 24.9 us -> 1.93 us
  waiting for transfers between devices: 0.39 us -> 13.1 us
  starting transfers between devices: 22.5 us -> 13.5 us
  between operations: 20.6 us -> 14.2 us
    pallas_call x4 -> x5, Pallas kernels: 147 us -> 169 us  [the longest x1 61.3 us: attend_back(): pl.pallas_call(functools.partial(attend_back_kernel, groups), grid_spec=p...]
    gather x2 -> x0, local copies, waits for them, and re-layouts: 15.4 us -> none  [pack(): taken = jnp.take(array.reshape(rows, width), picked, axis=0)]
    ppermute x10, waiting for transfers between devices: 0.03 us -> 13.1 us  [swap(): return lax.ppermute(array, 'tensor', [(i, i ^ step) for i in range(size)])]
    all_to_all x2 -> x1, starting transfers between devices: 15.9 us -> 7.21 us  [over_dp(): return lax.all_to_all(array, 'dp', split_axis=0, concat_axis=0, tiled=True)]
    select_n x5 -> x0, other arithmetic: 6.66 us -> none  [the longest x2 3.54 us: fill(): body = jnp.where(fix[..., None], spare[None, :, None, :], received)]
    slice x4 -> x0, local copies, waits for them, and re-layouts: 5.14 us -> none  [the longest x1 2.35 us: local(): x_own = x_rel[0]]
  transfers between devices with their start and end apart: 13 -> 12, of which waited for: 1 -> 4; matrix products, arithmetic and copies ran while one was open for 13% -> 1% of each run, Pallas kernels for 56% -> 66%
where the time goes in v3:
time: 463 us
  Pallas kernels  409 us (88%)
  between operations  14.2 us (3%)
  starting transfers between devices  13.5 us (3%)
  waiting for transfers between devices  13.1 us (3%)
  local copies, waits for them, and re-layouts  11.1 us (2%)
    pallas_call x1, Pallas kernels, settle(): pl.pallas_call(functools.partial(settle_kernel, groups, size), in_specs=[...  107 us
    pallas_call x1, Pallas kernels, attend_back(): pl.pallas_call(functools.partial(attend_back_kernel, groups), grid_spec=p...  61.3 us
    pallas_call x1, Pallas kernels, grads(): pl.pallas_call(functools.partial(grads_kernel, groups, size), grid=(size,...  55.2 us
    pallas_call x1, Pallas kernels, middle(): pl.pallas_call(functools.partial(middle_kernel, size, groups), grid=(rows...  47.8 us
    pallas_call x1, Pallas kernels, route(): pl.pallas_call(functools.partial(route_kernel, groups, size), in_specs=[a...  45 us
    pallas_call x1, Pallas kernels, attend(): pl.pallas_call(functools.partial(attend_kernel, groups), grid_spec=pltpu....  34.7 us
    pallas_call x2, Pallas kernels, unpack(): pl.pallas_call(unpack_kernel, grid_spec=pltpu.PrefetchScalarGridSpec(num_...  21.3 us
    pallas_call x1, Pallas kernels, pack(): pl.pallas_call(functools.partial(pack_kernel, groups, size), grid_spec=pl...  14.3 us
  transfers between devices with their start and end apart: 12, of which 4 were waited for; matrix products, arithmetic and copies ran while one was open for 1% of the time, Pallas kernels for 66%

profile of v3, /device:TPU:0, one launch (start us, length us, event | category | flops | bytes accessed | tf_op | source)
XLA Modules:
  0.0 462.9 jit_solution(751565214591935232)
XLA Ops:
  7.2 3.0 collective-permute-start.1
  10.2 0.1 collective-permute-start
  10.3 0.6 pad_add_fusion.ids
  10.8 14.3 %pack.1 = (bf16[8,96,768]{2,1,0:T(8,128)(2,1)}, bf16[8,1,768]{2,1,0:T(2,128)(2,1)}, bf16[8,112,768]{2,1,0:T(8,128)(2,1)}, s32[16]{0:T(128)}, s32[4,17]{1,0:T(4,128)}, /*index=5*/f32[64]{0:T(128)}) custom-call(s32[16]{0:T(128)} %lengths.1, s32[16]{0:T(128)} %dealing.1, s32[2]{0:T(128)} %pad_add_fusion.ids, bf16[3072,768]{1,0:T(8,128)(2,1)} %bitcast.24, ...), custom_call_target="tpu_custom_call" | custom-call | bytes 20971520 | tf_op jit(solution)/shard_map/pack/pallas_call | solution.py:138
  25.2 0.0 copy-start
  25.2 45.0 %route.1 = (bf16[4,8,96,768]{3,2,1,0:T(8,128)(2,1)}, bf16[8,1,768]{2,1,0:T(2,128)(2,1)}) custom-call(bf16[8,96,768]{2,1,0:T(8,128)(2,1)} %get-tuple-element.62.send_ref, bf16[8,1,768]{2,1,0:T(2,128)(2,1)} %get-tuple-element.63.over_ref), custom_call_target="tpu_custom_call" | custom-call | bytes 62914560 | tf_op jit(solution)/shard_map/route/pallas_call | solution.py:1248
  70.1 0.0 collective-permute-done.refs_8_
  70.2 0.0 collective-permute-done.1.refs_16_
  70.2 0.0 copy-start.7
  70.2 7.2 %all-to-all-start = ((bf16[8,112,768]{2,1,0:T(8,128)(2,1)}), bf16[8,112,768]{2,1,0:T(8,128)(2,1)}, u32[]{:S(2)}, u32[]{:S(2)}) async-start(bf16[8,112,768]{2,1,0:T(8,128)(2,1)} %get-tuple-element.74), calls=%async_computation | async-start | bytes 2752512 | tf_op jit(solution)/shard_map/all_to_all | solution.py:1553
  77.4 0.0 reduce-scatter.2.cloned.1.call-start
  77.4 0.0 copy-done
  77.4 1.8 copy.30
  79.3 0.0 copy-done.7
  79.3 1.2 collective-permute-start.2
  80.4 0.6 multiply_power_fusion.freq_ref
  81.0 0.0 collective-permute-start.5
  81.0 11.0 %project.1 = (bf16[192,3072]{1,0:T(8,128)(2,1)}, bf16[192,3072]{1,0:T(8,128)(2,1)}, bf16[240,3072]{1,0:T(8,128)(2,1)}, bf16[3,3072,64]{2,1,0:T(8,128)(2,1)}, bf1...) custom-call(s32[16]{0:T(128)} %get-tuple-element.60.meta.info, ...), custom_call_target="tpu_custom_call" | custom-call | flops 2717908992 | bytes 16777216 | tf_op jit(solution)/shard_map/project/pallas_call | solution.py:285
  92.1 0.0 copy-start.6
  92.1 0.0 copy-start.2
  92.1 0.0 copy-start.3
  92.1 34.7 %attend.1 = (bf16[12,192,256]{2,1,0:T(8,128)(2,1)}, f32[3,3072]{1,0:T(4,128)}) custom-call(s32[16]{0:T(128)} %get-tuple-element.60.meta.info, bf16[192,3072]{1,0:T(8,128)(2,1)} %get-tuple-element.69.q_ref, bf16[3,3072,64]{2,1,0:T(8,128)(2,1)} %get-tuple-element.70.k_ref.krow_ref, bf16[240,3072]{1,0:T(8,128)(2,1)} %get-tuple-element.71.v_ref), custom_call_target="tpu_custom_call" | custom-call | flops 14495514624 | bytes 8388608 | tf_op jit(solution)/shard_map/attend/pallas_call | solution.py:382
  126.8 5.9 %collective-permute-done.2.refs_12_ = bf16[768,1536]{1,0:T(8,128)(2,1)S(1)} collective-permute-done((bf16[768,1536]{1,0:T(8,128)(2,1)}, bf16[768,1536]{1,0:T(8,128)(2,1)S(1)}, u32[]{:S(2)}, u32[]{:S(2)}) %collective-permute-start.2) | collective-permute-done | bytes 2359328 | tf_op jit(solution)/shard_map/ppermute | solution.py:1178
  132.7 0.0 all-to-all-done.refs_2_.refs_3_
  132.7 0.0 collective-permute-start.6
  132.7 0.0 copy-done.6
  132.7 0.5 collective-permute-start.7
  133.2 0.1 collective-permute-start.8
  133.3 0.4 collective-permute-start.3
  133.7 5.1 %collective-permute-done.3.refs_7_ = bf16[192,768]{1,0:T(8,128)(2,1)} collective-permute-done((bf16[192,768]{1,0:T(8,128)(2,1)}, bf16[192,768]{1,0:T(8,128)(2,1)}, u32[]{:S(2)}, u32[]{:S(2)}) %collective-permute-start.3) | collective-permute-done | bytes 294944 | tf_op jit(solution)/shard_map/ppermute | solution.py:1178
  138.9 0.1 collective-permute-start.4
  139.0 0.0 copy-done.2
  139.0 0.0 copy-done.3
  139.0 0.6 pad_maximum_fusion.refs_4_
  139.6 1.4 collective-permute-done.7.refs_15_
  141.0 0.6 collective-permute-done.4.refs_9_
  141.7 0.0 collective-permute-done.8.refs_17_
  141.7 0.0 collective-permute-done.5.refs_11_
  141.7 0.0 collective-permute-done.6.refs_13_
  141.7 0.7 copy-done.10
  142.4 0.4 copy-done.9
  142.8 1.0 copy-done.5
  143.8 47.8 %middle.1 = (bf16[768,768]{1,0:T(8,128)(2,1)}, f32[768,768]{1,0:T(8,128)}, bf16[4,192,768]{2,1,0:T(8,128)(2,1)}, bf16[4,192,768]{2,1,0:T(8,128)(2,1)}, bf16[768,...) custom-call(bf16[768,768]{1,0:T(8,128)(2,1)} %get-tuple-element.68.r, ...), custom_call_target="tpu_custom_call" | custom-call | flops 23555211264 | bytes 41943040 | tf_op jit(solution)/shard_map/middle/pallas_call | solution.py:842
  191.6 55.2 %grads.1 = (bf16[2,768,2560]{2,1,0:T(8,128)(2,1)}, bf16[4,192,768]{2,1,0:T(8,128)(2,1)}, bf16[4,8,3,32,768]{4,3,2,1,0:T(8,128)(2,1)}, bf16[4,8,1,768]{3,2,1,0:T(2,128)(2,1)}) custom-call(f32[64]{0:T(128)} %get-tuple-element.59.match_ref.refs_1_, bf16[768,768]{1,0:T(8,128)(2,1)} %get-tuple-element.80.refs_0_, bf16[768,768]{1,0:T(8,128)(2,1)} %get-tuple-element.81.refs_1_, ...), custom_call_target="tpu_custom_call" | custom-call | flops 11777605632 | bytes 83886080 | tf_op jit(solution)/shard_map/grads/pallas_call | solution.py:1112
  246.8 0.0 reduce-scatter.2.cloned.1.call-update
  246.9 61.3 %attend_back.1.d_ref = bf16[4,576,768]{2,1,0:T(8,128)(2,1)} custom-call(s32[16]{0:T(128)} %get-tuple-element.60.meta.info, bf16[192,3072]{1,0:T(8,128)(2,1)} %get-tuple-element.69.q_ref, bf16[3,3072,64]{2,1,0:T(8,128)(2,1)} %get-tuple-element.70.k_ref.krow_ref, bf16[192,3072]{1,0:T(8,128)(2,1)} %get-tuple-element.92.k_ref, ...), custom_call_target="tpu_custom_call" | custom-call | flops 36238786560 | bytes 16777216 | tf_op jit(solution)/shard_map/attend_back/pallas_call | solution.py:510
  308.1 11.8 %project_back.1 = (bf16[4,768,768]{2,1,0:T(8,128)(2,1)}, bf16[768,576]{1,0:T(8,128)(2,1)}) custom-call(s32[16]{0:T(128)} %get-tuple-element.60.meta.info, bf16[4,576,768]{2,1,0:T(8,128)(2,1)} %attend_back.1.d_ref, bf16[4,768,768]{2,1,0:T(8,128)(2,1)} %get-tuple-element.98.x_ref, bf16[576,768]{1,0:T(8,128)(2,1)} %bitcast.36), custom_call_target="tpu_custom_call" | custom-call | flops 5435817984 | bytes 15728640 | tf_op jit(solution)/shard_map/project_back/pallas_call | solution.py:568
  319.9 106.6 %settle.1 = (bf16[4,8,3,32,768]{4,3,2,1,0:T(8,128)(2,1)}, bf16[4,8,1,768]{3,2,1,0:T(2,128)(2,1)}, f32[96,576]{1,0:T(8,128)}) custom-call(f32[64]{0:T(128)} %get-tuple-element.59.match_ref.refs_1_, bf16[4,768,768]{2,1,0:T(8,128)(2,1)} %get-tuple-element.99.back_ref, f32[768,768]{1,0:T(8,128)} %get-tuple-element.100.one_ref, bf16[8,96,576]{2,1,0:T(8,128)(2,1)} %bitcast.32), custom_call_target="tpu_custom_call" | custom-call | bytes 157286400 | tf_op jit(solution)/shard_map/settle/pallas_call | solution.py:1429
  426.6 0.0 reduce-scatter.2.cloned.1.call-done
  426.6 1.1 slice_bitcast_fusion
  427.7 0.9 collective-permute-start.9
  428.6 1.1 copy.26
  429.7 0.9 copy.27
  430.6 10.6 %unpack.2 = bf16[3072,768]{1,0:T(8,128)(2,1)} custom-call(s32[4,17]{1,0:T(4,128)} %get-tuple-element.58.info, bf16[4,8,96,768]{3,2,1,0:T(8,128)(2,1)} %bitcast.26, bf16[4,8,1,768]{3,2,1,0:T(2,128)(2,1)} %get-tuple-element.90.over_ref), custom_call_target="tpu_custom_call" | custom-call | bytes 31457280 | tf_op jit(solution)/shard_map/unpack/pallas_call | solution.py:1508
  441.1 10.7 %unpack.3 = bf16[3072,768]{1,0:T(8,128)(2,1)} custom-call(s32[4,17]{1,0:T(4,128)} %get-tuple-element.58.info, bf16[4,8,96,768]{3,2,1,0:T(8,128)(2,1)} %bitcast.29, bf16[4,8,1,768]{3,2,1,0:T(2,128)(2,1)} %get-tuple-element.105.over_ref), custom_call_target="tpu_custom_call" | custom-call | bytes 31457280 | tf_op jit(solution)/shard_map/unpack/pallas_call | solution.py:1508
  451.8 0.0 collective-permute-done.9
  451.8 0.1 convert_add_fusion
  452.0 0.6 slice.32
  452.7 0.7 slice.34
  453.4 0.1 slice.35
  453.5 1.2 reshape.81
  454.7 0.1 fusion
  454.8 0.6 copy.28
  455.4 0.6 copy.29
  (10 shorter events, 0.1 us)
Async XLA Ops:
  7.2 63.0 %collective-permute-start.1 = (bf16[768,768]{1,0:T(8,128)(2,1)}, bf16[768,768]{1,0:T(8,128)(2,1)S(1)}, u32[]{:S(2)}, u32[]{:S(2)}) collective-permute-start(bf16[768,768]{1,0:T(8,128)(2,1)} %refs_14_.1), channel_id=1, source_target_pairs={{0,2},{1,3},{2,0},{3,1},{4,6},{5,7},{6,4},{7,5},{8,10},{9,11},{10,... | collective-permute-start | bytes 3538952 | tf_op jit(solution)/shard_map/ppermute | solution.py:1178
  10.2 60.0 %collective-permute-start = (bf16[192,768]{1,0:T(8,128)(2,1)}, bf16[192,768]{1,0:T(8,128)(2,1)}, u32[]{:S(2)}, u32[]{:S(2)}) collective-permute-start(bf16[192,768]{1,0:T(8,128)(2,1)} %bitcast.37), channel_id=1, source_target_pairs={{0,2},{1,3},{2,0},{3,1},{4,6},{5,7},{6,4},{7,5},{8,10},{9,11},{10,... | collective-permute-start | bytes 884744 | tf_op jit(solution)/shard_map/ppermute | solution.py:1178
  25.2 52.3 %copy-start = (bf16[768,2,768]{2,1,0:T(2,128)(2,1)S(1)}, bf16[768,2,768]{2,1,0:T(2,128)(2,1)}, u32[]{:S(2)}) copy-start(bf16[768,2,768]{2,1,0:T(2,128)(2,1)} %param.16) | copy-start | bytes 7077892
  70.2 9.1 %copy-start.7 = (bf16[768,768]{1,0:T(8,128)(2,1)}, bf16[768,768]{1,0:T(8,128)(2,1)S(1)}, u32[]{:S(2)}) copy-start(bf16[768,768]{1,0:T(8,128)(2,1)S(1)} %collective-permute-done.1.refs_16_) | copy-start | bytes 3538948
  70.2 62.5 %all-to-all-start = ((bf16[8,112,768]{2,1,0:T(8,128)(2,1)}), bf16[8,112,768]{2,1,0:T(8,128)(2,1)}, u32[]{:S(2)}, u32[]{:S(2)}) async-start(bf16[8,112,768]{2,1,0:T(8,128)(2,1)} %get-tuple-element.74), calls=%async_computation | async-start | bytes 2752512 | tf_op jit(solution)/shard_map/all_to_all | solution.py:1553
  77.4 349.2 %reduce-scatter.2.cloned.1.call-start = ((), (), s32[]{:S(2)}) async-start(), calls=%async_computation.2 | async-start | bytes 8847360 | tf_op jit(solution)/shard_map/reduce_scatter | solution.py:1625
  79.3 53.4 %collective-permute-start.2 = (bf16[768,1536]{1,0:T(8,128)(2,1)}, bf16[768,1536]{1,0:T(8,128)(2,1)S(1)}, u32[]{:S(2)}, u32[]{:S(2)}) collective-permute-start(bf16[768,1536]{1,0:T(8,128)(2,1)} %bitcast.21.refs_10_), channel_id=1, source_target_pairs={{0,2},{1,3},{2,0},{3,1},{4,6},{5,7},{6,4},{7,5},{8,10},{9,11},{10,... | collective-permute-start | bytes 7077896 | tf_op jit(solution)/shard_map/ppermute | solution.py:1178
  81.0 60.6 %collective-permute-start.5 = (bf16[768,1536]{1,0:T(8,128)(2,1)}, bf16[768,1536]{1,0:T(8,128)(2,1)}, u32[]{:S(2)}, u32[]{:S(2)}) collective-permute-start(bf16[768,1536]{1,0:T(8,128)(2,1)} %bitcast.21.refs_10_), channel_id=1, source_target_pairs={{0,1},{1,0},{2,3},{3,2},{4,5},{5,4},{6,7},{7,6},{8,9},{9,8},{10,11... | collective-permute-start | bytes 7077896 | tf_op jit(solution)/shard_map/ppermute | solution.py:1178
  92.1 40.6 %copy-start.6 = (bf16[768,768]{1,0:T(8,128)(2,1)S(1)}, bf16[768,768]{1,0:T(8,128)(2,1)}, u32[]{:S(2)}) copy-start(bf16[768,768]{1,0:T(8,128)(2,1)} %refs_14_.1) | copy-start | bytes 3538948
  92.1 46.9 %copy-start.2 = (f32[768,2]{0,1:T(2,128)S(1)}, f32[768,2]{0,1:T(2,128)}, u32[]{:S(2)}) copy-start(f32[768,2]{0,1:T(2,128)} %param.19) | copy-start | bytes 18436
  92.1 46.9 %copy-start.3 = (f32[768,2]{0,1:T(2,128)S(1)}, f32[768,2]{0,1:T(2,128)}, u32[]{:S(2)}) copy-start(f32[768,2]{0,1:T(2,128)} %param.18) | copy-start | bytes 18436
  132.7 9.7 %copy-start.4 = (bf16[768,1536]{1,0:T(8,128)(2,1)}, bf16[768,1536]{1,0:T(8,128)(2,1)S(1)}, u32[]{:S(2)}) copy-start(bf16[768,1536]{1,0:T(8,128)(2,1)S(1)} %collective-permute-done.2.refs_12_) | copy-start | bytes 7077892
  132.7 9.0 %collective-permute-start.6 = (bf16[768,1536]{1,0:T(8,128)(2,1)S(1)}, bf16[768,1536]{1,0:T(8,128)(2,1)S(1)}, u32[]{:S(2)}, u32[]{:S(2)}) collective-permute-start(bf16[768,1536]{1,0:T(8,128)(2,1)S(1)} %collective-permute-done.2.refs_12_), channel_id=1, source_target_pairs={{0,1},{1,0},{2,3},{3,2},{4,5},{5,4},{6,7},{7,6},{8,9},{9,8},{10,11... | collective-permute-start | bytes 7077896 | tf_op jit(solution)/shard_map/ppermute | solution.py:1178
  132.7 8.3 %collective-permute-start.7 = (bf16[768,768]{1,0:T(8,128)(2,1)S(1)}, bf16[768,768]{1,0:T(8,128)(2,1)S(1)}, u32[]{:S(2)}, u32[]{:S(2)}) collective-permute-start(bf16[768,768]{1,0:T(8,128)(2,1)S(1)} %copy-done.6), channel_id=1, source_target_pairs={{0,1},{1,0},{2,3},{3,2},{4,5},{5,4},{6,7},{7,6},{8,9},{9,8},{10,11... | collective-permute-start | bytes 3538952 | tf_op jit(solution)/shard_map/ppermute | solution.py:1178
  133.2 8.5 %collective-permute-start.8 = (bf16[768,768]{1,0:T(8,128)(2,1)}, bf16[768,768]{1,0:T(8,128)(2,1)S(1)}, u32[]{:S(2)}, u32[]{:S(2)}) collective-permute-start(bf16[768,768]{1,0:T(8,128)(2,1)} %copy-done.7), channel_id=1, source_target_pairs={{0,1},{1,0},{2,3},{3,2},{4,5},{5,4},{6,7},{7,6},{8,9},{9,8},{10,11... | collective-permute-start | bytes 3538952 | tf_op jit(solution)/shard_map/ppermute | solution.py:1178
  133.3 5.6 %collective-permute-start.3 = (bf16[192,768]{1,0:T(8,128)(2,1)}, bf16[192,768]{1,0:T(8,128)(2,1)}, u32[]{:S(2)}, u32[]{:S(2)}) collective-permute-start(bf16[192,768]{1,0:T(8,128)(2,1)} %bitcast.38), channel_id=1, source_target_pairs={{0,1},{1,0},{2,3},{3,2},{4,5},{5,4},{6,7},{7,6},{8,9},{9,8},{10,11... | collective-permute-start | bytes 884744 | tf_op jit(solution)/shard_map/ppermute | solution.py:1178
  138.9 2.8 collective-permute-start.4
  141.0 1.4 copy-start.8
  141.7 0.7 copy-start.10
  141.7 1.1 copy-start.9
  142.4 1.4 copy-start.5
  427.7 24.1 %collective-permute-start.9 = (bf16[96,2560]{1,0:T(8,128)(2,1)S(1)}, bf16[96,2560]{1,0:T(8,128)(2,1)S(1)}, u32[]{:S(2)}, u32[]{:S(2)}) collective-permute-start(bf16[96,2560]{1,0:T(8,128)(2,1)S(1)} %slice_bitcast_fusion), channel_id=1, source_target_pairs={{0,2},{1,3},{2,0},{3,1},{4,6},{5,7},{6,4},{7,5},{8,10},{9,11},{10,... | collective-permute-start | bytes 1474568 | tf_op jit(solution)/shard_map/ppermute | solution.py:1178
  441.1 10.7 %copy-start.1 = (bf16[2,96,2560]{2,1,0:T(8,128)(2,1)S(1)}, bf16[2,96,2560]{2,1,0:T(8,128)(2,1)}, u32[]{:S(2)}) copy-start(bf16[2,96,2560]{2,1,0:T(8,128)(2,1)} %reduce-scatter.2.cloned.1.call-done) | copy-start | bytes 2949124
Sparse Core Ops, SparseCore 0:
  247.0 167.1 reduce-scatter.1

commit v4 on v3

--- a/solution.py
+++ b/solution.py
@@ -27,11 +27,24 @@
 
 
 HOLES = 8
+ROWS = 128
+
+
+def div(value, size):
+    if size & (size - 1) == 0:
+        return lax.shift_right_arithmetic(value, jnp.int32(size.bit_length() - 1))
+    return lax.div(value, size)
+
+
+def rem(value, size):
+    if size & (size - 1) == 0:
+        return lax.bitwise_and(value, jnp.int32(size - 1))
+    return lax.rem(value, size)
 
 
 def extra_of(source, offset, length, groups):
-    turned = lax.rem(source - offset + groups, groups)
-    return turned, jnp.where(turned < lax.rem(length, groups), 1, 0)
+    turned = rem(source - offset + groups, groups)
+    return turned, jnp.where(turned < rem(length, groups), 1, 0)
 
 
 def pack_kernel(
@@ -48,6 +61,7 @@
     meta_ref,
     table_ref,
     match_ref,
+    spots_ref,
 ):
     d = ids[0]
     t = ids[1]
@@ -62,15 +76,23 @@
         return seq, offset, lengths[seq]
 
     def span(offset, length):
-        low = lax.div(offset - d + groups - 1, groups)
-        return low, lax.div(offset + length - d + groups - 1, groups) - low
-
-    def load(ref, row, count):
+        low = div(offset - d + groups - 1, groups)
+        return low, div(offset + length - d + groups - 1, groups) - low
+
+    def window_at(row):
         start = jnp.clip(jnp.bitwise_and(row, -16), 0, rows - window)
-        shift = jnp.clip(row - start, 1 - window, window - 1)
-        loaded = ref[pl.ds(pl.multiple_of(start, 16), window), :].astype(F32)
-        return pltpu.roll(loaded, lax.rem(window - shift, window), 0)[:count]
-
+        return pl.ds(pl.multiple_of(start, 16), window), row - start
+
+    def one_hot(steps, shift, wanted):
+        return jnp.where((steps == shift) & wanted, 1.0, 0.0).astype(BF)
+
+    def steps_of(count):
+        shape = (count, window)
+        return lax.broadcasted_iota(jnp.int32, shape, 1) - lax.broadcasted_iota(jnp.int32, shape, 0)
+
+    steps = steps_of(share)
+    spare_steps = steps_of(16)
+    top = lax.broadcasted_iota(jnp.int32, (16, 1), 0) == 0
     table_ref[0, 0] = t
     slot_ids = lax.broadcasted_iota(jnp.int32, (share, 1), 0) + t * share
 
@@ -84,20 +106,41 @@
             for i, entry in enumerate(entries):
                 table_ref[i, 1 + seq] = jnp.int32(entry)
         shifted = low_b - count_a
+        at_a, shift_a = window_at(low_a + t * share)
+        at_b, shift_b = window_at(shifted + t * share)
+        at_over, shift_over = window_at(shifted + slots)
+        hot_a = one_hot(steps, shift_a, slot_ids < count_a)
+        hot_b = one_hot(steps, shift_b, slot_ids >= count_a)
+        hot_over = one_hot(spare_steps, shift_over, top)
         for ref, out_ref in ((x_ref, send_x_ref), (c_ref, send_c_ref)):
-            first = load(ref, low_a + t * share, share)
-            second = load(ref, shifted + t * share, share)
-            out_ref[g, :share] = jnp.where(slot_ids < count_a, first, second).astype(BF)
-        over_x_ref[g] = load(x_ref, shifted + slots, 1).astype(BF)
-        spare = send_c_ref.shape[1] - share
-        send_c_ref[g, share:] = load(c_ref, shifted + slots, spare).astype(BF)
+            picked = mm(hot_a, ref[at_a, :], 1, 0) + mm(hot_b, ref[at_b, :], 1, 0)
+            out_ref[g, :share] = picked.astype(BF)
+        over_x_ref[g] = mm(hot_over, x_ref[at_over, :], 1, 0)[:1].astype(BF)
+        send_c_ref[g, share:] = mm(hot_over, c_ref[at_over, :], 1, 0).astype(BF)
+
+    count = lengths.shape[0]
+
+    @pl.loop(0, rows // ROWS)
+    def _(i):
+        row = i * ROWS
+        begun = lambda j, total: total + jnp.where(table_ref[0, 1 + j] <= row, 1, 0)
+        here = lax.fori_loop(0, count, begun, jnp.int32(0)) - 1
+        after = jnp.minimum(here + 1, count - 1)
+        for k, j in enumerate((here, after)):
+            slot = row + table_ref[3, 1 + j] - table_ref[0, 1 + j]
+            start = jnp.clip(jnp.bitwise_and(slot, -16), 0, slots - ROWS)
+            spots_ref[8 * i + 3 * k] = table_ref[2, 1 + j]
+            spots_ref[8 * i + 3 * k + 1] = div(start, 16)
+            spots_ref[8 * i + 3 * k + 2] = slot - start
+        spots_ref[8 * i + 6] = jnp.where(here + 1 < count, table_ref[0, 1 + after] - row, ROWS)
+        spots_ref[8 * i + 7] = jnp.int32(0)
 
     _, off_a, len_a = lookup(2 * d)
     _, off_b, len_b = lookup(2 * d + 1)
-    off_a = lax.rem(off_a, groups)
-    off_b = lax.rem(off_b, groups)
-    meta_ref[0] = lax.div(len_a, BLOCK)
-    meta_ref[1] = lax.div(len_a + BLOCK - 1, BLOCK)
+    off_a = rem(off_a, groups)
+    off_b = rem(off_b, groups)
+    meta_ref[0] = div(len_a, BLOCK)
+    meta_ref[1] = div(len_a + BLOCK - 1, BLOCK)
     meta_ref[2] = t
     meta_ref[3] = off_a
     meta_ref[4] = off_b
@@ -106,8 +149,8 @@
     meta_ref[7] = jnp.int32(0)
 
     def counts(source):
-        first = lax.div(len_a, groups) + extra_of(source, off_a, len_a, groups)[1]
-        second = lax.div(len_b, groups) + extra_of(source, off_b, len_b, groups)[1]
+        first = div(len_a, groups) + extra_of(source, off_a, len_a, groups)[1]
+        second = div(len_b, groups) + extra_of(source, off_b, len_b, groups)[1]
         return first, first + second
 
     @pl.loop(0, groups)
@@ -141,13 +184,14 @@
             num_scalar_prefetch=3,
             grid=(1,),
             in_specs=[whole(rows, width)] * 2,
-            out_specs=[whole(*shape) for shape in shapes] + [smem] * 3,
+            out_specs=[whole(*shape) for shape in shapes] + [smem] * 4,
         ),
         out_shape=[jax.ShapeDtypeStruct(shape, BF) for shape in shapes]
         + [
             jax.ShapeDtypeStruct((HOLES + groups,), jnp.int32),
             jax.ShapeDtypeStruct((4, 1 + lengths.shape[0]), jnp.int32),
             jax.ShapeDtypeStruct((groups * groups,), F32),
+            jax.ShapeDtypeStruct((rows // ROWS * 8,), jnp.int32),
         ],
         compiler_params=pltpu.CompilerParams(vmem_limit_bytes=VMEM_LIMIT),
         cost_estimate=pl.CostEstimate(flops=0, bytes_accessed=20 << 20, transcendentals=0),
@@ -157,13 +201,13 @@
 
 def place(row, groups):
     sub = BLOCK // groups
-    inside = lax.rem(row, BLOCK)
-    return lax.div(inside, sub), lax.div(row, BLOCK) * sub + lax.rem(inside, sub)
+    inside = rem(row, BLOCK)
+    return div(inside, sub), div(row, BLOCK) * sub + rem(inside, sub)
 
 
 def count_first(meta, source, groups):
     turned, extra = extra_of(source, meta[3], meta[5], groups)
-    return turned, lax.div(meta[5], groups) + extra
+    return turned, div(meta[5], groups) + extra
 
 
 def in_second(meta, row, groups):
@@ -174,7 +218,7 @@
 def positions_of(meta, row, groups, slots):
     source, slot = place(row, groups)
     turned, count = count_first(meta, source, groups)
-    turned_b = lax.rem(source - meta[4] + groups, groups)
+    turned_b = rem(source - meta[4] + groups, groups)
     position = jnp.where(slot < count, slot * groups + turned, (slot - count) * groups + turned_b)
     for g in range(groups):
         fills = meta[HOLES + g]
@@ -679,7 +723,7 @@
 
 def middle_kernel(size, groups, *refs):
     x_ref, match_ref, cot_ref, over_ref, norm_ref, blocks_ref = refs[:6]
-    out_hbm, gu_hbm, down_hbm = (refs[6 + i * size : 6 + (i + 1) * size] for i in range(3))
+    weights_hbm = refs[6:12]
     (
         result_ref,
         grad_one_ref,
@@ -701,22 +745,29 @@
         sends,
         recvs,
         keep,
-    ) = refs[6 + 3 * size :]
+    ) = refs[12:]
     index = pl.program_id(0)
     first = index == 0
     d = lax.axis_index("dp")
     t = lax.axis_index("tensor")
     subs, local, _ = arrived_ref.shape[1:]
-    inner = down_hbm[0].shape[1]
-    ids = range(size)
-    part = [slice(r * local, (r + 1) * local) for r in ids]
-    copies_out = [
-        pltpu.make_async_copy(out_hbm[r], w_out_ref.at[part[r]], sems.at[0, r]) for r in ids
-    ]
-    copies_gu = [pltpu.make_async_copy(gu_hbm[r], w_gu_ref.at[r], sems.at[1, r]) for r in ids]
-    copies_down = [
-        pltpu.make_async_copy(down_hbm[r], w_down_ref.at[r], sems.at[2, r]) for r in ids
-    ]
+    inner = w_down_ref.shape[2]
+    ids = (0, 2, 1, 3)
+    part = [slice(r * local, (r + 1) * local) for r in range(size)]
+    core = (d, jnp.bitwise_xor(t, 1))
+    targets = (lambda r: w_out_ref.at[part[r]], lambda r: w_gu_ref.at[r], lambda r: w_down_ref.at[r])
+
+    def weight_copy(kind, r):
+        source = weights_hbm[2 * kind + r // 2]
+        if r % 2 == 0:
+            return pltpu.make_async_copy(source, targets[kind](r), sems.at[kind, r])
+        return remote(source, targets[kind](r), sems.at[kind, r - 1 + size], sems.at[kind, r], core)
+
+    def weight_wait(kind, r):
+        if r % 2 == 0:
+            weight_copy(kind, r).wait()
+        else:
+            weight_copy(kind, r).wait_recv()
 
     def heads_copy(r, i):
         other = jnp.bitwise_xor(t, r)
@@ -733,25 +784,28 @@
     @pl.when(first)
     def _():
         own_copy.start()
-        for copy in copies_out:
-            copy.start()
+        for r in (0, 2):
+            weight_copy(0, r).start()
         greet(1, (1, 2, 3), d, t)
         for i in range(subs):
             for r in (2, 3, 1):
                 heads_copy(r, i).start()
+            if i == 0:
+                for r in (1, 3):
+                    weight_copy(0, r).start()
+        for r in ids:
+            for kind in (1, 2):
+                weight_copy(kind, r).start()
         own_copy.wait()
         for r in ids:
-            copies_gu[r].start()
-            copies_down[r].start()
-        for copy in copies_out:
-            copy.wait()
+            weight_wait(0, r)
 
     for r in ids[1:]:
         heads_copy(r, index).wait_recv()
         heads_copy(r, index).wait_send()
     for r in ids:
         heads_ref[r] = arrived_ref[r, index]
-    heads_out = jnp.concatenate([arrived_ref[r, index] for r in ids], 0)
+    heads_out = jnp.concatenate([arrived_ref[r, index] for r in range(size)], 0)
     attn = mm(heads_out, w_out_ref[...], 0, 0)
     gain_one, gain_two, shift_one, shift_two = (norm_ref[i : i + 1, :] for i in range(4))
     normed_one, unit_one, inverse_one = norm_forward(
@@ -764,8 +818,8 @@
 
         @pl.when(first)
         def _():
-            copies_gu[r].wait()
-            copies_down[r].wait()
+            weight_wait(1, r)
+            weight_wait(2, r)
 
         both = mm(normed, w_gu_ref[r], 1, 0)
         gate = both[:, :inner]
@@ -816,15 +870,20 @@
     def _():
         norm_grad_ref[...] = jnp.zeros_like(norm_grad_ref)
 
+    @pl.when(index == subs - 1)
+    def _():
+        for kind in range(3):
+            for r in (1, 3):
+                weight_copy(kind, r).wait_send()
+
     for i, grad in enumerate((d_gain_one, d_gain_two, d_shift_one, d_shift_two)):
         norm_grad_ref[i : i + 1, :] += grad
 
 
-def middle(x_own, match, cot, norms, o_blocks, w_out_parts, gu_parts, down_parts):
+def middle(x_own, match, cot, norms, o_blocks, size, *weights):
     rows, width = x_own.shape
-    size = len(gu_parts)
     local = o_blocks.shape[1]
-    inner = down_parts[0].shape[1]
+    inner = weights[-1].shape[1]
     block = pl.BlockSpec((BLOCK, width), lambda i: (i, 0))
     turned = pl.BlockSpec((width, BLOCK), lambda i: (0, i))
     anywhere = pl.BlockSpec(memory_space=pl.ANY)
@@ -845,7 +904,7 @@
         in_specs=[block, pl.BlockSpec(memory_space=pltpu.SMEM)]
         + cot_specs
         + [pl.BlockSpec(norms.shape, lambda i: (0, 0))]
-        + [anywhere] * (1 + 3 * size),
+        + [anywhere] * (1 + len(weights)),
         out_specs=[
             block,
             block,
@@ -877,7 +936,7 @@
             pltpu.VMEM((size, BLOCK, inner), F32),
             pltpu.VMEM((size, BLOCK, inner), F32),
             pltpu.VMEM((size, rows // BLOCK, local, BLOCK), BF),
-            pltpu.SemaphoreType.DMA((3, size)),
+            pltpu.SemaphoreType.DMA((3, 2 * size)),
             pltpu.SemaphoreType.DMA((size, rows // BLOCK)),
             pltpu.SemaphoreType.DMA((size, rows // BLOCK)),
             pltpu.SemaphoreType.DMA,
@@ -891,7 +950,7 @@
             transcendentals=rows * size * inner,
         ),
         name="middle",
-    )(x_own, match, cot, cot, norms, o_blocks, *w_out_parts, *gu_parts, *down_parts)
+    )(x_own, match, cot, cot, norms, o_blocks, *weights)
 
 
 def weight_grads_tile(
@@ -953,6 +1012,8 @@
     (
         d_heads_ref,
         result_ref,
+        gu_own_ref,
+        gu_other_ref,
         pair_ref,
         do_ref,
         home_ref,
@@ -994,22 +1055,16 @@
     def own_copy(c):
         return pltpu.make_async_copy(own_ref.at[c, d], home_ref.at[0, d, c], keep.at[c])
 
-    load = pltpu.make_async_copy(result_ref, own_ref, keep.at[chunks])
-    own_heads = pltpu.make_async_copy(d_heads_ref.at[0], do_ref.at[0], keep.at[chunks + 1])
-    own_over = pltpu.make_async_copy(spare_ref.at[d], over_ref.at[0, d], keep.at[chunks + 2])
-
     def pass_on(c):
         own_copy(c).wait()
         for k in range(groups):
             if k > 0:
                 body.arrival(own_ref.at[c, 0], k, (c,), (c,)).wait_recv()
             body.across(k, (c,), (c,)).start()
-            body.beside(0, k, (c,), (c,)).start()
-
-    def pass_far(c):
-        for k in range(groups):
-            body.across(k, (c,), (c,)).wait_recv()
-            body.beside(2, k, (c,), (c,)).start()
+
+    load = pltpu.make_async_copy(result_ref, own_ref, keep.at[chunks])
+    own_heads = pltpu.make_async_copy(d_heads_ref.at[0], do_ref.at[0], keep.at[chunks + 1])
+    own_over = pltpu.make_async_copy(spare_ref.at[d], over_ref.at[0, d], keep.at[chunks + 2])
 
     @pl.when(step == 0)
     def _():
@@ -1033,7 +1088,7 @@
         for k in range(1, groups):
             extra.arrival(spare_ref.at[lax.rem(d + k, groups)], k, (), ()).start()
 
-    for c in range(2):
+    for c in range(chunks - 1):
 
         @pl.when(step == c + 2)
         def _():
@@ -1047,28 +1102,30 @@
         weight_grads_tile(*tile_refs, store)
         grad_copy(step).start()
 
-    @pl.when(step >= 2)
-    def _():
-        grad_copy(step - 2).wait_recv()
-
-        def store(low, high, value):
-            other = got_ref[step - 2, :, low:high].astype(F32)
-            pair_ref[0, :, low:high] = (value + other).astype(BF)
-
-        weight_grads_tile(*tile_refs, store)
+    gu_wide = gu_own_ref.shape[1]
+    for i, gu_ref in ((0, gu_own_ref), (1, gu_other_ref)):
+
+        @pl.when(step == 2 + i)
+        def _():
+            grad_copy(i).wait_recv()
+
+            def store(low, high, value):
+                total = (value + got_ref[i, :, low:high].astype(F32)).astype(BF)
+                if high <= gu_wide:
+                    gu_ref[:, low:high] = total
+                else:
+                    pair_ref[0, :, low - gu_wide : high - gu_wide] = total
+
+            weight_grads_tile(*tile_refs, store)
 
     @pl.when(step == size - 1)
     def _():
-        for c in range(2, chunks):
-            pass_on(c)
         own_over.wait()
         for k in range(groups):
             if k > 0:
                 extra.arrival(spare_ref.at[0], k, (), ()).wait_recv()
             extra.across(k, (), ()).start()
             extra.beside(0, k, (), ()).start()
-        for c in range(chunks):
-            pass_far(c)
         for k in range(groups):
             extra.across(k, (), ()).wait_recv()
             extra.beside(2, k, (), ()).start()
@@ -1078,15 +1135,17 @@
             heads_copy(r).wait_send()
         for i in range(2):
             grad_copy(i).wait_send()
-        for k in range(groups):
-            for c in range(chunks):
-                body.beside(0, k, (c,), (c,)).wait_recv()
-                body.beside(2, k, (c,), (c,)).wait_recv()
+        own_copy(chunks - 1).wait()
+        for c in range(chunks):
+            for k in range(groups):
+                if k > 0 and c == chunks - 1:
+                    body.arrival(own_ref.at[c, 0], k, (c,), (c,)).wait_recv()
                 if k > 0:
                     body.arrival(own_ref.at[c, 0], k, (c,), (c,)).wait_send()
-                body.across(k, (c,), (c,)).wait_send()
-                body.beside(0, k, (c,), (c,)).wait_send()
-                body.beside(2, k, (c,), (c,)).wait_send()
+                if c < chunks - 1:
+                    body.across(k, (c,), (c,)).wait_recv()
+                    body.across(k, (c,), (c,)).wait_send()
+        for k in range(groups):
             extra.beside(0, k, (), ()).wait_recv()
             extra.beside(2, k, (), ()).wait_recv()
             if k > 0:
@@ -1125,15 +1184,19 @@
             anywhere,
         ],
         out_specs=[
-            pl.BlockSpec((1, width, wide), lambda i: (jnp.maximum(i - 2, 0), 0, 0)),
+            pl.BlockSpec((width, 2 * inner), lambda i: (0, 0)),
+            pl.BlockSpec((width, 2 * inner), lambda i: (0, 0)),
+            pl.BlockSpec((1, width, wide - 2 * inner), lambda i: (jnp.maximum(i - 2, 0), 0, 0)),
             anywhere,
             anywhere,
             anywhere,
         ],
         out_shape=[
-            jax.ShapeDtypeStruct((2, width, wide), BF),
+            jax.ShapeDtypeStruct((width, 2 * inner), BF),
+            jax.ShapeDtypeStruct((width, 2 * inner), BF),
+            jax.ShapeDtypeStruct((2, width, wide - 2 * inner), BF),
             jax.ShapeDtypeStruct(d_heads.shape, BF),
-            jax.ShapeDtypeStruct((size, groups, chunks, sub, width), BF),
+            jax.ShapeDtypeStruct((3, groups, chunks, sub, width), BF),
             jax.ShapeDtypeStruct((size, groups, 1, width), BF),
         ],
         scratch_shapes=[
@@ -1145,8 +1208,8 @@
             dma((2,)),
             dma((size,)),
             dma((size,)),
-            dma((4, groups, chunks)),
-            dma((4, groups, chunks)),
+            dma((3, groups, chunks)),
+            dma((3, groups, chunks)),
             dma((4, groups)),
             dma((4, groups)),
             dma((chunks + 3,)),
@@ -1196,6 +1259,70 @@
     other = (pieces[2].astype(F32) + far.astype(F32)).astype(BF)
     across = swap(other, size, 2)
     return pieces[0].astype(F32) + near.astype(F32) + across.astype(F32)
+
+
+def unpack_block(spots_ref, src_ref, i):
+    window = ROWS + 16
+    shape = (ROWS, window)
+    rows = lax.broadcasted_iota(jnp.int32, shape, 0)
+    steps = lax.broadcasted_iota(jnp.int32, shape, 1) - rows
+    bound = spots_ref[8 * i + 6]
+    total = None
+    for k in range(2):
+        group, start, shift = (spots_ref[8 * i + 3 * k + j] for j in range(3))
+        wanted = rows < bound if k == 0 else rows >= bound
+        hot = jnp.where((steps == shift) & wanted, 1.0, 0.0).astype(BF)
+        tiles = [src_ref[group, start + j] for j in range(window // 16)]
+        part = mm(hot, jnp.concatenate(tiles, 0), 1, 0)
+        total = part if k == 0 else total + part
+    return total.astype(BF)
+
+
+def store_over(src_ref, over_ref, last):
+    top = lax.broadcasted_iota(jnp.int32, (16, 1), 0) == 0
+    end = src_ref.shape[1] - 1
+    for g in range(src_ref.shape[0]):
+        src_ref[g, end] = jnp.where(top, over_ref[last, g].astype(F32), 0.0).astype(BF)
+
+
+def unpack_kernel(size, spots, me, home_ref, over_ref, out_ref, src_ref, sems):
+    tiles = home_ref.shape[2]
+
+    def load(r):
+        at = pl.ds(jnp.bitwise_xor(me[0], r) * tiles, tiles)
+        return pltpu.make_async_copy(home_ref.at[r], src_ref.at[:, at], sems.at[r])
+
+    for r in range(size):
+        load(r).start()
+    store_over(src_ref, over_ref, jnp.bitwise_xor(size - 1, me[0]))
+    for r in range(size):
+        load(r).wait()
+    for i in range(out_ref.shape[0] // ROWS):
+        out_ref[i * ROWS : (i + 1) * ROWS, :] = unpack_block(spots, src_ref, i)
+
+
+def unpack(spots, me, home, over):
+    size, groups, share, width = home.shape
+    rows = size * groups * share
+    home = home.reshape(size, groups, share // 16, 16, width)
+    whole = lambda *shape: pl.BlockSpec(shape, lambda i, *refs: (0,) * len(shape))
+    return pl.pallas_call(
+        functools.partial(unpack_kernel, size),
+        grid_spec=pltpu.PrefetchScalarGridSpec(
+            num_scalar_prefetch=2,
+            grid=(1,),
+            in_specs=[pl.BlockSpec(memory_space=pl.ANY), whole(*over.shape)],
+            out_specs=whole(rows, width),
+            scratch_shapes=[
+                pltpu.VMEM((groups, size * share // 16 + 1, 16, width), BF),
+                pltpu.SemaphoreType.DMA((size,)),
+            ],
+        ),
+        out_shape=jax.ShapeDtypeStruct((rows, width), BF),
+        compiler_params=pltpu.CompilerParams(vmem_limit_bytes=VMEM_LIMIT),
+        cost_estimate=pl.CostEstimate(flops=0, bytes_accessed=30 << 20, transcendentals=0),
+        name="unpack",
+    )(spots, me, home, over)
 
 
 def route_kernel(groups, size, send_ref, over_ref, out_ref, over_out_ref, sends, recvs, keep):
@@ -1264,67 +1391,254 @@
     )(send, over)
 
 
+class Halving:
+    def __init__(self, fetch, bits, refs, sems, d, t):
+        self.fetch, self.bits, self.d, self.t = fetch, bits, d, t
+        self.out, self.got, self.held = refs
+        self.send, self.recv = sems
+
+    def mine(self, step):
+        return lax.rem(lax.div(self.d, self.bits[step]), 2)
+
+    def block(self, first, i):
+        one, two, three = self.bits
+        return first * one + lax.rem(i, 2) * two + lax.div(i, 2) * three
+
+    def copy(self, i):
+        step = 0 if i < 4 else 1 if i < 6 else 2
+        return remote(
+            self.out.at[i],
+            self.got.at[i],
+            self.send.at[i],
+            self.recv.at[i],
+            (jnp.bitwise_xor(self.d, self.bits[step]), self.t),
+        )
+
+    def start(self):
+        for i in range(4):
+            self.out[i] = self.fetch(self.block(1 - self.mine(0), jnp.int32(i))).astype(BF)
+            self.copy(i).start()
+
+    def second(self):
+        for i in range(4):
+            self.copy(i).wait_recv()
+        own = self.mine(1)
+        for keep in (False, True):
+            for j in range(2):
+                i = (own if keep else 1 - own) + 2 * j
+                value = self.fetch(self.block(self.mine(0), i)) + self.got[i].astype(F32)
+                if keep:
+                    self.held[j] = value
+                else:
+                    self.out[4 + j] = value.astype(BF)
+                    self.copy(4 + j).start()
+
+    def third(self):
+        for j in range(2):
+            self.copy(4 + j).wait_recv()
+        other = 1 - self.mine(2)
+        self.out[6] = (self.held[other] + self.got[4 + other].astype(F32)).astype(BF)
+        self.copy(6).start()
+
+    def total(self):
+        self.copy(6).wait_recv()
+        own = self.mine(2)
+        return self.held[own] + self.got[4 + own].astype(F32) + self.got[6].astype(F32)
+
+    def finish(self):
+        for i in range(7):
+            self.copy(i).wait_send()
+
+
 def settle_kernel(
     groups,
     size,
     match_ref,
-    back_ref,
-    one_ref,
-    gq_ref,
+    spots_ref,
+    res_over_ref,
+    d_hbm,
+    x_hbm,
+    w_hbm,
+    one_hbm,
+    gu_own_hbm,
+    gu_other_hbm,
+    res_hbm,
     home_ref,
     over_ref,
-    sum_ref,
-    far_ref,
-    near_ref,
+    result_hbm,
+    gq_sum_ref,
+    gu_sum_ref,
+    d_ref,
+    x_ref,
+    w_ref,
+    one_ref,
+    gu_own_ref,
+    gu_other_ref,
+    src_ref,
+    out_ref,
+    to_core_ref,
+    from_core_ref,
     pair_ref,
     other_ref,
     own_ref,
     spare_ref,
-    gqr_ref,
-    sends,
-    recvs,
-    s_over,
-    r_over,
-    s_sum,
-    r_sum,
-    s_gq,
-    r_gq,
-    keep,
+    gq_ref,
+    *refs,
 ):
+    halving_refs = (refs[:3], refs[3:6], refs[6:9])
+    (
+        loads,
+        s_res,
+        r_res,
+        s_half,
+        r_half,
+        sends,
+        recvs,
+        s_over,
+        r_over,
+        s_sum,
+        r_sum,
+        keep,
+    ) = refs[9:]
     d = lax.axis_index("dp")
     t = lax.axis_index("tensor")
     chunks, _, sub, width = own_ref.shape
-    greet(groups, (1, 2), d, t)
+    tiles = res_hbm.shape[2]
+    sent = (chunks - 1) * tiles // chunks
+    rest = tiles - sent
     core = (d, jnp.bitwise_xor(t, 1))
     chip = (d, jnp.bitwise_xor(t, 2))
 
+    def load(source, target, i):
+        return pltpu.make_async_copy(source, target, loads.at[i])
+
+    def load_d(r):
+        part = jnp.bitwise_xor(t, r)
+        return load(d_hbm.at[part], d_ref.at[part], r)
+
+    load_w = load(w_hbm, w_ref, 4)
+    load_x = load(x_hbm, x_ref, 5)
+    load_one = load(one_hbm, one_ref, 6)
+    load_gu = (load(gu_own_hbm, gu_own_ref, 7), load(gu_other_hbm, gu_other_ref, 8))
+
+    def slots_of(r, low, count):
+        return pl.ds(jnp.bitwise_xor(t, r) * tiles + low, count)
+
+    def source_of(r, low, count):
+        return res_hbm.at[r, :, pl.ds(low, count)]
+
+    def in_src(r, low, count):
+        return src_ref.at[:, slots_of(r, low, count)]
+
+    load_res = (
+        load(source_of(0, 0, tiles), in_src(0, 0, tiles), 9),
+        load(source_of(2, 0, sent), in_src(2, 0, sent), 10),
+    )
+    beside_res = (
+        remote(source_of(0, 0, tiles), in_src(0, 0, tiles), s_res.at[0], r_res.at[0], core),
+        remote(source_of(2, 0, sent), in_src(2, 0, sent), s_res.at[1], r_res.at[1], core),
+        remote(in_src(2, sent, rest), in_src(2, sent, rest), s_res.at[2], r_res.at[2], core),
+    )
+    across_res = remote(
+        source_of(0, sent, rest), in_src(0, sent, rest), s_res.at[3], r_res.at[3], chip
+    )
+
+    load_w.start()
+    for r in (3, 2, 1, 0):
+        load_d(r).start()
+    load_gu[0].start()
+    load_gu[1].start()
+    load_x.start()
+    load_one.start()
+    load_res[0].start()
+    load_res[1].start()
+    greet(groups, (1, 2), d, t)
+    across_res.start()
+
     def rows(c):
-        return pl.ds(c * BLOCK, BLOCK)
-
-    def far(c):
-        return remote(back_ref.at[3, rows(c)], far_ref.at[c], s_sum.at[0, c], r_sum.at[0, c], core)
-
-    def near(c):
-        return remote(back_ref.at[1, rows(c)], near_ref.at[c], s_sum.at[1, c], r_sum.at[1, c], core)
+        return slice(c * BLOCK, (c + 1) * BLOCK)
+
+    def piece(r, c):
+        return mm(d_ref[jnp.bitwise_xor(t, r), :, rows(c)], w_ref[...], 0, 0)
+
+    def to_core(i, c):
+        return remote(
+            to_core_ref.at[i, c], from_core_ref.at[i, c], s_sum.at[i, c], r_sum.at[i, c], core
+        )
 
     def other(c):
         return remote(pair_ref.at[c], other_ref.at[c], s_sum.at[2, c], r_sum.at[2, c], chip)
 
-    def gq(k):
-        to = lax.rem(d + k, groups)
-        return remote(gq_ref.at[to], gqr_ref.at[d], s_gq.at[k], r_gq.at[k], (to, t))
-
+    load_w.wait()
+    load_d(3).wait()
     for c in range(chunks):
-        far(c).start()
+        to_core_ref[0, c] = piece(3, c).astype(BF)
+        to_core(0, c).start()
+    load_d(2).wait()
     for c in range(chunks):
-        near(c).start()
+        value = piece(2, c)
+        to_core(0, c).wait_recv()
+        pair_ref[c] = (value + from_core_ref[0, c].astype(F32)).astype(BF)
+        other(c).start()
+    block_rows = gu_sum_ref.shape[0]
+
+    wide = gu_sum_ref.shape[1] // 2
+
+    def gu_rows(low, block):
+        at = pl.ds(pl.multiple_of(block * block_rows, block_rows), block_rows)
+        columns = slice(low, low + wide)
+        return gu_own_ref[at, columns].astype(F32) + gu_other_ref[at, columns].astype(F32)
+
+    sums = [
+        Halving(fetch, bits, halving_refs[i], (s_half.at[i], r_half.at[i]), d, t)
+        for i, (fetch, bits) in enumerate(
+            (
+                (functools.partial(gu_rows, 0), (1, 2, 4)),
+                (functools.partial(gu_rows, wide), (2, 1, 4)),
+                (lambda block: gq_ref[block].astype(F32), (1, 2, 4)),
+            )
+        )
+    ]
+
+    load_gu[0].wait()
+    load_gu[1].wait()
+    sums[0].start()
+    sums[1].start()
+    load_d(1).wait()
     for c in range(chunks):
-        far(c).wait_recv()
-        pair = back_ref[2, rows(c), :].astype(F32) + far_ref[c].astype(F32)
-        pair_ref[c] = pair.astype(BF)
-        other(c).start()
-    own_gq = pltpu.make_async_copy(gq_ref.at[d], gqr_ref.at[d], keep.at[chunks])
-    own_gq.start()
+        to_core_ref[1, c] = piece(1, c).astype(BF)
+        to_core(1, c).start()
+    load_d(0).wait()
+    load_one.wait()
+    for c in range(chunks):
+        one_ref[rows(c), :] += piece(0, c)
+
+    def start_gq():
+        load_x.wait()
+        total = mm(d_ref[0], x_ref[0], 1, 0)
+        for part in range(1, size):
+            total = total + mm(d_ref[part], x_ref[part], 1, 0)
+        total = total.T.astype(BF)
+        for g in range(groups):
+            gq_ref[g] = total[g * block_rows : (g + 1) * block_rows]
+        sums[2].start()
+
+    def store_result(i):
+        at = pl.ds(i * ROWS, ROWS)
+        return pltpu.make_async_copy(out_ref.at[at], result_hbm.at[at], keep.at[chunks + 1 + i])
+
+    blocks = out_ref.shape[0] // ROWS
+
+    def arrange_result():
+        for copy in load_res:
+            copy.wait()
+        for copy in beside_res:
+            copy.wait_recv()
+        for i in range(blocks):
+            out_ref[i * ROWS : (i + 1) * ROWS, :] = unpack_block(spots_ref, src_ref, i)
+            store_result(i).start()
+
+    store_over(src_ref, res_over_ref, jnp.bitwise_xor(size - 1, t))
 
     body = Spread(home_ref, (sends, recvs), groups, d, t)
     extra = Spread(over_ref, (s_over, r_over), groups, d, t)
@@ -1332,7 +1646,7 @@
     def own_copy(c):
         return pltpu.make_async_copy(own_ref.at[c, d], home_ref.at[0, d, c], keep.at[c])
 
-    own_over = pltpu.make_async_copy(spare_ref.at[d], over_ref.at[0, d], keep.at[chunks + 1])
+    own_over = pltpu.make_async_copy(spare_ref.at[d], over_ref.at[0, d], keep.at[chunks])
 
     def pass_on(c):
         own_copy(c).wait()
@@ -1348,10 +1662,8 @@
             body.beside(2, k, (c,), (c,)).start()
 
     for c in range(chunks):
-        near(c).wait_recv()
-        partial = (
-            one_ref[rows(c), :] + back_ref[0, rows(c), :].astype(F32) + near_ref[c].astype(F32)
-        )
+        to_core(1, c).wait_recv()
+        partial = one_ref[rows(c), :] + from_core_ref[1, c].astype(F32)
         other(c).wait_recv()
         done = (partial + other_ref[c].astype(F32)).astype(BF)
         for g in range(groups):
@@ -1360,9 +1672,7 @@
         for k in range(1, groups):
             body.arrival(own_ref.at[c, lax.rem(d + k, groups)], k, (c,), (c,)).start()
         if c == chunks - 1:
-            last = [
-                own_ref[c, g, sub - 16 :, :].astype(F32)[15:16] for g in range(groups)
-            ]
+            last = [own_ref[c, g, sub - 16 :, :].astype(F32)[15:16] for g in range(groups)]
             for to in range(groups):
                 spare = last[0] * match_ref[to]
                 for g in range(1, groups):
@@ -1372,31 +1682,45 @@
             for k in range(1, groups):
                 extra.arrival(spare_ref.at[lax.rem(d + k, groups)], k, (), ()).start()
         if c == 0:
-            for k in range(1, groups):
-                gq(k).start()
+            across_res.wait_recv()
+            for copy in beside_res:
+                copy.start()
+            start_gq()
+            sums[0].second()
+            sums[1].second()
         else:
             pass_on(c - 1)
+        if c == 1:
+            sums[0].third()
+            sums[1].third()
+    sums[2].second()
     pass_on(chunks - 1)
+    sums[2].third()
+    arrange_result()
     own_over.wait()
     for k in range(groups):
         if k > 0:
             extra.arrival(spare_ref.at[0], k, (), ()).wait_recv()
         extra.across(k, (), ()).start()
         extra.beside(0, k, (), ()).start()
-    own_gq.wait()
-    total = gqr_ref[d].astype(F32)
-    for k in range(1, groups):
-        gq(k).wait_recv()
-        total = total + gqr_ref[lax.rem(d - k + groups, groups)].astype(F32)
-    sum_ref[...] = total
+    gu_sum_ref[:, :wide] = sums[0].total()
+    gu_sum_ref[:, wide:] = sums[1].total()
+    gq_sum_ref[...] = sums[2].total()
     for c in range(chunks):
         pass_far(c)
     for k in range(groups):
         extra.across(k, (), ()).wait_recv()
         extra.beside(2, k, (), ()).start()
+    across_res.wait_send()
+    for copy in beside_res:
+        copy.wait_send()
+    for i in range(blocks):
+        store_result(i).wait()
+    for each in sums:
+        each.finish()
     for c in range(chunks):
-        far(c).wait_send()
-        near(c).wait_send()
+        to_core(0, c).wait_send()
+        to_core(1, c).wait_send()
         other(c).wait_send()
     for k in range(groups):
         for c in range(chunks):
@@ -1410,118 +1734,84 @@
         extra.beside(0, k, (), ()).wait_recv()
         extra.beside(2, k, (), ()).wait_recv()
         if k > 0:
-            gq(k).wait_send()
             extra.arrival(spare_ref.at[0], k, (), ()).wait_send()
         extra.across(k, (), ()).wait_send()
         extra.beside(0, k, (), ()).wait_send()
         extra.beside(2, k, (), ()).wait_send()
 
 
-def settle(match, back_rel, grad_one, grad_qkv):
-    size, rows, width = back_rel.shape
-    groups, part, local = grad_qkv.shape
+def settle(match, spots, res_over, d_qkv_t, x_all, w_t, grad_one, gu_own, gu_other, res):
+    size, local, rows = d_qkv_t.shape
+    _, groups, share, width = res.shape
+    res = res.reshape(-1, groups, share // 16, 16, width)
     chunks = rows // BLOCK
     sub = BLOCK // groups
+    part = width // groups
+    wide = gu_own.shape[1]
+    total_rows = size * rows
     anywhere = pl.BlockSpec(memory_space=pl.ANY)
     vmem = pl.BlockSpec(memory_space=pltpu.VMEM)
+    smem = pl.BlockSpec(memory_space=pltpu.SMEM)
     dma = pltpu.SemaphoreType.DMA
+    shape = jax.ShapeDtypeStruct
     buffer = pltpu.VMEM((chunks, BLOCK, width), BF)
+    pair_buffer = pltpu.VMEM((2, chunks, BLOCK, width), BF)
+    halving = lambda columns: [
+        pltpu.VMEM((7, part, columns), BF),
+        pltpu.VMEM((7, part, columns), BF),
+        pltpu.VMEM((2, part, columns), F32),
+    ]
     return pl.pallas_call(
         functools.partial(settle_kernel, groups, size),
-        in_specs=[pl.BlockSpec(memory_space=pltpu.SMEM), vmem, vmem, anywhere],
-        out_specs=[anywhere, anywhere, vmem],
+        in_specs=[smem, smem, vmem] + [anywhere] * 7,
+        out_specs=[anywhere, anywhere, anywhere, vmem, vmem],
         out_shape=[
-            jax.ShapeDtypeStruct((size, groups, chunks, sub, width), BF),
-            jax.ShapeDtypeStruct((size, groups, 1, width), BF),
-            jax.ShapeDtypeStruct((part, local), F32),
+            shape((size, groups, chunks, sub, width), BF),
+            shape((size, groups, 1, width), BF),
+            shape((total_rows, width), BF),
+            shape((part, local), F32),
+            shape((part, wide), F32),
         ],
         scratch_shapes=[
-            buffer,
-            buffer,
+            pltpu.VMEM(d_qkv_t.shape, BF),
+            pltpu.VMEM(x_all.shape, BF),
+            pltpu.VMEM(w_t.shape, BF),
+            pltpu.VMEM(grad_one.shape, F32),
+            pltpu.VMEM(gu_own.shape, BF),
+            pltpu.VMEM(gu_own.shape, BF),
+            pltpu.VMEM((groups, size * share // 16 + 1, 16, width), BF),
+            pltpu.VMEM((total_rows, width), BF),
+            pair_buffer,
+            pair_buffer,
             buffer,
             buffer,
             pltpu.VMEM((chunks, groups, sub, width), BF),
             pltpu.VMEM((groups, 1, width), BF),
             pltpu.VMEM((groups, part, local), BF),
+            *halving(wide // 2),
+            *halving(wide // 2),
+            *halving(local),
+            dma((11,)),
+            dma((4,)),
+            dma((4,)),
+            dma((3, 7)),
+            dma((3, 7)),
             dma((4, groups, chunks)),
             dma((4, groups, chunks)),
             dma((4, groups)),
             dma((4, groups)),
             dma((3, chunks)),
             dma((3, chunks)),
-            dma((groups,)),
-            dma((groups,)),
-            dma((chunks + 2,)),
+            dma((chunks + 1 + total_rows // ROWS,)),
         ],
         compiler_params=pltpu.CompilerParams(
             collective_id=1, has_side_effects=True, vmem_limit_bytes=VMEM_LIMIT
         ),
-        cost_estimate=pl.CostEstimate(flops=0, bytes_accessed=150 << 20, transcendentals=0),
+        cost_estimate=pl.CostEstimate(
+            flops=4 * size * rows * local * width, bytes_accessed=150 << 20, transcendentals=0
+        ),
         name="settle",
-    )(match, back_rel, grad_one, grad_qkv)
-
-
-ROWS = 32
-
-
-def unpack_kernel(info, home_ref, over_ref, out_ref, src_ref, dst_ref):
-    size, groups, share, _ = home_ref.shape
-    rows = out_ref.shape[0]
-    slots = size * share
-    me = info[0, 0]
-
-    @pl.loop(0, size)
-    def _(part):
-        source = jnp.bitwise_xor(part, me)
-        at = pl.ds(pl.multiple_of(ROWS + part * share, 8), share)
-        for g in range(groups):
-            src_ref[g, at, :] = home_ref[source, g].astype(F32)
-
-    last = jnp.bitwise_xor(size - 1, me)
-    for g in range(groups):
-        src_ref[g, ROWS + slots : ROWS + slots + 1, :] = over_ref[last, g].astype(F32)
-    row_ids = lax.broadcasted_iota(jnp.int32, (ROWS, 1), 0)
-
-    @pl.loop(0, info.shape[1] - 1)
-    def _(j):
-        low = info[0, 1 + j]
-        count = info[1, 1 + j]
-        group = info[2, 1 + j]
-        first = info[3, 1 + j]
-
-        @pl.loop(low // ROWS, (low + count + ROWS - 1) // ROWS)
-        def _(i):
-            start = i * ROWS + first - low + ROWS
-            offset = jnp.bitwise_and(start, 7)
-            loaded = src_ref[group, pl.ds(pl.multiple_of(start - offset, 8), ROWS + 8), :]
-            moved = pltpu.roll(loaded, ROWS + 8 - offset, 0)[:ROWS]
-            at = pl.ds(pl.multiple_of(i * ROWS, ROWS), ROWS)
-            dst_ref[at, :] = jnp.where(row_ids >= low - i * ROWS, moved, dst_ref[at, :])
-
-    out_ref[...] = dst_ref[:rows, :].astype(BF)
-
-
-def unpack(info, home, over):
-    size, groups, share, width = home.shape
-    rows = size * groups * share
-    whole = lambda *shape: pl.BlockSpec(shape, lambda i, info: (0,) * len(shape))
-    return pl.pallas_call(
-        unpack_kernel,
-        grid_spec=pltpu.PrefetchScalarGridSpec(
-            num_scalar_prefetch=1,
-            grid=(1,),
-            in_specs=[whole(*home.shape), whole(*over.shape)],
-            out_specs=whole(rows, width),
-            scratch_shapes=[
-                pltpu.VMEM((groups, size * share + 4 * ROWS, width), F32),
-                pltpu.VMEM((rows + ROWS, width), F32),
-            ],
-        ),
-        out_shape=jax.ShapeDtypeStruct((rows, width), BF),
-        compiler_params=pltpu.CompilerParams(vmem_limit_bytes=VMEM_LIMIT),
-        cost_estimate=pl.CostEstimate(flops=0, bytes_accessed=30 << 20, transcendentals=0),
-        name="unpack",
-    )(info, home, over)
+    )(match, spots, res_over, d_qkv_t, x_all, w_t, grad_one, gu_own, gu_other, res)
 
 
 def local(tokens, cotangent, lengths, dealing, w_qkv, w_out, w_gu, w_down, gains, shifts):
@@ -1535,11 +1825,11 @@
     own_rows = rows // size
     subs = own_rows // BLOCK
     sub = share // subs
-    fused = sub % 16 == 0
+    fused = groups == 8 and sub % 16 == 0
     i32 = jnp.int32
 
     ids = jnp.stack([lax.axis_index("dp"), me]).astype(i32)
-    send_x, over_x, send_c, meta, table, match = pack(
+    send_x, over_x, send_c, meta, table, match, spots = pack(
         lengths,
         dealing,
         ids,
@@ -1587,10 +1877,6 @@
     o_blocks, lse = attend(meta, q, k_rows, v, groups)
     o_blocks, far_gu, cot = lax.optimization_barrier((o_blocks, far_gu, cot))
 
-    spread_parts = lambda near, far: [near, swap(near, size, 1), far, swap(far, size, 1)]
-    w_out_parts = spread_parts(w_out.T, far_out)
-    down_parts = spread_parts(w_down, far_down)
-    gu_parts = spread_parts(near_gu, far_gu)
     norms = jnp.concatenate([gains.T, shifts.T], 0)
     (
         result_own,
@@ -1603,13 +1889,27 @@
         hidden,
         d_gu,
         norm_grads,
-    ) = middle(x_own, match, cot, norms, o_blocks, w_out_parts, gu_parts, down_parts)
+    ) = middle(
+        x_own,
+        match,
+        cot,
+        norms,
+        o_blocks,
+        size,
+        w_out.T,
+        far_out,
+        near_gu,
+        far_gu,
+        w_down,
+        far_down,
+    )
     grad_args = (normed_t, d_branch_t, d_attn_t, hidden, d_gu, heads_own, norm_grads)
     if fused:
-        pair, do_rel, home_result, over_result = grads(
+        gu_own, gu_other, pair, do_rel, home_result, over_result = grads(
             match, groups, *grad_args, d_heads, result_own
         )
-        home_result = (home_result.reshape(size, groups, share, width), over_result)
+        home_result = home_result.reshape(3, groups, share, width)
+        gu_other = swap(gu_other, size, 2)
     else:
         sent_grads = weight_grads(1, *grad_args)
         kept_grads = weight_grads(0, *grad_args)
@@ -1619,9 +1919,6 @@
     d_qkv_t = attend_back(
         meta, q, k_rows, k, v_rows, o_blocks, do_rel, lse, cosine, sine, groups
     )
-    back_rel, grad_qkv = project_back(meta, d_qkv_t, x_all, w_qkv_t)
-    grad_qkv = grad_qkv.reshape(groups, width // groups, 3 * local_width)
-
     pair = lax.psum_scatter(pair, "dp", scatter_dimension=1, tiled=True)
     def send_back(own):
         body = own.reshape(subs, groups, sub, width).transpose(1, 0, 2, 3)
@@ -1636,12 +1933,23 @@
         return tuple(jnp.stack(gather_members(a)) for a in pair)
 
     if fused:
-        home_input, home_over, qkv_sum = settle(
-            match, back_rel, grad_one, grad_qkv
+        home_input, home_over, result, qkv_sum, gu_sum = settle(
+            match,
+            spots,
+            over_result,
+            d_qkv_t,
+            x_all,
+            w_qkv_t,
+            grad_one,
+            gu_own,
+            gu_other,
+            home_result,
         )
-        home_input = (home_input.reshape(size, groups, share, width), home_over)
+        home_input = home_input.reshape(size, groups, share, width)
         pair, home_input = lax.optimization_barrier((pair, home_input))
     else:
+        back_rel, grad_qkv = project_back(meta, d_qkv_t, x_all, w_qkv_t)
+        grad_qkv = grad_qkv.reshape(groups, width // groups, 3 * local_width)
         home_result = send_back(result_own)
         input_own = grad_one + reduce_members([back_rel[r] for r in range(size)])
         home_input = send_back(input_own.astype(BF))
@@ -1650,15 +1958,17 @@
     qkv_sum = qkv_sum.reshape(-1, 3, local_width)
     summed = pair[0].astype(F32) + swap(pair[1], size, 2).astype(F32)
     inner = w_down.shape[1]
-    gu_sum = summed[:, : 2 * inner].reshape(-1, 2, inner)
-    down_sum = summed[:, 2 * inner : 3 * inner]
-    out_sum = summed[:, 3 * inner : 3 * inner + local_width]
-    norm_sum = summed[:, 3 * inner + local_width : 3 * inner + local_width + 4]
+    if not fused:
+        gu_sum, summed = summed[:, : 2 * inner], summed[:, 2 * inner :]
+    gu_sum = gu_sum.reshape(-1, 2, inner)
+    down_sum = summed[:, :inner]
+    out_sum = summed[:, inner : inner + local_width]
+    norm_sum = summed[:, inner + local_width : inner + local_width + 4]
     norm_sum = lax.dynamic_slice_in_dim(
         norm_sum, me * (norm_sum.shape[0] // size), norm_sum.shape[0] // size, 0
     )
     if fused:
-        arrange = functools.partial(unpack, table)
+        input_grad = unpack(spots, me[None], home_input, home_over)
     else:
         row_ids = jnp.arange(rows, dtype=i32)[None, :]
         low, count, group, first = (table[i, 1:][:, None] for i in range(4))
@@ -1672,8 +1982,10 @@
             every = jnp.concatenate([home, over], 2).reshape(-1, width)
             return jnp.take(every, flat, axis=0)
 
-    result = arrange(*home_result).reshape(rows, 1, width)
-    input_grad = arrange(*home_input).reshape(rows, 1, width)
+        result = arrange(*home_result)
+        input_grad = arrange(*home_input)
+    result = result.reshape(rows, 1, width)
+    input_grad = input_grad.reshape(rows, 1, width)
     return (
         result,
         input_grad,

time: 463 us -> 405 us (0.87); the launches traced: 463 us -> 399 us
  Pallas kernels: 409 us -> 343 us
  local copies, waits for them, and re-layouts: 11.1 us -> 17.7 us
  waiting for transfers between devices: 13.1 us -> 6.91 us
    pallas_call x1, Pallas kernels: 107 us -> 76.1 us  [settle(): pl.pallas_call(functools.partial(settle_kernel, groups, size), in_specs=[...]
    pallas_call x3 -> x1, Pallas kernels: 33.1 us -> 8.93 us  [unpack(): pl.pallas_call(functools.partial(unpack_kernel, size), grid_spec=pltpu.Pr...]
    pallas_call x1, Pallas kernels: 55.2 us -> 46.3 us  [grads(): pl.pallas_call(functools.partial(grads_kernel, groups, size), grid=(size,...]
    ppermute x10 -> x5, waiting for transfers between devices: 13.1 us -> 6.87 us  [swap(): return lax.ppermute(array, 'tensor', [(i, i ^ step) for i in range(size)])]
    unnamed x26 -> x23, local copies, waits for them, and re-layouts: 6.13 us -> 11.8 us
  transfers between devices with their start and end apart: 12 -> 7, of which waited for: 4 -> 1; matrix products, arithmetic and copies ran while one was open for 1% -> 2% of each run, Pallas kernels for 66% -> 62%
where the time goes in v4:
time: 405 us; the launch traced here: 399 us
  Pallas kernels  343 us (85%)
  local copies, waits for them, and re-layouts  17.7 us (4%)
  starting transfers between devices  15.2 us (4%)
  between operations  14.8 us (4%)
  waiting for transfers between devices  6.91 us (2%)
    pallas_call x1, Pallas kernels, settle(): pl.pallas_call(functools.partial(settle_kernel, groups, size), in_specs=[...  76.1 us
    pallas_call x1, Pallas kernels, attend_back(): pl.pallas_call(functools.partial(attend_back_kernel, groups), grid_spec=p...  58.5 us
    pallas_call x1, Pallas kernels, middle(): pl.pallas_call(functools.partial(middle_kernel, size, groups), grid=(rows...  49.9 us
    pallas_call x1, Pallas kernels, grads(): pl.pallas_call(functools.partial(grads_kernel, groups, size), grid=(size,...  46.3 us
    pallas_call x1, Pallas kernels, route(): pl.pallas_call(functools.partial(route_kernel, groups, size), in_specs=[a...  45.2 us
    pallas_call x1, Pallas kernels, attend(): pl.pallas_call(functools.partial(attend_kernel, groups), grid_spec=pltpu....  32.8 us
    pallas_call x1, Pallas kernels, pack(): pl.pallas_call(functools.partial(pack_kernel, groups, size), grid_spec=pl...  14.1 us
    unnamed x23, local copies, waits for them, and re-layouts  11.8 us
  transfers between devices with their start and end apart: 7, of which 1 were waited for; matrix products, arithmetic and copies ran while one was open for 2% of the time, Pallas kernels for 62%

profile of v4, /device:TPU:0, one launch (start us, length us, event | category | flops | bytes accessed | tf_op | source)
XLA Modules:
  0.0 399.3 jit_solution(5030591128829218693)
XLA Ops:
  7.2 3.0 collective-permute-start.1
  10.2 0.1 collective-permute-start
  10.3 0.6 pad_add_fusion.ids
  10.8 14.1 %pack.1 = (bf16[8,96,768]{2,1,0:T(8,128)(2,1)}, bf16[8,1,768]{2,1,0:T(2,128)(2,1)}, bf16[8,112,768]{2,1,0:T(8,128)(2,1)}, s32[16]{0:T(128)}, s32[4,17]{1,0:T(4,128)}, /*index=5*/f32[64]{0:T(128)}, s32[192]{0:T(256)}) custom-call(s32[16]{0:T(128)} %lengths.1, s32[16]{0:T(128)} %dealing.1, s32[2]{0:T(128)} %pad_add_fusion.ids, bf16[3072,768]{1,0:T(8,128)(2,1)} %bitcast.24, ...), custom_call_target="tpu_custom_call" | custom-call | bytes 20971520 | tf_op jit(solution)/shard_map/pack/pallas_call | solution.py:181
  25.0 0.0 copy-start
  25.0 45.2 %route.1 = (bf16[4,8,96,768]{3,2,1,0:T(8,128)(2,1)}, bf16[8,1,768]{2,1,0:T(2,128)(2,1)}) custom-call(bf16[8,96,768]{2,1,0:T(8,128)(2,1)} %get-tuple-element.63.send_ref, bf16[8,1,768]{2,1,0:T(2,128)(2,1)} %get-tuple-element.64.over_ref), custom_call_target="tpu_custom_call" | custom-call | bytes 62914560 | tf_op jit(solution)/shard_map/route/pallas_call | solution.py:1375
  70.1 0.0 collective-permute-done.refs_7_
  70.2 0.0 collective-permute-done.1.refs_11_
  70.2 0.0 copy-start.8
  70.2 7.1 %all-to-all-start = ((bf16[8,112,768]{2,1,0:T(8,128)(2,1)}), bf16[8,112,768]{2,1,0:T(8,128)(2,1)}, u32[]{:S(2)}, u32[]{:S(2)}) async-start(bf16[8,112,768]{2,1,0:T(8,128)(2,1)} %get-tuple-element.75), calls=%async_computation | async-start | bytes 2752512 | tf_op jit(solution)/shard_map/all_to_all | solution.py:1843
  77.3 0.0 reduce-scatter.2.cloned.1.call-start
  77.3 0.0 copy-done
  77.3 0.0 copy-start.3
  77.3 0.0 copy-start.4
  77.4 0.4 copy.30
  77.8 0.0 copy-done.8
  77.8 0.0 copy-start.1
  77.8 1.3 collective-permute-start.2
  79.1 0.0 copy-done.3
  79.1 0.0 copy-done.4
  79.1 0.6 pad_maximum_fusion.refs_4_
  79.7 0.6 multiply_power_fusion.freq_ref
  80.4 11.0 %project.1 = (bf16[192,3072]{1,0:T(8,128)(2,1)}, bf16[192,3072]{1,0:T(8,128)(2,1)}, bf16[240,3072]{1,0:T(8,128)(2,1)}, bf16[3,3072,64]{2,1,0:T(8,128)(2,1)}, bf1...) custom-call(s32[16]{0:T(128)} %get-tuple-element.61.meta.info, ...), custom_call_target="tpu_custom_call" | custom-call | flops 2717908992 | bytes 16777216 | tf_op jit(solution)/shard_map/project/pallas_call | solution.py:329
  91.4 0.0 copy-done.1
  91.4 32.8 %attend.1 = (bf16[12,192,256]{2,1,0:T(8,128)(2,1)}, f32[3,3072]{1,0:T(4,128)}) custom-call(s32[16]{0:T(128)} %get-tuple-element.61.meta.info, bf16[192,3072]{1,0:T(8,128)(2,1)} %get-tuple-element.70.q_ref, bf16[3,3072,64]{2,1,0:T(8,128)(2,1)} %get-tuple-element.71.k_ref.krow_ref, bf16[240,3072]{1,0:T(8,128)(2,1)} %get-tuple-element.72.v_ref), custom_call_target="tpu_custom_call" | custom-call | flops 14495514624 | bytes 8388608 | tf_op jit(solution)/shard_map/attend/pallas_call | solution.py:426
  124.3 6.9 %collective-permute-done.2.refs_9_ = bf16[768,1536]{1,0:T(8,128)(2,1)S(1)} collective-permute-done((bf16[768,1536]{1,0:T(8,128)(2,1)S(1)}, bf16[768,1536]{1,0:T(8,128)(2,1)S(1)}, u32[]{:S(2)}, u32[]{:S(2)}) %collective-permute-start.2) | collective-permute-done | bytes 2359328 | tf_op jit(solution)/shard_map/ppermute | solution.py:1241
  131.1 0.0 copy-start.5
  131.1 0.0 all-to-all-done.refs_2_.refs_3_
  131.1 1.4 copy-done.5
  132.5 49.9 %middle.1 = (bf16[768,768]{1,0:T(8,128)(2,1)}, f32[768,768]{1,0:T(8,128)}, bf16[4,192,768]{2,1,0:T(8,128)(2,1)}, bf16[4,192,768]{2,1,0:T(8,128)(2,1)}, bf16[768,...) custom-call(bf16[768,768]{1,0:T(8,128)(2,1)} %get-tuple-element.69.r, ...), custom_call_target="tpu_custom_call" | custom-call | flops 23555211264 | bytes 41943040 | tf_op jit(solution)/shard_map/middle/pallas_call | solution.py:901
  182.4 46.3 %grads.1 = (bf16[768,1536]{1,0:T(8,128)(2,1)}, bf16[768,1536]{1,0:T(8,128)(2,1)}, bf16[2,768,1024]{2,1,0:T(8,128)(2,1)}, bf16[4,192,768]{2,1,0:T(8,128)(2,1)}, b...) custom-call(f32[64]{0:T(128)} %get-tuple-element.59.match_ref.refs_1_, ...), custom_call_target="tpu_custom_call" | custom-call | flops 11777605632 | bytes 83886080 | tf_op jit(solution)/shard_map/grads/pallas_call | solution.py:1171
  228.8 0.0 copy-start.6
  228.8 0.0 reduce-scatter.2.cloned.1.call-update
  228.8 1.6 copy-done.6
  230.4 1.2 collective-permute-start.3
  231.7 58.5 %attend_back.1.d_hbm = bf16[4,576,768]{2,1,0:T(8,128)(2,1)} custom-call(s32[16]{0:T(128)} %get-tuple-element.61.meta.info, bf16[192,3072]{1,0:T(8,128)(2,1)} %get-tuple-element.70.q_ref, bf16[3,3072,64]{2,1,0:T(8,128)(2,1)} %get-tuple-element.71.k_ref.krow_ref, bf16[192,3072]{1,0:T(8,128)(2,1)} %get-tuple-element.91.k_ref, ...), custom_call_target="tpu_custom_call" | custom-call | flops 36238786560 | bytes 16777216 | tf_op jit(solution)/shard_map/attend_back/pallas_call | solution.py:554
  290.2 0.0 collective-permute-done.3.gu_other_hbm
  290.2 0.0 copy-start.7
  290.2 1.4 copy-done.7
  291.6 76.1 %settle.1 = (bf16[4,8,3,32,768]{4,3,2,1,0:T(8,128)(2,1)}, bf16[4,8,1,768]{3,2,1,0:T(2,128)(2,1)}, bf16[3072,768]{1,0:T(8,128)(2,1)}, f32[96,576]{1,0:T(8,128)}, f32[96,1536]{1,0:T(8,128)}) custom-call(f32[64]{0:T(128)} %get-tuple-element.59.match_ref.refs_1_, s32[192]{0:T(256)} %get-tuple-element.60.spots_ref.spots, ...), custom_call_target="tpu_custom_call" | custom-call | flops 5435817984 | bytes 157286400 | tf_op jit(solution)/shard_map/settle/pallas_call | solution.py:1764
  367.7 0.0 reduce-scatter.2.cloned.1.call-done
  367.7 0.9 slice_bitcast_fusion
  368.7 2.4 collective-permute-start.4
  371.1 1.1 copy.26
  372.2 0.9 copy.27
  373.1 2.3 reshape.77
  375.3 0.0 copy-start.2
  375.3 8.9 %unpack.1 = bf16[3072,768]{1,0:T(8,128)(2,1)} custom-call(s32[192]{0:T(256)} %get-tuple-element.60.spots_ref.spots, s32[1]{0:T(128)} %bitcast.1.me, bf16[4,8,6,16,768]{4,3,2,1,0:T(8,128)(2,1)} %bitcast.26, bf16[4,8,1,768]{3,2,1,0:T(2,128)(2,1)} %get-tuple-element.106.over_ref), custom_call_target="tpu_custom_call" | custom-call | bytes 31457280 | tf_op jit(solution)/shard_map/unpack/pallas_call | solution.py:1309
  384.3 0.0 collective-permute-done.4
  384.3 0.0 copy-done.2
  384.4 0.6 slice.28
  385.0 0.7 slice.29
  385.7 0.1 slice.30
  385.8 0.1 fusion
  385.9 0.6 copy.28
  386.5 0.6 copy.29
  387.2 4.8 %copy.32 = bf16[3072,1,768]{2,0,1:T(8,128)(2,1)} copy(bf16[3072,1,768]{2,0,1:T(8,128)(2,1)} %bitcast.28) | data formatting | bytes 9437184
  (1 shorter events, 0.0 us)
Async XLA Ops:
  7.2 63.0 %collective-permute-start.1 = (bf16[768,768]{1,0:T(8,128)(2,1)}, bf16[768,768]{1,0:T(8,128)(2,1)S(1)}, u32[]{:S(2)}, u32[]{:S(2)}) collective-permute-start(bf16[768,768]{1,0:T(8,128)(2,1)} %refs_10_.1), channel_id=1, source_target_pairs={{0,2},{1,3},{2,0},{3,1},{4,6},{5,7},{6,4},{7,5},{8,10},{9,11},{10,... | collective-permute-start | bytes 3538952 | tf_op jit(solution)/shard_map/ppermute | solution.py:1241
  10.2 60.0 %collective-permute-start = (bf16[192,768]{1,0:T(8,128)(2,1)}, bf16[192,768]{1,0:T(8,128)(2,1)}, u32[]{:S(2)}, u32[]{:S(2)}) collective-permute-start(bf16[192,768]{1,0:T(8,128)(2,1)} %bitcast.37), channel_id=1, source_target_pairs={{0,2},{1,3},{2,0},{3,1},{4,6},{5,7},{6,4},{7,5},{8,10},{9,11},{10,... | collective-permute-start | bytes 884744 | tf_op jit(solution)/shard_map/ppermute | solution.py:1241
  25.0 52.4 %copy-start = (bf16[768,2,768]{2,1,0:T(2,128)(2,1)S(1)}, bf16[768,2,768]{2,1,0:T(2,128)(2,1)}, u32[]{:S(2)}) copy-start(bf16[768,2,768]{2,1,0:T(2,128)(2,1)} %param.16) | copy-start | bytes 7077892
  70.2 7.6 %copy-start.8 = (bf16[768,768]{1,0:T(8,128)(2,1)}, bf16[768,768]{1,0:T(8,128)(2,1)S(1)}, u32[]{:S(2)}) copy-start(bf16[768,768]{1,0:T(8,128)(2,1)S(1)} %collective-permute-done.1.refs_11_) | copy-start | bytes 3538948
  70.2 60.9 %all-to-all-start = ((bf16[8,112,768]{2,1,0:T(8,128)(2,1)}), bf16[8,112,768]{2,1,0:T(8,128)(2,1)}, u32[]{:S(2)}, u32[]{:S(2)}) async-start(bf16[8,112,768]{2,1,0:T(8,128)(2,1)} %get-tuple-element.75), calls=%async_computation | async-start | bytes 2752512 | tf_op jit(solution)/shard_map/all_to_all | solution.py:1843
  77.3 290.4 %reduce-scatter.2.cloned.1.call-start = ((), (), s32[]{:S(2)}) async-start(), calls=%async_computation.2 | async-start | bytes 3538944 | tf_op jit(solution)/shard_map/reduce_scatter | solution.py:1922
  77.3 1.8 copy-start.3
  77.3 1.8 copy-start.4
  77.8 13.6 %copy-start.1 = (bf16[96,8,2,768]{3,1,2,0:T(8,128)(2,1)}, bf16[96,8,2,768]{3,1,2,0:T(8,128)(2,1)S(1)}, u32[]{:S(2)}) copy-start(bf16[96,8,2,768]{3,1,2,0:T(8,128)(2,1)S(1)} %copy.30) | copy-start | bytes 7077892
  77.8 53.3 %collective-permute-start.2 = (bf16[768,1536]{1,0:T(8,128)(2,1)S(1)}, bf16[768,1536]{1,0:T(8,128)(2,1)S(1)}, u32[]{:S(2)}, u32[]{:S(2)}) collective-permute-start(bf16[768,1536]{1,0:T(8,128)(2,1)S(1)} %bitcast.30), channel_id=1, source_target_pairs={{0,2},{1,3},{2,0},{3,1},{4,6},{5,7},{6,4},{7,5},{8,10},{9,11},{10,... | collective-permute-start | bytes 7077896 | tf_op jit(solution)/shard_map/ppermute | solution.py:1241
  131.1 1.4 copy-start.5
  228.8 1.7 copy-start.6
  230.4 59.8 %collective-permute-start.3 = (bf16[768,1536]{1,0:T(8,128)(2,1)S(1)}, bf16[768,1536]{1,0:T(8,128)(2,1)S(1)}, u32[]{:S(2)}, u32[]{:S(2)}) collective-permute-start(bf16[768,1536]{1,0:T(8,128)(2,1)S(1)} %copy-done.6), channel_id=1, source_target_pairs={{0,2},{1,3},{2,0},{3,1},{4,6},{5,7},{6,4},{7,5},{8,10},{9,11},{10,... | collective-permute-start | bytes 7077896 | tf_op jit(solution)/shard_map/ppermute | solution.py:1241
  290.2 1.4 copy-start.7
  368.7 15.6 %collective-permute-start.4 = (bf16[96,1024]{1,0:T(8,128)(2,1)S(1)}, bf16[96,1024]{1,0:T(8,128)(2,1)S(1)}, u32[]{:S(2)}, u32[]{:S(2)}) collective-permute-start(bf16[96,1024]{1,0:T(8,128)(2,1)S(1)} %slice_bitcast_fusion), channel_id=1, source_target_pairs={{0,2},{1,3},{2,0},{3,1},{4,6},{5,7},{6,4},{7,5},{8,10},{9,11},{10,... | collective-permute-start | bytes 589832 | tf_op jit(solution)/shard_map/ppermute | solution.py:1241
  375.3 9.0 %copy-start.2 = (bf16[2,96,1024]{2,1,0:T(8,128)(2,1)S(1)}, bf16[2,96,1024]{2,1,0:T(8,128)(2,1)}, u32[]{:S(2)}) copy-start(bf16[2,96,1024]{2,1,0:T(8,128)(2,1)} %reduce-scatter.2.cloned.1.call-done) | copy-start | bytes 1179652
Sparse Core Ops, SparseCore 0:
  228.9 72.4 reduce-scatter.1

commit v5 on v4

--- a/solution.py
+++ b/solution.py
@@ -2,6 +2,7 @@
 
 import jax
 import jax.numpy as jnp
+import numpy as np
 from jax import lax
 from jax.experimental import pallas as pl
 from jax.experimental.pallas import tpu as pltpu
@@ -28,6 +29,9 @@
 
 HOLES = 8
 ROWS = 128
+WIDE = 1664
+WIDE_PARTS = (896, 768)
+TILE = 256
 
 
 def div(value, size):
@@ -62,6 +66,7 @@
     table_ref,
     match_ref,
     spots_ref,
+    places,
 ):
     d = ids[0]
     t = ids[1]
@@ -70,10 +75,17 @@
     share = slots // size
     window = (share + 31) // 16 * 16
 
+    count = lengths.shape[0]
+
+    def place_of(j, offset):
+        places[0, j] = offset
+        return offset + lengths[j]
+
+    lax.fori_loop(0, count, place_of, jnp.int32(0), unroll=True)
+
     def lookup(q):
         seq = dealing[q]
-        offset = lax.fori_loop(0, seq, lambda j, total: total + lengths[j], jnp.int32(0))
-        return seq, offset, lengths[seq]
+        return seq, places[0, seq], lengths[seq]
 
     def span(offset, length):
         low = div(offset - d + groups - 1, groups)
@@ -96,7 +108,7 @@
     table_ref[0, 0] = t
     slot_ids = lax.broadcasted_iota(jnp.int32, (share, 1), 0) + t * share
 
-    @pl.loop(0, groups)
+    @pl.loop(0, groups, unroll=4)
     def _(g):
         seq_a, off_a, len_a = lookup(2 * g)
         seq_b, off_b, len_b = lookup(2 * g + 1)
@@ -118,13 +130,10 @@
         over_x_ref[g] = mm(hot_over, x_ref[at_over, :], 1, 0)[:1].astype(BF)
         send_c_ref[g, share:] = mm(hot_over, c_ref[at_over, :], 1, 0).astype(BF)
 
-    count = lengths.shape[0]
-
-    @pl.loop(0, rows // ROWS)
-    def _(i):
+    def spot(i, here):
         row = i * ROWS
-        begun = lambda j, total: total + jnp.where(table_ref[0, 1 + j] <= row, 1, 0)
-        here = lax.fori_loop(0, count, begun, jnp.int32(0)) - 1
+        following = jnp.minimum(here + 1, count - 1)
+        here = jnp.where(table_ref[0, 1 + following] <= row, following, here)
         after = jnp.minimum(here + 1, count - 1)
         for k, j in enumerate((here, after)):
             slot = row + table_ref[3, 1 + j] - table_ref[0, 1 + j]
@@ -132,8 +141,11 @@
             spots_ref[8 * i + 3 * k] = table_ref[2, 1 + j]
             spots_ref[8 * i + 3 * k + 1] = div(start, 16)
             spots_ref[8 * i + 3 * k + 2] = slot - start
-        spots_ref[8 * i + 6] = jnp.where(here + 1 < count, table_ref[0, 1 + after] - row, ROWS)
+        spots_ref[8 * i + 6] = jnp.where(after > here, table_ref[0, 1 + after] - row, ROWS)
         spots_ref[8 * i + 7] = jnp.int32(0)
+        return here
+
+    lax.fori_loop(0, rows // ROWS, spot, jnp.int32(0), unroll=4)
 
     _, off_a, len_a = lookup(2 * d)
     _, off_b, len_b = lookup(2 * d + 1)
@@ -153,23 +165,29 @@
         second = div(len_b, groups) + extra_of(source, off_b, len_b, groups)[1]
         return first, first + second
 
-    @pl.loop(0, groups)
-    def _(hole):
-        lacks = lambda source: jnp.where(counts(source)[1] < slots, 1, 0)
-        rank = lax.fori_loop(0, hole, lambda j, total: total + lacks(j), jnp.int32(0))
-        rank = jnp.where(lacks(hole) == 1, rank, -1)
-
-        def scan(source, carry):
-            seen, found = carry
-            over = jnp.where(counts(source)[1] > slots, 1, 0)
-            hit = (over == 1) & (seen == rank)
-            match_ref[hole * groups + source] = jnp.where(hit, jnp.float32(1.0), jnp.float32(0.0))
-            return seen + over, jnp.where(hit, source, found)
-
-        _, found = lax.fori_loop(0, groups, scan, (jnp.int32(0), jnp.int32(-1)))
-        source = jnp.maximum(found, 0)
+    def clear(i, carry):
+        match_ref[i] = jnp.float32(0.0)
+        return carry
+
+    lax.fori_loop(0, groups * groups, clear, 0, unroll=8)
+
+    def sort_out(source, carry):
+        holes, overs = carry
+        total = counts(source)[1]
+        places[1, holes] = source
+        places[2, overs] = source
+        meta_ref[HOLES + source] = jnp.int32(-1)
+        return holes + jnp.where(total < slots, 1, 0), overs + jnp.where(total > slots, 1, 0)
+
+    holes, _ = lax.fori_loop(0, groups, sort_out, (jnp.int32(0), jnp.int32(0)), unroll=8)
+
+    @pl.loop(0, holes)
+    def _(i):
+        hole = places[1, i]
+        source = places[2, i]
+        match_ref[hole * groups + source] = jnp.float32(1.0)
         position = (slots - counts(source)[0]) * groups + extra_of(source, off_b, len_b, groups)[0]
-        meta_ref[HOLES + hole] = jnp.where(found >= 0, position, -1)
+        meta_ref[HOLES + hole] = position
 
 
 def pack(lengths, dealing, ids, x, cotangent, groups, size):
@@ -185,6 +203,7 @@
             grid=(1,),
             in_specs=[whole(rows, width)] * 2,
             out_specs=[whole(*shape) for shape in shapes] + [smem] * 4,
+            scratch_shapes=[pltpu.SMEM((3, max(lengths.shape[0], groups + 1)), jnp.int32)],
         ),
         out_shape=[jax.ShapeDtypeStruct(shape, BF) for shape in shapes]
         + [
@@ -365,7 +384,7 @@
         ],
         compiler_params=pltpu.CompilerParams(vmem_limit_bytes=VMEM_LIMIT),
         cost_estimate=pl.CostEstimate(
-            flops=2 * rows * width * 3 * local, bytes_accessed=16 << 20, transcendentals=0
+            flops=rows * width, bytes_accessed=1 << 20, transcendentals=0
         ),
         name="project",
     )(meta, match, x_rel, over, w_t, freq)
@@ -445,9 +464,9 @@
         ],
         compiler_params=pltpu.CompilerParams(vmem_limit_bytes=VMEM_LIMIT),
         cost_estimate=pl.CostEstimate(
-            flops=2 * 2 * rows * rows * 256 * heads // 2,
+            flops=2 * rows * rows * HEAD * heads,
             bytes_accessed=8 << 20,
-            transcendentals=heads * rows * rows // 2,
+            transcendentals=0,
         ),
         name="attend",
     )(info, q, k_rows, v)
@@ -461,23 +480,10 @@
     ).astype(BF)
 
 
-def attend_back_kernel(
-    groups,
-    info,
-    q_ref,
-    krow_ref,
-    k_ref,
-    vrow_ref,
-    o_ref,
-    do_ref,
-    lse_ref,
-    cos_ref,
-    sin_ref,
-    out_ref,
-    dq_ref,
-    dk_ref,
-    dv_ref,
-):
+def attend_back_kernel(groups, info, q_ref, krow_ref, k_ref, vrow_ref, o_ref, *refs):
+    count = QUERIES // BLOCK
+    do_refs = refs[:count]
+    lse_ref, cos_ref, sin_ref, out_ref, up_ref, dq_ref, dk_ref, dv_ref = refs[count:]
     index = pl.program_id(0)
     heads, rows, _ = krow_ref.shape
     width = heads * HEAD
@@ -492,43 +498,48 @@
         dv_ref[...] = jnp.zeros_like(dv_ref)
 
     dq_ref[...] = jnp.zeros_like(dq_ref)
-    query_ids = lax.broadcasted_iota(jnp.int32, (1, BLOCK), 1) + index * BLOCK
+    query_ids = lax.broadcasted_iota(jnp.int32, (1, QUERIES), 1) + index * QUERIES
     key_ids = lax.broadcasted_iota(jnp.int32, (KEYS, 1), 0)
-    delta = [
-        jnp.sum(do_ref[0, p, :].astype(F32) * o_ref[0, p, :].astype(F32), 0, keepdims=True)
-        for p in part
-    ]
-    spans_ = visible(info, index, 1, KEYS // BLOCK, rows // KEYS)
+    deltas = []
+    for i, ref in enumerate(do_refs):
+        columns = slice(i * BLOCK, (i + 1) * BLOCK)
+        up_ref[:, columns] = ref[0]
+        terms = ref[0].astype(F32) * o_ref[i].astype(F32)
+        deltas.append([jnp.sum(terms[p], 0, keepdims=True) for p in part])
+    delta = [jnp.concatenate([halves[h] for halves in deltas], 1) for h in ids]
+    spans_ = visible(info, index, QUERIES // BLOCK, KEYS // BLOCK, rows // KEYS)
 
     def step(masked, j, carry):
         keys = pl.ds(pl.multiple_of(j * KEYS, KEYS), KEYS)
-        scores = [mm(krow_ref[h, keys, :], q_ref[part[h], :], 1, 0) for h in ids]
-        grad_soft = [mm(vrow_ref[h, keys, :], do_ref[0, part[h], :], 1, 0) for h in ids]
         if masked:
             same = in_second(info, key_ids + j * KEYS, groups) == in_second(info, query_ids, groups)
-            scores = [jnp.where(same, s, NEGATIVE) for s in scores]
-        soft = [jnp.exp2(scores[h] - lse_ref[h : h + 1, :]) for h in ids]
-        grad_scores = [(soft[h] * (grad_soft[h] - delta[h])).astype(BF) for h in ids]
-        soft = [s.astype(BF) for s in soft]
-        dv = [mm(do_ref[0, part[h], :], soft[h], 1, 1) for h in ids]
-        dk = [mm(q_ref[part[h], :], grad_scores[h], 1, 1) for h in ids]
-        dq = [mm(k_ref[part[h], keys], grad_scores[h], 1, 0) for h in ids]
         for h in ids:
-            dv_ref[part[h], keys] += dv[h]
-            dk_ref[part[h], keys] += dk[h]
-            dq_ref[part[h], :] += dq[h]
+            queries = q_ref[part[h], :]
+            upstream = up_ref[part[h], :]
+            scores = mm(krow_ref[h, keys, :], queries, 1, 0)
+            grad_soft = mm(vrow_ref[h, keys, :], upstream, 1, 0)
+            if masked:
+                scores = jnp.where(same, scores, NEGATIVE)
+            soft = jnp.exp2(scores - lse_ref[h : h + 1, :])
+            grad_scores = (soft * (grad_soft - delta[h])).astype(BF)
+            dv_ref[part[h], keys] += mm(upstream, soft.astype(BF), 1, 1)
+            dk_ref[part[h], keys] += mm(queries, grad_scores, 1, 1)
+            dq_ref[part[h], :] += mm(k_ref[part[h], keys], grad_scores, 1, 0)
         return carry
 
     lax.fori_loop(spans_[0], spans_[1], functools.partial(step, False), 0)
     lax.fori_loop(spans_[2], spans_[3], functools.partial(step, True), 0)
 
-    owner = index // each
-    columns = pl.ds(pl.multiple_of(index * BLOCK, BLOCK), BLOCK)
-    inside = pl.ds(pl.multiple_of(index % each * BLOCK, BLOCK), BLOCK)
-    for h in ids:
-        out_ref[owner, part[h], inside] = unturn(
-            dq_ref[part[h], :] * HEAD ** (-0.5), cos_ref[:, columns], sin_ref[:, columns]
-        )
+    for i in range(QUERIES // BLOCK):
+        block = index * (QUERIES // BLOCK) + i
+        columns = pl.ds(pl.multiple_of(block * BLOCK, BLOCK), BLOCK)
+        inside = pl.ds(pl.multiple_of(lax.rem(block, each) * BLOCK, BLOCK), BLOCK)
+        for h in ids:
+            out_ref[lax.div(block, each), part[h], inside] = unturn(
+                dq_ref[part[h], i * BLOCK : (i + 1) * BLOCK] * HEAD ** (-0.5),
+                cos_ref[:, columns],
+                sin_ref[:, columns],
+            )
 
     @pl.when(index == pl.num_programs(0) - 1)
     def _():
@@ -551,28 +562,35 @@
     blocks = rows // BLOCK
     each = blocks // parts
     whole = lambda *shape: pl.BlockSpec(shape, lambda i, info: (0,) * len(shape))
+    count = QUERIES // BLOCK
+
+    def upstream_spec(k):
+        def pick(i, info):
+            block = i * count + k
+            return jnp.bitwise_xor(block // each, info[2]), 0, block % each
+
+        return pl.BlockSpec((1, local, BLOCK), pick)
+
     return pl.pallas_call(
         functools.partial(attend_back_kernel, groups),
         grid_spec=pltpu.PrefetchScalarGridSpec(
             num_scalar_prefetch=1,
-            grid=(blocks,),
+            grid=(rows // QUERIES,),
             in_specs=[
-                pl.BlockSpec((local, BLOCK), lambda i, info: (0, i)),
+                pl.BlockSpec((local, QUERIES), lambda i, info: (0, i)),
                 whole(heads, rows, HEAD),
                 whole(local, rows),
                 whole(heads, rows, HEAD),
-                pl.BlockSpec((1, local, BLOCK), lambda i, info: (i, 0, 0)),
-                pl.BlockSpec(
-                    (1, local, BLOCK),
-                    lambda i, info: (jnp.bitwise_xor(i // each, info[2]), 0, i % each),
-                ),
-                pl.BlockSpec((heads, BLOCK), lambda i, info: (0, i)),
+                pl.BlockSpec((count, local, BLOCK), lambda i, info: (i, 0, 0)),
+                *[upstream_spec(k) for k in range(count)],
+                pl.BlockSpec((heads, QUERIES), lambda i, info: (0, i)),
                 whole(HALF, rows),
                 whole(HALF, rows),
             ],
             out_specs=whole(parts, 3 * local, rows // parts),
             scratch_shapes=[
-                pltpu.VMEM((local, BLOCK), F32),
+                pltpu.VMEM((local, QUERIES), BF),
+                pltpu.VMEM((local, QUERIES), F32),
                 pltpu.VMEM((local, rows), F32),
                 pltpu.VMEM((local, rows), F32),
             ],
@@ -585,7 +603,7 @@
             transcendentals=heads * rows * rows // 2,
         ),
         name="attend_back",
-    )(info, q, k_rows, k, v_rows, o, do, lse, cosine, sine)
+    )(info, q, k_rows, k, v_rows, o, *[do] * count, lse, cosine, sine)
 
 
 def project_back_kernel(meta, d_ref, x_ref, w_ref, back_ref, grad_ref, acc_ref):
@@ -721,9 +739,9 @@
     )
 
 
-def middle_kernel(size, groups, *refs):
+def middle_kernel(size, groups, count, *refs):
     x_ref, match_ref, cot_ref, over_ref, norm_ref, blocks_ref = refs[:6]
-    weights_hbm = refs[6:12]
+    weights_hbm = refs[6 : 6 + count]
     (
         result_ref,
         grad_one_ref,
@@ -740,12 +758,14 @@
         w_down_ref,
         slope_ref,
         swish_ref,
+        normed_ref,
+        sum_ref,
         arrived_ref,
         sems,
         sends,
         recvs,
         keep,
-    ) = refs[12:]
+    ) = refs[6 + count :]
     index = pl.program_id(0)
     first = index == 0
     d = lax.axis_index("dp")
@@ -757,17 +777,34 @@
     core = (d, jnp.bitwise_xor(t, 1))
     targets = (lambda r: w_out_ref.at[part[r]], lambda r: w_gu_ref.at[r], lambda r: w_down_ref.at[r])
 
-    def weight_copy(kind, r):
-        source = weights_hbm[2 * kind + r // 2]
-        if r % 2 == 0:
-            return pltpu.make_async_copy(source, targets[kind](r), sems.at[kind, r])
-        return remote(source, targets[kind](r), sems.at[kind, r - 1 + size], sems.at[kind, r], core)
+    def weight_copies(kind, r):
+        target = targets[kind](r)
+        pieces = [(weights_hbm[2 * kind + r // 2], target)]
+        if kind == 2 and r >= 2:
+            pieces = []
+            for i in range(2):
+                half = weights_hbm[5 + i]
+                low = pl.multiple_of(lax.rem(d + i, 2) * half.shape[0], 16)
+                pieces.append((half, target.at[pl.ds(low, half.shape[0])]))
+        copies = []
+        for i, (source, place) in enumerate(pieces):
+            recv = sems.at[kind, r, i]
+            if r == 1 or r == 3:
+                copies.append(remote(source, place, sems.at[kind, r - 1 + size, i], recv, core))
+            else:
+                copies.append(pltpu.make_async_copy(source, place, recv))
+        return copies
+
+    def weight_start(kind, r):
+        for copy in weight_copies(kind, r):
+            copy.start()
 
     def weight_wait(kind, r):
-        if r % 2 == 0:
-            weight_copy(kind, r).wait()
-        else:
-            weight_copy(kind, r).wait_recv()
+        for copy in weight_copies(kind, r):
+            if r % 2 == 0:
+                copy.wait()
+            else:
+                copy.wait_recv()
 
     def heads_copy(r, i):
         other = jnp.bitwise_xor(t, r)
@@ -785,24 +822,32 @@
     def _():
         own_copy.start()
         for r in (0, 2):
-            weight_copy(0, r).start()
+            weight_start(0, r)
         greet(1, (1, 2, 3), d, t)
-        for i in range(subs):
-            for r in (2, 3, 1):
-                heads_copy(r, i).start()
-            if i == 0:
-                for r in (1, 3):
-                    weight_copy(0, r).start()
+        for r in (2, 3, 1):
+            heads_copy(r, 0).start()
+        for r in (1, 3):
+            weight_start(0, r)
         for r in ids:
             for kind in (1, 2):
-                weight_copy(kind, r).start()
+                weight_start(kind, r)
         own_copy.wait()
         for r in ids:
             weight_wait(0, r)
 
+    @pl.when(first)
+    def _():
+        norm_grad_ref[...] = jnp.zeros_like(norm_grad_ref)
+
     for r in ids[1:]:
         heads_copy(r, index).wait_recv()
         heads_copy(r, index).wait_send()
+
+    @pl.when(index < subs - 1)
+    def _():
+        for r in (2, 3, 1):
+            heads_copy(r, index + 1).start()
+
     for r in ids:
         heads_ref[r] = arrived_ref[r, index]
     heads_out = jnp.concatenate([arrived_ref[r, index] for r in range(size)], 0)
@@ -811,27 +856,32 @@
     normed_one, unit_one, inverse_one = norm_forward(
         x_ref[...].astype(F32) + attn, gain_one, shift_one
     )
-    normed = normed_one.astype(BF)
+    normed_ref[...] = normed_one.astype(BF)
     normed_t_ref[...] = normed_one.T.astype(BF)
-    branch = jnp.zeros(normed_one.shape, F32)
-    for r in ids:
-
-        @pl.when(first)
-        def _():
-            weight_wait(1, r)
-            weight_wait(2, r)
-
-        both = mm(normed, w_gu_ref[r], 1, 0)
+    sum_ref[...] = normed_one
+
+    @pl.loop(0, size)
+    def _(i):
+        r = lax.rem(i, 2) * 2 + lax.div(i, 2)
+        for k in ids:
+
+            @pl.when(first & (r == k))
+            def _():
+                weight_wait(1, k)
+                weight_wait(2, k)
+
+        both = mm(normed_ref[...], w_gu_ref[r], 1, 0)
         gate = both[:, :inner]
         up = both[:, inner:]
-        sig = jax.nn.sigmoid(gate)
+        sig = 0.5 + 0.5 * jnp.tanh(0.5 * gate)
         swish = gate * sig
         hidden = (swish * up).astype(BF)
         swish_ref[r] = swish
-        slope_ref[r] = up * sig * (1.0 + gate * (1.0 - sig))
+        slope_ref[r] = up * (sig + swish * (1.0 - sig))
         hidden_ref[r] = hidden
-        branch = branch + mm(hidden, w_down_ref[r], 1, 1)
-    result, unit_two, inverse_two = norm_forward(normed_one + branch, gain_two, shift_two)
+        sum_ref[...] += mm(hidden, w_down_ref[r], 1, 1)
+
+    result, unit_two, inverse_two = norm_forward(sum_ref[...], gain_two, shift_two)
     result_ref[...] = result.astype(BF)
     if groups:
         sub = BLOCK // groups
@@ -848,42 +898,43 @@
     else:
         cot = cot_ref[...].astype(F32)
     grad_two, d_gain_two, d_shift_two = norm_backward(cot, unit_two, inverse_two, gain_two)
-    d_branch = grad_two.astype(BF)
+    normed_ref[...] = grad_two.astype(BF)
     d_branch_t_ref[...] = grad_two.T.astype(BF)
-    back = grad_two
-    for r in ids:
-        grad_hidden = mm(d_branch, w_down_ref[r], 1, 0)
+    sum_ref[...] = grad_two
+
+    @pl.loop(0, size)
+    def _(r):
+        grad_hidden = mm(normed_ref[...], w_down_ref[r], 1, 0)
         d_gate = (grad_hidden * slope_ref[r]).astype(BF)
         d_up = (grad_hidden * swish_ref[r]).astype(BF)
         d_gu_ref[r, :, :inner] = d_gate
         d_gu_ref[r, :, inner:] = d_up
-        back = back + mm(jnp.concatenate([d_gate, d_up], 1), w_gu_ref[r], 1, 1)
-    grad_one, d_gain_one, d_shift_one = norm_backward(back, unit_one, inverse_one, gain_one)
+        sum_ref[...] += mm(jnp.concatenate([d_gate, d_up], 1), w_gu_ref[r], 1, 1)
+
+    grad_one, d_gain_one, d_shift_one = norm_backward(
+        sum_ref[...], unit_one, inverse_one, gain_one
+    )
     grad_one_ref[...] = grad_one
     d_attn_t = grad_one.T.astype(BF)
     d_attn_t_ref[...] = d_attn_t
     d_heads = mm(w_out_ref[...], d_attn_t, 1, 0).astype(BF)
     for r in ids:
         d_heads_ref[r] = d_heads[part[r]]
-
-    @pl.when(first)
-    def _():
-        norm_grad_ref[...] = jnp.zeros_like(norm_grad_ref)
+    for i, grad in enumerate((d_gain_one, d_gain_two, d_shift_one, d_shift_two)):
+        norm_grad_ref[i : i + 1, :] += grad
 
     @pl.when(index == subs - 1)
     def _():
         for kind in range(3):
             for r in (1, 3):
-                weight_copy(kind, r).wait_send()
-
-    for i, grad in enumerate((d_gain_one, d_gain_two, d_shift_one, d_shift_two)):
-        norm_grad_ref[i : i + 1, :] += grad
+                for copy in weight_copies(kind, r):
+                    copy.wait_send()
 
 
 def middle(x_own, match, cot, norms, o_blocks, size, *weights):
     rows, width = x_own.shape
     local = o_blocks.shape[1]
-    inner = weights[-1].shape[1]
+    inner = weights[4].shape[1]
     block = pl.BlockSpec((BLOCK, width), lambda i: (i, 0))
     turned = pl.BlockSpec((width, BLOCK), lambda i: (0, i))
     anywhere = pl.BlockSpec(memory_space=pl.ANY)
@@ -899,7 +950,7 @@
     else:
         cot_specs = [block, pl.BlockSpec((16, width), lambda i: (0, 0))]
     return pl.pallas_call(
-        functools.partial(middle_kernel, size, groups),
+        functools.partial(middle_kernel, size, groups, len(weights)),
         grid=(rows // BLOCK,),
         in_specs=[block, pl.BlockSpec(memory_space=pltpu.SMEM)]
         + cot_specs
@@ -935,8 +986,10 @@
             pltpu.VMEM((size, width, inner), BF),
             pltpu.VMEM((size, BLOCK, inner), F32),
             pltpu.VMEM((size, BLOCK, inner), F32),
+            pltpu.VMEM((BLOCK, width), BF),
+            pltpu.VMEM((BLOCK, width), F32),
             pltpu.VMEM((size, rows // BLOCK, local, BLOCK), BF),
-            pltpu.SemaphoreType.DMA((3, 2 * size)),
+            pltpu.SemaphoreType.DMA((3, 2 * size, 2)),
             pltpu.SemaphoreType.DMA((size, rows // BLOCK)),
             pltpu.SemaphoreType.DMA((size, rows // BLOCK)),
             pltpu.SemaphoreType.DMA,
@@ -953,26 +1006,37 @@
     )(x_own, match, cot, cot, norms, o_blocks, *weights)
 
 
+def product_tiles(left_ref, right_ref, store):
+    @pl.loop(0, right_ref.shape[2] // TILE)
+    def _(i):
+        columns = pl.ds(pl.multiple_of(i * TILE, TILE), TILE)
+        store(columns, mm(left_ref[...], right_ref[0, :, columns], 1, 0))
+
+
 def weight_grads_tile(
     normed_t_ref, d_branch_t_ref, d_attn_t_ref, hidden_ref, d_gu_ref, heads_ref, norm_ref, store
 ):
-    inner = hidden_ref.shape[2]
+    wide = d_gu_ref.shape[2]
     local = heads_ref.shape[1]
-    width = normed_t_ref.shape[0]
-    store(0, 2 * inner, mm(normed_t_ref[...], d_gu_ref[0], 1, 0))
-    store(2 * inner, 3 * inner, mm(d_branch_t_ref[...], hidden_ref[0], 1, 0))
+    product_tiles(normed_t_ref, d_gu_ref, store)
     d_out = mm(d_attn_t_ref[...], heads_ref[0], 1, 1)
     norm = norm_ref[...].T
     spare = -(local + norm.shape[1]) % 128
-    tail = jnp.concatenate([d_out, norm, jnp.zeros((width, spare), F32)], 1)
-    store(3 * inner, 3 * inner + tail.shape[1], tail)
+    tail = jnp.concatenate([d_out, norm, jnp.zeros((norm.shape[0], spare), F32)], 1)
+    store(pl.ds(wide, tail.shape[1]), tail)
+    base = wide + tail.shape[1]
+
+    def shifted(columns, value):
+        store(pl.ds(pl.multiple_of(base + columns.start, 128), columns.size), value)
+
+    product_tiles(d_branch_t_ref, hidden_ref, shifted)
 
 
 def weight_grads_kernel(*refs):
     out_ref = refs[-1]
 
-    def store(low, high, value):
-        out_ref[0, :, low:high] = value.astype(BF)
+    def store(columns, value):
+        out_ref[0, :, columns] = value.astype(BF)
 
     weight_grads_tile(*refs[:-1], store)
 
@@ -1012,9 +1076,9 @@
     (
         d_heads_ref,
         result_ref,
-        gu_own_ref,
-        gu_other_ref,
-        pair_ref,
+        wide_own_ref,
+        wide_other_ref,
+        down_ref,
         do_ref,
         home_ref,
         over_ref,
@@ -1031,6 +1095,7 @@
         s_over,
         r_over,
         keep,
+        outs,
     ) = refs[7:]
     step = pl.program_id(0)
     d = lax.axis_index("dp")
@@ -1055,11 +1120,14 @@
     def own_copy(c):
         return pltpu.make_async_copy(own_ref.at[c, d], home_ref.at[0, d, c], keep.at[c])
 
+    def arrival(c, k):
+        return body.arrival(own_ref.at[c, lax.rem(d + k, groups)], k, (c,), (c,))
+
     def pass_on(c):
         own_copy(c).wait()
         for k in range(groups):
             if k > 0:
-                body.arrival(own_ref.at[c, 0], k, (c,), (c,)).wait_recv()
+                arrival(c, k).wait_recv()
             body.across(k, (c,), (c,)).start()
 
     load = pltpu.make_async_copy(result_ref, own_ref, keep.at[chunks])
@@ -1077,7 +1145,7 @@
         for c in range(chunks):
             own_copy(c).start()
             for k in range(1, groups):
-                body.arrival(own_ref.at[c, lax.rem(d + k, groups)], k, (c,), (c,)).start()
+                arrival(c, k).start()
         last = [own_ref[chunks - 1, g, sub - 16 :, :].astype(F32)[15:16] for g in range(groups)]
         for to in range(groups):
             spare = last[0] * match_ref[to]
@@ -1096,30 +1164,48 @@
 
     @pl.when(step < 2)
     def _():
-        def store(low, high, value):
-            sent_ref[step, :, low:high] = value.astype(BF)
+        def store(columns, value):
+            sent_ref[step, :, columns] = value.astype(BF)
 
         weight_grads_tile(*tile_refs, store)
         grad_copy(step).start()
 
-    gu_wide = gu_own_ref.shape[1]
-    for i, gu_ref in ((0, gu_own_ref), (1, gu_other_ref)):
+    @pl.when(step >= 2)
+    def _():
+        grad_copy(step - 2).wait_recv()
+        grad_copy(step - 2).wait_send()
+
+        def store(columns, value):
+            sent_ref[step - 2, :, columns] = (
+                value + got_ref[step - 2, :, columns].astype(F32)
+            ).astype(BF)
+
+        weight_grads_tile(*tile_refs, store)
+
+    part = down_ref.shape[2]
+
+    def leave(i):
+        copies = [(sent_ref.at[i, :, pl.ds(0, WIDE)], (wide_own_ref, wide_other_ref)[i])]
+        for g in range(groups):
+            rest = sent_ref.at[i, pl.ds(g * part, part), pl.ds(WIDE, down_ref.shape[3])]
+            copies.append((rest, down_ref.at[g, i]))
+        return [
+            pltpu.make_async_copy(source, target, outs.at[i, j])
+            for j, (source, target) in enumerate(copies)
+        ]
+
+    for i in range(2):
 
         @pl.when(step == 2 + i)
         def _():
-            grad_copy(i).wait_recv()
-
-            def store(low, high, value):
-                total = (value + got_ref[i, :, low:high].astype(F32)).astype(BF)
-                if high <= gu_wide:
-                    gu_ref[:, low:high] = total
-                else:
-                    pair_ref[0, :, low - gu_wide : high - gu_wide] = total
-
-            weight_grads_tile(*tile_refs, store)
+            for copy in leave(i):
+                copy.start()
 
     @pl.when(step == size - 1)
     def _():
+        for i in range(2):
+            for copy in leave(i):
+                copy.wait()
         own_over.wait()
         for k in range(groups):
             if k > 0:
@@ -1133,15 +1219,13 @@
         for r in range(1, size):
             heads_copy(r).wait_recv()
             heads_copy(r).wait_send()
-        for i in range(2):
-            grad_copy(i).wait_send()
         own_copy(chunks - 1).wait()
         for c in range(chunks):
             for k in range(groups):
                 if k > 0 and c == chunks - 1:
-                    body.arrival(own_ref.at[c, 0], k, (c,), (c,)).wait_recv()
+                    arrival(c, k).wait_recv()
                 if k > 0:
-                    body.arrival(own_ref.at[c, 0], k, (c,), (c,)).wait_send()
+                    arrival(c, k).wait_send()
                 if c < chunks - 1:
                     body.across(k, (c,), (c,)).wait_recv()
                     body.across(k, (c,), (c,)).wait_send()
@@ -1163,8 +1247,9 @@
     width = normed_t.shape[0]
     chunks = rows // BLOCK
     sub = BLOCK // groups
-    wide = 3 * inner + (local + norm_grads.shape[0] + 127) // 128 * 128
-    flat = pl.BlockSpec((width, rows), lambda i: (0, 0))
+    total = 3 * inner + (local + norm_grads.shape[0] + 127) // 128 * 128
+    part = width // groups
+    whole = lambda *shape: pl.BlockSpec(shape, lambda i: (0,) * len(shape))
     pick = lambda i: (jnp.where(i < 2, 2 * i + 1, 2 * i - 4), 0, 0)
     anywhere = pl.BlockSpec(memory_space=pl.ANY)
     dma = pltpu.SemaphoreType.DMA
@@ -1173,35 +1258,35 @@
         grid=(size,),
         in_specs=[
             pl.BlockSpec(memory_space=pltpu.SMEM),
-            flat,
-            flat,
-            flat,
+            whole(width, rows),
+            whole(width, rows),
+            whole(width, rows),
             pl.BlockSpec((1, rows, inner), pick),
             pl.BlockSpec((1, rows, 2 * inner), pick),
             pl.BlockSpec((1, local, rows), pick),
-            pl.BlockSpec(norm_grads.shape, lambda i: (0, 0)),
+            whole(*norm_grads.shape),
             anywhere,
             anywhere,
         ],
         out_specs=[
-            pl.BlockSpec((width, 2 * inner), lambda i: (0, 0)),
-            pl.BlockSpec((width, 2 * inner), lambda i: (0, 0)),
-            pl.BlockSpec((1, width, wide - 2 * inner), lambda i: (jnp.maximum(i - 2, 0), 0, 0)),
+            anywhere,
+            anywhere,
+            anywhere,
             anywhere,
             anywhere,
             anywhere,
         ],
         out_shape=[
-            jax.ShapeDtypeStruct((width, 2 * inner), BF),
-            jax.ShapeDtypeStruct((width, 2 * inner), BF),
-            jax.ShapeDtypeStruct((2, width, wide - 2 * inner), BF),
+            jax.ShapeDtypeStruct((width, WIDE), BF),
+            jax.ShapeDtypeStruct((width, WIDE), BF),
+            jax.ShapeDtypeStruct((groups, 2, part, total - WIDE), BF),
             jax.ShapeDtypeStruct(d_heads.shape, BF),
             jax.ShapeDtypeStruct((3, groups, chunks, sub, width), BF),
             jax.ShapeDtypeStruct((size, groups, 1, width), BF),
         ],
         scratch_shapes=[
-            pltpu.VMEM((2, width, wide), BF),
-            pltpu.VMEM((2, width, wide), BF),
+            pltpu.VMEM((2, width, total), BF),
+            pltpu.VMEM((2, width, total), BF),
             pltpu.VMEM((chunks, groups, sub, width), BF),
             pltpu.VMEM((groups, 1, width), BF),
             dma((2,)),
@@ -1213,6 +1298,7 @@
             dma((4, groups)),
             dma((4, groups)),
             dma((chunks + 3,)),
+            dma((2, groups + 1)),
         ],
         compiler_params=pltpu.CompilerParams(
             collective_id=3, has_side_effects=True, vmem_limit_bytes=VMEM_LIMIT
@@ -1285,88 +1371,123 @@
         src_ref[g, end] = jnp.where(top, over_ref[last, g].astype(F32), 0.0).astype(BF)
 
 
-def unpack_kernel(size, spots, me, home_ref, over_ref, out_ref, src_ref, sems):
+def unpack_kernel(
+    size, spots, me, home_ref, over_ref, result_ref, out_ref, result_out_ref, src_ref, sems
+):
     tiles = home_ref.shape[2]
+    step = pl.program_id(0)
+    each = out_ref.shape[0] // ROWS
 
     def load(r):
         at = pl.ds(jnp.bitwise_xor(me[0], r) * tiles, tiles)
         return pltpu.make_async_copy(home_ref.at[r], src_ref.at[:, at], sems.at[r])
 
-    for r in range(size):
-        load(r).start()
-    store_over(src_ref, over_ref, jnp.bitwise_xor(size - 1, me[0]))
-    for r in range(size):
-        load(r).wait()
-    for i in range(out_ref.shape[0] // ROWS):
-        out_ref[i * ROWS : (i + 1) * ROWS, :] = unpack_block(spots, src_ref, i)
-
-
-def unpack(spots, me, home, over):
+    @pl.when(step == 0)
+    def _():
+        for r in range(size):
+            load(r).start()
+        store_over(src_ref, over_ref, jnp.bitwise_xor(size - 1, me[0]))
+        for r in range(size):
+            load(r).wait()
+
+    for i in range(each):
+        out_ref[i * ROWS : (i + 1) * ROWS, :] = unpack_block(spots, src_ref, step * each + i)
+    result_out_ref[...] = result_ref[...]
+
+
+def unpack(spots, me, home, over, result):
     size, groups, share, width = home.shape
     rows = size * groups * share
     home = home.reshape(size, groups, share // 16, 16, width)
     whole = lambda *shape: pl.BlockSpec(shape, lambda i, *refs: (0,) * len(shape))
+    anywhere = pl.BlockSpec(memory_space=pl.ANY)
+    each = 4 * ROWS
+    block = pl.BlockSpec((each, width), lambda i, *refs: (i, 0))
     return pl.pallas_call(
         functools.partial(unpack_kernel, size),
         grid_spec=pltpu.PrefetchScalarGridSpec(
             num_scalar_prefetch=2,
-            grid=(1,),
-            in_specs=[pl.BlockSpec(memory_space=pl.ANY), whole(*over.shape)],
-            out_specs=whole(rows, width),
+            grid=(rows // each,),
+            in_specs=[anywhere, whole(*over.shape), block],
+            out_specs=[block, block],
             scratch_shapes=[
                 pltpu.VMEM((groups, size * share // 16 + 1, 16, width), BF),
                 pltpu.SemaphoreType.DMA((size,)),
             ],
         ),
-        out_shape=jax.ShapeDtypeStruct((rows, width), BF),
+        out_shape=[jax.ShapeDtypeStruct((rows, width), BF)] * 2,
         compiler_params=pltpu.CompilerParams(vmem_limit_bytes=VMEM_LIMIT),
         cost_estimate=pl.CostEstimate(flops=0, bytes_accessed=30 << 20, transcendentals=0),
         name="unpack",
-    )(spots, me, home, over)
-
-
-def route_kernel(groups, size, send_ref, over_ref, out_ref, over_out_ref, sends, recvs, keep):
+    )(spots, me, home, over, result)
+
+
+def route_kernel(groups, size, send_ref, over_ref, out_ref, over_out_ref, sends, recvs, s_over, r_over, keep):
     d = lax.axis_index("dp")
     t = lax.axis_index("tensor")
+    chunks = sends.shape[2]
+    count = send_ref.shape[1] // chunks
     greet(groups, (1, 2), d, t)
     spread = Spread(out_ref, (sends, recvs), groups, d, t)
-    own = pltpu.make_async_copy(send_ref.at[d], out_ref.at[0, d], keep.at[0])
-    own_over = pltpu.make_async_copy(over_ref.at[d], over_out_ref.at[d], keep.at[1])
-    own.start()
-    own_over.start()
+
+    def rows(c):
+        return pl.ds(c * count, count)
+
+    def own(c):
+        return pltpu.make_async_copy(
+            send_ref.at[d, rows(c)], out_ref.at[0, d, rows(c)], keep.at[c]
+        )
+
+    def arrival(c, k):
+        return spread.arrival(send_ref.at[lax.rem(d + k, groups), rows(c)], k, (rows(c),), (c,))
+
+    def across(c, k):
+        return spread.across(k, (rows(c),), (c,))
+
+    def beside(r, c, k):
+        return spread.beside(r, k, (rows(c),), (c,))
 
     def over_copy(k):
         to = lax.rem(d + k, groups)
-        return remote(
-            over_ref.at[to], over_out_ref.at[d], sends.at[4, k], recvs.at[4, k], (to, t)
-        )
-
-    for k in range(1, groups):
-        spread.arrival(send_ref.at[lax.rem(d + k, groups)], k, (), ()).start()
+        return remote(over_ref.at[to], over_out_ref.at[d], s_over.at[k], r_over.at[k], (to, t))
+
+    def pass_far(c):
+        for k in range(groups):
+            across(c, k).wait_recv()
+            beside(2, c, k).start()
+
+    own_over = pltpu.make_async_copy(over_ref.at[d], over_out_ref.at[d], keep.at[chunks])
+    for c in range(chunks):
+        own(c).start()
+    own_over.start()
+    for c in range(chunks):
+        for k in range(1, groups):
+            arrival(c, k).start()
     for k in range(1, groups):
         over_copy(k).start()
-    own.wait()
-    for k in range(groups):
-        if k > 0:
-            spread.arrival(send_ref.at[0], k, (), ()).wait_recv()
-        spread.across(k, (), ()).start()
-        spread.beside(0, k, (), ()).start()
-        if k > 0:
-            spread.across(k - 1, (), ()).wait_recv()
-            spread.beside(2, k - 1, (), ()).start()
-    spread.across(groups - 1, (), ()).wait_recv()
-    spread.beside(2, groups - 1, (), ()).start()
+    for c in range(chunks):
+        own(c).wait()
+        for k in range(groups):
+            if k > 0:
+                arrival(c, k).wait_recv()
+            across(c, k).start()
+            beside(0, c, k).start()
+        if c > 0:
+            pass_far(c - 1)
+    pass_far(chunks - 1)
     own_over.wait()
     for k in range(groups):
-        spread.beside(0, k, (), ()).wait_recv()
-        spread.beside(2, k, (), ()).wait_recv()
+        for c in range(chunks):
+            beside(0, c, k).wait_recv()
+            beside(2, c, k).wait_recv()
+            if k > 0:
+                arrival(c, k).wait_send()
+            across(c, k).wait_send()
+            beside(0, c, k).wait_send()
+            beside(2, c, k).wait_send()
         if k > 0:
             over_copy(k).wait_recv()
             over_copy(k).wait_send()
-            spread.arrival(send_ref.at[0], k, (), ()).wait_send()
-        spread.across(k, (), ()).wait_send()
-        spread.beside(0, k, (), ()).wait_send()
-        spread.beside(2, k, (), ()).wait_send()
 
 
 def route(send, over, size):
@@ -1381,9 +1502,11 @@
             jax.ShapeDtypeStruct(over.shape, BF),
         ],
         scratch_shapes=[
-            pltpu.SemaphoreType.DMA((5, groups)),
-            pltpu.SemaphoreType.DMA((5, groups)),
-            pltpu.SemaphoreType.DMA((2,)),
+            pltpu.SemaphoreType.DMA((4, groups, 3)),
+            pltpu.SemaphoreType.DMA((4, groups, 3)),
+            pltpu.SemaphoreType.DMA((groups,)),
+            pltpu.SemaphoreType.DMA((groups,)),
+            pltpu.SemaphoreType.DMA((4,)),
         ],
         compiler_params=pltpu.CompilerParams(collective_id=0, has_side_effects=True),
         cost_estimate=pl.CostEstimate(flops=0, bytes_accessed=60 << 20, transcendentals=0),
@@ -1392,62 +1515,52 @@
 
 
 class Halving:
-    def __init__(self, fetch, bits, refs, sems, d, t):
-        self.fetch, self.bits, self.d, self.t = fetch, bits, d, t
+    def __init__(self, fetch, links, refs, sems):
+        self.fetch, self.links = fetch, links
         self.out, self.got, self.held = refs
         self.send, self.recv = sems
-
-    def mine(self, step):
-        return lax.rem(lax.div(self.d, self.bits[step]), 2)
-
-    def block(self, first, i):
-        one, two, three = self.bits
-        return first * one + lax.rem(i, 2) * two + lax.div(i, 2) * three
-
-    def copy(self, i):
-        step = 0 if i < 4 else 1 if i < 6 else 2
+        self.counts = [2 ** (len(links) - 1 - step) for step in range(len(links))]
+        self.first = [sum(self.counts[:step]) for step in range(len(links))]
+
+    def term(self, side, i):
+        rest = [lax.rem(lax.div(i, 2**j), 2) for j in range(len(self.links) - 1)]
+        return self.fetch(side, *rest)
+
+    def copy(self, step, i):
+        at = self.first[step] + i
         return remote(
-            self.out.at[i],
-            self.got.at[i],
-            self.send.at[i],
-            self.recv.at[i],
-            (jnp.bitwise_xor(self.d, self.bits[step]), self.t),
+            self.out.at[at], self.got.at[at], self.send.at[at], self.recv.at[at], self.links[step][1]
         )
 
     def start(self):
-        for i in range(4):
-            self.out[i] = self.fetch(self.block(1 - self.mine(0), jnp.int32(i))).astype(BF)
-            self.copy(i).start()
-
-    def second(self):
-        for i in range(4):
-            self.copy(i).wait_recv()
-        own = self.mine(1)
+        for i in range(self.counts[0]):
+            self.out[i] = self.term(1 - self.links[0][0], jnp.int32(i)).astype(BF)
+            self.copy(0, i).start()
+
+    def advance(self, step):
+        for i in range(self.counts[step - 1]):
+            self.copy(step - 1, i).wait_recv()
+        own = self.links[step][0]
         for keep in (False, True):
-            for j in range(2):
+            for j in range(self.counts[step]):
                 i = (own if keep else 1 - own) + 2 * j
-                value = self.fetch(self.block(self.mine(0), i)) + self.got[i].astype(F32)
+                value = self.term(self.links[0][0], i) if step == 1 else self.held[i]
+                value = value + self.got[self.first[step - 1] + i].astype(F32)
                 if keep:
                     self.held[j] = value
                 else:
-                    self.out[4 + j] = value.astype(BF)
-                    self.copy(4 + j).start()
-
-    def third(self):
-        for j in range(2):
-            self.copy(4 + j).wait_recv()
-        other = 1 - self.mine(2)
-        self.out[6] = (self.held[other] + self.got[4 + other].astype(F32)).astype(BF)
-        self.copy(6).start()
+                    self.out[self.first[step] + j] = value.astype(BF)
+                    self.copy(step, j).start()
 
     def total(self):
-        self.copy(6).wait_recv()
-        own = self.mine(2)
-        return self.held[own] + self.got[4 + own].astype(F32) + self.got[6].astype(F32)
+        last = len(self.links) - 1
+        self.copy(last, 0).wait_recv()
+        return self.held[0] + self.got[self.first[last]].astype(F32)
 
     def finish(self):
-        for i in range(7):
-            self.copy(i).wait_send()
+        for step, count in enumerate(self.counts):
+            for i in range(count):
+                self.copy(step, i).wait_send()
 
 
 def settle_kernel(
@@ -1460,20 +1573,27 @@
     x_hbm,
     w_hbm,
     one_hbm,
-    gu_own_hbm,
-    gu_other_hbm,
+    wide_own_hbm,
+    wide_other_hbm,
+    down_hbm,
     res_hbm,
     home_ref,
     over_ref,
     result_hbm,
     gq_sum_ref,
     gu_sum_ref,
+    down_sum_ref,
+    out_sum_ref,
+    norm_sum_ref,
     d_ref,
     x_ref,
     w_ref,
     one_ref,
-    gu_own_ref,
-    gu_other_ref,
+    wide_own_ref,
+    wide_other_ref,
+    down_ref,
+    down_sent_ref,
+    down_got_ref,
     src_ref,
     out_ref,
     to_core_ref,
@@ -1483,9 +1603,10 @@
     own_ref,
     spare_ref,
     gq_ref,
+    gq_acc_ref,
     *refs,
 ):
-    halving_refs = (refs[:3], refs[3:6], refs[6:9])
+    halving_refs = tuple(refs[3 * i : 3 * i + 3] for i in range(3))
     (
         loads,
         s_res,
@@ -1503,9 +1624,8 @@
     d = lax.axis_index("dp")
     t = lax.axis_index("tensor")
     chunks, _, sub, width = own_ref.shape
-    tiles = res_hbm.shape[2]
-    sent = (chunks - 1) * tiles // chunks
-    rest = tiles - sent
+    sent = (chunks - 1) * sub // 16
+    rest = sub // 16
     core = (d, jnp.bitwise_xor(t, 1))
     chip = (d, jnp.bitwise_xor(t, 2))
 
@@ -1519,44 +1639,45 @@
     load_w = load(w_hbm, w_ref, 4)
     load_x = load(x_hbm, x_ref, 5)
     load_one = load(one_hbm, one_ref, 6)
-    load_gu = (load(gu_own_hbm, gu_own_ref, 7), load(gu_other_hbm, gu_other_ref, 8))
-
-    def slots_of(r, low, count):
-        return pl.ds(jnp.bitwise_xor(t, r) * tiles + low, count)
+    load_wide = (load(wide_own_hbm, wide_own_ref, 7), load(wide_other_hbm, wide_other_ref, 8))
+    load_down = load(down_hbm, down_ref, 11)
+    down_copy = remote(down_sent_ref, down_got_ref, s_res.at[4], r_res.at[4], chip)
+
+    def down_sum(member):
+        total = down_ref[0, member].astype(F32)
+        for g in range(1, groups):
+            total = total + down_ref[g, member].astype(F32)
+        return total
+
+
+    def in_src(r, low, count):
+        base = jnp.bitwise_xor(t, r) * (sent + rest)
+        return src_ref.at[:, pl.ds(base + low, count)]
 
     def source_of(r, low, count):
         return res_hbm.at[r, :, pl.ds(low, count)]
 
-    def in_src(r, low, count):
-        return src_ref.at[:, slots_of(r, low, count)]
-
-    load_res = (
-        load(source_of(0, 0, tiles), in_src(0, 0, tiles), 9),
-        load(source_of(2, 0, sent), in_src(2, 0, sent), 10),
+    res_parts = (
+        (source_of(0, 0, sent + rest), in_src(0, 0, sent + rest)),
+        (source_of(2, 0, sent), in_src(2, 0, sent)),
+        (in_src(2, sent, rest), in_src(2, sent, rest)),
     )
-    beside_res = (
-        remote(source_of(0, 0, tiles), in_src(0, 0, tiles), s_res.at[0], r_res.at[0], core),
-        remote(source_of(2, 0, sent), in_src(2, 0, sent), s_res.at[1], r_res.at[1], core),
-        remote(in_src(2, sent, rest), in_src(2, sent, rest), s_res.at[2], r_res.at[2], core),
-    )
+    load_res = [load(source, target, 9 + i) for i, (source, target) in enumerate(res_parts[:2])]
+    beside_res = [
+        remote(source, target, s_res.at[i], r_res.at[i], core)
+        for i, (source, target) in enumerate(res_parts)
+    ]
     across_res = remote(
         source_of(0, sent, rest), in_src(0, sent, rest), s_res.at[3], r_res.at[3], chip
     )
 
     load_w.start()
-    for r in (3, 2, 1, 0):
-        load_d(r).start()
-    load_gu[0].start()
-    load_gu[1].start()
-    load_x.start()
-    load_one.start()
-    load_res[0].start()
-    load_res[1].start()
+    load_d(3).start()
+    load_d(2).start()
     greet(groups, (1, 2), d, t)
-    across_res.start()
 
     def rows(c):
-        return slice(c * BLOCK, (c + 1) * BLOCK)
+        return pl.ds(pl.multiple_of(c * BLOCK, BLOCK), BLOCK)
 
     def piece(r, c):
         return mm(d_ref[jnp.bitwise_xor(t, r), :, rows(c)], w_ref[...], 0, 0)
@@ -1571,60 +1692,92 @@
 
     load_w.wait()
     load_d(3).wait()
-    for c in range(chunks):
+    load_d(1).start()
+    load_d(0).start()
+    load_wide[0].start()
+    load_wide[1].start()
+    load_d(2).wait()
+
+    @pl.loop(0, chunks)
+    def _(c):
         to_core_ref[0, c] = piece(3, c).astype(BF)
         to_core(0, c).start()
-    load_d(2).wait()
-    for c in range(chunks):
         value = piece(2, c)
         to_core(0, c).wait_recv()
         pair_ref[c] = (value + from_core_ref[0, c].astype(F32)).astype(BF)
-        other(c).start()
-    block_rows = gu_sum_ref.shape[0]
-
-    wide = gu_sum_ref.shape[1] // 2
-
-    def gu_rows(low, block):
+
+        @pl.when(c == 0)
+        def _():
+            other(0).start()
+
+    block_rows, _, inner = gu_sum_ref.shape
+
+    def wide_rows(part, block):
         at = pl.ds(pl.multiple_of(block * block_rows, block_rows), block_rows)
-        columns = slice(low, low + wide)
-        return gu_own_ref[at, columns].astype(F32) + gu_other_ref[at, columns].astype(F32)
-
+        columns = slice(part * WIDE_PARTS[0], WIDE_PARTS[0] + part * WIDE_PARTS[1])
+        return wide_own_ref[at, columns].astype(F32) + wide_other_ref[at, columns].astype(F32)
+
+    def gq_rows(y, low, high):
+        return gq_ref[y + 2 * low + 4 * high].astype(F32)
+
+    link_y, link_low, link_high = (
+        (lax.rem(lax.div(d, step), 2), (jnp.bitwise_xor(d, step), t)) for step in (1, 2, 4)
+    )
     sums = [
-        Halving(fetch, bits, halving_refs[i], (s_half.at[i], r_half.at[i]), d, t)
-        for i, (fetch, bits) in enumerate(
+        Halving(fetch, links, halving_refs[i], (s_half.at[i], r_half.at[i]))
+        for i, (fetch, links) in enumerate(
             (
-                (functools.partial(gu_rows, 0), (1, 2, 4)),
-                (functools.partial(gu_rows, wide), (2, 1, 4)),
-                (lambda block: gq_ref[block].astype(F32), (1, 2, 4)),
+                (
+                    lambda y, low, high: wide_rows(0, y + 2 * low + 4 * high),
+                    (link_y, link_low, link_high),
+                ),
+                (
+                    lambda low, y, high: wide_rows(1, y + 2 * low + 4 * high),
+                    (link_low, link_y, link_high),
+                ),
+                (gq_rows, (link_y, link_low, link_high)),
             )
         )
     ]
 
-    load_gu[0].wait()
-    load_gu[1].wait()
+    load_wide[0].wait()
+    load_wide[1].wait()
+    load_x.start()
+    load_one.start()
+    load_down.start()
+    for copy in load_res:
+        copy.start()
     sums[0].start()
     sums[1].start()
     load_d(1).wait()
-    for c in range(chunks):
+
+    @pl.loop(0, chunks)
+    def _(c):
         to_core_ref[1, c] = piece(1, c).astype(BF)
         to_core(1, c).start()
+
     load_d(0).wait()
     load_one.wait()
-    for c in range(chunks):
+
+    @pl.loop(0, chunks)
+    def _(c):
         one_ref[rows(c), :] += piece(0, c)
 
     def start_gq():
         load_x.wait()
-        total = mm(d_ref[0], x_ref[0], 1, 0)
-        for part in range(1, size):
-            total = total + mm(d_ref[part], x_ref[part], 1, 0)
-        total = total.T.astype(BF)
+        gq_acc_ref[...] = jnp.zeros_like(gq_acc_ref)
+
+        @pl.loop(0, size)
+        def _(part):
+            gq_acc_ref[...] += mm(d_ref[part], x_ref[part], 1, 0)
+
+        total = gq_acc_ref[...].T.astype(BF)
         for g in range(groups):
             gq_ref[g] = total[g * block_rows : (g + 1) * block_rows]
         sums[2].start()
 
     def store_result(i):
-        at = pl.ds(i * ROWS, ROWS)
+        at = pl.ds(pl.multiple_of(i * ROWS, ROWS), ROWS)
         return pltpu.make_async_copy(out_ref.at[at], result_hbm.at[at], keep.at[chunks + 1 + i])
 
     blocks = out_ref.shape[0] // ROWS
@@ -1634,8 +1787,11 @@
             copy.wait()
         for copy in beside_res:
             copy.wait_recv()
-        for i in range(blocks):
-            out_ref[i * ROWS : (i + 1) * ROWS, :] = unpack_block(spots_ref, src_ref, i)
+
+        @pl.loop(0, blocks)
+        def _(i):
+            at = pl.ds(pl.multiple_of(i * ROWS, ROWS), ROWS)
+            out_ref[at, :] = unpack_block(spots_ref, src_ref, i)
             store_result(i).start()
 
     store_over(src_ref, res_over_ref, jnp.bitwise_xor(size - 1, t))
@@ -1661,7 +1817,7 @@
             body.across(k, (c,), (c,)).wait_recv()
             body.beside(2, k, (c,), (c,)).start()
 
-    for c in range(chunks):
+    def send_home(c):
         to_core(1, c).wait_recv()
         partial = one_ref[rows(c), :] + from_core_ref[1, c].astype(F32)
         other(c).wait_recv()
@@ -1681,47 +1837,72 @@
             own_over.start()
             for k in range(1, groups):
                 extra.arrival(spare_ref.at[lax.rem(d + k, groups)], k, (), ()).start()
-        if c == 0:
-            across_res.wait_recv()
-            for copy in beside_res:
-                copy.start()
-            start_gq()
-            sums[0].second()
-            sums[1].second()
-        else:
-            pass_on(c - 1)
-        if c == 1:
-            sums[0].third()
-            sums[1].third()
-    sums[2].second()
-    pass_on(chunks - 1)
-    sums[2].third()
-    arrange_result()
+
+    other(0).wait_send()
+    other(1).start()
+    send_home(0)
+    start_gq()
+    other(1).wait_send()
+    other(2).start()
+    send_home(1)
+    sums[0].advance(1)
+    sums[1].advance(1)
+    other(2).wait_send()
+    pass_on(0)
+    across_res.start()
+    send_home(2)
+    sums[0].advance(2)
+    sums[1].advance(2)
+    sums[2].advance(1)
+    pass_on(1)
+    across_res.wait_recv()
+    for copy in beside_res:
+        copy.start()
+    load_down.wait()
+    down_sent_ref[...] = down_sum(1).astype(BF)
+    down_copy.start()
+    pass_on(2)
     own_over.wait()
     for k in range(groups):
         if k > 0:
             extra.arrival(spare_ref.at[0], k, (), ()).wait_recv()
         extra.across(k, (), ()).start()
         extra.beside(0, k, (), ()).start()
-    gu_sum_ref[:, :wide] = sums[0].total()
-    gu_sum_ref[:, wide:] = sums[1].total()
-    gq_sum_ref[...] = sums[2].total()
-    for c in range(chunks):
-        pass_far(c)
+    sums[2].advance(2)
+    pass_far(0)
+    pass_far(1)
+    arrange_result()
+    down_copy.wait_recv()
+    totals = jnp.concatenate(
+        [sums[0].total(), sums[1].total(), down_sum(0) + down_got_ref[...].astype(F32)], 1
+    )
+    gu_sum_ref[:, 0, :] = totals[:, :inner]
+    gu_sum_ref[:, 1, :] = totals[:, inner : 2 * inner]
+    total = sums[2].total()
+    local = gq_sum_ref.shape[2]
+    for i in range(3):
+        gq_sum_ref[i] = total[:, i * local : (i + 1) * local]
+    out_sum_ref[...] = totals[:, 2 * inner : 2 * inner + local]
+    norm_sum_ref[...] = totals[:, 2 * inner + local : 2 * inner + local + norm_sum_ref.shape[1]]
+    down_sum_ref[...] = totals[:, totals.shape[1] - inner :]
+    pass_far(2)
     for k in range(groups):
         extra.across(k, (), ()).wait_recv()
         extra.beside(2, k, (), ()).start()
+    down_copy.wait_send()
     across_res.wait_send()
     for copy in beside_res:
         copy.wait_send()
-    for i in range(blocks):
+
+    @pl.loop(0, blocks)
+    def _(i):
         store_result(i).wait()
+
     for each in sums:
         each.finish()
     for c in range(chunks):
         to_core(0, c).wait_send()
         to_core(1, c).wait_send()
-        other(c).wait_send()
     for k in range(groups):
         for c in range(chunks):
             body.beside(0, k, (c,), (c,)).wait_recv()
@@ -1740,14 +1921,26 @@
         extra.beside(2, k, (), ()).wait_send()
 
 
-def settle(match, spots, res_over, d_qkv_t, x_all, w_t, grad_one, gu_own, gu_other, res):
+def settle(
+    match,
+    spots,
+    res_over,
+    d_qkv_t,
+    x_all,
+    w_t,
+    grad_one,
+    wide_own,
+    wide_other,
+    down,
+    inner,
+    res,
+):
     size, local, rows = d_qkv_t.shape
-    _, groups, share, width = res.shape
+    _, groups, _, sub, width = res.shape
+    share = res.shape[2] * sub
     res = res.reshape(-1, groups, share // 16, 16, width)
     chunks = rows // BLOCK
-    sub = BLOCK // groups
     part = width // groups
-    wide = gu_own.shape[1]
     total_rows = size * rows
     anywhere = pl.BlockSpec(memory_space=pl.ANY)
     vmem = pl.BlockSpec(memory_space=pltpu.VMEM)
@@ -1756,29 +1949,35 @@
     shape = jax.ShapeDtypeStruct
     buffer = pltpu.VMEM((chunks, BLOCK, width), BF)
     pair_buffer = pltpu.VMEM((2, chunks, BLOCK, width), BF)
-    halving = lambda columns: [
-        pltpu.VMEM((7, part, columns), BF),
-        pltpu.VMEM((7, part, columns), BF),
-        pltpu.VMEM((2, part, columns), F32),
+    halving = lambda columns, steps: [
+        pltpu.VMEM((2**steps - 1, part, columns), BF),
+        pltpu.VMEM((2**steps - 1, part, columns), BF),
+        pltpu.VMEM((2 ** (steps - 2), part, columns), F32),
     ]
     return pl.pallas_call(
         functools.partial(settle_kernel, groups, size),
-        in_specs=[smem, smem, vmem] + [anywhere] * 7,
-        out_specs=[anywhere, anywhere, anywhere, vmem, vmem],
+        in_specs=[smem, smem, vmem] + [anywhere] * 8,
+        out_specs=[anywhere, anywhere, anywhere] + [vmem] * 5,
         out_shape=[
             shape((size, groups, chunks, sub, width), BF),
             shape((size, groups, 1, width), BF),
             shape((total_rows, width), BF),
-            shape((part, local), F32),
-            shape((part, wide), F32),
+            shape((3, part, local // 3), F32),
+            shape((part, 2, inner), F32),
+            shape((part, inner), F32),
+            shape((part, local // 3), F32),
+            shape((part, 4), F32),
         ],
         scratch_shapes=[
             pltpu.VMEM(d_qkv_t.shape, BF),
             pltpu.VMEM(x_all.shape, BF),
             pltpu.VMEM(w_t.shape, BF),
             pltpu.VMEM(grad_one.shape, F32),
-            pltpu.VMEM(gu_own.shape, BF),
-            pltpu.VMEM(gu_own.shape, BF),
+            pltpu.VMEM(wide_own.shape, BF),
+            pltpu.VMEM(wide_own.shape, BF),
+            pltpu.VMEM(down.shape, BF),
+            pltpu.VMEM(down.shape[2:], BF),
+            pltpu.VMEM(down.shape[2:], BF),
             pltpu.VMEM((groups, size * share // 16 + 1, 16, width), BF),
             pltpu.VMEM((total_rows, width), BF),
             pair_buffer,
@@ -1788,12 +1987,13 @@
             pltpu.VMEM((chunks, groups, sub, width), BF),
             pltpu.VMEM((groups, 1, width), BF),
             pltpu.VMEM((groups, part, local), BF),
-            *halving(wide // 2),
-            *halving(wide // 2),
-            *halving(local),
-            dma((11,)),
-            dma((4,)),
-            dma((4,)),
+            pltpu.VMEM((local, width), F32),
+            *halving(WIDE_PARTS[0], 3),
+            *halving(WIDE_PARTS[1], 3),
+            *halving(local, 3),
+            dma((15,)),
+            dma((5,)),
+            dma((5,)),
             dma((3, 7)),
             dma((3, 7)),
             dma((4, groups, chunks)),
@@ -1811,7 +2011,19 @@
             flops=4 * size * rows * local * width, bytes_accessed=150 << 20, transcendentals=0
         ),
         name="settle",
-    )(match, spots, res_over, d_qkv_t, x_all, w_t, grad_one, gu_own, gu_other, res)
+    )(
+        match,
+        spots,
+        res_over,
+        d_qkv_t,
+        x_all,
+        w_t,
+        grad_one,
+        wide_own,
+        wide_other,
+        down,
+        res,
+    )
 
 
 def local(tokens, cotangent, lengths, dealing, w_qkv, w_out, w_gu, w_down, gains, shifts):
@@ -1842,7 +2054,9 @@
     def over_dp(array):
         return lax.all_to_all(array, "dp", split_axis=0, concat_axis=0, tiled=True)
 
-    far_out, far_down = swap(w_out.T, size, 2), swap(w_down, size, 2)
+    half = w_down.shape[0] // 2
+    down_half = lax.dynamic_slice_in_dim(w_down, ids[0] % 2 * half, half, 0)
+    far_out, far_down = swap(w_out.T, size, 2), swap(down_half, size, 2)
     match_square = match.reshape(groups, groups)
 
     def fill(received, over, last):
@@ -1862,20 +2076,23 @@
         x_rel = jnp.stack(gather_members(over_dp(send_x)))
         relative = jnp.bitwise_xor(jnp.arange(size, dtype=i32), me)
         x_rel = fill(x_rel, over_dp(over_x)[:, 0], relative == size - 1)
-    cot = over_dp(send_c)
-    if not fused:
-        cot = fill(cot[None, :, :share], cot[:, share], (me == size - 1)[None])[0]
-
     local_width = w_qkv.shape[2]
     w_qkv_t = w_qkv.transpose(1, 2, 0).reshape(3 * local_width, width)
     x_rel, near_gu = lax.optimization_barrier((x_rel, w_gu.reshape(width, -1)))
     far_gu = swap(near_gu, size, 2)
-    frequency = 1000.0 ** (-(jnp.arange(HALF, dtype=F32) * 2.0) / HEAD)
+    other_down = lax.ppermute(far_down, "dp", [(i, i ^ 1) for i in range(groups)])
+    cot = over_dp(send_c)
+    if not fused:
+        cot = fill(cot[None, :, :share], cot[:, share], (me == size - 1)[None])[0]
+    frequency = np.float32(1000.0) ** (-(np.arange(HALF, dtype=np.float32) * 2) / HEAD)
+    frequency = jnp.asarray(frequency.astype(np.float32))
     q, k, v, k_rows, v_rows, cosine, sine, x_all, x_own = project(
         meta, match, x_rel, over_x, w_qkv_t, frequency[:, None], groups, fused
     )
     o_blocks, lse = attend(meta, q, k_rows, v, groups)
-    o_blocks, far_gu, cot = lax.optimization_barrier((o_blocks, far_gu, cot))
+    o_blocks, far_gu, other_down, cot = lax.optimization_barrier(
+        (o_blocks, far_gu, other_down, cot)
+    )
 
     norms = jnp.concatenate([gains.T, shifts.T], 0)
     (
@@ -1902,14 +2119,15 @@
         far_gu,
         w_down,
         far_down,
+        other_down,
     )
     grad_args = (normed_t, d_branch_t, d_attn_t, hidden, d_gu, heads_own, norm_grads)
     if fused:
-        gu_own, gu_other, pair, do_rel, home_result, over_result = grads(
+        wide_own, wide_other, down, do_rel, home_result, over_result = grads(
             match, groups, *grad_args, d_heads, result_own
         )
-        home_result = home_result.reshape(3, groups, share, width)
-        gu_other = swap(gu_other, size, 2)
+        wide_other = swap(wide_other, size, 2)
+        down = over_dp(down)
     else:
         sent_grads = weight_grads(1, *grad_args)
         kept_grads = weight_grads(0, *grad_args)
@@ -1919,7 +2137,6 @@
     d_qkv_t = attend_back(
         meta, q, k_rows, k, v_rows, o_blocks, do_rel, lse, cosine, sine, groups
     )
-    pair = lax.psum_scatter(pair, "dp", scatter_dimension=1, tiled=True)
     def send_back(own):
         body = own.reshape(subs, groups, sub, width).transpose(1, 0, 2, 3)
         body = body.reshape(groups, share, width)
@@ -1933,7 +2150,7 @@
         return tuple(jnp.stack(gather_members(a)) for a in pair)
 
     if fused:
-        home_input, home_over, result, qkv_sum, gu_sum = settle(
+        home_input, home_over, result, qkv_sum, gu_sum, down_sum, out_sum, norm_sum = settle(
             match,
             spots,
             over_result,
@@ -1941,12 +2158,13 @@
             x_all,
             w_qkv_t,
             grad_one,
-            gu_own,
-            gu_other,
+            wide_own,
+            wide_other,
+            down,
+            w_down.shape[1],
             home_result,
         )
         home_input = home_input.reshape(size, groups, share, width)
-        pair, home_input = lax.optimization_barrier((pair, home_input))
     else:
         back_rel, grad_qkv = project_back(meta, d_qkv_t, x_all, w_qkv_t)
         grad_qkv = grad_qkv.reshape(groups, width // groups, 3 * local_width)
@@ -1955,20 +2173,22 @@
         home_input = send_back(input_own.astype(BF))
         grad_qkv = lax.all_to_all(grad_qkv, "dp", split_axis=0, concat_axis=0, tiled=True)
         qkv_sum = jnp.sum(grad_qkv.astype(F32), 0)
-    qkv_sum = qkv_sum.reshape(-1, 3, local_width)
-    summed = pair[0].astype(F32) + swap(pair[1], size, 2).astype(F32)
-    inner = w_down.shape[1]
-    if not fused:
-        gu_sum, summed = summed[:, : 2 * inner], summed[:, 2 * inner :]
-    gu_sum = gu_sum.reshape(-1, 2, inner)
-    down_sum = summed[:, :inner]
-    out_sum = summed[:, inner : inner + local_width]
-    norm_sum = summed[:, inner + local_width : inner + local_width + 4]
+        pair = lax.psum_scatter(pair, "dp", scatter_dimension=1, tiled=True)
+        summed = pair[0].astype(F32) + swap(pair[1], size, 2).astype(F32)
+    if fused:
+        qkv_sum = qkv_sum.transpose(1, 0, 2)
+    else:
+        qkv_sum = qkv_sum.reshape(-1, 3, local_width)
+        inner = w_down.shape[1]
+        gu_sum = summed[:, : 2 * inner].reshape(-1, 2, inner)
+        out_sum = summed[:, 2 * inner : 2 * inner + local_width]
+        norm_sum = summed[:, 2 * inner + local_width : 2 * inner + local_width + 4]
+        down_sum = summed[:, -inner:]
     norm_sum = lax.dynamic_slice_in_dim(
         norm_sum, me * (norm_sum.shape[0] // size), norm_sum.shape[0] // size, 0
     )
     if fused:
-        input_grad = unpack(spots, me[None], home_input, home_over)
+        input_grad, result = unpack(spots, me[None], home_input, home_over, result)
     else:
         row_ids = jnp.arange(rows, dtype=i32)[None, :]
         low, count, group, first = (table[i, 1:][:, None] for i in range(4))

time: 405 us -> 388 us (0.958); the launches traced: 399 us -> 387 us
  between operations: 14.8 us -> 0.82 us
  local copies, waits for them, and re-layouts: 17.7 us -> 9.5 us
    pallas_call x1, Pallas kernels: 76.1 us -> 86.1 us  [settle(): pl.pallas_call(functools.partial(settle_kernel, groups, size), in_specs=[...]
    pallas_call x1, Pallas kernels: 14.1 us -> 8.58 us  [pack(): pl.pallas_call(functools.partial(pack_kernel, groups, size), grid_spec=pl...]
    all_to_all x1 -> x2, waiting for transfers between devices: 0.01 us -> 4.42 us  [over_dp(): return lax.all_to_all(array, 'dp', split_axis=0, concat_axis=0, tiled=True)]
    unnamed x23 -> x31, local copies, waits for them, and re-layouts: 11.8 us -> 7.53 us
    all_to_all x1 -> x2, starting transfers between devices: 7.11 us -> 11.3 us  [over_dp(): return lax.all_to_all(array, 'dp', split_axis=0, concat_axis=0, tiled=True)]
  transfers between devices with their start and end apart: 7 -> 7, of which waited for: 1 -> 2; matrix products, arithmetic and copies ran while one was open for 2% -> 0% of each run, Pallas kernels for 62% -> 39%
where the time goes in v5:
time: 388 us; the launch traced here: 387 us
  Pallas kernels  347 us (89%)
  starting transfers between devices  17.5 us (5%)
  waiting for transfers between devices  10.6 us (3%)
  local copies, waits for them, and re-layouts  9.5 us (2%)
    pallas_call x1, Pallas kernels, settle(): pl.pallas_call(functools.partial(settle_kernel, groups, size), in_specs=[...  86.1 us
    pallas_call x1, Pallas kernels, attend_back(): pl.pallas_call(functools.partial(attend_back_kernel, groups), grid_spec=p...  57.8 us
    pallas_call x1, Pallas kernels, middle(): pl.pallas_call(functools.partial(middle_kernel, size, groups, len(weights...  53.2 us
    pallas_call x1, Pallas kernels, grads(): pl.pallas_call(functools.partial(grads_kernel, groups, size), grid=(size,...  44.6 us
    pallas_call x1, Pallas kernels, route(): pl.pallas_call(functools.partial(route_kernel, groups, size), in_specs=[a...  41.8 us
    pallas_call x1, Pallas kernels, attend(): pl.pallas_call(functools.partial(attend_kernel, groups), grid_spec=pltpu....  32.8 us
    pallas_call x1, Pallas kernels, unpack(): pl.pallas_call(functools.partial(unpack_kernel, size), grid_spec=pltpu.Pr...  11.5 us
    all_to_all x2, starting transfers between devices, over_dp(): return lax.all_to_all(array, 'dp', split_axis=0, concat_axis=0, tiled=True)  11.3 us
  transfers between devices with their start and end apart: 7, of which 2 were waited for; matrix products, arithmetic and copies ran while one was open for 0% of the time, Pallas kernels for 39%

profile of v5, /device:TPU:0, one launch (start us, length us, event | category | flops | bytes accessed | tf_op | source)
XLA Modules:
  0.0 387.1 jit_solution(16994831114901615886)
XLA Ops:
  0.6 1.1 constant_dynamic-slice_fusion.1
  1.8 3.0 collective-permute-start.1
  4.8 0.1 collective-permute-start
  4.8 0.6 pad_add_fusion.ids
  5.4 8.6 %pack.1 = (bf16[8,96,768]{2,1,0:T(8,128)(2,1)}, bf16[8,1,768]{2,1,0:T(2,128)(2,1)}, bf16[8,112,768]{2,1,0:T(8,128)(2,1)}, s32[16]{0:T(128)}, s32[4,17]{1,0:T(4,128)}, /*index=5*/f32[64]{0:T(128)}, s32[192]{0:T(256)}) custom-call(s32[16]{0:T(128)} %lengths.1, s32[16]{0:T(128)} %dealing.1, s32[2]{0:T(128)} %pad_add_fusion.ids, bf16[3072,768]{1,0:T(8,128)(2,1)} %bitcast.18, ...), custom_call_target="tpu_custom_call" | custom-call | bytes 20971520 | tf_op jit(solution)/shard_map/pack/pallas_call | solution.py:199
  14.0 0.0 copy-start.1
  14.0 41.8 %route.1 = (bf16[4,8,96,768]{3,2,1,0:T(8,128)(2,1)}, bf16[8,1,768]{2,1,0:T(2,128)(2,1)}) custom-call(bf16[8,96,768]{2,1,0:T(8,128)(2,1)} %get-tuple-element.67.send_ref, bf16[8,1,768]{2,1,0:T(2,128)(2,1)} %get-tuple-element.68.over_ref), custom_call_target="tpu_custom_call" | custom-call | bytes 62914560 | tf_op jit(solution)/shard_map/route/pallas_call | solution.py:1496
  55.9 0.0 collective-permute-done.refs_7_
  55.9 0.0 collective-permute-done.1.refs_11_
  55.9 0.0 copy-start.10
  55.9 5.6 %all-to-all-start = ((bf16[8,112,768]{2,1,0:T(8,128)(2,1)}), bf16[8,112,768]{2,1,0:T(8,128)(2,1)}, u32[]{:S(2)}, u32[]{:S(2)}) async-start(bf16[8,112,768]{2,1,0:T(8,128)(2,1)} %get-tuple-element.80), calls=%async_computation | async-start | bytes 2752512 | tf_op jit(solution)/shard_map/all_to_all | solution.py:2055
  61.5 0.0 copy-done.1
  61.5 0.0 copy-start.7
  61.5 0.0 copy-start.8
  61.5 0.4 copy.21
  61.9 0.0 copy-start.2
  61.9 0.6 collective-permute-start.2
  62.5 0.0 copy-done.10
  62.5 2.0 collective-permute-start.3
  64.5 0.0 copy-done.7
  64.5 0.0 copy-done.8
  64.6 0.6 pad_maximum_fusion.refs_4_
  65.2 11.0 %project.1 = (bf16[192,3072]{1,0:T(8,128)(2,1)}, bf16[192,3072]{1,0:T(8,128)(2,1)}, bf16[240,3072]{1,0:T(8,128)(2,1)}, bf16[3,3072,64]{2,1,0:T(8,128)(2,1)}, bf1...) custom-call(s32[16]{0:T(128)} %get-tuple-element.65.meta.info, ...), custom_call_target="tpu_custom_call" | custom-call | flops 2359296 | bytes 1048576 | tf_op jit(solution)/shard_map/project/pallas_call | solution.py:348
  76.2 0.0 copy-done.2
  76.2 32.8 %attend.1 = (bf16[12,192,256]{2,1,0:T(8,128)(2,1)}, f32[3,3072]{1,0:T(4,128)}) custom-call(s32[16]{0:T(128)} %get-tuple-element.65.meta.info, bf16[192,3072]{1,0:T(8,128)(2,1)} %get-tuple-element.74.q_ref, bf16[3,3072,64]{2,1,0:T(8,128)(2,1)} %get-tuple-element.75.k_ref.krow_ref, bf16[240,3072]{1,0:T(8,128)(2,1)} %get-tuple-element.76.v_ref), custom_call_target="tpu_custom_call" | custom-call | flops 3623878656 | bytes 8388608 | tf_op jit(solution)/shard_map/attend/pallas_call | solution.py:445
  109.0 0.0 collective-permute-done.3.refs_12_
  109.0 0.0 copy-start.11
  109.0 6.2 %collective-permute-done.2.refs_9_ = bf16[768,1536]{1,0:T(8,128)(2,1)S(1)} collective-permute-done((bf16[768,1536]{1,0:T(8,128)(2,1)S(1)}, bf16[768,1536]{1,0:T(8,128)(2,1)S(1)}, u32[]{:S(2)}, u32[]{:S(2)}) %collective-permute-start.2) | collective-permute-done | bytes 2359328 | tf_op jit(solution)/shard_map/ppermute | solution.py:1327
  115.2 0.0 copy-start.9
  115.2 0.0 all-to-all-done.refs_2_.refs_3_
  115.2 0.0 copy-done.11
  115.2 1.4 copy-done.9
  116.6 53.2 %middle.1 = (bf16[768,768]{1,0:T(8,128)(2,1)}, f32[768,768]{1,0:T(8,128)}, bf16[4,192,768]{2,1,0:T(8,128)(2,1)}, bf16[4,192,768]{2,1,0:T(8,128)(2,1)}, bf16[768,...) custom-call(bf16[768,768]{1,0:T(8,128)(2,1)} %get-tuple-element.73.r, ...), custom_call_target="tpu_custom_call" | custom-call | flops 23555211264 | bytes 41943040 | tf_op jit(solution)/shard_map/middle/pallas_call | solution.py:952
  169.8 44.6 %grads.1 = (bf16[768,1664]{1,0:T(8,128)(2,1)}, bf16[768,1664]{1,0:T(8,128)(2,1)}, bf16[8,2,96,896]{3,2,1,0:T(8,128)(2,1)}, bf16[4,192,768]{2,1,0:T(8,128)(2,1)},...) custom-call(f32[64]{0:T(128)} %get-tuple-element.64.match_ref.refs_1_, ...), custom_call_target="tpu_custom_call" | custom-call | flops 11777605632 | bytes 83886080 | tf_op jit(solution)/shard_map/grads/pallas_call | solution.py:1256
  214.4 5.8 %all-to-all-start.1 = ((bf16[8,2,96,896]{3,2,1,0:T(8,128)(2,1)}), bf16[8,2,96,896]{3,2,1,0:T(8,128)(2,1)S(1)}, u32[]{:S(2)}, u32[]{:S(2)}) async-start(bf16[8,2,96,896]{3,2,1,0:T(8,128)(2,1)} %get-tuple-element.106), calls=%async_computation.1 | async-start | bytes 5505024 | tf_op jit(solution)/shard_map/all_to_all | solution.py:2055
  220.1 0.5 collective-permute-start.4
  220.7 57.8 %attend_back.1.d_hbm = bf16[4,576,768]{2,1,0:T(8,128)(2,1)} custom-call(s32[16]{0:T(128)} %get-tuple-element.65.meta.info, bf16[192,3072]{1,0:T(8,128)(2,1)} %get-tuple-element.74.q_ref, bf16[3,3072,64]{2,1,0:T(8,128)(2,1)} %get-tuple-element.75.k_ref.krow_ref, bf16[192,3072]{1,0:T(8,128)(2,1)} %get-tuple-element.96.k_ref, ...), custom_call_target="tpu_custom_call" | custom-call | flops 36238786560 | bytes 16777216 | tf_op jit(solution)/shard_map/attend_back/pallas_call | solution.py:574
  278.5 0.0 collective-permute-done.4.wide_other_hbm
  278.5 4.4 %all-to-all-done.1.down_hbm = bf16[8,2,96,896]{3,2,1,0:T(8,128)(2,1)S(1)} async-done(((bf16[8,2,96,896]{3,2,1,0:T(8,128)(2,1)}), bf16[8,2,96,896]{3,2,1,0:T(8,128)(2,1)S(1)}, u32[]{:S(2)}, u32[]{:S(2)}) %all-to-all-start.1) | async-done | bytes 2752544 | tf_op jit(solution)/shard_map/all_to_all | solution.py:2055
  282.9 0.0 copy-start
  282.9 1.5 copy-done
  284.4 86.1 %settle.1 = (bf16[4,8,3,32,768]{4,3,2,1,0:T(8,128)(2,1)}, bf16[4,8,1,768]{3,2,1,0:T(2,128)(2,1)}, bf16[3072,768]{1,0:T(8,128)(2,1)}, f32[3,96,192]{2,1,0:T(8,128...) custom-call(f32[64]{0:T(128)} %get-tuple-element.64.match_ref.refs_1_, ...), custom_call_target="tpu_custom_call" | custom-call | flops 5435817984 | bytes 157286400 | tf_op jit(solution)/shard_map/settle/pallas_call | solution.py:1957
  370.5 0.9 fusion
  371.4 0.6 copy.19
  372.1 0.6 copy.20
  372.7 0.0 copy-start.5
  372.7 0.0 copy-start.6
  372.7 0.0 copy-start.3
  372.7 0.0 copy-start.4
  372.7 11.5 %unpack.1 = (bf16[3072,768]{1,0:T(8,128)(2,1)}, bf16[3072,768]{1,0:T(8,128)(2,1)}) custom-call(s32[192]{0:T(256)} %get-tuple-element.63.spots_ref.spots, s32[1]{0:T(128)} %bitcast.1.me, bf16[4,8,6,16,768]{4,3,2,1,0:T(8,128)(2,1)} %bitcast.20, bf16[4,8,1,768]{3,2,1,0:T(2,128)(2,1)} %get-tuple-element.109.over_ref, bf16[3072,768]{1,0:T(8,128)(2,1)} %get-tuple-element.110.result_ref), custom_call_target="tpu_custom_call" | custom-call | bytes 31457280 | tf_op jit(solution)/shard_map/unpack/pallas_call | solution.py:1406
  384.2 0.0 copy-done.5
  384.2 0.7 copy.26
  384.9 0.0 copy-done.6
  384.9 0.6 copy.27
  385.6 0.0 copy-done.3
  385.6 0.8 copy.28
  386.4 0.0 copy-done.4
  386.4 0.7 copy.29
Async XLA Ops:
  1.8 54.1 %collective-permute-start.1 = (bf16[384,768]{1,0:T(8,128)(2,1)S(1)}, bf16[384,768]{1,0:T(8,128)(2,1)S(1)}, u32[]{:S(2)}, u32[]{:S(2)}) collective-permute-start(bf16[384,768]{1,0:T(8,128)(2,1)S(1)} %constant_dynamic-slice_fusion.1), channel_id=1, source_target_pairs={{0,2},{1,3},{2,0},{3,1},{4,6},{5,7},{6,4},{7,5},{8,10},{9,11},{10,... | collective-permute-start | bytes 1769480 | tf_op jit(solution)/shard_map/ppermute | solution.py:1327
  4.8 51.1 %collective-permute-start = (bf16[192,768]{1,0:T(8,128)(2,1)}, bf16[192,768]{1,0:T(8,128)(2,1)}, u32[]{:S(2)}, u32[]{:S(2)}) collective-permute-start(bf16[192,768]{1,0:T(8,128)(2,1)} %bitcast.32), channel_id=1, source_target_pairs={{0,2},{1,3},{2,0},{3,1},{4,6},{5,7},{6,4},{7,5},{8,10},{9,11},{10,... | collective-permute-start | bytes 884744 | tf_op jit(solution)/shard_map/ppermute | solution.py:1327
  14.0 47.4 %copy-start.1 = (bf16[768,2,768]{2,1,0:T(2,128)(2,1)S(1)}, bf16[768,2,768]{2,1,0:T(2,128)(2,1)}, u32[]{:S(2)}) copy-start(bf16[768,2,768]{2,1,0:T(2,128)(2,1)} %param.17) | copy-start | bytes 7077892
  55.9 6.6 %copy-start.10 = (bf16[384,768]{1,0:T(8,128)(2,1)}, bf16[384,768]{1,0:T(8,128)(2,1)S(1)}, u32[]{:S(2)}) copy-start(bf16[384,768]{1,0:T(8,128)(2,1)S(1)} %collective-permute-done.1.refs_11_) | copy-start | bytes 1769476
  55.9 59.3 %all-to-all-start = ((bf16[8,112,768]{2,1,0:T(8,128)(2,1)}), bf16[8,112,768]{2,1,0:T(8,128)(2,1)}, u32[]{:S(2)}, u32[]{:S(2)}) async-start(bf16[8,112,768]{2,1,0:T(8,128)(2,1)} %get-tuple-element.80), calls=%async_computation | async-start | bytes 2752512 | tf_op jit(solution)/shard_map/all_to_all | solution.py:2055
  61.5 3.1 copy-start.7
  61.5 3.1 copy-start.8
  61.9 14.3 %copy-start.2 = (bf16[96,8,2,768]{3,1,2,0:T(8,128)(2,1)}, bf16[96,8,2,768]{3,1,2,0:T(8,128)(2,1)S(1)}, u32[]{:S(2)}) copy-start(bf16[96,8,2,768]{3,1,2,0:T(8,128)(2,1)S(1)} %copy.21) | copy-start | bytes 7077892
  61.9 53.3 %collective-permute-start.2 = (bf16[768,1536]{1,0:T(8,128)(2,1)S(1)}, bf16[768,1536]{1,0:T(8,128)(2,1)S(1)}, u32[]{:S(2)}, u32[]{:S(2)}) collective-permute-start(bf16[768,1536]{1,0:T(8,128)(2,1)S(1)} %bitcast.25), channel_id=1, source_target_pairs={{0,2},{1,3},{2,0},{3,1},{4,6},{5,7},{6,4},{7,5},{8,10},{9,11},{10,... | collective-permute-start | bytes 7077896 | tf_op jit(solution)/shard_map/ppermute | solution.py:1327
  62.5 46.5 %collective-permute-start.3 = (bf16[384,768]{1,0:T(8,128)(2,1)S(1)}, bf16[384,768]{1,0:T(8,128)(2,1)S(1)}, u32[]{:S(2)}, u32[]{:S(2)}) collective-permute-start(bf16[384,768]{1,0:T(8,128)(2,1)S(1)} %collective-permute-done.1.refs_11_), channel_id=1, source_target_pairs={{0,4},{4,0},{8,12},{12,8},{16,20},{20,16},{24,28},{28,24},{1,5},{5... | collective-permute-start | bytes 1769480 | tf_op jit(solution)/shard_map/ppermute | solution.py:2083
  109.0 6.2 %copy-start.11 = (bf16[384,768]{1,0:T(8,128)(2,1)}, bf16[384,768]{1,0:T(8,128)(2,1)S(1)}, u32[]{:S(2)}) copy-start(bf16[384,768]{1,0:T(8,128)(2,1)S(1)} %collective-permute-done.3.refs_12_) | copy-start | bytes 1769476
  115.2 1.4 copy-start.9
  214.4 68.6 %all-to-all-start.1 = ((bf16[8,2,96,896]{3,2,1,0:T(8,128)(2,1)}), bf16[8,2,96,896]{3,2,1,0:T(8,128)(2,1)S(1)}, u32[]{:S(2)}, u32[]{:S(2)}) async-start(bf16[8,2,96,896]{3,2,1,0:T(8,128)(2,1)} %get-tuple-element.106), calls=%async_computation.1 | async-start | bytes 5505024 | tf_op jit(solution)/shard_map/all_to_all | solution.py:2055
  220.1 58.4 %collective-permute-start.4 = (bf16[768,1664]{1,0:T(8,128)(2,1)}, bf16[768,1664]{1,0:T(8,128)(2,1)}, u32[]{:S(2)}, u32[]{:S(2)}) collective-permute-start(bf16[768,1664]{1,0:T(8,128)(2,1)} %get-tuple-element.105), channel_id=1, source_target_pairs={{0,2},{1,3},{2,0},{3,1},{4,6},{5,7},{6,4},{7,5},{8,10},{9,11},{10,... | collective-permute-start | bytes 7667720 | tf_op jit(solution)/shard_map/ppermute | solution.py:1327
  282.9 1.5 copy-start
  372.7 11.5 %copy-start.5 = (f32[3,96,192]{2,1,0:T(8,128)S(1)}, f32[3,96,192]{2,1,0:T(8,128)}, u32[]{:S(2)}) copy-start(f32[3,96,192]{2,1,0:T(8,128)} %get-tuple-element.113) | copy-start | bytes 663556
  372.7 12.2 %copy-start.6 = (f32[96,192]{1,0:T(8,128)S(1)}, f32[96,192]{1,0:T(8,128)}, u32[]{:S(2)}) copy-start(f32[96,192]{1,0:T(8,128)} %get-tuple-element.139) | copy-start | bytes 221188
  372.7 12.9 %copy-start.3 = (f32[96,2,768]{2,1,0:T(2,128)S(1)}, f32[96,2,768]{2,1,0:T(2,128)}, u32[]{:S(2)}) copy-start(f32[96,2,768]{2,1,0:T(2,128)} %get-tuple-element.140) | copy-start | bytes 1769476
  372.7 13.7 %copy-start.4 = (f32[96,768]{1,0:T(8,128)S(1)}, f32[96,768]{1,0:T(8,128)}, u32[]{:S(2)}) copy-start(f32[96,768]{1,0:T(8,128)} %get-tuple-element.141) | copy-start | bytes 884740

commit v6 on v5

--- a/solution.py
+++ b/solution.py
@@ -1845,14 +1845,12 @@
     other(1).wait_send()
     other(2).start()
     send_home(1)
-    sums[0].advance(1)
-    sums[1].advance(1)
     other(2).wait_send()
     pass_on(0)
     across_res.start()
     send_home(2)
-    sums[0].advance(2)
-    sums[1].advance(2)
+    sums[0].advance(1)
+    sums[1].advance(1)
     sums[2].advance(1)
     pass_on(1)
     across_res.wait_recv()
@@ -1868,6 +1866,8 @@
             extra.arrival(spare_ref.at[0], k, (), ()).wait_recv()
         extra.across(k, (), ()).start()
         extra.beside(0, k, (), ()).start()
+    sums[0].advance(2)
+    sums[1].advance(2)
     sums[2].advance(2)
     pass_far(0)
     pass_far(1)

time: 388 us -> 383 us (0.987)
  Pallas kernels: 347 us -> 328 us
  waiting for transfers between devices: 10.6 us -> 25.7 us
    ppermute x4, waiting for transfers between devices: 6.2 us -> 20.6 us  [swap(): return lax.ppermute(array, 'tensor', [(i, i ^ step) for i in range(size)])]
    pallas_call x1, Pallas kernels: 57.8 us -> 48.4 us  [attend_back(): pl.pallas_call(functools.partial(attend_back_kernel, groups), grid_spec=p...]
    pallas_call x1, Pallas kernels: 32.8 us -> 27.2 us  [attend(): pl.pallas_call(functools.partial(attend_kernel, groups), grid_spec=pltpu....]
    pallas_call x1, Pallas kernels: 86.1 us -> 81.1 us  [settle(): pl.pallas_call(functools.partial(settle_kernel, groups, size), in_specs=[...]
  transfers between devices with their start and end apart: 7 -> 7, of which waited for: 2 -> 3; matrix products, arithmetic and copies ran while one was open for 0% -> 0% of each run, Pallas kernels for 39% -> 36%
where the time goes in v6:
time: 383 us; the launch traced here: 382 us
  Pallas kernels  328 us (86%)
  waiting for transfers between devices  25.7 us (7%)
  starting transfers between devices  17.5 us (5%)
  local copies, waits for them, and re-layouts  9.5 us (2%)
    pallas_call x1, Pallas kernels, settle(): pl.pallas_call(functools.partial(settle_kernel, groups, size), in_specs=[...  81.1 us
    pallas_call x1, Pallas kernels, middle(): pl.pallas_call(functools.partial(middle_kernel, size, groups, len(weights...  53.2 us
    pallas_call x1, Pallas kernels, attend_back(): pl.pallas_call(functools.partial(attend_back_kernel, groups), grid_spec=p...  48.4 us
    pallas_call x1, Pallas kernels, grads(): pl.pallas_call(functools.partial(grads_kernel, groups, size), grid=(size,...  44.6 us
    pallas_call x1, Pallas kernels, route(): pl.pallas_call(functools.partial(route_kernel, groups, size), in_specs=[a...  41.9 us
    pallas_call x1, Pallas kernels, attend(): pl.pallas_call(functools.partial(attend_kernel, groups), grid_spec=pltpu....  27.2 us
    ppermute x4, waiting for transfers between devices, swap(): return lax.ppermute(array, 'tensor', [(i, i ^ step) for i in range(size)])  20.6 us
    pallas_call x1, Pallas kernels, unpack(): pl.pallas_call(functools.partial(unpack_kernel, size), grid_spec=pltpu.Pr...  11.5 us
  transfers between devices with their start and end apart: 7, of which 3 were waited for; matrix products, arithmetic and copies ran while one was open for 0% of the time, Pallas kernels for 36%

profile of v6, /device:TPU:0, one launch (start us, length us, event | category | flops | bytes accessed | tf_op | source)
XLA Modules:
  0.0 382.2 jit_solution(8796868422463519151)
XLA Ops:
  0.6 1.1 constant_dynamic-slice_fusion.1
  1.8 3.0 collective-permute-start.1
  4.8 0.1 collective-permute-start
  4.8 0.6 pad_add_fusion.ids
  5.4 8.6 %pack.1 = (bf16[8,96,768]{2,1,0:T(8,128)(2,1)}, bf16[8,1,768]{2,1,0:T(2,128)(2,1)}, bf16[8,112,768]{2,1,0:T(8,128)(2,1)}, s32[16]{0:T(128)}, s32[4,17]{1,0:T(4,128)}, /*index=5*/f32[64]{0:T(128)}, s32[192]{0:T(256)}) custom-call(s32[16]{0:T(128)} %lengths.1, s32[16]{0:T(128)} %dealing.1, s32[2]{0:T(128)} %pad_add_fusion.ids, bf16[3072,768]{1,0:T(8,128)(2,1)} %bitcast.18, ...), custom_call_target="tpu_custom_call" | custom-call | bytes 20971520 | tf_op jit(solution)/shard_map/pack/pallas_call | solution.py:199
  14.0 0.0 copy-start.1
  14.0 41.9 %route.1 = (bf16[4,8,96,768]{3,2,1,0:T(8,128)(2,1)}, bf16[8,1,768]{2,1,0:T(2,128)(2,1)}) custom-call(bf16[8,96,768]{2,1,0:T(8,128)(2,1)} %get-tuple-element.67.send_ref, bf16[8,1,768]{2,1,0:T(2,128)(2,1)} %get-tuple-element.68.over_ref), custom_call_target="tpu_custom_call" | custom-call | bytes 62914560 | tf_op jit(solution)/shard_map/route/pallas_call | solution.py:1496
  56.0 0.0 collective-permute-done.refs_7_
  56.0 0.0 collective-permute-done.1.refs_11_
  56.0 0.0 copy-start.10
  56.0 5.5 %all-to-all-start = ((bf16[8,112,768]{2,1,0:T(8,128)(2,1)}), bf16[8,112,768]{2,1,0:T(8,128)(2,1)}, u32[]{:S(2)}, u32[]{:S(2)}) async-start(bf16[8,112,768]{2,1,0:T(8,128)(2,1)} %get-tuple-element.80), calls=%async_computation | async-start | bytes 2752512 | tf_op jit(solution)/shard_map/all_to_all | solution.py:2055
  61.5 0.0 copy-done.1
  61.5 0.0 copy-start.7
  61.5 0.0 copy-start.8
  61.5 0.4 copy.21
  62.0 0.0 copy-start.2
  62.0 0.6 collective-permute-start.2
  62.6 0.0 copy-done.10
  62.6 2.0 collective-permute-start.3
  64.6 0.0 copy-done.7
  64.6 0.0 copy-done.8
  64.6 0.6 pad_maximum_fusion.refs_4_
  65.2 11.0 %project.1 = (bf16[192,3072]{1,0:T(8,128)(2,1)}, bf16[192,3072]{1,0:T(8,128)(2,1)}, bf16[240,3072]{1,0:T(8,128)(2,1)}, bf16[3,3072,64]{2,1,0:T(8,128)(2,1)}, bf1...) custom-call(s32[16]{0:T(128)} %get-tuple-element.65.meta.info, ...), custom_call_target="tpu_custom_call" | custom-call | flops 2359296 | bytes 1048576 | tf_op jit(solution)/shard_map/project/pallas_call | solution.py:348
  76.2 0.0 copy-done.2
  76.2 27.2 %attend.1 = (bf16[12,192,256]{2,1,0:T(8,128)(2,1)}, f32[3,3072]{1,0:T(4,128)}) custom-call(s32[16]{0:T(128)} %get-tuple-element.65.meta.info, bf16[192,3072]{1,0:T(8,128)(2,1)} %get-tuple-element.74.q_ref, bf16[3,3072,64]{2,1,0:T(8,128)(2,1)} %get-tuple-element.75.k_ref.krow_ref, bf16[240,3072]{1,0:T(8,128)(2,1)} %get-tuple-element.76.v_ref), custom_call_target="tpu_custom_call" | custom-call | flops 3623878656 | bytes 8388608 | tf_op jit(solution)/shard_map/attend/pallas_call | solution.py:445
  103.4 0.0 collective-permute-done.3.refs_12_
  103.4 0.0 copy-start.11
  103.4 11.8 %collective-permute-done.2.refs_9_ = bf16[768,1536]{1,0:T(8,128)(2,1)S(1)} collective-permute-done((bf16[768,1536]{1,0:T(8,128)(2,1)S(1)}, bf16[768,1536]{1,0:T(8,128)(2,1)S(1)}, u32[]{:S(2)}, u32[]{:S(2)}) %collective-permute-start.2) | collective-permute-done | bytes 2359328 | tf_op jit(solution)/shard_map/ppermute | solution.py:1327
  115.3 0.0 copy-start.9
  115.3 0.0 all-to-all-done.refs_2_.refs_3_
  115.3 0.0 copy-done.11
  115.3 1.4 copy-done.9
  116.6 53.2 %middle.1 = (bf16[768,768]{1,0:T(8,128)(2,1)}, f32[768,768]{1,0:T(8,128)}, bf16[4,192,768]{2,1,0:T(8,128)(2,1)}, bf16[4,192,768]{2,1,0:T(8,128)(2,1)}, bf16[768,...) custom-call(bf16[768,768]{1,0:T(8,128)(2,1)} %get-tuple-element.73.r, ...), custom_call_target="tpu_custom_call" | custom-call | flops 23555211264 | bytes 41943040 | tf_op jit(solution)/shard_map/middle/pallas_call | solution.py:952
  169.8 44.6 %grads.1 = (bf16[768,1664]{1,0:T(8,128)(2,1)}, bf16[768,1664]{1,0:T(8,128)(2,1)}, bf16[8,2,96,896]{3,2,1,0:T(8,128)(2,1)}, bf16[4,192,768]{2,1,0:T(8,128)(2,1)},...) custom-call(f32[64]{0:T(128)} %get-tuple-element.64.match_ref.refs_1_, ...), custom_call_target="tpu_custom_call" | custom-call | flops 11777605632 | bytes 83886080 | tf_op jit(solution)/shard_map/grads/pallas_call | solution.py:1256
  214.4 5.8 %all-to-all-start.1 = ((bf16[8,2,96,896]{3,2,1,0:T(8,128)(2,1)}), bf16[8,2,96,896]{3,2,1,0:T(8,128)(2,1)S(1)}, u32[]{:S(2)}, u32[]{:S(2)}) async-start(bf16[8,2,96,896]{3,2,1,0:T(8,128)(2,1)} %get-tuple-element.106), calls=%async_computation.1 | async-start | bytes 5505024 | tf_op jit(solution)/shard_map/all_to_all | solution.py:2055
  220.2 0.5 collective-permute-start.4
  220.7 48.4 %attend_back.1.d_hbm = bf16[4,576,768]{2,1,0:T(8,128)(2,1)} custom-call(s32[16]{0:T(128)} %get-tuple-element.65.meta.info, bf16[192,3072]{1,0:T(8,128)(2,1)} %get-tuple-element.74.q_ref, bf16[3,3072,64]{2,1,0:T(8,128)(2,1)} %get-tuple-element.75.k_ref.krow_ref, bf16[192,3072]{1,0:T(8,128)(2,1)} %get-tuple-element.96.k_ref, ...), custom_call_target="tpu_custom_call" | custom-call | flops 36238786560 | bytes 16777216 | tf_op jit(solution)/shard_map/attend_back/pallas_call | solution.py:574
  269.1 8.8 %collective-permute-done.4.wide_other_hbm = bf16[768,1664]{1,0:T(8,128)(2,1)} collective-permute-done((bf16[768,1664]{1,0:T(8,128)(2,1)}, bf16[768,1664]{1,0:T(8,128)(2,1)}, u32[]{:S(2)}, u32[]{:S(2)}) %collective-permute-start.4) | collective-permute-done | bytes 2555936 | tf_op jit(solution)/shard_map/ppermute | solution.py:1327
  277.9 5.0 %all-to-all-done.1.down_hbm = bf16[8,2,96,896]{3,2,1,0:T(8,128)(2,1)S(1)} async-done(((bf16[8,2,96,896]{3,2,1,0:T(8,128)(2,1)}), bf16[8,2,96,896]{3,2,1,0:T(8,128)(2,1)S(1)}, u32[]{:S(2)}, u32[]{:S(2)}) %all-to-all-start.1) | async-done | bytes 2752544 | tf_op jit(solution)/shard_map/all_to_all | solution.py:2055
  282.9 0.0 copy-start
  282.9 1.5 copy-done
  284.5 81.1 %settle.1 = (bf16[4,8,3,32,768]{4,3,2,1,0:T(8,128)(2,1)}, bf16[4,8,1,768]{3,2,1,0:T(2,128)(2,1)}, bf16[3072,768]{1,0:T(8,128)(2,1)}, f32[3,96,192]{2,1,0:T(8,128...) custom-call(f32[64]{0:T(128)} %get-tuple-element.64.match_ref.refs_1_, ...), custom_call_target="tpu_custom_call" | custom-call | flops 5435817984 | bytes 157286400 | tf_op jit(solution)/shard_map/settle/pallas_call | solution.py:1957
  365.6 0.9 fusion
  366.5 0.6 copy.19
  367.1 0.6 copy.20
  367.7 0.0 copy-start.5
  367.7 0.0 copy-start.6
  367.7 0.0 copy-start.3
  367.7 0.0 copy-start.4
  367.7 11.5 %unpack.1 = (bf16[3072,768]{1,0:T(8,128)(2,1)}, bf16[3072,768]{1,0:T(8,128)(2,1)}) custom-call(s32[192]{0:T(256)} %get-tuple-element.63.spots_ref.spots, s32[1]{0:T(128)} %bitcast.1.me, bf16[4,8,6,16,768]{4,3,2,1,0:T(8,128)(2,1)} %bitcast.20, bf16[4,8,1,768]{3,2,1,0:T(2,128)(2,1)} %get-tuple-element.109.over_ref, bf16[3072,768]{1,0:T(8,128)(2,1)} %get-tuple-element.110.result_ref), custom_call_target="tpu_custom_call" | custom-call | bytes 31457280 | tf_op jit(solution)/shard_map/unpack/pallas_call | solution.py:1406
  379.3 0.0 copy-done.5
  379.3 0.7 copy.26
  380.0 0.0 copy-done.6
  380.0 0.6 copy.27
  380.6 0.0 copy-done.3
  380.6 0.8 copy.28
  381.4 0.0 copy-done.4
  381.4 0.7 copy.29
Async XLA Ops:
  1.8 54.2 %collective-permute-start.1 = (bf16[384,768]{1,0:T(8,128)(2,1)S(1)}, bf16[384,768]{1,0:T(8,128)(2,1)S(1)}, u32[]{:S(2)}, u32[]{:S(2)}) collective-permute-start(bf16[384,768]{1,0:T(8,128)(2,1)S(1)} %constant_dynamic-slice_fusion.1), channel_id=1, source_target_pairs={{0,2},{1,3},{2,0},{3,1},{4,6},{5,7},{6,4},{7,5},{8,10},{9,11},{10,... | collective-permute-start | bytes 1769480 | tf_op jit(solution)/shard_map/ppermute | solution.py:1327
  4.8 51.2 %collective-permute-start = (bf16[192,768]{1,0:T(8,128)(2,1)}, bf16[192,768]{1,0:T(8,128)(2,1)}, u32[]{:S(2)}, u32[]{:S(2)}) collective-permute-start(bf16[192,768]{1,0:T(8,128)(2,1)} %bitcast.32), channel_id=1, source_target_pairs={{0,2},{1,3},{2,0},{3,1},{4,6},{5,7},{6,4},{7,5},{8,10},{9,11},{10,... | collective-permute-start | bytes 884744 | tf_op jit(solution)/shard_map/ppermute | solution.py:1327
  14.0 47.5 %copy-start.1 = (bf16[768,2,768]{2,1,0:T(2,128)(2,1)S(1)}, bf16[768,2,768]{2,1,0:T(2,128)(2,1)}, u32[]{:S(2)}) copy-start(bf16[768,2,768]{2,1,0:T(2,128)(2,1)} %param.17) | copy-start | bytes 7077892
  56.0 6.6 %copy-start.10 = (bf16[384,768]{1,0:T(8,128)(2,1)}, bf16[384,768]{1,0:T(8,128)(2,1)S(1)}, u32[]{:S(2)}) copy-start(bf16[384,768]{1,0:T(8,128)(2,1)S(1)} %collective-permute-done.1.refs_11_) | copy-start | bytes 1769476
  56.0 59.3 %all-to-all-start = ((bf16[8,112,768]{2,1,0:T(8,128)(2,1)}), bf16[8,112,768]{2,1,0:T(8,128)(2,1)}, u32[]{:S(2)}, u32[]{:S(2)}) async-start(bf16[8,112,768]{2,1,0:T(8,128)(2,1)} %get-tuple-element.80), calls=%async_computation | async-start | bytes 2752512 | tf_op jit(solution)/shard_map/all_to_all | solution.py:2055
  61.5 3.1 copy-start.7
  61.5 3.1 copy-start.8
  62.0 14.3 %copy-start.2 = (bf16[96,8,2,768]{3,1,2,0:T(8,128)(2,1)}, bf16[96,8,2,768]{3,1,2,0:T(8,128)(2,1)S(1)}, u32[]{:S(2)}) copy-start(bf16[96,8,2,768]{3,1,2,0:T(8,128)(2,1)S(1)} %copy.21) | copy-start | bytes 7077892
  62.0 53.3 %collective-permute-start.2 = (bf16[768,1536]{1,0:T(8,128)(2,1)S(1)}, bf16[768,1536]{1,0:T(8,128)(2,1)S(1)}, u32[]{:S(2)}, u32[]{:S(2)}) collective-permute-start(bf16[768,1536]{1,0:T(8,128)(2,1)S(1)} %bitcast.25), channel_id=1, source_target_pairs={{0,2},{1,3},{2,0},{3,1},{4,6},{5,7},{6,4},{7,5},{8,10},{9,11},{10,... | collective-permute-start | bytes 7077896 | tf_op jit(solution)/shard_map/ppermute | solution.py:1327
  62.6 40.9 %collective-permute-start.3 = (bf16[384,768]{1,0:T(8,128)(2,1)S(1)}, bf16[384,768]{1,0:T(8,128)(2,1)S(1)}, u32[]{:S(2)}, u32[]{:S(2)}) collective-permute-start(bf16[384,768]{1,0:T(8,128)(2,1)S(1)} %collective-permute-done.1.refs_11_), channel_id=1, source_target_pairs={{0,4},{4,0},{8,12},{12,8},{16,20},{20,16},{24,28},{28,24},{1,5},{5... | collective-permute-start | bytes 1769480 | tf_op jit(solution)/shard_map/ppermute | solution.py:2083
  103.4 11.8 %copy-start.11 = (bf16[384,768]{1,0:T(8,128)(2,1)}, bf16[384,768]{1,0:T(8,128)(2,1)S(1)}, u32[]{:S(2)}) copy-start(bf16[384,768]{1,0:T(8,128)(2,1)S(1)} %collective-permute-done.3.refs_12_) | copy-start | bytes 1769476
  115.3 1.4 copy-start.9
  214.4 68.6 %all-to-all-start.1 = ((bf16[8,2,96,896]{3,2,1,0:T(8,128)(2,1)}), bf16[8,2,96,896]{3,2,1,0:T(8,128)(2,1)S(1)}, u32[]{:S(2)}, u32[]{:S(2)}) async-start(bf16[8,2,96,896]{3,2,1,0:T(8,128)(2,1)} %get-tuple-element.106), calls=%async_computation.1 | async-start | bytes 5505024 | tf_op jit(solution)/shard_map/all_to_all | solution.py:2055
  220.2 57.7 %collective-permute-start.4 = (bf16[768,1664]{1,0:T(8,128)(2,1)}, bf16[768,1664]{1,0:T(8,128)(2,1)}, u32[]{:S(2)}, u32[]{:S(2)}) collective-permute-start(bf16[768,1664]{1,0:T(8,128)(2,1)} %get-tuple-element.105), channel_id=1, source_target_pairs={{0,2},{1,3},{2,0},{3,1},{4,6},{5,7},{6,4},{7,5},{8,10},{9,11},{10,... | collective-permute-start | bytes 7667720 | tf_op jit(solution)/shard_map/ppermute | solution.py:1327
  282.9 1.5 copy-start
  367.7 11.5 %copy-start.5 = (f32[3,96,192]{2,1,0:T(8,128)S(1)}, f32[3,96,192]{2,1,0:T(8,128)}, u32[]{:S(2)}) copy-start(f32[3,96,192]{2,1,0:T(8,128)} %get-tuple-element.113) | copy-start | bytes 663556
  367.7 12.2 %copy-start.6 = (f32[96,192]{1,0:T(8,128)S(1)}, f32[96,192]{1,0:T(8,128)}, u32[]{:S(2)}) copy-start(f32[96,192]{1,0:T(8,128)} %get-tuple-element.139) | copy-start | bytes 221188
  367.7 12.9 %copy-start.3 = (f32[96,2,768]{2,1,0:T(2,128)S(1)}, f32[96,2,768]{2,1,0:T(2,128)}, u32[]{:S(2)}) copy-start(f32[96,2,768]{2,1,0:T(2,128)} %get-tuple-element.140) | copy-start | bytes 1769476
  367.7 13.7 %copy-start.4 = (f32[96,768]{1,0:T(8,128)S(1)}, f32[96,768]{1,0:T(8,128)}, u32[]{:S(2)}) copy-start(f32[96,768]{1,0:T(8,128)} %get-tuple-element.141) | copy-start | bytes 884740

commit v7 on v6

--- a/solution.py
+++ b/solution.py
@@ -860,7 +860,7 @@
     normed_t_ref[...] = normed_one.T.astype(BF)
     sum_ref[...] = normed_one
 
-    @pl.loop(0, size)
+    @pl.loop(0, size, unroll=2)
     def _(i):
         r = lax.rem(i, 2) * 2 + lax.div(i, 2)
         for k in ids:
@@ -902,7 +902,7 @@
     d_branch_t_ref[...] = grad_two.T.astype(BF)
     sum_ref[...] = grad_two
 
-    @pl.loop(0, size)
+    @pl.loop(0, size, unroll=2)
     def _(r):
         grad_hidden = mm(normed_ref[...], w_down_ref[r], 1, 0)
         d_gate = (grad_hidden * slope_ref[r]).astype(BF)

time: 383 us -> 380 us (level)
  no operation moved by 1% of the time
where the time goes in v7:
time: 380 us
  Pallas kernels  325 us (86%)
  waiting for transfers between devices  25.7 us (7%)
  starting transfers between devices  17.4 us (5%)
  local copies, waits for them, and re-layouts  9.5 us (2%)
    pallas_call x1, Pallas kernels, settle(): pl.pallas_call(functools.partial(settle_kernel, groups, size), in_specs=[...  81.1 us
    pallas_call x1, Pallas kernels, middle(): pl.pallas_call(functools.partial(middle_kernel, size, groups, len(weights...  50.6 us
    pallas_call x1, Pallas kernels, attend_back(): pl.pallas_call(functools.partial(attend_back_kernel, groups), grid_spec=p...  48.4 us
    pallas_call x1, Pallas kernels, grads(): pl.pallas_call(functools.partial(grads_kernel, groups, size), grid=(size,...  44.6 us
    pallas_call x1, Pallas kernels, route(): pl.pallas_call(functools.partial(route_kernel, groups, size), in_specs=[a...  42 us
    pallas_call x1, Pallas kernels, attend(): pl.pallas_call(functools.partial(attend_kernel, groups), grid_spec=pltpu....  27.2 us
    ppermute x4, waiting for transfers between devices, swap(): return lax.ppermute(array, 'tensor', [(i, i ^ step) for i in range(size)])  20.6 us
    pallas_call x1, Pallas kernels, unpack(): pl.pallas_call(functools.partial(unpack_kernel, size), grid_spec=pltpu.Pr...  11.5 us
  transfers between devices with their start and end apart: 7, of which 3 were waited for; matrix products, arithmetic and copies ran while one was open for 0% of the time, Pallas kernels for 36%

profile of v7, /device:TPU:0, one launch (start us, length us, event | category | flops | bytes accessed | tf_op | source)
XLA Modules:
  0.0 379.6 jit_solution(11484458004431784336)
XLA Ops:
  0.6 1.1 constant_dynamic-slice_fusion.1
  1.8 3.0 collective-permute-start.1
  4.8 0.1 collective-permute-start
  4.8 0.6 pad_add_fusion.ids
  5.4 8.5 %pack.1 = (bf16[8,96,768]{2,1,0:T(8,128)(2,1)}, bf16[8,1,768]{2,1,0:T(2,128)(2,1)}, bf16[8,112,768]{2,1,0:T(8,128)(2,1)}, s32[16]{0:T(128)}, s32[4,17]{1,0:T(4,128)}, /*index=5*/f32[64]{0:T(128)}, s32[192]{0:T(256)}) custom-call(s32[16]{0:T(128)} %lengths.1, s32[16]{0:T(128)} %dealing.1, s32[2]{0:T(128)} %pad_add_fusion.ids, bf16[3072,768]{1,0:T(8,128)(2,1)} %bitcast.18, ...), custom_call_target="tpu_custom_call" | custom-call | bytes 20971520 | tf_op jit(solution)/shard_map/pack/pallas_call | solution.py:199
  14.0 0.0 copy-start.1
  14.0 42.0 %route.1 = (bf16[4,8,96,768]{3,2,1,0:T(8,128)(2,1)}, bf16[8,1,768]{2,1,0:T(2,128)(2,1)}) custom-call(bf16[8,96,768]{2,1,0:T(8,128)(2,1)} %get-tuple-element.67.send_ref, bf16[8,1,768]{2,1,0:T(2,128)(2,1)} %get-tuple-element.68.over_ref), custom_call_target="tpu_custom_call" | custom-call | bytes 62914560 | tf_op jit(solution)/shard_map/route/pallas_call | solution.py:1496
  56.0 0.0 collective-permute-done.refs_7_
  56.0 0.0 collective-permute-done.1.refs_11_
  56.0 0.0 copy-start.10
  56.0 5.5 %all-to-all-start = ((bf16[8,112,768]{2,1,0:T(8,128)(2,1)}), bf16[8,112,768]{2,1,0:T(8,128)(2,1)}, u32[]{:S(2)}, u32[]{:S(2)}) async-start(bf16[8,112,768]{2,1,0:T(8,128)(2,1)} %get-tuple-element.80), calls=%async_computation | async-start | bytes 2752512 | tf_op jit(solution)/shard_map/all_to_all | solution.py:2055
  61.5 0.0 copy-done.1
  61.5 0.0 copy-start.7
  61.5 0.0 copy-start.8
  61.5 0.4 copy.21
  61.9 0.0 copy-start.2
  62.0 0.6 collective-permute-start.2
  62.5 0.0 copy-done.10
  62.5 2.0 collective-permute-start.3
  64.6 0.0 copy-done.7
  64.6 0.0 copy-done.8
  64.6 0.6 pad_maximum_fusion.refs_4_
  65.2 11.0 %project.1 = (bf16[192,3072]{1,0:T(8,128)(2,1)}, bf16[192,3072]{1,0:T(8,128)(2,1)}, bf16[240,3072]{1,0:T(8,128)(2,1)}, bf16[3,3072,64]{2,1,0:T(8,128)(2,1)}, bf1...) custom-call(s32[16]{0:T(128)} %get-tuple-element.65.meta.info, ...), custom_call_target="tpu_custom_call" | custom-call | flops 2359296 | bytes 1048576 | tf_op jit(solution)/shard_map/project/pallas_call | solution.py:348
  76.2 0.0 copy-done.2
  76.2 27.2 %attend.1 = (bf16[12,192,256]{2,1,0:T(8,128)(2,1)}, f32[3,3072]{1,0:T(4,128)}) custom-call(s32[16]{0:T(128)} %get-tuple-element.65.meta.info, bf16[192,3072]{1,0:T(8,128)(2,1)} %get-tuple-element.74.q_ref, bf16[3,3072,64]{2,1,0:T(8,128)(2,1)} %get-tuple-element.75.k_ref.krow_ref, bf16[240,3072]{1,0:T(8,128)(2,1)} %get-tuple-element.76.v_ref), custom_call_target="tpu_custom_call" | custom-call | flops 3623878656 | bytes 8388608 | tf_op jit(solution)/shard_map/attend/pallas_call | solution.py:445
  103.4 0.0 collective-permute-done.3.refs_12_
  103.4 0.0 copy-start.11
  103.4 11.8 %collective-permute-done.2.refs_9_ = bf16[768,1536]{1,0:T(8,128)(2,1)S(1)} collective-permute-done((bf16[768,1536]{1,0:T(8,128)(2,1)S(1)}, bf16[768,1536]{1,0:T(8,128)(2,1)S(1)}, u32[]{:S(2)}, u32[]{:S(2)}) %collective-permute-start.2) | collective-permute-done | bytes 2359328 | tf_op jit(solution)/shard_map/ppermute | solution.py:1327
  115.2 0.0 copy-start.9
  115.2 0.0 all-to-all-done.refs_2_.refs_3_
  115.3 0.0 copy-done.11
  115.3 1.4 copy-done.9
  116.6 50.6 %middle.1 = (bf16[768,768]{1,0:T(8,128)(2,1)}, f32[768,768]{1,0:T(8,128)}, bf16[4,192,768]{2,1,0:T(8,128)(2,1)}, bf16[4,192,768]{2,1,0:T(8,128)(2,1)}, bf16[768,...) custom-call(bf16[768,768]{1,0:T(8,128)(2,1)} %get-tuple-element.73.r, ...), custom_call_target="tpu_custom_call" | custom-call | flops 23555211264 | bytes 41943040 | tf_op jit(solution)/shard_map/middle/pallas_call | solution.py:952
  167.2 44.6 %grads.1 = (bf16[768,1664]{1,0:T(8,128)(2,1)}, bf16[768,1664]{1,0:T(8,128)(2,1)}, bf16[8,2,96,896]{3,2,1,0:T(8,128)(2,1)}, bf16[4,192,768]{2,1,0:T(8,128)(2,1)},...) custom-call(f32[64]{0:T(128)} %get-tuple-element.64.match_ref.refs_1_, ...), custom_call_target="tpu_custom_call" | custom-call | flops 11777605632 | bytes 83886080 | tf_op jit(solution)/shard_map/grads/pallas_call | solution.py:1256
  211.9 5.8 %all-to-all-start.1 = ((bf16[8,2,96,896]{3,2,1,0:T(8,128)(2,1)}), bf16[8,2,96,896]{3,2,1,0:T(8,128)(2,1)S(1)}, u32[]{:S(2)}, u32[]{:S(2)}) async-start(bf16[8,2,96,896]{3,2,1,0:T(8,128)(2,1)} %get-tuple-element.106), calls=%async_computation.1 | async-start | bytes 5505024 | tf_op jit(solution)/shard_map/all_to_all | solution.py:2055
  217.6 0.5 collective-permute-start.4
  218.2 48.4 %attend_back.1.d_hbm = bf16[4,576,768]{2,1,0:T(8,128)(2,1)} custom-call(s32[16]{0:T(128)} %get-tuple-element.65.meta.info, bf16[192,3072]{1,0:T(8,128)(2,1)} %get-tuple-element.74.q_ref, bf16[3,3072,64]{2,1,0:T(8,128)(2,1)} %get-tuple-element.75.k_ref.krow_ref, bf16[192,3072]{1,0:T(8,128)(2,1)} %get-tuple-element.96.k_ref, ...), custom_call_target="tpu_custom_call" | custom-call | flops 36238786560 | bytes 16777216 | tf_op jit(solution)/shard_map/attend_back/pallas_call | solution.py:574
  266.6 8.8 %collective-permute-done.4.wide_other_hbm = bf16[768,1664]{1,0:T(8,128)(2,1)} collective-permute-done((bf16[768,1664]{1,0:T(8,128)(2,1)}, bf16[768,1664]{1,0:T(8,128)(2,1)}, u32[]{:S(2)}, u32[]{:S(2)}) %collective-permute-start.4) | collective-permute-done | bytes 2555936 | tf_op jit(solution)/shard_map/ppermute | solution.py:1327
  275.4 5.0 %all-to-all-done.1.down_hbm = bf16[8,2,96,896]{3,2,1,0:T(8,128)(2,1)S(1)} async-done(((bf16[8,2,96,896]{3,2,1,0:T(8,128)(2,1)}), bf16[8,2,96,896]{3,2,1,0:T(8,128)(2,1)S(1)}, u32[]{:S(2)}, u32[]{:S(2)}) %all-to-all-start.1) | async-done | bytes 2752544 | tf_op jit(solution)/shard_map/all_to_all | solution.py:2055
  280.4 0.0 copy-start
  280.4 1.5 copy-done
  281.9 81.1 %settle.1 = (bf16[4,8,3,32,768]{4,3,2,1,0:T(8,128)(2,1)}, bf16[4,8,1,768]{3,2,1,0:T(2,128)(2,1)}, bf16[3072,768]{1,0:T(8,128)(2,1)}, f32[3,96,192]{2,1,0:T(8,128...) custom-call(f32[64]{0:T(128)} %get-tuple-element.64.match_ref.refs_1_, ...), custom_call_target="tpu_custom_call" | custom-call | flops 5435817984 | bytes 157286400 | tf_op jit(solution)/shard_map/settle/pallas_call | solution.py:1957
  363.1 0.9 fusion
  363.9 0.6 copy.19
  364.6 0.6 copy.20
  365.2 0.0 copy-start.5
  365.2 0.0 copy-start.6
  365.2 0.0 copy-start.3
  365.2 0.0 copy-start.4
  365.2 11.5 %unpack.1 = (bf16[3072,768]{1,0:T(8,128)(2,1)}, bf16[3072,768]{1,0:T(8,128)(2,1)}) custom-call(s32[192]{0:T(256)} %get-tuple-element.63.spots_ref.spots, s32[1]{0:T(128)} %bitcast.1.me, bf16[4,8,6,16,768]{4,3,2,1,0:T(8,128)(2,1)} %bitcast.20, bf16[4,8,1,768]{3,2,1,0:T(2,128)(2,1)} %get-tuple-element.109.over_ref, bf16[3072,768]{1,0:T(8,128)(2,1)} %get-tuple-element.110.result_ref), custom_call_target="tpu_custom_call" | custom-call | bytes 31457280 | tf_op jit(solution)/shard_map/unpack/pallas_call | solution.py:1406
  376.7 0.0 copy-done.5
  376.7 0.7 copy.26
  377.5 0.0 copy-done.6
  377.5 0.6 copy.27
  378.1 0.0 copy-done.3
  378.1 0.8 copy.28
  378.9 0.0 copy-done.4
  378.9 0.7 copy.29
Async XLA Ops:
  1.8 54.2 %collective-permute-start.1 = (bf16[384,768]{1,0:T(8,128)(2,1)S(1)}, bf16[384,768]{1,0:T(8,128)(2,1)S(1)}, u32[]{:S(2)}, u32[]{:S(2)}) collective-permute-start(bf16[384,768]{1,0:T(8,128)(2,1)S(1)} %constant_dynamic-slice_fusion.1), channel_id=1, source_target_pairs={{0,2},{1,3},{2,0},{3,1},{4,6},{5,7},{6,4},{7,5},{8,10},{9,11},{10,... | collective-permute-start | bytes 1769480 | tf_op jit(solution)/shard_map/ppermute | solution.py:1327
  4.8 51.2 %collective-permute-start = (bf16[192,768]{1,0:T(8,128)(2,1)}, bf16[192,768]{1,0:T(8,128)(2,1)}, u32[]{:S(2)}, u32[]{:S(2)}) collective-permute-start(bf16[192,768]{1,0:T(8,128)(2,1)} %bitcast.32), channel_id=1, source_target_pairs={{0,2},{1,3},{2,0},{3,1},{4,6},{5,7},{6,4},{7,5},{8,10},{9,11},{10,... | collective-permute-start | bytes 884744 | tf_op jit(solution)/shard_map/ppermute | solution.py:1327
  14.0 47.5 %copy-start.1 = (bf16[768,2,768]{2,1,0:T(2,128)(2,1)S(1)}, bf16[768,2,768]{2,1,0:T(2,128)(2,1)}, u32[]{:S(2)}) copy-start(bf16[768,2,768]{2,1,0:T(2,128)(2,1)} %param.17) | copy-start | bytes 7077892
  56.0 6.5 %copy-start.10 = (bf16[384,768]{1,0:T(8,128)(2,1)}, bf16[384,768]{1,0:T(8,128)(2,1)S(1)}, u32[]{:S(2)}) copy-start(bf16[384,768]{1,0:T(8,128)(2,1)S(1)} %collective-permute-done.1.refs_11_) | copy-start | bytes 1769476
  56.0 59.2 %all-to-all-start = ((bf16[8,112,768]{2,1,0:T(8,128)(2,1)}), bf16[8,112,768]{2,1,0:T(8,128)(2,1)}, u32[]{:S(2)}, u32[]{:S(2)}) async-start(bf16[8,112,768]{2,1,0:T(8,128)(2,1)} %get-tuple-element.80), calls=%async_computation | async-start | bytes 2752512 | tf_op jit(solution)/shard_map/all_to_all | solution.py:2055
  61.5 3.1 copy-start.7
  61.5 3.1 copy-start.8
  61.9 14.3 %copy-start.2 = (bf16[96,8,2,768]{3,1,2,0:T(8,128)(2,1)}, bf16[96,8,2,768]{3,1,2,0:T(8,128)(2,1)S(1)}, u32[]{:S(2)}) copy-start(bf16[96,8,2,768]{3,1,2,0:T(8,128)(2,1)S(1)} %copy.21) | copy-start | bytes 7077892
  62.0 53.3 %collective-permute-start.2 = (bf16[768,1536]{1,0:T(8,128)(2,1)S(1)}, bf16[768,1536]{1,0:T(8,128)(2,1)S(1)}, u32[]{:S(2)}, u32[]{:S(2)}) collective-permute-start(bf16[768,1536]{1,0:T(8,128)(2,1)S(1)} %bitcast.25), channel_id=1, source_target_pairs={{0,2},{1,3},{2,0},{3,1},{4,6},{5,7},{6,4},{7,5},{8,10},{9,11},{10,... | collective-permute-start | bytes 7077896 | tf_op jit(solution)/shard_map/ppermute | solution.py:1327
  62.5 40.9 %collective-permute-start.3 = (bf16[384,768]{1,0:T(8,128)(2,1)S(1)}, bf16[384,768]{1,0:T(8,128)(2,1)S(1)}, u32[]{:S(2)}, u32[]{:S(2)}) collective-permute-start(bf16[384,768]{1,0:T(8,128)(2,1)S(1)} %collective-permute-done.1.refs_11_), channel_id=1, source_target_pairs={{0,4},{4,0},{8,12},{12,8},{16,20},{20,16},{24,28},{28,24},{1,5},{5... | collective-permute-start | bytes 1769480 | tf_op jit(solution)/shard_map/ppermute | solution.py:2083
  103.4 11.8 %copy-start.11 = (bf16[384,768]{1,0:T(8,128)(2,1)}, bf16[384,768]{1,0:T(8,128)(2,1)S(1)}, u32[]{:S(2)}) copy-start(bf16[384,768]{1,0:T(8,128)(2,1)S(1)} %collective-permute-done.3.refs_12_) | copy-start | bytes 1769476
  115.2 1.4 copy-start.9
  211.9 68.6 %all-to-all-start.1 = ((bf16[8,2,96,896]{3,2,1,0:T(8,128)(2,1)}), bf16[8,2,96,896]{3,2,1,0:T(8,128)(2,1)S(1)}, u32[]{:S(2)}, u32[]{:S(2)}) async-start(bf16[8,2,96,896]{3,2,1,0:T(8,128)(2,1)} %get-tuple-element.106), calls=%async_computation.1 | async-start | bytes 5505024 | tf_op jit(solution)/shard_map/all_to_all | solution.py:2055
  217.6 57.7 %collective-permute-start.4 = (bf16[768,1664]{1,0:T(8,128)(2,1)}, bf16[768,1664]{1,0:T(8,128)(2,1)}, u32[]{:S(2)}, u32[]{:S(2)}) collective-permute-start(bf16[768,1664]{1,0:T(8,128)(2,1)} %get-tuple-element.105), channel_id=1, source_target_pairs={{0,2},{1,3},{2,0},{3,1},{4,6},{5,7},{6,4},{7,5},{8,10},{9,11},{10,... | collective-permute-start | bytes 7667720 | tf_op jit(solution)/shard_map/ppermute | solution.py:1327
  280.4 1.5 copy-start
  365.2 11.5 %copy-start.5 = (f32[3,96,192]{2,1,0:T(8,128)S(1)}, f32[3,96,192]{2,1,0:T(8,128)}, u32[]{:S(2)}) copy-start(f32[3,96,192]{2,1,0:T(8,128)} %get-tuple-element.113) | copy-start | bytes 663556
  365.2 12.2 %copy-start.6 = (f32[96,192]{1,0:T(8,128)S(1)}, f32[96,192]{1,0:T(8,128)}, u32[]{:S(2)}) copy-start(f32[96,192]{1,0:T(8,128)} %get-tuple-element.139) | copy-start | bytes 221188
  365.2 12.9 %copy-start.3 = (f32[96,2,768]{2,1,0:T(2,128)S(1)}, f32[96,2,768]{2,1,0:T(2,128)}, u32[]{:S(2)}) copy-start(f32[96,2,768]{2,1,0:T(2,128)} %get-tuple-element.140) | copy-start | bytes 1769476
  365.2 13.7 %copy-start.4 = (f32[96,768]{1,0:T(8,128)S(1)}, f32[96,768]{1,0:T(8,128)}, u32[]{:S(2)}) copy-start(f32[96,768]{1,0:T(8,128)} %get-tuple-element.141) | copy-start | bytes 884740
